TPU v7x, 32 devices: a whole 2x2x4 slice. The times are simulated.
32 devices in a mesh: req: 8 (over y, x, core), exp: 4 (over z).
Axes of the slice: x: 2, y: 2, z: 4, core: 2. Of those that a mesh axis runs over, the one named last changes fastest.
Arguments:
- attention_out: bfloat16 [1024, 4096], P('req'), may hold values from -6 to 6
- residual: bfloat16 [1024, 4096], P('req', 'exp'), may hold values from -6 to 6
- w_out: bfloat16 [4096, 4096], P('req', 'exp'), may hold values from -0.09375 to 0.09375
- router_w: float32 [4096, 4], P('exp'), may hold values from -0.09375 to 0.09375
- norm_gain: float32 [4096], P('exp'), may hold values from 0.5 to 1.5
- page_pool: bfloat16 [2048, 8, 2048], P('req', None, 'exp'), may hold values from -6 to 6
- page_table: int32 [1024, 2], P('req'), may hold values from 0 to 255, as said below
- cache_len: int32 [1024], P('req'), may hold values from 1 to 16
- came_from: int32 [1024], replicated, may hold values from 0 to 1023, as said below
- routes: int32 [1024, 2], P('req'), may hold values from 0 to 3, all different within a row; in each aligned block of 128 rows (0 to 127, 128 to 255, ...) at most 64 rows name the same one
- w_gate: bfloat16 [8, 4096, 7168], P('req', None, 'exp'), as said below
- w_up: bfloat16 [8, 4096, 7168], P('req', None, 'exp'), as said below
- w_down: bfloat16 [8, 7168, 4096], P('req', 'exp'), as said below
Outputs:
- mixed: float32 [1024, 4096], P('req', 'exp')
- new_pages: bfloat16 [1024, 2, 8, 2048], P('req', None, None, 'exp')
Inputs may be any that keep to these rules, and one draw needn't show every extreme that they name: page_table's entries for the requests of one req group are distinct. came_from is a permutation; from each req group 4 rows go to each of the other 7 groups, each group receives 4 rows from each of them, and all other rows keep their place. `routes`: within the rows of one req group every expert is named by at most 64 rows, and some expert by exactly 64 rows in some group. `w_gate`: slices e and e + 4 along the first dimension are equal. `w_up`: slices e and e + 4 along the first dimension are equal. `w_down`: slices e and e + 4 along the first dimension are equal.
All inputs are finite; a program needn't handle non-finite values.
Results may differ from a plain program's by a relative error of at most 0.0055.
Values may be sent and summed in bfloat16 or wider, within the bound.
No kernel may reach another device: no remote copies, remote signals or barrier semaphores. Data moves between devices by JAX's collectives and lax.ppermute only.
A program may use at most 128 MiB of HBM per device.

v0:
```python
import jax
import jax.numpy as jnp
from jax import lax
from jax.sharding import PartitionSpec as P

D = 4096
CAP = 32
MIG_PAIR = 4


EPSILON = 1e-05


def pick_rows(source, row_index, live_slot):
    taken_rows = jnp.take(source, row_index, axis=0)
    return jnp.where(live_slot[:, None], taken_rows, jnp.zeros((), source.dtype))


def body(
    attention_out,
    residual,
    w_out,
    router_w,
    norm_gain,
    page_pool,
    page_table,
    cache_len,
    came_from,
    routes,
    w_gate,
    w_up,
    w_down,
):
    groups = lax.axis_size("req")
    own_group = lax.axis_index("req")
    row_req = attention_out.shape[0]
    rows_all = came_from.shape[0]
    pages_req = page_table.shape[1]
    page_len = page_pool.shape[1]
    kv_slice = page_pool.shape[2]
    experts = groups // 2
    targets = jnp.arange(groups, dtype=jnp.int32)
    local_ids = jnp.arange(row_req, dtype=jnp.int32)
    dest_of = (
        jnp.zeros((rows_all,), jnp.int32).at[came_from].set(jnp.arange(rows_all, dtype=jnp.int32))
    )
    dest_group = dest_of // row_req
    dest_hot = (
        (dest_group[:, None] == targets[None, :]).astype(jnp.int32).reshape(groups, row_req, groups)
    )
    pair_rank = jnp.sum((jnp.cumsum(dest_hot, axis=1) - dest_hot) * dest_hot, axis=2).reshape(
        rows_all
    )
    own_dest = lax.dynamic_slice_in_dim(dest_group, own_group * row_req, row_req)
    own_rank = lax.dynamic_slice_in_dim(pair_rank, own_group * row_req, row_req)
    chosen_send = (
        (own_dest[None, None, :] == targets[:, None, None])
        & (own_rank[None, None, :] == jnp.arange(MIG_PAIR, dtype=jnp.int32)[None, :, None])
        & (targets[:, None, None] != own_group)
    )
    send_index = jnp.sum(jnp.where(chosen_send, local_ids[None, None, :], 0), axis=2).reshape(-1)
    send_live = jnp.any(chosen_send, axis=2).reshape(-1)
    page_rows = jnp.take(page_pool, page_table.reshape(-1), axis=0).reshape(
        row_req, pages_req, page_len, kv_slice
    )
    position = (
        jnp.arange(pages_req, dtype=jnp.int32)[:, None] * page_len
        + jnp.arange(page_len, dtype=jnp.int32)[None, :]
    )
    kept_mask = position[None, :, :] < cache_len[:, None, None]
    page_rows = jnp.where(kept_mask[..., None], page_rows, jnp.zeros((), page_rows.dtype)).reshape(
        row_req, -1
    )
    moved_attn, moved_resid, moved_pages = (
        lax.all_to_all(
            pick_rows(attention_out, send_index, send_live),
            "req",
            split_axis=0,
            concat_axis=0,
            tiled=True,
        ),
        lax.all_to_all(
            pick_rows(residual, send_index, send_live),
            "req",
            split_axis=0,
            concat_axis=0,
            tiled=True,
        ),
        lax.all_to_all(
            pick_rows(page_rows, send_index, send_live),
            "req",
            split_axis=0,
            concat_axis=0,
            tiled=True,
        ),
    )
    new_source = lax.dynamic_slice_in_dim(came_from, own_group * row_req, row_req)
    source_group = new_source // row_req
    stays_home = source_group == own_group
    arrival = jnp.where(
        stays_home,
        new_source - own_group * row_req,
        row_req + source_group * MIG_PAIR + jnp.take(pair_rank, new_source),
    )
    attn_new = jnp.take(jnp.concatenate([attention_out, moved_attn], axis=0), arrival, axis=0)
    resid_new = jnp.take(jnp.concatenate([residual, moved_resid], axis=0), arrival, axis=0)
    new_pages = jnp.take(
        jnp.concatenate([page_rows, moved_pages], axis=0), arrival, axis=0
    ).reshape(row_req, pages_req, page_len, kv_slice)
    projected = jnp.dot(
        attn_new,
        lax.all_gather(w_out, "req", axis=0, tiled=True),
        preferred_element_type=jnp.float32,
    )
    hidden = resid_new.astype(jnp.float32) + projected
    squares = jnp.sum(hidden * hidden, axis=1)
    scaled = hidden * norm_gain[None, :]
    total_sq = lax.psum(squares, "exp")
    inverse = lax.rsqrt(total_sq / D + EPSILON)
    normed = scaled * inverse[:, None]
    logits = lax.psum(jnp.dot(normed, router_w, precision=lax.Precision.HIGHEST), "exp")
    normed_rows = normed.astype(jnp.bfloat16)
    expert_ids = jnp.arange(experts, dtype=jnp.int32)
    chosen = jnp.sum(
        jnp.where(routes[:, :, None] == expert_ids[None, None, :], logits[:, None, :], 0.0), axis=2
    )
    gate_first = jax.nn.sigmoid(chosen[:, 0] - chosen[:, 1])
    gate_second = jax.nn.sigmoid(chosen[:, 1] - chosen[:, 0])
    flat_routes = routes.reshape(-1)
    expert_hot = (flat_routes[:, None] == expert_ids[None, :]).astype(jnp.int32)
    expert_rank = jnp.sum((jnp.cumsum(expert_hot, axis=0) - expert_hot) * expert_hot, axis=1)
    target_dev = flat_routes + experts * (expert_rank % 2)
    slot_index = expert_rank // 2
    assign_ids = jnp.arange(flat_routes.shape[0], dtype=jnp.int32)
    chosen_slot = (target_dev[None, None, :] == targets[:, None, None]) & (
        slot_index[None, None, :] == jnp.arange(CAP, dtype=jnp.int32)[None, :, None]
    )
    slot_source = jnp.sum(
        jnp.where(chosen_slot, assign_ids[None, None, :] // 2, 0), axis=2
    ).reshape(-1)
    slot_live = jnp.any(chosen_slot, axis=2).reshape(-1)
    outgoing = pick_rows(normed_rows, slot_source, slot_live)
    arrived = lax.all_to_all(outgoing, "req", split_axis=0, concat_axis=0, tiled=True)
    rows_full = lax.all_gather(arrived, "exp", axis=1, tiled=True)
    gate_h = jnp.dot(rows_full, w_gate[0], preferred_element_type=jnp.float32)
    up_h = jnp.dot(rows_full, w_up[0], preferred_element_type=jnp.float32)
    active = (jax.nn.silu(gate_h) * up_h).astype(jnp.bfloat16)
    partial_value = lax.optimization_barrier(
        jnp.dot(active, w_down[0], preferred_element_type=jnp.float32).astype(jnp.bfloat16)
    )
    lookup = target_dev * CAP + slot_index
    returned = lax.all_to_all(partial_value, "req", split_axis=0, concat_axis=0, tiled=True)
    taken_rows = jnp.take(returned, lookup, axis=0).reshape(row_req, 2, -1)
    weighted = gate_first[:, None] * taken_rows[:, 0].astype(jnp.float32) + gate_second[
        :, None
    ] * taken_rows[:, 1].astype(jnp.float32)
    expert_part = lax.psum_scatter(
        weighted.astype(jnp.bfloat16), "exp", scatter_dimension=1, tiled=True
    ).astype(jnp.float32)
    mixed = hidden + expert_part
    return (mixed, new_pages)


def solution(mesh):
    in_specs = (
        P("req", None),
        P("req", "exp"),
        P("req", "exp"),
        P("exp", None),
        P("exp"),
        P("req", None, "exp"),
        P("req", None),
        P("req"),
        P(),
        P("req", None),
        P("req", None, "exp"),
        P("req", None, "exp"),
        P("req", "exp", None),
    )
    out_specs = (P("req", "exp"), P("req", None, None, "exp"))
    return jax.shard_map(body, mesh=mesh, in_specs=in_specs, out_specs=out_specs, check_vma=False)
```

profile of v0, /device:TPU:0, one launch (start us, length us, event | category | flops | bytes accessed | tf_op | source)
XLA Modules:
  0.0 242.4 jit_solution(17611403964226083101)
XLA Ops:
  7.2 0.7 all-gather.3.cloned.1.call-update
  7.9 0.7 compare_select_fusion.1
  8.6 4.3 %scatter_custom_fusion = s32[1024]{0:T(1024)S(1)} fusion(s32[1024]{0:T(1024)S(1)} %compare_select_fusion.1, s32[1024]{0:T(1024)S(1)} %iota.72, s32[]{:T(128)} %constant.210.clone.1), kind=kCustom, calls=%fused_computation.105 | custom fusion | bytes 4100 | tf_op jit(solution)/shard_map/scatter | solution.py:45
  13.1 2.5 %select_reduce_fusion = s32[8,128]{0,1:T(8,128)S(1)} fusion(s32[8,128]{0,1:T(8,128)S(1)} %copy.127), kind=kOutput, calls=%fused_computation.43 | output fusion | flops 1096704 | bytes 8192 | tf_op jit(solution)/shard_map/jit(cumsum)/reduce_window_sum | solution.py:51
  15.8 0.2 select_reduce_fusion.1
  16.3 0.2 fusion.30
  16.7 1.7 gather_fusion.1
  18.4 0.7 select_select_fusion.4
  19.1 5.2 %all-to-all-start = ((bf16[8,4,1024]{2,1,0:T(4,128)(2,1)}), bf16[8,4,1024]{2,1,0:T(4,128)(2,1)S(1)}, u32[]{:S(2)}, u32[]{:S(2)}) async-start(bf16[8,4,1024]{2,1,0:T(4,128)(2,1)} %select_select_fusion.4), calls=%async_computation | async-start | bytes 131072 | tf_op jit(solution)/shard_map/all_to_all | solution.py:82
  24.6 0.7 eq.150
  25.3 1.4 gather_fusion.3
  26.7 1.1 gather.59
  27.8 0.8 compare_select_fusion.14
  28.5 1.0 gather_fusion
  29.5 0.7 compare_convert_fusion
  30.2 1.2 reduce-window.6
  32.2 0.8 and_reduce_fusion
  32.9 1.3 compare_and_fusion.4
  34.3 0.5 compare_and_fusion
  34.8 1.6 select_select_fusion.3
  36.5 4.2 %all-to-all-start.1 = ((bf16[8,4,4096]{2,1,0:T(4,128)(2,1)}), bf16[8,4,4096]{2,1,0:T(4,128)(2,1)S(1)}, u32[]{:S(2)}, u32[]{:S(2)}) async-start(bf16[8,4,4096]{2,1,0:T(4,128)(2,1)} %select_select_fusion.3), calls=%async_computation.1 | async-start | bytes 524288 | tf_op jit(solution)/shard_map/all_to_all | solution.py:75
  40.7 0.6 pad_clamp_fusion.2
  41.4 1.6 gather_fusion.2
  42.9 7.4 %all-to-all-done.1 = bf16[8,4,4096]{2,1,0:T(4,128)(2,1)S(1)} async-done(((bf16[8,4,4096]{2,1,0:T(4,128)(2,1)}), bf16[8,4,4096]{2,1,0:T(4,128)(2,1)S(1)}, u32[]{:S(2)}, u32[]{:S(2)}) %all-to-all-start.1) | async-done | bytes 262176 | tf_op jit(solution)/shard_map/all_to_all | solution.py:75
  50.4 0.8 all_to_all.35
  51.1 1.4 pad_maximum_fusion.1
  52.5 2.2 gather_fusion.4
  54.7 15.9 %all-gather.3.cloned.1.call-done = bf16[4096,1024]{1,0:T(8,128)(2,1)} async-done(((bf16[512,1024]{1,0:T(8,128)(2,1)}), bf16[4096,1024]{1,0:T(8,128)(2,1)}) %all-gather.3.cloned.1.call-update) | async-done | bytes 8388624 | tf_op jit(solution)/shard_map/all_gather | solution.py:112
  70.6 5.1 %multiply_reduce_fusion = (f32[128]{0:T(128)S(1)}, f32[128,1024]{1,0:T(8,128)S(1)}) fusion(bf16[4096,1024]{1,0:T(8,128)(2,1)} %all-gather.3.cloned.1.call-done, bf16[128,4096]{1,0:T(8,128)(2,1)} %gather_fusion.4, pred[128]{0:T(512)(128)(4,1)S(1)} %copy-done.15, bf16[128,1024]{1,0:T(8,128)(2,1)} %gather_fusion.2), kind=kOutput, calls=%fused_computation.40 | convolution fusion | flops 1074921344 | bytes 10224256 | tf_op jit(solution)/shard_map/dot_general | solution.py:110
  75.6 11.7 %psum.14 = f32[128]{0:T(128)S(1)} all-reduce(f32[128]{0:T(128)S(1)} %get-tuple-element.10), channel_id=1, replica_groups=mesh['req'=8,'exp'=4] {'exp'}, use_global_device_ids=true, to_apply=%region_6.7 | all-reduce | flops 128 | bytes 1024 | tf_op jit(solution)/shard_map/psum | solution.py:118
  87.5 2.1 gather_fusion.5
  89.6 1.2 select_select_fusion.2
  90.8 12.8 %all_to_all.48 = bf16[8,32,1024]{2,1,0:T(8,128)(2,1)} all-to-all(bf16[8,32,1024]{2,1,0:T(8,128)(2,1)S(1)} %select_select_fusion.2), channel_id=1, replica_groups=mesh['req'=8,'exp'=4] {'req'}, dimensions={0} | all-to-all | bytes 1048576 | tf_op jit(solution)/shard_map/all_to_all | solution.py:143
  103.9 0.4 broadcast_in_dim.258
  104.4 2.0 copy.149
  106.6 0.4 broadcast_in_dim.260
  107.1 2.0 copy.150
  109.3 2.1 gather_fusion.7
  111.4 4.2 %gather.66 = bf16[128,8192]{1,0:T(8,128)(2,1)} reshape(bf16[256,8,512]{2,1,0:T(8,128)(2,1)} %gather_fusion.7) | data formatting | bytes 4194304 | tf_op jit(solution)/shard_map/jit(_take)/gather | solution.py:63
  115.6 30.5 %all-gather.5.cloned.1.call-done = bf16[256,4096]{1,0:T(8,128)(2,1)} async-done(((bf16[256,1024]{1,0:T(8,128)(2,1)}), bf16[256,4096]{1,0:T(8,128)(2,1)}) %all-gather.5.cloned.1.call-update) | async-done | bytes 2097168 | tf_op jit(solution)/shard_map/all_gather | solution.py:144
  146.0 8.5 %fusion.4 = f32[256,1792]{1,0:T(8,128)S(1)} fusion(bf16[256,4096]{1,0:T(8,128)(2,1)} %all-gather.5.cloned.1.call-done, bf16[1,4096,1792]{2,1,0:T(8,128)(2,1)} %param.23), kind=kOutput, calls=%fused_computation.15 | convolution fusion | flops 3758096384 | bytes 18612224 | tf_op jit(solution)/shard_map/dot_general | solution.py:145
  154.6 9.4 %fusion.12 = bf16[256,1792]{1,0:T(8,128)(2,1)S(1)} fusion(bf16[256,4096]{1,0:T(8,128)(2,1)S(1)} %copy-done.18, bf16[1,4096,1792]{2,1,0:T(8,128)(2,1)} %param.24, f32[256,1792]{1,0:T(8,128)S(1)} %fusion.4), kind=kOutput, calls=%fused_computation.20 | convolution fusion | flops 3760848896 | bytes 19529728 | tf_op jit(solution)/shard_map/dot_general | solution.py:146
  164.1 5.1 %fusion.6 = bf16[256,4096]{1,0:T(8,128)(2,1)} fusion(bf16[256,1792]{1,0:T(8,128)(2,1)S(1)} %fusion.12, bf16[1,1792,4096]{2,1,0:T(8,128)(2,1)S(1)} %bitcast.93), kind=kOutput, calls=%fused_computation.17 | convolution fusion | flops 3759144960 | bytes 17694720 | tf_op jit(solution)/shard_map/dot_general | solution.py:149
  169.2 3.7 %all-to-all-start.3 = ((bf16[8,32,4096]{2,1,0:T(8,128)(2,1)}), bf16[8,32,4096]{2,1,0:T(8,128)(2,1)S(1)}, u32[]{:S(2)}, u32[]{:S(2)}) async-start(bf16[8,32,4096]{2,1,0:T(8,128)(2,1)} %bitcast.85), calls=%async_computation.3 | async-start | bytes 4194304 | tf_op jit(solution)/shard_map/all_to_all | solution.py:152
  172.9 0.3 reduce-scatter.2.cloned.1.call-start
  173.1 4.0 %select_select_fusion = bf16[128,8192]{1,0:T(8,128)(2,1)} fusion(pred[128,8192]{1,0:T(8,128)(4,1)} %bitcast.82, pred[128,8192]{1,0:T(8,128)(4,1)} %bitcast.83, bf16[128,8192]{1,0:T(8,128)(2,1)} %gather.66), kind=kLoop, calls=%fused_computation.26 | loop fusion | flops 2097152 | bytes 6291456 | tf_op jit(solution)/shard_map/jit(_where)/select_n | solution.py:71
  177.4 3.4 %gather_fusion.8 = bf16[32,8192]{1,0:T(8,128)(2,1)S(1)} fusion(bf16[128,8192]{1,0:T(8,128)(2,1)} %select_select_fusion, s32[1024]{0:T(1024)} %copy-done.12), kind=kCustom, calls=%fused_computation.8 | custom fusion | bytes 1048704 | tf_op jit(solution)/shard_map/jit(_take)/gather | solution.py:15
  180.8 1.0 gather.68
  181.9 0.6 fusion.25
  182.5 9.5 %psum.15 = f32[128,4]{0,1:T(4,128)S(1)} all-reduce(f32[128,4]{0,1:T(4,128)S(1)} %fusion.25), channel_id=1, replica_groups=mesh['req'=8,'exp'=4] {'exp'}, use_global_device_ids=true, to_apply=%region_7.8 | all-reduce | flops 512 | bytes 4096 | tf_op jit(solution)/shard_map/psum | solution.py:121
  192.0 7.6 %all-to-all-done.3 = bf16[8,32,4096]{2,1,0:T(8,128)(2,1)S(1)} async-done(((bf16[8,32,4096]{2,1,0:T(8,128)(2,1)}), bf16[8,32,4096]{2,1,0:T(8,128)(2,1)S(1)}, u32[]{:S(2)}, u32[]{:S(2)}) %all-to-all-start.3) | async-done | bytes 2097184 | tf_op jit(solution)/shard_map/all_to_all | solution.py:152
  199.5 3.2 %gather_fusion.6 = bf16[256,4096]{1,0:T(8,128)(2,1)} fusion(bf16[256,4096]{1,0:T(8,128)(2,1)S(1)} %bitcast.75, s32[1024]{0:T(1024)S(1)} %pad_clamp_fusion.1), kind=kCustom, calls=%fused_computation.6 | custom fusion | bytes 4195328 | tf_op jit(solution)/shard_map/jit(_take)/gather | solution.py:153
  202.7 3.2 %gather.64 = bf16[128,2,4096]{2,1,0:T(2,128)(2,1)S(1)} reshape(bf16[256,4096]{1,0:T(8,128)(2,1)} %gather_fusion.6) | data formatting | bytes 4194304 | tf_op jit(solution)/shard_map/jit(_take)/gather | solution.py:153
  205.9 2.4 %copy_select_fusion = bf16[128,2,4096]{2,0,1:T(8,128)(2,1)S(1)} fusion(bf16[128,2,4096]{2,1,0:T(2,128)(2,1)S(1)} %gather.64, pred[128,2]{0,1:T(4,128)(4,1)S(1)} %compare_and_fusion.2), kind=kLoop, calls=%fused_computation.25 | loop fusion | flops 1048576 | bytes 4194560 | tf_op jit(solution)/shard_map/jit(_take)/select_n | solution.py:153
  208.3 1.5 fusion.16
  209.8 0.3 select_select_fusion.1
  210.2 12.2 %all_to_all.49 = bf16[8,4,8192]{2,1,0:T(4,128)(2,1)S(1)} all-to-all(bf16[8,4,8192]{2,1,0:T(4,128)(2,1)S(1)} %select_select_fusion.1), channel_id=1, replica_groups=mesh['req'=8,'exp'=4] {'req'}, dimensions={0} | all-to-all | bytes 1048576 | tf_op jit(solution)/shard_map/all_to_all | solution.py:89
  222.3 0.9 all_to_all.42
  223.2 2.0 pad_maximum_fusion
  225.2 3.2 %gather_fusion.9 = bf16[128,8192]{1,0:T(8,128)(2,1)} fusion(bf16[160,8192]{1,0:T(8,128)(2,1)S(1)} %pad_maximum_fusion, s32[1024]{0:T(1024)S(1)} %pad_clamp_fusion.3), kind=kCustom, calls=%fused_computation.9 | custom fusion | bytes 4194816 | tf_op jit(solution)/shard_map/jit(_take)/gather | solution.py:107
  228.4 2.4 copy.151
  230.8 1.6 broadcast_select_fusion
  232.4 1.6 reduce-scatter.2.cloned.1.call-done
  234.0 1.8 convert_add_fusion
  (108 shorter events, 3.2 us)
Async XLA Ops:
  7.2 102.1 %copy-start = (bf16[256,8,512]{2,1,0:T(8,128)(2,1)S(1)}, bf16[256,8,512]{2,1,0:T(8,128)(2,1)}, u32[]{:S(2)}) copy-start(bf16[256,8,512]{2,1,0:T(8,128)(2,1)} %param.18) | copy-start | bytes 6291460
  7.2 17.1 %copy-start.7 = (s32[128,2]{0,1:T(2,128)S(1)}, s32[128,2]{0,1:T(2,128)}, u32[]{:S(2)}) copy-start(s32[128,2]{0,1:T(2,128)} %param.22) | copy-start | bytes 3076
  7.2 18.1 %copy-start.2 = (bf16[128,4096]{1,0:T(8,128)(2,1)S(1)}, bf16[128,4096]{1,0:T(8,128)(2,1)}, u32[]{:S(2)}) copy-start(bf16[128,4096]{1,0:T(8,128)(2,1)} %param.13) | copy-start | bytes 3145732
  7.2 63.4 %all-gather.3.cloned.1.call-start = ((), (), s32[]{:S(2)}) async-start(), calls=%async_computation.6 | async-start | bytes 9437184 | tf_op jit(solution)/shard_map/all_gather | solution.py:112
  16.3 8.2 %copy-start.8 = (pred[8,4]{1,0:T(8,128)(4,1)}, pred[8,4]{1,0:T(8,128)(4,1)S(1)}, u32[]{:S(2)}) copy-start(pred[8,4]{1,0:T(8,128)(4,1)S(1)} %copy.130) | copy-start | bytes 100
  16.7 7.9 %copy-start.10 = (pred[8,4]{1,0:T(8,128)(4,1)}, pred[8,4]{1,0:T(8,128)(4,1)S(1)}, u32[]{:S(2)}) copy-start(pred[8,4]{1,0:T(8,128)(4,1)S(1)} %copy.129) | copy-start | bytes 100
  16.7 12.8 %copy-start.12 = (s32[1024]{0:T(1024)}, s32[1024]{0:T(1024)S(1)}, u32[]{:S(2)}) copy-start(s32[1024]{0:T(1024)S(1)} %pad_clamp_fusion.4) | copy-start | bytes 12292
  19.1 17.3 %all-to-all-start = ((bf16[8,4,1024]{2,1,0:T(4,128)(2,1)}), bf16[8,4,1024]{2,1,0:T(4,128)(2,1)S(1)}, u32[]{:S(2)}, u32[]{:S(2)}) async-start(bf16[8,4,1024]{2,1,0:T(4,128)(2,1)} %select_select_fusion.4), calls=%async_computation | async-start | bytes 131072 | tf_op jit(solution)/shard_map/all_to_all | solution.py:82
  25.3 16.0 %copy-start.3 = (bf16[128,1024]{1,0:T(8,128)(2,1)S(1)}, bf16[128,1024]{1,0:T(8,128)(2,1)}, u32[]{:S(2)}) copy-start(bf16[128,1024]{1,0:T(8,128)(2,1)} %param.14) | copy-start | bytes 786436
  36.5 13.9 %all-to-all-start.1 = ((bf16[8,4,4096]{2,1,0:T(4,128)(2,1)}), bf16[8,4,4096]{2,1,0:T(4,128)(2,1)S(1)}, u32[]{:S(2)}, u32[]{:S(2)}) async-start(bf16[8,4,4096]{2,1,0:T(4,128)(2,1)} %select_select_fusion.3), calls=%async_computation.1 | async-start | bytes 524288 | tf_op jit(solution)/shard_map/all_to_all | solution.py:75
  40.7 105.4 %all-gather.5.cloned.1.call-start = ((), (), s32[]{:S(2)}) async-start(), calls=%async_computation.7 | async-start | bytes 2621440 | tf_op jit(solution)/shard_map/all_gather | solution.py:144
  52.5 18.0 %copy-start.15 = (pred[128]{0:T(512)(128)(4,1)S(1)}, pred[128]{0:T(512)(128)(4,1)}, u32[]{:S(2)}) copy-start(pred[128]{0:T(512)(128)(4,1)} %get-tuple-element.2) | copy-start | bytes 388
  70.6 16.8 %copy-start.5 = (f32[1024]{0:T(1024)S(1)}, f32[1024]{0:T(1024)}, u32[]{:S(2)}) copy-start(f32[1024]{0:T(1024)} %param.17) | copy-start | bytes 12292
  87.4 2.1 copy-start.13
  87.5 2.1 copy-start.14
  89.6 14.1 %copy-start.17 = (s32[128]{0:T(128)S(1)}, s32[128]{0:T(128)}, u32[]{:S(2)}) copy-start(s32[128]{0:T(128)} %param.20) | copy-start | bytes 1540
  103.6 2.8 %copy-start.16 = (s32[128,2]{0,1:T(2,128)S(1)}, s32[128,2]{0,1:T(2,128)}, u32[]{:S(2)}) copy-start(s32[128,2]{0,1:T(2,128)} %param.19) | copy-start | bytes 3076
  146.0 8.6 %copy-start.18 = (bf16[256,4096]{1,0:T(8,128)(2,1)S(1)}, bf16[256,4096]{1,0:T(8,128)(2,1)}, u32[]{:S(2)}) copy-start(bf16[256,4096]{1,0:T(8,128)(2,1)} %all-gather.5.cloned.1.call-done) | copy-start | bytes 6291460
  146.0 18.0 %slice-start = ((s8[14680064]{0:T(1024)(128)(4,1)}), s8[4194304]{0:T(1024)(128)(4,1)S(1)}, s32[]{:S(2)}) async-start(s8[14680064]{0:T(1024)(128)(4,1)} %bitcast.92), calls=%async_computation.9 | async-start | bytes 8388608
  146.0 18.0 %slice-start.1 = ((s8[14680064]{0:T(1024)(128)(4,1)}), s8[4194304]{0:T(1024)(128)(4,1)S(1)}, s32[]{:S(2)}) async-start(s8[14680064]{0:T(1024)(128)(4,1)} %bitcast.92), calls=%async_computation.10 | async-start | bytes 8388608
  154.6 9.5 %slice-start.2 = ((s8[14680064]{0:T(1024)(128)(4,1)}), s8[4194304]{0:T(1024)(128)(4,1)S(1)}, s32[]{:S(2)}) async-start(s8[14680064]{0:T(1024)(128)(4,1)} %bitcast.92), calls=%async_computation.11 | async-start | bytes 8388608
  154.6 9.5 %slice-start.3 = ((s8[14680064]{0:T(1024)(128)(4,1)}), s8[2097152]{0:T(1024)(128)(4,1)S(1)}, s32[]{:S(2)}) async-start(s8[14680064]{0:T(1024)(128)(4,1)} %bitcast.92), calls=%async_computation.12 | async-start | bytes 4194304
  169.2 30.3 %all-to-all-start.3 = ((bf16[8,32,4096]{2,1,0:T(8,128)(2,1)}), bf16[8,32,4096]{2,1,0:T(8,128)(2,1)S(1)}, u32[]{:S(2)}, u32[]{:S(2)}) async-start(bf16[8,32,4096]{2,1,0:T(8,128)(2,1)} %bitcast.85), calls=%async_computation.3 | async-start | bytes 4194304 | tf_op jit(solution)/shard_map/all_to_all | solution.py:152
  172.9 61.2 %reduce-scatter.2.cloned.1.call-start = ((), (), s32[]{:S(2)}) async-start(), calls=%async_computation.8 | async-start | bytes 1310720 | tf_op jit(solution)/shard_map/reduce_scatter | solution.py:157
  177.4 4.4 %copy-start.6 = (f32[1024,4]{0,1:T(4,128)S(1)}, f32[1024,4]{0,1:T(4,128)}, u32[]{:S(2)}) copy-start(f32[1024,4]{0,1:T(4,128)} %param.16) | copy-start | bytes 49156
  208.3 1.5 copy-start.4
  208.3 1.5 copy-start.9
  208.3 1.5 copy-start.11
  230.8 5.0 %copy-start.1 = (bf16[256,8,512]{2,1,0:T(8,128)(2,1)S(1)}, bf16[256,8,512]{2,1,0:T(8,128)(2,1)}, u32[]{:S(2)}) copy-start(bf16[256,8,512]{2,1,0:T(8,128)(2,1)} %param.18) | copy-start | bytes 6291460
Sparse Core Ops, SparseCore 0:
  9.9 60.5 all-gather.2
  103.7 42.2 all-gather.4
  209.9 24.0 reduce-scatter.1
where the time goes:
time: 243 us; the launch traced here: 242 us
  waiting for transfers between devices  63.7 us (26%)
  local copies, waits for them, and re-layouts  47.3 us (19%)
  blocking collectives  46.2 us (19%)
  other arithmetic  29 us (12%)
  matrix products  28.7 us (12%)
  between operations  14.2 us (6%)
  starting transfers between devices  13.4 us (6%)
    all_gather x1, waiting for transfers between devices, body(): rows_full = lax.all_gather(arrived, 'exp', axis=1, tiled=True)  30.5 us
    all_gather x1, waiting for transfers between devices, body(): lax.all_gather(w_out, 'req', axis=0, tiled=True)  15.9 us
    all_to_all x1, blocking collectives, body(): lax.all_to_all(outgoing, 'req', split_axis=0, concat_axis=0, tiled=True)  12.8 us
    all_to_all x1, blocking collectives, body(): lax.all_to_all(pick_rows(page_rows, send_index, send_live), 'req', split_...  12.2 us
    psum x1, blocking collectives, body(): total_sq = lax.psum(squares, 'exp')  11.7 us
    gather x7, local copies, waits for them, and re-layouts, pick_rows(): taken_rows = jnp.take(source, row_index, axis=0)  10.6 us
    psum x1, blocking collectives, body(): lax.psum(jnp.dot(normed, router_w, precision=lax.Precision.HIGHEST), 'exp')  9.47 us
    dot_general x1, matrix products, body(): up_h = jnp.dot(rows_full, w_up[0], preferred_element_type=jnp.float32)  9.4 us
  transfers between devices with their start and end apart: 6, of which 5 were waited for; matrix products, arithmetic and copies ran while one was open for 25% of the time, Pallas kernels for 0%

commit v1 on v0

v1 whole, which is shorter than its diff:
```python
import jax
import jax.numpy as jnp
from jax import lax
from jax.experimental import pallas as pl
from jax.experimental.pallas import tpu as pltpu
from jax.sharding import PartitionSpec as P

D = 4096
SLOTS = 64
MIG = 4
EPSILON = 1e-05
BF = jnp.bfloat16
F32 = jnp.float32
I32 = jnp.int32


def swap(x, axis, s):
    n = lax.axis_size(axis)
    return lax.ppermute(x, axis, [(i, i ^ s) for i in range(n)])


def hot(index, count):
    return (index[..., None] == jnp.arange(count, dtype=I32)).astype(BF)


def pick(selector, rows):
    return jnp.dot(selector, rows, preferred_element_type=F32)


def page_kernel(pool, moved, rows, slot, table, length, out):
    count, pages, page_len, width = out.shape
    token = lax.broadcasted_iota(I32, (page_len, width), 0)

    @pl.loop(0, count)
    def _(j):
        at = slot[j]

        @pl.when(at >= 0)
        def _():
            for p in range(pages):
                out[j, p] = moved[at, p]

        @pl.when(at < 0)
        def _():
            i = rows[j]
            for p in range(pages):
                page = pool[table[i * pages + p]].astype(F32)
                out[j, p] = jnp.where(token + p * page_len < length[i], page, 0.0).astype(out.dtype)


def take_pages(pool, moved, rows, slot, table, length):
    pages = table.shape[0] // length.shape[0]
    count = rows.shape[0]
    return pl.pallas_call(
        page_kernel,
        out_shape=jax.ShapeDtypeStruct((count, pages) + pool.shape[1:], pool.dtype),
        in_specs=[pl.BlockSpec(memory_space=pltpu.VMEM)] * 2
        + [pl.BlockSpec(memory_space=pltpu.SMEM)] * 4,
        out_specs=pl.BlockSpec(memory_space=pltpu.VMEM),
        compiler_params=pltpu.CompilerParams(vmem_limit_bytes=16 * 2**20),
        cost_estimate=pl.CostEstimate(flops=0, bytes_accessed=6 * 2**20, transcendentals=0),
    )(pool, moved, rows, slot, table, length)


def body(
    attention_out,
    residual,
    w_out,
    router_w,
    norm_gain,
    page_pool,
    page_table,
    cache_len,
    came_from,
    routes,
    w_gate,
    w_up,
    w_down,
):
    n = lax.axis_size("req")
    ne = lax.axis_size("exp")
    me = lax.axis_index("req")
    ze = lax.axis_index("exp")
    half = n // 2
    q, k = me // 2, me % 2
    rows = attention_out.shape[0]
    feats = residual.shape[1]
    kblock = D // half
    experts = n // 2

    def column_block(x, s):
        return lax.dynamic_slice_in_dim(x, (q ^ s) * kblock, kblock, axis=1)

    attn_blocks = [column_block(attention_out, s) for s in range(half)]
    attn_blocks = attn_blocks[:1] + [swap(attn_blocks[s], "req", 2 * s) for s in range(1, half)]
    w_other = swap(w_out, "req", 1)
    w_pair = jnp.where(
        k == 0,
        jnp.concatenate([w_out, w_other], axis=0),
        jnp.concatenate([w_other, w_out], axis=0),
    )

    local = jnp.arange(rows, dtype=I32)
    in_new = came_from[None, :] == (me * rows + local)[:, None]
    new_ids = jnp.arange(came_from.shape[0], dtype=I32)
    dest = jnp.sum(jnp.where(in_new, new_ids[None, :], 0), axis=1) // rows
    dest_rank = jnp.sum((dest[:, None] == dest[None, :]) & (local[None, :] < local[:, None]), axis=1)
    dest_rel, dest_par = (dest // 2) ^ q, dest % 2
    send_slot = jnp.where(
        dest_par != k,
        dest_rel * MIG + dest_rank,
        jnp.where(dest_rel != 0, (half + dest_rel - 1) * MIG + dest_rank, -1),
    )
    n_pair, n_send = half * MIG, (2 * half - 1) * MIG
    send_hot = (jnp.arange(n_send, dtype=I32)[:, None] == send_slot[None, :])
    send_row = jnp.sum(jnp.where(send_hot, local[None, :], 0), axis=1)
    send_pick = send_hot.astype(BF)

    source = jnp.stack(
        [lax.dynamic_slice_in_dim(came_from, (2 * (q ^ t) + k) * rows, rows) for t in range(half)]
    )
    src_group, src_local = source // rows, source % rows
    src_rank = jnp.sum(
        (src_group[:, :, None] == src_group[:, None, :]) & (source[:, None, :] < source[:, :, None]),
        axis=2,
    )
    src_rel, src_par = (src_group // 2) ^ q, src_group % 2
    t_ids = jnp.arange(half, dtype=I32)[:, None]
    attn_at = jnp.where(
        src_par == k,
        src_rel * rows + src_local,
        half * rows + src_rel * n_pair + (t_ids ^ src_rel) * MIG + src_rank,
    ).reshape(-1)
    own_stays = src_group[0] == me
    own_slot = src_rel[0] * 2 * MIG + jnp.where(src_par[0] == k, 0, MIG) + src_rank[0]
    own_at = jnp.where(own_stays, src_local[0], rows + own_slot)

    pair_attn = swap(pick(send_pick[:n_pair], attention_out).astype(BF), "req", 1)
    late_blocks = [column_block(pair_attn, s) for s in range(half)]
    late_blocks = late_blocks[:1] + [swap(late_blocks[s], "req", 2 * s) for s in range(1, half)]

    def relay(moving):
        pair = swap(moving[:n_pair], "req", 1)
        blocks = []
        for s in range(half):
            first = moving[n_pair + (s - 1) * MIG : n_pair + s * MIG] if s else pair[:MIG]
            both = jnp.concatenate([first, pair[s * MIG : (s + 1) * MIG]], axis=0)
            blocks.append(swap(both, "req", 2 * s) if s else both)
        return jnp.concatenate(blocks, axis=0)

    moved_resid = relay(pick(send_pick, residual).astype(BF))
    resid_new = pick(
        hot(own_at, rows + 2 * MIG * half), jnp.concatenate([residual, moved_resid], axis=0)
    )

    attn_new = pick(
        hot(attn_at, half * (rows + n_pair)), jnp.concatenate(attn_blocks + late_blocks, axis=0)
    ).astype(BF)
    part = jnp.dot(attn_new, w_pair, preferred_element_type=F32).reshape(half, rows, feats)
    hidden = resid_new + part[0]
    for s in range(1, half):
        hidden = hidden + swap(part[s].astype(BF), "req", 2 * s).astype(F32)

    scaled = hidden * norm_gain[None, :]
    scaled_rows = scaled.astype(BF)
    stats = jnp.concatenate(
        [
            jnp.sum(hidden * hidden, axis=1, keepdims=True),
            jnp.dot(scaled, router_w, precision=lax.Precision.HIGHEST),
        ],
        axis=1,
    )
    stats_all = stats
    for s in range(1, ne):
        stats_all = stats_all + swap(stats, "exp", s)
    full = jnp.zeros((rows, D), BF)
    for s in range(ne):
        block = swap(scaled_rows, "exp", s) if s else scaled_rows
        full = lax.dynamic_update_slice_in_dim(full, block, (ze ^ s) * feats, axis=1)
    inverse = lax.rsqrt(stats_all[:, 0] / D + EPSILON)
    logits = stats_all[:, 1:] * inverse[:, None]
    expert_ids = jnp.arange(experts, dtype=I32)
    chosen = jnp.sum(
        jnp.where(routes[:, :, None] == expert_ids[None, None, :], logits[:, None, :], 0.0), axis=2
    )
    gates = jax.nn.sigmoid(chosen - chosen[:, ::-1])

    names = routes[:, :, None] == expert_ids[None, None, :]
    named = jnp.any(names, axis=1)
    before = jnp.sum(
        jnp.where((local[None, :] < local[:, None])[:, :, None], named[None, :, :], False), axis=1
    )
    rank = jnp.sum(jnp.where(names, before[:, None, :], 0), axis=2)
    slot_of = ((routes ^ (me % experts)) * SLOTS + rank).astype(I32)
    slot_ids = jnp.arange(experts * SLOTS, dtype=I32)
    slot_hot = slot_ids[:, None, None] == slot_of[None, :, :]
    slot_pick = jnp.any(slot_hot, axis=2)
    slot_scale = jnp.sum(jnp.where(slot_pick, inverse[None, :], 0.0), axis=1)
    outgoing = (pick(slot_pick.astype(BF), full) * slot_scale[:, None]).astype(BF)
    outgoing = outgoing.reshape(experts, SLOTS, D)
    arrived = jnp.concatenate(
        [swap(outgoing[s], "req", s) if s else outgoing[s] for s in range(experts)], axis=0
    )

    gate_h = jnp.dot(arrived, w_gate[0], preferred_element_type=F32)
    up_h = jnp.dot(arrived, w_up[0], preferred_element_type=F32)
    active = (jax.nn.silu(gate_h) * up_h).astype(BF)
    down = jnp.dot(active, w_down[0], preferred_element_type=F32).astype(BF)
    down = down.reshape(experts, SLOTS, D)
    back = jnp.concatenate(
        [swap(down[s], "req", s) if s else down[s] for s in range(experts)], axis=0
    )
    gate_slots = jnp.sum(
        jnp.where(slot_of[:, :, None] == slot_ids[None, None, :], gates[:, :, None], 0.0), axis=1
    )
    gate_high = gate_slots.astype(BF)
    gate_low = (gate_slots - gate_high.astype(F32)).astype(BF)
    weighted = pick(gate_high, back) + pick(gate_low, back)
    mixed = hidden + lax.dynamic_slice_in_dim(weighted, ze * feats, feats, axis=1)
    weighted = weighted.astype(BF)
    for s in range(1, ne):
        block = lax.dynamic_slice_in_dim(weighted, (ze ^ s) * feats, feats, axis=1)
        mixed = mixed + swap(block, "exp", s).astype(F32)

    table = page_table.reshape(-1)
    none = jnp.full((n_send,), -1, I32)
    moving_pages = take_pages(page_pool, page_pool[:2].reshape((1, 2) + page_pool.shape[1:]), send_row, none, table, cache_len)
    moved_pages = relay(moving_pages)
    new_pages = take_pages(
        page_pool,
        moved_pages,
        jnp.where(own_stays, src_local[0], 0),
        jnp.where(own_stays, -1, own_slot),
        table,
        cache_len,
    )
    return (mixed, new_pages)


def solution(mesh):
    in_specs = (
        P("req", None),
        P("req", "exp"),
        P("req", "exp"),
        P("exp", None),
        P("exp"),
        P("req", None, "exp"),
        P("req", None),
        P("req"),
        P(),
        P("req", None),
        P("req", None, "exp"),
        P("req", None, "exp"),
        P("req", "exp", None),
    )
    out_specs = (P("req", "exp"), P("req", None, None, "exp"))
    return jax.shard_map(body, mesh=mesh, in_specs=in_specs, out_specs=out_specs, check_vma=False)
```

time: 243 us -> 196 us (0.81)
  blocking collectives: 46.2 us -> 0 us
  local copies, waits for them, and re-layouts: 47.3 us -> 18 us
  starting transfers between devices: 13.4 us -> 39.2 us
  waiting for transfers between devices: 63.7 us -> 85 us
  other arithmetic: 29 us -> 7.81 us
  between operations: 14.2 us -> 1.25 us
  matrix products: 28.7 us -> 37.4 us
  Pallas kernels: 0 us -> 6.53 us
    ppermute x0 -> x34, waiting for transfers between devices: none -> 85 us  [swap(): return lax.ppermute(x, axis, [(i, i ^ s) for i in range(n)])]
    all_gather x2 -> x0, waiting for transfers between devices: 46.3 us -> none  [the longest x1 30.5 us: body(): rows_full = lax.all_gather(arrived, 'exp', axis=1, tiled=True)]
    ppermute x0 -> x34, starting transfers between devices: none -> 39.2 us  [swap(): return lax.ppermute(x, axis, [(i, i ^ s) for i in range(n)])]
    gather x15 -> x0, local copies, waits for them, and re-layouts: 31.1 us -> none  [the longest x7 10.6 us: pick_rows(): taken_rows = jnp.take(source, row_index, axis=0)]
    all_to_all x2 -> x0, blocking collectives: 25 us -> none  [the longest x1 12.8 us: body(): lax.all_to_all(outgoing, 'req', split_axis=0, concat_axis=0, tiled=True)]
    psum x2 -> x0, blocking collectives: 21.2 us -> none  [the longest x1 11.7 us: body(): total_sq = lax.psum(squares, 'exp')]
    all_to_all x3 -> x0, waiting for transfers between devices: 15 us -> none  [the longest x1 7.56 us: body(): lax.all_to_all(partial_value, 'req', split_axis=0, concat_axis=0, tiled=T...]
    all_to_all x3 -> x0, starting transfers between devices: 13 us -> none  [the longest x1 5.17 us: body(): lax.all_to_all(pick_rows(residual, send_index, send_live), 'req', split_a...]
  transfers between devices with their start and end apart: 6 -> 34, of which waited for: 5 -> 11; matrix products, arithmetic and copies ran while one was open for 25% -> 31% of each run, Pallas kernels for 0% -> 3%
where the time goes in v1:
time: 196 us; the launch traced here: 195 us
  waiting for transfers between devices  85 us (43%)
  starting transfers between devices  39.2 us (20%)
  matrix products  37.4 us (19%)
  local copies, waits for them, and re-layouts  18 us (9%)
  other arithmetic  7.81 us (4%)
  Pallas kernels  6.53 us (3%)
    ppermute x34, waiting for transfers between devices, swap(): return lax.ppermute(x, axis, [(i, i ^ s) for i in range(n)])  85 us
    ppermute x34, starting transfers between devices, swap(): return lax.ppermute(x, axis, [(i, i ^ s) for i in range(n)])  39.2 us
    dot_general x1, matrix products, body(): down = jnp.dot(active, w_down[0], preferred_element_type=F32).astype(BF)  9.78 us
    dot_general x6, matrix products, pick(): return jnp.dot(selector, rows, preferred_element_type=F32)  8.51 us
    dot_general x1, matrix products, body(): up_h = jnp.dot(arrived, w_up[0], preferred_element_type=F32)  8.02 us
    unnamed x43, local copies, waits for them, and re-layouts  7.39 us
    pallas_call x2, Pallas kernels, take_pages(): pl.pallas_call(page_kernel, out_shape=jax.ShapeDtypeStruct((count, pages)...  6.53 us
    dot_general x1, matrix products, body(): jnp.dot(attn_new, w_pair, preferred_element_type=F32)  6.45 us
  transfers between devices with their start and end apart: 34, of which 11 were waited for; matrix products, arithmetic and copies ran while one was open for 31% of the time, Pallas kernels for 3%

profile of v1, /device:TPU:0, one launch (start us, length us, event | category | flops | bytes accessed | tf_op | source)
XLA Modules:
  0.0 195.1 jit_solution(5903118938409152891)
XLA Ops:
  1.2 1.1 select_reduce_fusion
  2.6 2.1 %convolution_convert_fusion = bf16[16,4096]{1,0:T(8,128)(2,1)} fusion(bf16[128,4096]{1,0:T(8,128)(2,1)} %param.13, pred[28,128]{1,0:T(8,128)(4,1)S(1)} %iota_compare_fusion.9), kind=kOutput, calls=%fused_computation.10 | convolution fusion | flops 16842752 | bytes 1181696 | tf_op jit(solution)/shard_map/dot_general | solution.py:27
  4.7 2.1 %constant_dynamic-slice_fusion.6 = (bf16[128,1024]{1,0:T(8,128)(2,1)S(1)}, bf16[128,1024]{1,0:T(8,128)(2,1)S(1)}, bf16[128,1024]{1,0:T(8,128)(2,1)}, bf16[576,1024]{1,0:T(8,128)(2,1)}) fusion(bf16[128,4096]{1,0:T(8,128)(2,1)} %param.13, s32[]{:T(128)S(6)} %select_n.249, s32[]{:T(128)S(6)} %select_n.248, s32[]{:T(128)S(6)} %select_n.247, s32[]{:T(128)S(6)} %select_n.246), kind=kLoop, calls=%fused_computation.93 | loop fusion | bytes 2097168 | tf_op jit(solution)/shard_map/dynamic_slice | solution.py:92
  6.8 2.8 %collective-permute-start.4 = (bf16[128,1024]{1,0:T(8,128)(2,1)}, bf16[128,1024]{1,0:T(8,128)(2,1)}, u32[]{:S(2)}, u32[]{:S(2)}) collective-permute-start(bf16[128,1024]{1,0:T(8,128)(2,1)} %get-tuple-element.24), channel_id=1, source_target_pairs={{0,8},{4,12},{8,0},{12,4},{16,24},{20,28},{24,16},{28,20},{1,9},{5... | collective-permute-start | bytes 786440 | tf_op jit(solution)/shard_map/ppermute | solution.py:19
  9.6 1.5 collective-permute-start.5
  11.8 0.6 fusion.34
  13.3 0.6 fusion.38
  14.2 1.3 shard_map.140
  15.6 0.7 fusion.59
  16.2 0.7 bitcast_select_fusion
  17.5 1.7 constant_dynamic-update-slice_fusion.5
  19.2 1.7 constant_dynamic-update-slice_fusion.4
  20.9 6.2 %collective-permute-done.6 = bf16[128,1024]{1,0:T(8,128)(2,1)S(1)} collective-permute-done((bf16[128,1024]{1,0:T(8,128)(2,1)S(1)}, bf16[128,1024]{1,0:T(8,128)(2,1)S(1)}, u32[]{:S(2)}, u32[]{:S(2)}) %collective-permute-start.6) | collective-permute-done | bytes 262176 | tf_op jit(solution)/shard_map/ppermute | solution.py:19
  27.1 0.7 constant_dynamic-update-slice_fusion.3
  27.8 1.4 constant_dynamic-slice_fusion.3
  29.8 1.6 collective-permute-start.1
  31.9 1.5 collective-permute-start.10
  33.4 0.6 constant_dynamic-update-slice_fusion.2
  34.0 1.3 collective-permute-done.9
  35.3 0.6 constant_dynamic-update-slice_fusion.1
  35.9 0.8 collective-permute-done.10
  36.7 0.6 constant_dynamic-update-slice_fusion
  37.3 6.4 %fusion.63 = (bf16[512,1024]{1,0:T(8,128)(2,1)}, f32[512,1024]{1,0:T(8,128)}) fusion(bf16[512,1024]{1,0:T(8,128)(2,1)} %collective-permute-done.11, bf16[512,1024]{1,0:T(8,128)(2,1)} %param.15, pred[]{:T(512)S(6)} %eq.197, bf16[576,1024]{1,0:T(8,128)(2,1)} %constant_dynamic-update-slice_fusion, s32[512]{0:T(512)} %fusion.38), kind=kOutput, calls=%fused_computation.180 | convolution fusion | flops 1688502272 | bytes 6424577 | tf_op jit(solution)/shard_map/dot_general | solution.py:159
  43.7 2.0 %fusion.58 = (bf16[128,1024]{1,0:T(8,128)(2,1)}, bf16[128,1024]{1,0:T(8,128)(2,1)}, bf16[128,1024]{1,0:T(8,128)(2,1)}) fusion(bf16[512,1024]{1,0:T(8,128)(2,1)} %get-tuple-element.51), kind=kLoop, calls=%fused_computation.175 | loop fusion | bytes 1572864 | tf_op jit(solution)/shard_map/slice | solution.py:162
  45.7 1.5 collective-permute-start.14
  47.5 1.7 collective-permute-start.12
  49.2 1.6 collective-permute-start.2
  51.3 0.7 slice.187
  52.0 7.1 %collective-permute-done.2 = bf16[8,1024]{1,0:T(8,128)(2,1)S(1)} collective-permute-done((bf16[8,1024]{1,0:T(8,128)(2,1)S(1)}, bf16[8,1024]{1,0:T(8,128)(2,1)S(1)}, u32[]{:S(2)}, u32[]{:S(2)}) %collective-permute-start.2) | collective-permute-done | bytes 16416 | tf_op jit(solution)/shard_map/ppermute | solution.py:19
  59.4 1.6 constant_dynamic-update-slice_fusion.12
  61.7 3.7 %collective-permute-start.17 = (f32[128,5]{0,1:T(8,128)S(1)}, f32[128,5]{0,1:T(8,128)S(1)}, u32[]{:S(2)}, u32[]{:S(2)}) collective-permute-start(f32[128,5]{0,1:T(8,128)S(1)} %pad_maximum_fusion.12), channel_id=1, source_target_pairs={{0,3},{1,2},{2,1},{3,0},{4,7},{5,6},{6,5},{7,4},{8,11},{9,10},{10,... | collective-permute-start | bytes 7688 | tf_op jit(solution)/shard_map/ppermute | solution.py:19
  65.4 0.8 collective-permute-start.15
  66.2 1.0 fusion.60
  67.1 1.3 collective-permute-start.18
  68.4 2.9 %collective-permute-start.19 = (bf16[128,1024]{1,0:T(8,128)(2,1)S(1)}, bf16[128,1024]{1,0:T(8,128)(2,1)S(1)}, u32[]{:S(2)}, u32[]{:S(2)}) collective-permute-start(bf16[128,1024]{1,0:T(8,128)(2,1)S(1)} %get-tuple-element.5), channel_id=1, source_target_pairs={{0,2},{1,3},{2,0},{3,1},{4,6},{5,7},{6,4},{7,5},{8,10},{9,11},{10,... | collective-permute-start | bytes 786440 | tf_op jit(solution)/shard_map/ppermute | solution.py:19
  71.7 8.4 %collective-permute-done.18 = bf16[128,1024]{1,0:T(8,128)(2,1)S(1)} collective-permute-done((bf16[128,1024]{1,0:T(8,128)(2,1)S(1)}, bf16[128,1024]{1,0:T(8,128)(2,1)S(1)}, u32[]{:S(2)}, u32[]{:S(2)}) %collective-permute-start.18) | collective-permute-done | bytes 262176 | tf_op jit(solution)/shard_map/ppermute | solution.py:19
  80.1 9.6 %collective-permute-done.19 = bf16[128,1024]{1,0:T(8,128)(2,1)S(1)} collective-permute-done((bf16[128,1024]{1,0:T(8,128)(2,1)S(1)}, bf16[128,1024]{1,0:T(8,128)(2,1)S(1)}, u32[]{:S(2)}, u32[]{:S(2)}) %collective-permute-start.19) | collective-permute-done | bytes 262176 | tf_op jit(solution)/shard_map/ppermute | solution.py:19
  89.8 0.7 fusion.9
  90.8 0.8 collective-permute-start.22
  91.6 1.1 collective-permute-start.21
  92.7 0.7 pad_maximum_fusion.6
  93.3 0.7 collective-permute-start.31
  94.1 1.6 collective-permute-start.32
  95.7 0.7 pad_maximum_fusion.8
  96.3 0.8 slice_dynamic-update-slice_fusion.1
  97.2 7.8 %collective-permute-done.23 = bf16[64,4096]{1,0:T(8,128)(2,1)S(1)} collective-permute-done((bf16[64,4096]{1,0:T(8,128)(2,1)S(1)}, bf16[64,4096]{1,0:T(8,128)(2,1)S(1)}, u32[]{:S(2)}, u32[]{:S(2)}) %collective-permute-start.23) | collective-permute-done | bytes 524320 | tf_op jit(solution)/shard_map/ppermute | solution.py:19
  105.0 9.8 %collective-permute-done.22 = bf16[64,4096]{1,0:T(8,128)(2,1)S(1)} collective-permute-done((bf16[64,4096]{1,0:T(8,128)(2,1)S(1)}, bf16[64,4096]{1,0:T(8,128)(2,1)S(1)}, u32[]{:S(2)}, u32[]{:S(2)}) %collective-permute-start.22) | collective-permute-done | bytes 524320 | tf_op jit(solution)/shard_map/ppermute | solution.py:19
  114.8 8.0 %fusion.2 = f32[256,1792]{1,0:T(8,128)S(1)} fusion(bf16[1,4096,1792]{2,1,0:T(8,128)(2,1)} %param.24, bf16[64,4096]{1,0:T(8,128)(2,1)S(1)} %collective-permute-done.23, bf16[64,4096]{1,0:T(8,128)(2,1)S(1)} %collective-permute-done.22, bf16[64,4096]{1,0:T(8,128)(2,1)S(1)} %collective-permute-done.21, bf16[64,4096]{1,0:T(8,128)(2,1)S(1)} %get-tuple-element.12), kind=kOutput, calls=%fused_computation.2 | convolution fusion | flops 3766484992 | bytes 18612224 | tf_op jit(solution)/shard_map/dot_general | solution.py:206
  123.1 4.1 %fusion.4 = f32[256,1792]{1,0:T(8,128)S(1)} fusion(bf16[1,4096,1792]{2,1,0:T(8,128)(2,1)S(1)} %bitcast.76, bf16[64,4096]{1,0:T(8,128)(2,1)S(1)} %collective-permute-done.23, bf16[64,4096]{1,0:T(8,128)(2,1)S(1)} %collective-permute-done.22, bf16[64,4096]{1,0:T(8,128)(2,1)S(1)} %collective-permute-done.21, bf16[64,4096]{1,0:T(8,128)(2,1)S(1)} %get-tuple-element.12), kind=kOutput, calls=%fused_computation.4 | convolution fusion | flops 3766484992 | bytes 18612224 | tf_op jit(solution)/shard_map/dot_general | solution.py:205
  127.2 9.8 %fusion.6 = bf16[256,4096]{1,0:T(8,128)(2,1)S(1)} fusion(bf16[1,1792,4096]{2,1,0:T(8,128)(2,1)} %param.25, f32[256,1792]{1,0:T(8,128)S(1)} %fusion.2, f32[256,1792]{1,0:T(8,128)S(1)} %fusion.4), kind=kOutput, calls=%fused_computation.7 | convolution fusion | flops 3761897472 | bytes 20447232 | tf_op jit(solution)/shard_map/dot_general | solution.py:208
  137.0 1.4 fusion.56
  138.3 1.9 collective-permute-start.26
  140.2 1.3 collective-permute-start.25
  141.7 11.1 %collective-permute-done.26 = bf16[64,4096]{1,0:T(8,128)(2,1)} collective-permute-done((bf16[64,4096]{1,0:T(8,128)(2,1)}, bf16[64,4096]{1,0:T(8,128)(2,1)}, u32[]{:S(2)}, u32[]{:S(2)}) %collective-permute-start.26) | collective-permute-done | bytes 524320 | tf_op jit(solution)/shard_map/ppermute | solution.py:19
  152.8 2.0 %collective-permute-start.33 = (bf16[8,2,8,512]{3,2,1,0:T(8,128)(2,1)}, bf16[8,2,8,512]{3,2,1,0:T(8,128)(2,1)S(1)}, u32[]{:S(2)}, u32[]{:S(2)}) collective-permute-start(bf16[8,2,8,512]{3,2,1,0:T(8,128)(2,1)} %pad_maximum_fusion.8), channel_id=1, source_target_pairs={{0,24},{4,28},{8,16},{12,20},{16,8},{20,12},{24,0},{28,4},{1,25},{... | collective-permute-start | bytes 393224 | tf_op jit(solution)/shard_map/ppermute | solution.py:19
  154.8 10.9 %collective-permute-done.25 = bf16[64,4096]{1,0:T(8,128)(2,1)} collective-permute-done((bf16[64,4096]{1,0:T(8,128)(2,1)}, bf16[64,4096]{1,0:T(8,128)(2,1)}, u32[]{:S(2)}, u32[]{:S(2)}) %collective-permute-start.25) | collective-permute-done | bytes 524320 | tf_op jit(solution)/shard_map/ppermute | solution.py:19
  165.6 2.0 %fusion.25 = f32[128,4096]{1,0:T(8,128)S(1)} fusion(bf16[64,4096]{1,0:T(8,128)(2,1)} %collective-permute-done.26, bf16[64,4096]{1,0:T(8,128)(2,1)} %collective-permute-done.25, bf16[64,4096]{1,0:T(8,128)(2,1)} %collective-permute-done.24, bf16[64,4096]{1,0:T(8,128)(2,1)} %get-tuple-element.8, f32[128,256]{1,0:T(8,128)S(1)} %select_reduce_fusion.1), kind=kOutput, calls=%fused_computation.37 | convolution fusion | flops 276955136 | bytes 4325376 | tf_op jit(solution)/shard_map/dot_general | solution.py:27
  167.7 1.9 fusion.64
  169.6 2.5 %collective-permute-start.29 = (bf16[128,1024]{1,0:T(8,128)(2,1)S(1)}, bf16[128,1024]{1,0:T(8,128)(2,1)S(1)}, u32[]{:S(2)}, u32[]{:S(2)}) collective-permute-start(bf16[128,1024]{1,0:T(8,128)(2,1)S(1)} %get-tuple-element.17), channel_id=1, source_target_pairs={{0,3},{1,2},{2,1},{3,0},{4,7},{5,6},{6,5},{7,4},{8,11},{9,10},{10,... | collective-permute-start | bytes 786440 | tf_op jit(solution)/shard_map/ppermute | solution.py:19
  172.1 3.9 %collective-permute-start.28 = (bf16[128,1024]{1,0:T(8,128)(2,1)S(1)}, bf16[128,1024]{1,0:T(8,128)(2,1)S(1)}, u32[]{:S(2)}, u32[]{:S(2)}) collective-permute-start(bf16[128,1024]{1,0:T(8,128)(2,1)S(1)} %get-tuple-element.18), channel_id=1, source_target_pairs={{0,2},{1,3},{2,0},{3,1},{4,6},{5,7},{6,4},{7,5},{8,10},{9,11},{10,... | collective-permute-start | bytes 786440 | tf_op jit(solution)/shard_map/ppermute | solution.py:19
  176.1 0.9 constant_dynamic-update-slice_fusion.7
  177.1 5.2 %shard_map.141 = bf16[128,2,8,512]{3,2,1,0:T(8,128)(2,1)} custom-call(bf16[256,8,512]{2,1,0:T(8,128)(2,1)S(1)} %copy-done.2, bf16[32,2,8,512]{3,2,1,0:T(8,128)(2,1)S(1)} %constant_dynamic-update-slice_fusion.6.moved, s32[128]{0:T(128)S(1)} %get-tuple-element.44.rows, s32[128]{0:T(128)S(1)} %get-tuple-element.2.slot, s32[256]{0:T(256)S(1)} %reshape.524.table, ...), custom_call_target="tpu_custom_call" | custom-call | bytes 6291456 | tf_op jit(solution)/shard_map/pallas_call | solution.py:54
  182.3 11.9 %collective-permute-done.28 = bf16[128,1024]{1,0:T(8,128)(2,1)S(1)} collective-permute-done((bf16[128,1024]{1,0:T(8,128)(2,1)S(1)}, bf16[128,1024]{1,0:T(8,128)(2,1)S(1)}, u32[]{:S(2)}, u32[]{:S(2)}) %collective-permute-start.28) | collective-permute-done | bytes 262176 | tf_op jit(solution)/shard_map/ppermute | solution.py:19
  194.1 1.0 convert_add_fusion
  (120 shorter events, 7.2 us)
Async XLA Ops:
  0.6 60.4 %copy-start = (f32[1024,4]{0,1:T(4,128)S(1)}, f32[1024,4]{0,1:T(4,128)}, u32[]{:S(2)}) copy-start(f32[1024,4]{0,1:T(4,128)} %param.16) | copy-start | bytes 49156
  0.6 11.1 %copy-start.9 = (s32[1024]{0:T(1024)S(1)}, s32[1024]{0:T(1024)}, u32[]{:S(2)}) copy-start(s32[1024]{0:T(1024)} %param.21) | copy-start | bytes 12292
  0.7 10.4 %copy-start.4 = (bf16[128,1024]{1,0:T(8,128)(2,1)S(1)}, bf16[128,1024]{1,0:T(8,128)(2,1)}, u32[]{:S(2)}) copy-start(bf16[128,1024]{1,0:T(8,128)(2,1)} %param.14) | copy-start | bytes 786436
  0.7 10.9 %copy-start.10 = (s32[128,2]{0,1:T(2,128)S(1)}, s32[128,2]{0,1:T(2,128)}, u32[]{:S(2)}) copy-start(s32[128,2]{0,1:T(2,128)} %param.22) | copy-start | bytes 3076
  0.7 13.3 %copy-start.2 = (bf16[256,8,512]{2,1,0:T(8,128)(2,1)S(1)}, bf16[256,8,512]{2,1,0:T(8,128)(2,1)}, u32[]{:S(2)}) copy-start(bf16[256,8,512]{2,1,0:T(8,128)(2,1)} %pool.3) | copy-start | bytes 6291460
  0.7 13.3 %copy-start.12 = (s32[128,2]{0,1:T(2,128)S(1)}, s32[128,2]{0,1:T(2,128)}, u32[]{:S(2)}) copy-start(s32[128,2]{0,1:T(2,128)} %param.19) | copy-start | bytes 3076
  0.7 13.5 %copy-start.3 = (s32[128]{0:T(128)S(1)}, s32[128]{0:T(128)}, u32[]{:S(2)}) copy-start(s32[128]{0:T(128)} %length.3) | copy-start | bytes 1540
  0.7 36.6 %collective-permute-start.11 = (bf16[512,1024]{1,0:T(8,128)(2,1)}, bf16[512,1024]{1,0:T(8,128)(2,1)}, u32[]{:S(2)}, u32[]{:S(2)}) collective-permute-start(bf16[512,1024]{1,0:T(8,128)(2,1)} %param.15), channel_id=1, source_target_pairs={{0,4},{4,0},{8,12},{12,8},{16,20},{20,16},{24,28},{28,24},{1,5},{5... | collective-permute-start | bytes 3145736 | tf_op jit(solution)/shard_map/ppermute | solution.py:19
  4.7 23.1 %collective-permute-start.7 = (bf16[16,4096]{1,0:T(8,128)(2,1)}, bf16[16,4096]{1,0:T(8,128)(2,1)}, u32[]{:S(2)}, u32[]{:S(2)}) collective-permute-start(bf16[16,4096]{1,0:T(8,128)(2,1)} %convolution_convert_fusion), channel_id=1, source_target_pairs={{0,4},{4,0},{8,12},{12,8},{16,20},{20,16},{24,28},{28,24},{1,5},{5... | collective-permute-start | bytes 393224 | tf_op jit(solution)/shard_map/ppermute | solution.py:19
  6.8 10.8 %collective-permute-start.4 = (bf16[128,1024]{1,0:T(8,128)(2,1)}, bf16[128,1024]{1,0:T(8,128)(2,1)}, u32[]{:S(2)}, u32[]{:S(2)}) collective-permute-start(bf16[128,1024]{1,0:T(8,128)(2,1)} %get-tuple-element.24), channel_id=1, source_target_pairs={{0,8},{4,12},{8,0},{12,4},{16,24},{20,28},{24,16},{28,20},{1,9},{5... | collective-permute-start | bytes 786440 | tf_op jit(solution)/shard_map/ppermute | solution.py:19
  9.6 9.7 %collective-permute-start.5 = (bf16[128,1024]{1,0:T(8,128)(2,1)S(1)}, bf16[128,1024]{1,0:T(8,128)(2,1)}, u32[]{:S(2)}, u32[]{:S(2)}) collective-permute-start(bf16[128,1024]{1,0:T(8,128)(2,1)S(1)} %get-tuple-element.23), channel_id=1, source_target_pairs={{0,16},{4,20},{8,24},{12,28},{16,0},{20,4},{24,8},{28,12},{1,17},{... | collective-permute-start | bytes 786440 | tf_op jit(solution)/shard_map/ppermute | solution.py:19
  11.3 6.2 %collective-permute-start = (bf16[16,1024]{1,0:T(8,128)(2,1)S(1)}, bf16[16,1024]{1,0:T(8,128)(2,1)S(1)}, u32[]{:S(2)}, u32[]{:S(2)}) collective-permute-start(bf16[16,1024]{1,0:T(8,128)(2,1)S(1)} %slice.166), channel_id=1, source_target_pairs={{0,4},{4,0},{8,12},{12,8},{16,20},{20,16},{24,28},{28,24},{1,5},{5... | collective-permute-start | bytes 98312 | tf_op jit(solution)/shard_map/ppermute | solution.py:19
  17.5 9.6 %collective-permute-start.6 = (bf16[128,1024]{1,0:T(8,128)(2,1)S(1)}, bf16[128,1024]{1,0:T(8,128)(2,1)S(1)}, u32[]{:S(2)}, u32[]{:S(2)}) collective-permute-start(bf16[128,1024]{1,0:T(8,128)(2,1)S(1)} %get-tuple-element.22), channel_id=1, source_target_pairs={{0,24},{4,28},{8,16},{12,20},{16,8},{20,12},{24,0},{28,4},{1,25},{... | collective-permute-start | bytes 786440 | tf_op jit(solution)/shard_map/ppermute | solution.py:19
  29.3 4.1 %collective-permute-start.8 = (bf16[16,1024]{1,0:T(8,128)(2,1)S(1)}, bf16[16,1024]{1,0:T(8,128)(2,1)S(1)}, u32[]{:S(2)}, u32[]{:S(2)}) collective-permute-start(bf16[16,1024]{1,0:T(8,128)(2,1)S(1)} %get-tuple-element.35), channel_id=1, source_target_pairs={{0,8},{4,12},{8,0},{12,4},{16,24},{20,28},{24,16},{28,20},{1,9},{5... | collective-permute-start | bytes 98312 | tf_op jit(solution)/shard_map/ppermute | solution.py:19
  29.8 21.1 %collective-permute-start.1 = (bf16[8,1024]{1,0:T(8,128)(2,1)S(1)}, bf16[8,1024]{1,0:T(8,128)(2,1)S(1)}, u32[]{:S(2)}, u32[]{:S(2)}) collective-permute-start(bf16[8,1024]{1,0:T(8,128)(2,1)S(1)} %pad_maximum_fusion.9), channel_id=1, source_target_pairs={{0,8},{4,12},{8,0},{12,4},{16,24},{20,28},{24,16},{28,20},{1,9},{5... | collective-permute-start | bytes 49160 | tf_op jit(solution)/shard_map/ppermute | solution.py:19
  31.4 3.9 %collective-permute-start.9 = (bf16[16,1024]{1,0:T(8,128)(2,1)S(1)}, bf16[16,1024]{1,0:T(8,128)(2,1)S(1)}, u32[]{:S(2)}, u32[]{:S(2)}) collective-permute-start(bf16[16,1024]{1,0:T(8,128)(2,1)S(1)} %get-tuple-element.34), channel_id=1, source_target_pairs={{0,16},{4,20},{8,24},{12,28},{16,0},{20,4},{24,8},{28,12},{1,17},{... | collective-permute-start | bytes 98312 | tf_op jit(solution)/shard_map/ppermute | solution.py:19
  31.9 4.8 %collective-permute-start.10 = (bf16[16,1024]{1,0:T(8,128)(2,1)S(1)}, bf16[16,1024]{1,0:T(8,128)(2,1)S(1)}, u32[]{:S(2)}, u32[]{:S(2)}) collective-permute-start(bf16[16,1024]{1,0:T(8,128)(2,1)S(1)} %get-tuple-element.33), channel_id=1, source_target_pairs={{0,24},{4,28},{8,16},{12,20},{16,8},{20,12},{24,0},{28,4},{1,25},{... | collective-permute-start | bytes 98312 | tf_op jit(solution)/shard_map/ppermute | solution.py:19
  43.7 15.6 %copy-start.8 = (f32[1024]{0:T(1024)S(1)}, f32[1024]{0:T(1024)}, u32[]{:S(2)}) copy-start(f32[1024]{0:T(1024)} %param.17) | copy-start | bytes 12292
  43.7 15.6 %copy-start.11 = (s32[128]{0:T(128)S(1)}, s32[128]{0:T(128)}, u32[]{:S(2)}) copy-start(s32[128]{0:T(128)} %get-tuple-element.45) | copy-start | bytes 1540
  45.7 13.5 %collective-permute-start.14 = (bf16[128,1024]{1,0:T(8,128)(2,1)}, bf16[128,1024]{1,0:T(8,128)(2,1)}, u32[]{:S(2)}, u32[]{:S(2)}) collective-permute-start(bf16[128,1024]{1,0:T(8,128)(2,1)} %get-tuple-element.20), channel_id=1, source_target_pairs={{0,24},{4,28},{8,16},{12,20},{16,8},{20,12},{24,0},{28,4},{1,25},{... | collective-permute-start | bytes 786440 | tf_op jit(solution)/shard_map/ppermute | solution.py:19
  47.2 12.0 %collective-permute-start.13 = (bf16[128,1024]{1,0:T(8,128)(2,1)}, bf16[128,1024]{1,0:T(8,128)(2,1)}, u32[]{:S(2)}, u32[]{:S(2)}) collective-permute-start(bf16[128,1024]{1,0:T(8,128)(2,1)} %get-tuple-element.21), channel_id=1, source_target_pairs={{0,16},{4,20},{8,24},{12,28},{16,0},{20,4},{24,8},{28,12},{1,17},{... | collective-permute-start | bytes 786440 | tf_op jit(solution)/shard_map/ppermute | solution.py:19
  47.5 11.7 %collective-permute-start.12 = (bf16[128,1024]{1,0:T(8,128)(2,1)}, bf16[128,1024]{1,0:T(8,128)(2,1)}, u32[]{:S(2)}, u32[]{:S(2)}) collective-permute-start(bf16[128,1024]{1,0:T(8,128)(2,1)} %get-tuple-element.19), channel_id=1, source_target_pairs={{0,8},{4,12},{8,0},{12,4},{16,24},{20,28},{24,16},{28,20},{1,9},{5... | collective-permute-start | bytes 786440 | tf_op jit(solution)/shard_map/ppermute | solution.py:19
  49.2 9.9 %collective-permute-start.2 = (bf16[8,1024]{1,0:T(8,128)(2,1)S(1)}, bf16[8,1024]{1,0:T(8,128)(2,1)S(1)}, u32[]{:S(2)}, u32[]{:S(2)}) collective-permute-start(bf16[8,1024]{1,0:T(8,128)(2,1)S(1)} %pad_maximum_fusion.10), channel_id=1, source_target_pairs={{0,16},{4,20},{8,24},{12,28},{16,0},{20,4},{24,8},{28,12},{1,17},{... | collective-permute-start | bytes 49160 | tf_op jit(solution)/shard_map/ppermute | solution.py:19
  50.9 8.2 %collective-permute-start.3 = (bf16[8,1024]{1,0:T(8,128)(2,1)S(1)}, bf16[8,1024]{1,0:T(8,128)(2,1)S(1)}, u32[]{:S(2)}, u32[]{:S(2)}) collective-permute-start(bf16[8,1024]{1,0:T(8,128)(2,1)S(1)} %pad_maximum_fusion.11), channel_id=1, source_target_pairs={{0,24},{4,28},{8,16},{12,20},{16,8},{20,12},{24,0},{28,4},{1,25},{... | collective-permute-start | bytes 49160 | tf_op jit(solution)/shard_map/ppermute | solution.py:19
  59.1 7.0 %collective-permute-start.30 = (bf16[16,2,8,512]{3,2,1,0:T(8,128)(2,1)}, bf16[16,2,8,512]{3,2,1,0:T(8,128)(2,1)}, u32[]{:S(2)}, u32[]{:S(2)}) collective-permute-start(bf16[16,2,8,512]{3,2,1,0:T(8,128)(2,1)} %slice.187), channel_id=1, source_target_pairs={{0,4},{4,0},{8,12},{12,8},{16,20},{20,16},{24,28},{28,24},{1,5},{5... | collective-permute-start | bytes 786440 | tf_op jit(solution)/shard_map/ppermute | solution.py:19
  61.7 9.6 %collective-permute-start.17 = (f32[128,5]{0,1:T(8,128)S(1)}, f32[128,5]{0,1:T(8,128)S(1)}, u32[]{:S(2)}, u32[]{:S(2)}) collective-permute-start(f32[128,5]{0,1:T(8,128)S(1)} %pad_maximum_fusion.12), channel_id=1, source_target_pairs={{0,3},{1,2},{2,1},{3,0},{4,7},{5,6},{6,5},{7,4},{8,11},{9,10},{10,... | collective-permute-start | bytes 7688 | tf_op jit(solution)/shard_map/ppermute | solution.py:19
  65.3 6.2 %collective-permute-start.16 = (f32[128,5]{0,1:T(8,128)S(1)}, f32[128,5]{0,1:T(8,128)S(1)}, u32[]{:S(2)}, u32[]{:S(2)}) collective-permute-start(f32[128,5]{0,1:T(8,128)S(1)} %pad_maximum_fusion.12), channel_id=1, source_target_pairs={{0,2},{1,3},{2,0},{3,1},{4,6},{5,7},{6,4},{7,5},{8,10},{9,11},{10,... | collective-permute-start | bytes 7688 | tf_op jit(solution)/shard_map/ppermute | solution.py:19
  65.4 6.2 %collective-permute-start.15 = (f32[128,5]{0,1:T(8,128)S(1)}, f32[128,5]{0,1:T(8,128)S(1)}, u32[]{:S(2)}, u32[]{:S(2)}) collective-permute-start(f32[128,5]{0,1:T(8,128)S(1)} %pad_maximum_fusion.12), channel_id=1, source_target_pairs={{0,1},{1,0},{2,3},{3,2},{4,5},{5,4},{6,7},{7,6},{8,9},{9,8},{10,11... | collective-permute-start | bytes 7688 | tf_op jit(solution)/shard_map/ppermute | solution.py:19
  67.1 13.0 %collective-permute-start.18 = (bf16[128,1024]{1,0:T(8,128)(2,1)S(1)}, bf16[128,1024]{1,0:T(8,128)(2,1)S(1)}, u32[]{:S(2)}, u32[]{:S(2)}) collective-permute-start(bf16[128,1024]{1,0:T(8,128)(2,1)S(1)} %get-tuple-element.5), channel_id=1, source_target_pairs={{0,1},{1,0},{2,3},{3,2},{4,5},{5,4},{6,7},{7,6},{8,9},{9,8},{10,11... | collective-permute-start | bytes 786440 | tf_op jit(solution)/shard_map/ppermute | solution.py:19
  68.4 21.4 %collective-permute-start.19 = (bf16[128,1024]{1,0:T(8,128)(2,1)S(1)}, bf16[128,1024]{1,0:T(8,128)(2,1)S(1)}, u32[]{:S(2)}, u32[]{:S(2)}) collective-permute-start(bf16[128,1024]{1,0:T(8,128)(2,1)S(1)} %get-tuple-element.5), channel_id=1, source_target_pairs={{0,2},{1,3},{2,0},{3,1},{4,6},{5,7},{6,4},{7,5},{8,10},{9,11},{10,... | collective-permute-start | bytes 786440 | tf_op jit(solution)/shard_map/ppermute | solution.py:19
  71.3 18.5 %collective-permute-start.20 = (bf16[128,1024]{1,0:T(8,128)(2,1)S(1)}, bf16[128,1024]{1,0:T(8,128)(2,1)S(1)}, u32[]{:S(2)}, u32[]{:S(2)}) collective-permute-start(bf16[128,1024]{1,0:T(8,128)(2,1)S(1)} %get-tuple-element.5), channel_id=1, source_target_pairs={{0,3},{1,2},{2,1},{3,0},{4,7},{5,6},{6,5},{7,4},{8,11},{9,10},{10,... | collective-permute-start | bytes 786440 | tf_op jit(solution)/shard_map/ppermute | solution.py:19
  90.5 2.1 %copy-start.7 = (bf16[4,2,8,512]{3,2,1,0:T(8,128)(2,1)S(1)}, bf16[4,2,8,512]{3,2,1,0:T(8,128)(2,1)}, u32[]{:S(2)}) copy-start(bf16[4,2,8,512]{3,2,1,0:T(8,128)(2,1)} %get-tuple-element.28) | copy-start | bytes 196612
  90.5 3.5 %copy-start.6 = (bf16[4,2,8,512]{3,2,1,0:T(8,128)(2,1)S(1)}, bf16[4,2,8,512]{3,2,1,0:T(8,128)(2,1)}, u32[]{:S(2)}) copy-start(bf16[4,2,8,512]{3,2,1,0:T(8,128)(2,1)} %get-tuple-element.27) | copy-start | bytes 196612
  90.7 14.2 %collective-permute-start.23 = (bf16[64,4096]{1,0:T(8,128)(2,1)S(1)}, bf16[64,4096]{1,0:T(8,128)(2,1)S(1)}, u32[]{:S(2)}, u32[]{:S(2)}) collective-permute-start(bf16[64,4096]{1,0:T(8,128)(2,1)S(1)} %get-tuple-element.13), channel_id=1, source_target_pairs={{0,12},{4,8},{8,4},{12,0},{16,28},{20,24},{24,20},{28,16},{1,13},{... | collective-permute-start | bytes 1572872 | tf_op jit(solution)/shard_map/ppermute | solution.py:19
  90.8 24.0 %collective-permute-start.22 = (bf16[64,4096]{1,0:T(8,128)(2,1)S(1)}, bf16[64,4096]{1,0:T(8,128)(2,1)S(1)}, u32[]{:S(2)}, u32[]{:S(2)}) collective-permute-start(bf16[64,4096]{1,0:T(8,128)(2,1)S(1)} %get-tuple-element.14), channel_id=1, source_target_pairs={{0,8},{4,12},{8,0},{12,4},{16,24},{20,28},{24,16},{28,20},{1,9},{5... | collective-permute-start | bytes 1572872 | tf_op jit(solution)/shard_map/ppermute | solution.py:19
  91.6 23.2 %collective-permute-start.21 = (bf16[64,4096]{1,0:T(8,128)(2,1)S(1)}, bf16[64,4096]{1,0:T(8,128)(2,1)S(1)}, u32[]{:S(2)}, u32[]{:S(2)}) collective-permute-start(bf16[64,4096]{1,0:T(8,128)(2,1)S(1)} %get-tuple-element.15), channel_id=1, source_target_pairs={{0,4},{4,0},{8,12},{12,8},{16,20},{20,16},{24,28},{28,24},{1,5},{5... | collective-permute-start | bytes 1572872 | tf_op jit(solution)/shard_map/ppermute | solution.py:19
  92.7 30.2 %slice-start = ((s8[14680064]{0:T(1024)(128)(4,1)}), s8[4194304]{0:T(1024)(128)(4,1)S(1)}, s32[]{:S(2)}) async-start(s8[14680064]{0:T(1024)(128)(4,1)} %bitcast.75), calls=%async_computation | async-start | bytes 8388608
  93.3 82.7 %collective-permute-start.31 = (bf16[8,2,8,512]{3,2,1,0:T(8,128)(2,1)}, bf16[8,2,8,512]{3,2,1,0:T(8,128)(2,1)S(1)}, u32[]{:S(2)}, u32[]{:S(2)}) collective-permute-start(bf16[8,2,8,512]{3,2,1,0:T(8,128)(2,1)} %pad_maximum_fusion.6), channel_id=1, source_target_pairs={{0,8},{4,12},{8,0},{12,4},{16,24},{20,28},{24,16},{28,20},{1,9},{5... | collective-permute-start | bytes 393224 | tf_op jit(solution)/shard_map/ppermute | solution.py:19
  94.1 82.0 %collective-permute-start.32 = (bf16[8,2,8,512]{3,2,1,0:T(8,128)(2,1)S(1)}, bf16[8,2,8,512]{3,2,1,0:T(8,128)(2,1)}, u32[]{:S(2)}, u32[]{:S(2)}) collective-permute-start(bf16[8,2,8,512]{3,2,1,0:T(8,128)(2,1)S(1)} %pad_maximum_fusion.7), channel_id=1, source_target_pairs={{0,16},{4,20},{8,24},{12,28},{16,0},{20,4},{24,8},{28,12},{1,17},{... | collective-permute-start | bytes 393224 | tf_op jit(solution)/shard_map/ppermute | solution.py:19
  114.8 8.1 %slice-start.1 = ((s8[14680064]{0:T(1024)(128)(4,1)}), s8[4194304]{0:T(1024)(128)(4,1)S(1)}, s32[]{:S(2)}) async-start(s8[14680064]{0:T(1024)(128)(4,1)} %bitcast.75), calls=%async_computation.1 | async-start | bytes 8388608
  114.8 8.1 %slice-start.2 = ((s8[14680064]{0:T(1024)(128)(4,1)}), s8[4194304]{0:T(1024)(128)(4,1)S(1)}, s32[]{:S(2)}) async-start(s8[14680064]{0:T(1024)(128)(4,1)} %bitcast.75), calls=%async_computation.2 | async-start | bytes 8388608
  114.8 8.2 %slice-start.3 = ((s8[14680064]{0:T(1024)(128)(4,1)}), s8[2097152]{0:T(1024)(128)(4,1)S(1)}, s32[]{:S(2)}) async-start(s8[14680064]{0:T(1024)(128)(4,1)} %bitcast.75), calls=%async_computation.3 | async-start | bytes 4194304
  138.3 14.4 %collective-permute-start.26 = (bf16[64,4096]{1,0:T(8,128)(2,1)}, bf16[64,4096]{1,0:T(8,128)(2,1)}, u32[]{:S(2)}, u32[]{:S(2)}) collective-permute-start(bf16[64,4096]{1,0:T(8,128)(2,1)} %get-tuple-element.9), channel_id=1, source_target_pairs={{0,12},{4,8},{8,4},{12,0},{16,28},{20,24},{24,20},{28,16},{1,13},{... | collective-permute-start | bytes 1572872 | tf_op jit(solution)/shard_map/ppermute | solution.py:19
  140.2 25.4 %collective-permute-start.25 = (bf16[64,4096]{1,0:T(8,128)(2,1)}, bf16[64,4096]{1,0:T(8,128)(2,1)}, u32[]{:S(2)}, u32[]{:S(2)}) collective-permute-start(bf16[64,4096]{1,0:T(8,128)(2,1)} %get-tuple-element.10), channel_id=1, source_target_pairs={{0,8},{4,12},{8,0},{12,4},{16,24},{20,28},{24,16},{28,20},{1,9},{5... | collective-permute-start | bytes 1572872 | tf_op jit(solution)/shard_map/ppermute | solution.py:19
  141.5 24.2 %collective-permute-start.24 = (bf16[64,4096]{1,0:T(8,128)(2,1)}, bf16[64,4096]{1,0:T(8,128)(2,1)}, u32[]{:S(2)}, u32[]{:S(2)}) collective-permute-start(bf16[64,4096]{1,0:T(8,128)(2,1)} %get-tuple-element.11), channel_id=1, source_target_pairs={{0,4},{4,0},{8,12},{12,8},{16,20},{20,16},{24,28},{28,24},{1,5},{5... | collective-permute-start | bytes 1572872 | tf_op jit(solution)/shard_map/ppermute | solution.py:19
  152.8 24.3 %collective-permute-start.33 = (bf16[8,2,8,512]{3,2,1,0:T(8,128)(2,1)}, bf16[8,2,8,512]{3,2,1,0:T(8,128)(2,1)S(1)}, u32[]{:S(2)}, u32[]{:S(2)}) collective-permute-start(bf16[8,2,8,512]{3,2,1,0:T(8,128)(2,1)} %pad_maximum_fusion.8), channel_id=1, source_target_pairs={{0,24},{4,28},{8,16},{12,20},{16,8},{20,12},{24,0},{28,4},{1,25},{... | collective-permute-start | bytes 393224 | tf_op jit(solution)/shard_map/ppermute | solution.py:19
  165.6 2.0 %copy-start.5 = (bf16[64,4096]{1,0:T(8,128)(2,1)S(1)}, bf16[64,4096]{1,0:T(8,128)(2,1)}, u32[]{:S(2)}) copy-start(bf16[64,4096]{1,0:T(8,128)(2,1)} %get-tuple-element.8) | copy-start | bytes 1572868
  169.6 12.6 %collective-permute-start.29 = (bf16[128,1024]{1,0:T(8,128)(2,1)S(1)}, bf16[128,1024]{1,0:T(8,128)(2,1)S(1)}, u32[]{:S(2)}, u32[]{:S(2)}) collective-permute-start(bf16[128,1024]{1,0:T(8,128)(2,1)S(1)} %get-tuple-element.17), channel_id=1, source_target_pairs={{0,3},{1,2},{2,1},{3,0},{4,7},{5,6},{6,5},{7,4},{8,11},{9,10},{10,... | collective-permute-start | bytes 786440 | tf_op jit(solution)/shard_map/ppermute | solution.py:19
  172.1 22.0 %collective-permute-start.28 = (bf16[128,1024]{1,0:T(8,128)(2,1)S(1)}, bf16[128,1024]{1,0:T(8,128)(2,1)S(1)}, u32[]{:S(2)}, u32[]{:S(2)}) collective-permute-start(bf16[128,1024]{1,0:T(8,128)(2,1)S(1)} %get-tuple-element.18), channel_id=1, source_target_pairs={{0,2},{1,3},{2,0},{3,1},{4,6},{5,7},{6,4},{7,5},{8,10},{9,11},{10,... | collective-permute-start | bytes 786440 | tf_op jit(solution)/shard_map/ppermute | solution.py:19
  176.0 18.1 %collective-permute-start.27 = (bf16[128,1024]{1,0:T(8,128)(2,1)S(1)}, bf16[128,1024]{1,0:T(8,128)(2,1)S(1)}, u32[]{:S(2)}, u32[]{:S(2)}) collective-permute-start(bf16[128,1024]{1,0:T(8,128)(2,1)S(1)} %get-tuple-element.16), channel_id=1, source_target_pairs={{0,1},{1,0},{2,3},{3,2},{4,5},{5,4},{6,7},{7,6},{8,9},{9,8},{10,11... | collective-permute-start | bytes 786440 | tf_op jit(solution)/shard_map/ppermute | solution.py:19
  177.1 18.1 %copy-start.1 = (f32[1024,4]{0,1:T(4,128)S(1)}, f32[1024,4]{0,1:T(4,128)}, u32[]{:S(2)}) copy-start(f32[1024,4]{0,1:T(4,128)} %param.16) | copy-start | bytes 49156

commit v2 on v1

--- a/solution.py
+++ b/solution.py
@@ -1,3 +1,5 @@
+import functools
+
 import jax
 import jax.numpy as jnp
 from jax import lax
@@ -12,6 +14,9 @@
 BF = jnp.bfloat16
 F32 = jnp.float32
 I32 = jnp.int32
+MIB = 2**20
+VMEM = pl.BlockSpec(memory_space=pltpu.VMEM)
+SMEM = pl.BlockSpec(memory_space=pltpu.SMEM)
 
 
 def swap(x, axis, s):
@@ -25,6 +30,26 @@
 
 def pick(selector, rows):
     return jnp.dot(selector, rows, preferred_element_type=F32)
+
+
+def lanes(start, width):
+    return pl.ds(pl.multiple_of(start, 128), width)
+
+
+def local_call(kernel, in_specs, args, outs, scratch=(), vmem=24, flops=0, moved=0):
+    return pl.pallas_call(
+        kernel,
+        out_shape=outs,
+        in_specs=in_specs,
+        out_specs=[VMEM] * len(outs),
+        scratch_shapes=list(scratch),
+        compiler_params=pltpu.CompilerParams(vmem_limit_bytes=vmem * MIB),
+        cost_estimate=pl.CostEstimate(flops=flops, bytes_accessed=moved, transcendentals=0),
+    )(*args)
+
+
+def shape(dims, dtype):
+    return jax.ShapeDtypeStruct(dims, dtype)
 
 
 def page_kernel(pool, moved, rows, slot, table, length, out):
@@ -50,16 +75,172 @@
 
 def take_pages(pool, moved, rows, slot, table, length):
     pages = table.shape[0] // length.shape[0]
-    count = rows.shape[0]
+    outs = [shape((rows.shape[0], pages) + pool.shape[1:], pool.dtype)]
+    args = (pool, moved, rows, slot, table, length)
+    return local_call(page_kernel, [VMEM] * 2 + [SMEM] * 4, args, outs, moved=5 * MIB)[0]
+
+
+def project_kernel(half, *refs):
+    odd, selector, own, other = refs[:4]
+    blocks = refs[4 : 4 + 2 * half]
+    outs = refs[4 + 2 * half : 4 + 3 * half]
+    buf, left = refs[4 + 3 * half :]
+    at = 0
+    for block in blocks:
+        buf[at : at + block.shape[0]] = block[...]
+        at += block.shape[0]
+    picked = pick(selector[...], buf[...]).astype(BF)
+    first, second = picked[:, : own.shape[0]], picked[:, own.shape[0] :]
+
+    @pl.when(odd[0] == 0)
+    def _():
+        left[...] = pick(first, own[...]) + pick(second, other[...])
+
+    @pl.when(odd[0] == 1)
+    def _():
+        left[...] = pick(first, other[...]) + pick(second, own[...])
+
+    rows = outs[0].shape[0]
+    for t, out in enumerate(outs):
+        out[...] = left[t * rows : (t + 1) * rows].astype(out.dtype)
+
+
+def norm_kernel(half, experts, wide, *refs):
+    resid, gain, selector = refs[:3]
+    parts = refs[3 : 3 + half]
+    hidden_out, early = refs[3 + half : 5 + half]
+    late = refs[5 + half :]
+    hidden = resid[...]
+    for part in parts:
+        hidden = hidden + part[...].astype(F32)
+    hidden_out[...] = hidden
+    scaled = (hidden * gain[...]).astype(BF)
+    early[...] = scaled[:, :wide]
+    chosen = pick(selector[...], scaled[:, wide:]).astype(BF)
+    for s in range(experts):
+        late[s][...] = chosen[s * SLOTS : (s + 1) * SLOTS]
+
+
+def dispatch_kernel(ne, experts, *refs):
+    place, selector = refs[:2]
+    blocks, outs = refs[2 : 2 + ne], refs[2 + ne :]
+    wide = blocks[0].shape[1]
+    for s in range(ne):
+        chosen = pick(selector[...], blocks[s][...]).astype(BF)
+        columns = lanes((place[0] ^ s) * wide, wide)
+        for t in range(experts):
+            outs[t][:, columns] = chosen[t * SLOTS : (t + 1) * SLOTS]
+
+
+def gate_up_kernel(ne, experts, *refs):
+    place, inverse_gain = refs[:2]
+    early, late = refs[2 : 2 + experts], refs[2 + experts : 2 + experts + ne]
+    gate, up, out, rows, scale = refs[2 + experts + ne :]
+    wide, rest = early[0].shape[1] // ne, late[0].shape[1]
+    feats = wide + rest
+
+    @pl.when(pl.program_id(0) == 0)
+    def _():
+        for t in range(experts):
+            for e in range(ne):
+                rows[t * SLOTS : (t + 1) * SLOTS, e * feats : e * feats + wide] = early[t][
+                    :, e * wide : (e + 1) * wide
+                ]
+        for s in range(ne):
+            rows[:, lanes((place[0] ^ s) * feats + wide, rest)] = late[s][...]
+        total = jnp.zeros((rows.shape[0], 1), F32)
+        step = min(1024, rows.shape[1])
+        for c in range(0, rows.shape[1], step):
+            plain = rows[:, c : c + step].astype(F32) * inverse_gain[:, c : c + step]
+            total = total + jnp.sum(plain * plain, axis=1, keepdims=True)
+        scale[...] = lax.rsqrt(total / D + EPSILON)
+
+    gate_h = pick(rows[...], gate[0]) * scale[...]
+    up_h = pick(rows[...], up[0]) * scale[...]
+    out[...] = (gate_h / (1.0 + jnp.exp(-gate_h)) * up_h).astype(out.dtype)
+
+
+def gate_up(place, inverse_gain, early, late, w_gate, w_up, ne):
+    hidden = w_gate.shape[2]
+    slots = late[0].shape[0]
+    tile = 256 if hidden % 256 == 0 else 128
+    whole = lambda a: pl.BlockSpec(a.shape, lambda f: (0,) * a.ndim)
+    weight = pl.BlockSpec((1, D, tile), lambda f: (0, 0, f))
     return pl.pallas_call(
-        page_kernel,
-        out_shape=jax.ShapeDtypeStruct((count, pages) + pool.shape[1:], pool.dtype),
-        in_specs=[pl.BlockSpec(memory_space=pltpu.VMEM)] * 2
-        + [pl.BlockSpec(memory_space=pltpu.SMEM)] * 4,
-        out_specs=pl.BlockSpec(memory_space=pltpu.VMEM),
-        compiler_params=pltpu.CompilerParams(vmem_limit_bytes=16 * 2**20),
-        cost_estimate=pl.CostEstimate(flops=0, bytes_accessed=6 * 2**20, transcendentals=0),
-    )(pool, moved, rows, slot, table, length)
+        functools.partial(gate_up_kernel, ne, len(early)),
+        grid=(hidden // tile,),
+        out_shape=shape((slots, hidden), BF),
+        in_specs=[SMEM] + [whole(a) for a in (inverse_gain, *early, *late)] + [weight] * 2,
+        out_specs=pl.BlockSpec((slots, tile), lambda f: (0, f)),
+        scratch_shapes=[pltpu.VMEM((slots, D), BF), pltpu.VMEM((slots, 1), F32)],
+        compiler_params=pltpu.CompilerParams(vmem_limit_bytes=40 * MIB),
+        cost_estimate=pl.CostEstimate(
+            flops=4 * slots * D * hidden, bytes_accessed=4 * D * hidden, transcendentals=0
+        ),
+    )(place, inverse_gain, *early, *late, w_gate, w_up)
+
+
+def down_late_kernel(ne, place, active, weight, *outs):
+    value = pick(active[...], weight[0]).astype(BF)
+    for s in range(ne):
+
+        @pl.when(pl.program_id(0) == s)
+        def _(s=s):
+            outs[s][...] = value
+
+
+def down_early_kernel(ne, place, active, weight, *outs):
+    value = pick(active[...], weight[0]).astype(BF)
+    wide = weight.shape[2]
+    for t, out in enumerate(outs):
+        out[:, lanes(pl.program_id(0) * wide, wide)] = value[t * SLOTS : (t + 1) * SLOTS]
+
+
+def down_call(kernel, place, active, w_down, width, column, out_shapes, ne):
+    slots, hidden = active.shape
+    return pl.pallas_call(
+        functools.partial(kernel, ne),
+        grid_spec=pltpu.PrefetchScalarGridSpec(
+            num_scalar_prefetch=1,
+            grid=(ne,),
+            in_specs=[
+                pl.BlockSpec((slots, hidden), lambda g, place: (0, 0)),
+                pl.BlockSpec((1, hidden, width), lambda g, place: (0, 0, column(g, place))),
+            ],
+            out_specs=[pl.BlockSpec(o.shape, lambda g, place: (0, 0)) for o in out_shapes],
+        ),
+        out_shape=out_shapes,
+        compiler_params=pltpu.CompilerParams(vmem_limit_bytes=32 * MIB),
+        cost_estimate=pl.CostEstimate(
+            flops=2 * slots * hidden * width * ne,
+            bytes_accessed=2 * hidden * width * ne,
+            transcendentals=0,
+        ),
+    )(place, active, w_down)
+
+
+def weigh_kernel(ne, experts, *refs):
+    place, high, low = refs[:3]
+    blocks, outs, buf, total = refs[3 : 3 + experts], refs[3 + experts : 3 + experts + ne], *refs[3 + experts + ne :]
+    for t in range(experts):
+        buf[t * SLOTS : (t + 1) * SLOTS] = blocks[t][...]
+    total[...] = pick(high[...], buf[...]) + pick(low[...], buf[...])
+    wide = outs[0].shape[1]
+    for s in range(ne):
+        outs[s][...] = total[:, lanes((place[0] ^ s) * wide, wide)].astype(outs[s].dtype)
+
+
+def finish_kernel(ne, experts, wide, *refs):
+    high, low, hidden = refs[:3]
+    early, late = refs[3 : 3 + ne], refs[3 + ne : 3 + ne + experts]
+    out, buf = refs[3 + ne + experts :]
+    first = hidden[:, :wide]
+    for block in early:
+        first = first + block[...].astype(F32)
+    out[:, :wide] = first
+    for t in range(experts):
+        buf[t * SLOTS : (t + 1) * SLOTS] = late[t][...]
+    out[:, wide:] = hidden[:, wide:] + pick(high[...], buf[...]) + pick(low[...], buf[...])
 
 
 def body(
@@ -87,18 +268,19 @@
     feats = residual.shape[1]
     kblock = D // half
     experts = n // 2
+    rest = feats // 2
+    wide = feats - rest
+    place = ze.reshape(1).astype(I32)
 
     def column_block(x, s):
         return lax.dynamic_slice_in_dim(x, (q ^ s) * kblock, kblock, axis=1)
 
     attn_blocks = [column_block(attention_out, s) for s in range(half)]
+    attn_blocks = list(lax.optimization_barrier(tuple(attn_blocks)))
+    came_from, _ = lax.optimization_barrier((came_from, attn_blocks[0]))
     attn_blocks = attn_blocks[:1] + [swap(attn_blocks[s], "req", 2 * s) for s in range(1, half)]
     w_other = swap(w_out, "req", 1)
-    w_pair = jnp.where(
-        k == 0,
-        jnp.concatenate([w_out, w_other], axis=0),
-        jnp.concatenate([w_other, w_out], axis=0),
-    )
+    gain_all = lax.all_gather(norm_gain, "exp", tiled=True)
 
     local = jnp.arange(rows, dtype=I32)
     in_new = came_from[None, :] == (me * rows + local)[:, None]
@@ -153,38 +335,7 @@
         hot(own_at, rows + 2 * MIG * half), jnp.concatenate([residual, moved_resid], axis=0)
     )
 
-    attn_new = pick(
-        hot(attn_at, half * (rows + n_pair)), jnp.concatenate(attn_blocks + late_blocks, axis=0)
-    ).astype(BF)
-    part = jnp.dot(attn_new, w_pair, preferred_element_type=F32).reshape(half, rows, feats)
-    hidden = resid_new + part[0]
-    for s in range(1, half):
-        hidden = hidden + swap(part[s].astype(BF), "req", 2 * s).astype(F32)
-
-    scaled = hidden * norm_gain[None, :]
-    scaled_rows = scaled.astype(BF)
-    stats = jnp.concatenate(
-        [
-            jnp.sum(hidden * hidden, axis=1, keepdims=True),
-            jnp.dot(scaled, router_w, precision=lax.Precision.HIGHEST),
-        ],
-        axis=1,
-    )
-    stats_all = stats
-    for s in range(1, ne):
-        stats_all = stats_all + swap(stats, "exp", s)
-    full = jnp.zeros((rows, D), BF)
-    for s in range(ne):
-        block = swap(scaled_rows, "exp", s) if s else scaled_rows
-        full = lax.dynamic_update_slice_in_dim(full, block, (ze ^ s) * feats, axis=1)
-    inverse = lax.rsqrt(stats_all[:, 0] / D + EPSILON)
-    logits = stats_all[:, 1:] * inverse[:, None]
     expert_ids = jnp.arange(experts, dtype=I32)
-    chosen = jnp.sum(
-        jnp.where(routes[:, :, None] == expert_ids[None, None, :], logits[:, None, :], 0.0), axis=2
-    )
-    gates = jax.nn.sigmoid(chosen - chosen[:, ::-1])
-
     names = routes[:, :, None] == expert_ids[None, None, :]
     named = jnp.any(names, axis=1)
     before = jnp.sum(
@@ -193,39 +344,116 @@
     rank = jnp.sum(jnp.where(names, before[:, None, :], 0), axis=2)
     slot_of = ((routes ^ (me % experts)) * SLOTS + rank).astype(I32)
     slot_ids = jnp.arange(experts * SLOTS, dtype=I32)
-    slot_hot = slot_ids[:, None, None] == slot_of[None, :, :]
-    slot_pick = jnp.any(slot_hot, axis=2)
-    slot_scale = jnp.sum(jnp.where(slot_pick, inverse[None, :], 0.0), axis=1)
-    outgoing = (pick(slot_pick.astype(BF), full) * slot_scale[:, None]).astype(BF)
-    outgoing = outgoing.reshape(experts, SLOTS, D)
-    arrived = jnp.concatenate(
-        [swap(outgoing[s], "req", s) if s else outgoing[s] for s in range(experts)], axis=0
-    )
-
-    gate_h = jnp.dot(arrived, w_gate[0], preferred_element_type=F32)
-    up_h = jnp.dot(arrived, w_up[0], preferred_element_type=F32)
-    active = (jax.nn.silu(gate_h) * up_h).astype(BF)
-    down = jnp.dot(active, w_down[0], preferred_element_type=F32).astype(BF)
-    down = down.reshape(experts, SLOTS, D)
-    back = jnp.concatenate(
-        [swap(down[s], "req", s) if s else down[s] for s in range(experts)], axis=0
-    )
+    slot_pick = jnp.any(slot_ids[:, None, None] == slot_of[None, :, :], axis=2).astype(BF)
+
+    total_rows = half * (rows + n_pair)
+    selector = hot(attn_at, total_rows)
+    parts = local_call(
+        functools.partial(project_kernel, half),
+        [SMEM] + [VMEM] * (3 + 2 * half),
+        (k.reshape(1).astype(I32), selector, w_out, w_other, *attn_blocks, *late_blocks),
+        [shape((rows, feats), F32)] + [shape((rows, feats), BF)] * (half - 1),
+        [pltpu.VMEM((total_rows, kblock), BF), pltpu.VMEM((half * rows, feats), F32)],
+        flops=2 * half * rows * (total_rows + feats) * kblock,
+        moved=6 * MIB,
+    )
+    parts = [parts[0]] + [swap(parts[s], "req", 2 * s) for s in range(1, half)]
+
+    normed = local_call(
+        functools.partial(norm_kernel, half, experts, wide),
+        [VMEM] * (3 + half),
+        (resid_new, norm_gain[None, :], slot_pick, *parts),
+        [shape((rows, feats), F32), shape((rows, wide), BF)] + [shape((SLOTS, rest), BF)] * experts,
+        flops=2 * experts * SLOTS * rows * rest,
+        moved=3 * MIB,
+    )
+    hidden, early = normed[:2]
+    early_blocks = [early] + [swap(early, "exp", s) for s in range(1, ne)]
+    late = [normed[2 + s] if s == 0 else swap(normed[2 + s], "req", s) for s in range(experts)]
+    late = jnp.concatenate(late, axis=0)
+    late_rows = [late] + [swap(late, "exp", s) for s in range(1, ne)]
+    outgoing = local_call(
+        functools.partial(dispatch_kernel, ne, experts),
+        [SMEM] + [VMEM] * (1 + ne),
+        (place, slot_pick, *early_blocks),
+        [shape((SLOTS, ne * wide), BF)] * experts,
+        flops=2 * experts * SLOTS * rows * ne * wide,
+        moved=3 * MIB,
+    )
+    early_rows = [swap(outgoing[s], "req", s) if s else outgoing[s] for s in range(experts)]
+
+    stats = jnp.concatenate(
+        [
+            jnp.sum(hidden * hidden, axis=1, keepdims=True),
+            jnp.dot(hidden * norm_gain[None, :], router_w, precision=lax.Precision.HIGHEST),
+        ],
+        axis=1,
+    )
+    stats = jnp.sum(lax.all_gather(stats, "exp"), axis=0)
+    logits = stats[:, 1:] * lax.rsqrt(stats[:, :1] / D + EPSILON)
+    chosen = jnp.sum(jnp.where(names, logits[:, None, :], 0.0), axis=2)
+    gates = jax.nn.sigmoid(chosen - chosen[:, ::-1])
     gate_slots = jnp.sum(
         jnp.where(slot_of[:, :, None] == slot_ids[None, None, :], gates[:, :, None], 0.0), axis=1
     )
     gate_high = gate_slots.astype(BF)
     gate_low = (gate_slots - gate_high.astype(F32)).astype(BF)
-    weighted = pick(gate_high, back) + pick(gate_low, back)
-    mixed = hidden + lax.dynamic_slice_in_dim(weighted, ze * feats, feats, axis=1)
-    weighted = weighted.astype(BF)
-    for s in range(1, ne):
-        block = lax.dynamic_slice_in_dim(weighted, (ze ^ s) * feats, feats, axis=1)
-        mixed = mixed + swap(block, "exp", s).astype(F32)
 
     table = page_table.reshape(-1)
     none = jnp.full((n_send,), -1, I32)
-    moving_pages = take_pages(page_pool, page_pool[:2].reshape((1, 2) + page_pool.shape[1:]), send_row, none, table, cache_len)
+    no_rows = page_pool[:2].reshape((1, 2) + page_pool.shape[1:])
+    moving_pages = take_pages(page_pool, no_rows, send_row, none, table, cache_len)
+    moving_pages, _ = lax.optimization_barrier((moving_pages, outgoing[0]))
     moved_pages = relay(moving_pages)
+
+    active = gate_up(place, 1.0 / gain_all[None, :], early_rows, late_rows, w_gate, w_up, ne)
+    per_owner = feats // rest
+    down_late = down_call(
+        down_late_kernel,
+        place,
+        active,
+        w_down,
+        rest,
+        lambda g, place: (g ^ place[0]) * per_owner + per_owner - 1,
+        [shape((experts * SLOTS, rest), BF)] * ne,
+        ne,
+    )
+    late_sum = down_late[0].astype(F32)
+    for s in range(1, ne):
+        late_sum = late_sum + swap(down_late[s], "exp", s).astype(F32)
+    late_sum = late_sum.astype(BF).reshape(experts, SLOTS, rest)
+    late_back = [swap(late_sum[s], "req", s) if s else late_sum[s] for s in range(experts)]
+    down_early = down_call(
+        down_early_kernel,
+        place,
+        active,
+        w_down,
+        wide,
+        lambda g, place: g * per_owner,
+        [shape((SLOTS, ne * wide), BF)] * experts,
+        ne,
+    )
+    early_back = [swap(down_early[s], "req", s) if s else down_early[s] for s in range(experts)]
+    weighted = local_call(
+        functools.partial(weigh_kernel, ne, experts),
+        [SMEM] + [VMEM] * (2 + experts),
+        (place, gate_high, gate_low, *early_back),
+        [shape((rows, wide), F32)] + [shape((rows, wide), BF)] * (ne - 1),
+        [pltpu.VMEM((experts * SLOTS, ne * wide), BF), pltpu.VMEM((rows, ne * wide), F32)],
+        flops=4 * rows * experts * SLOTS * ne * wide,
+        moved=3 * MIB,
+    )
+    early_parts = [weighted[0]] + [swap(weighted[s], "exp", s) for s in range(1, ne)]
+    mixed = local_call(
+        functools.partial(finish_kernel, ne, experts, wide),
+        [VMEM] * (3 + ne + experts),
+        (gate_high, gate_low, hidden, *early_parts, *late_back),
+        [shape((rows, feats), F32)],
+        [pltpu.VMEM((experts * SLOTS, rest), BF)],
+        flops=4 * rows * experts * SLOTS * rest,
+        moved=2 * MIB,
+    )[0]
+
     new_pages = take_pages(
         page_pool,
         moved_pages,

time: 196 us -> 181 us (0.923)
  waiting for transfers between devices: 85 us -> 46.3 us
  matrix products: 37.4 us -> 3.37 us
  Pallas kernels: 6.53 us -> 37.5 us
  blocking collectives: 0 us -> 27.1 us
  starting transfers between devices: 39.2 us -> 49.6 us
  other arithmetic: 7.81 us -> 2.49 us
  local copies, waits for them, and re-layouts: 18 us -> 12.8 us
    ppermute x34 -> x43, waiting for transfers between devices: 85 us -> 46.3 us  [swap(): return lax.ppermute(x, axis, [(i, i ^ s) for i in range(n)])]
    pallas_call x2 -> x10, Pallas kernels: 6.53 us -> 37.5 us  [the longest x1 16.2 us: gate_up(): pl.pallas_call(functools.partial(gate_up_kernel, ne, len(early)), grid=(h...]
    dot_general x5 -> x1, matrix products: 28.9 us -> 0.51 us  [body(): jnp.dot(hidden * norm_gain[None, :], router_w, precision=lax.Precision.HI...]
    all_gather x0 -> x2, blocking collectives: none -> 27.1 us  [the longest x1 13.8 us: body(): gain_all = lax.all_gather(norm_gain, 'exp', tiled=True)]
    ppermute x34 -> x43, starting transfers between devices: 39.2 us -> 49.6 us  [swap(): return lax.ppermute(x, axis, [(i, i ^ s) for i in range(n)])]
    dot_general x6 -> x3, matrix products: 8.51 us -> 2.86 us  [pick(): return jnp.dot(selector, rows, preferred_element_type=F32)]
    concatenate x1, local copies, waits for them, and re-layouts: 0.11 us -> 4.09 us  [body(): jnp.concatenate([residual, moved_resid], axis=0)]
    slice x3 -> x1, local copies, waits for them, and re-layouts: 3.55 us -> 0.02 us  [body(): late_sum[s]]
  transfers between devices with their start and end apart: 34 -> 43, of which waited for: 11 -> 14; matrix products, arithmetic and copies ran while one was open for 31% -> 6% of each run, Pallas kernels for 3% -> 19%
where the time goes in v2:
time: 181 us
  starting transfers between devices  49.6 us (27%)
  waiting for transfers between devices  46.3 us (26%)
  Pallas kernels  37.5 us (21%)
  blocking collectives  27.1 us (15%)
  local copies, waits for them, and re-layouts  12.8 us (7%)
  matrix products  3.37 us (2%)
  other arithmetic  2.49 us (1%)
    ppermute x43, starting transfers between devices, swap(): return lax.ppermute(x, axis, [(i, i ^ s) for i in range(n)])  49.6 us
    ppermute x43, waiting for transfers between devices, swap(): return lax.ppermute(x, axis, [(i, i ^ s) for i in range(n)])  46.3 us
    pallas_call x1, Pallas kernels, gate_up(): pl.pallas_call(functools.partial(gate_up_kernel, ne, len(early)), grid=(h...  16.2 us
    pallas_call x7, Pallas kernels, local_call(): pl.pallas_call(kernel, out_shape=outs, in_specs=in_specs, out_specs=[VMEM...  14.8 us
    all_gather x1, blocking collectives, body(): gain_all = lax.all_gather(norm_gain, 'exp', tiled=True)  13.8 us
    all_gather x1, blocking collectives, body(): stats = jnp.sum(lax.all_gather(stats, 'exp'), axis=0)  13.3 us
    pallas_call x2, Pallas kernels, down_call(): pl.pallas_call(functools.partial(kernel, ne), grid_spec=pltpu.PrefetchSca...  6.53 us
    unnamed x57, local copies, waits for them, and re-layouts  4.53 us
  transfers between devices with their start and end apart: 43, of which 14 were waited for; matrix products, arithmetic and copies ran while one was open for 6% of the time, Pallas kernels for 19%

profile of v2, /device:TPU:0, one launch (start us, length us, event | category | flops | bytes accessed | tf_op | source)
XLA Modules:
  0.0 180.6 jit_solution(15659928741118147948)
XLA Ops:
  0.7 2.3 %constant_dynamic-slice_fusion.4 = (bf16[128,1024]{1,0:T(8,128)(2,1)}, bf16[128,1024]{1,0:T(8,128)(2,1)}, bf16[128,1024]{1,0:T(8,128)(2,1)}, bf16[128,1024]{1,0:T(8,128)(2,1)}) fusion(bf16[128,4096]{1,0:T(8,128)(2,1)} %param.13, s32[]{:T(128)S(6)} %select_n.202, s32[]{:T(128)S(6)} %select_n.201, s32[]{:T(128)S(6)} %select_n.200, s32[]{:T(128)S(6)} %select_n.199), kind=kLoop, calls=%fused_computation.89 | loop fusion | bytes 2097168 | tf_op jit(solution)/shard_map/dynamic_slice | solution.py:276
  3.7 0.6 slice.123
  4.8 2.9 %collective-permute-start.5 = (bf16[128,1024]{1,0:T(8,128)(2,1)}, bf16[128,1024]{1,0:T(8,128)(2,1)S(1)}, u32[]{:S(2)}, u32[]{:S(2)}) collective-permute-start(bf16[128,1024]{1,0:T(8,128)(2,1)} %get-tuple-element.36), channel_id=1, source_target_pairs={{0,8},{4,12},{8,0},{12,4},{16,24},{20,28},{24,16},{28,20},{1,9},{5... | collective-permute-start | bytes 786440 | tf_op jit(solution)/shard_map/ppermute | solution.py:24
  7.8 1.5 collective-permute-start.6
  10.3 13.8 %all_gather.11 = f32[4096]{0:T(1024)S(1)} all-gather(f32[1024]{0:T(1024)S(1)} %copy-done.6), channel_id=1, replica_groups=mesh['req'=8,'exp'=4] {'exp'}, dimensions={0}, use_global_device_ids=true | all-gather | bytes 20480 | tf_op jit(solution)/shard_map/all_gather | solution.py:283
  24.2 0.6 bitcast_select_fusion.1
  24.7 1.5 convolution_convert_fusion
  26.3 0.8 fusion.30
  27.1 0.5 collective-permute-done.8
  27.7 1.6 collective-permute-start.9
  29.2 2.4 %collective-permute-done.9.refs_9_ = bf16[16,1024]{1,0:T(8,128)(2,1)S(1)} collective-permute-done((bf16[16,1024]{1,0:T(8,128)(2,1)S(1)}, bf16[16,1024]{1,0:T(8,128)(2,1)S(1)}, u32[]{:S(2)}, u32[]{:S(2)}) %collective-permute-start.9) | collective-permute-done | bytes 32800 | tf_op jit(solution)/shard_map/ppermute | solution.py:24
  31.6 1.5 collective-permute-start.10
  33.2 2.4 %collective-permute-done.10.refs_10_ = bf16[16,1024]{1,0:T(8,128)(2,1)S(1)} collective-permute-done((bf16[16,1024]{1,0:T(8,128)(2,1)S(1)}, bf16[16,1024]{1,0:T(8,128)(2,1)S(1)}, u32[]{:S(2)}, u32[]{:S(2)}) %collective-permute-start.10) | collective-permute-done | bytes 32800 | tf_op jit(solution)/shard_map/ppermute | solution.py:24
  35.6 2.4 %collective-permute-start.11 = (bf16[16,1024]{1,0:T(8,128)(2,1)S(1)}, bf16[16,1024]{1,0:T(8,128)(2,1)S(1)}, u32[]{:S(2)}, u32[]{:S(2)}) collective-permute-start(bf16[16,1024]{1,0:T(8,128)(2,1)S(1)} %get-tuple-element.87), channel_id=1, source_target_pairs={{0,24},{4,28},{8,16},{12,20},{16,8},{20,12},{24,0},{28,4},{1,25},{... | collective-permute-start | bytes 98312 | tf_op jit(solution)/shard_map/ppermute | solution.py:24
  38.0 2.4 %collective-permute-done.11.refs_11_ = bf16[16,1024]{1,0:T(8,128)(2,1)S(1)} collective-permute-done((bf16[16,1024]{1,0:T(8,128)(2,1)S(1)}, bf16[16,1024]{1,0:T(8,128)(2,1)S(1)}, u32[]{:S(2)}, u32[]{:S(2)}) %collective-permute-start.11) | collective-permute-done | bytes 32800 | tf_op jit(solution)/shard_map/ppermute | solution.py:24
  40.4 1.5 collective-permute-start.1
  41.9 0.7 copy-done.8
  42.6 1.5 collective-permute-start.2
  44.1 0.7 copy-done.10
  45.3 0.9 copy-done.5
  46.2 0.9 copy-done.9
  47.2 0.9 copy-done.11
  48.1 4.8 %shard_map.140 = (f32[128,1024]{1,0:T(8,128)S(1)}, bf16[128,1024]{1,0:T(8,128)(2,1)}, bf16[128,1024]{1,0:T(8,128)(2,1)}, bf16[128,1024]{1,0:T(8,128)(2,1)}) custom-call(s32[1]{0:T(128)} %bitcast.8.refs_0_, bf16[512,576]{1,0:T(8,128)(2,1)S(1)} %fusion.refs_1_, bf16[512,1024]{1,0:T(8,128)(2,1)} %refs_2_.1, bf16[512,1024]{1,0:T(8,128)(2,1)} %collective-permute-done.4.refs_3_, ...), custom_call_target="tpu_custom_call" | custom-call | flops 1677721600 | bytes 6291456 | tf_op jit(solution)/shard_map/pallas_call | solution.py:40
  52.9 1.5 collective-permute-start.12
  54.4 1.5 collective-permute-start.13
  56.8 1.3 shard_map.148
  58.2 4.1 %concatenate.59 = bf16[160,1024]{1,0:T(8,128)(2,1)} concatenate(bf16[128,1024]{1,0:T(8,128)(2,1)} %param.14, bf16[4,1024]{1,0:T(4,128)(2,1)S(1)} %get-tuple-element.97, bf16[4,1024]{1,0:T(4,128)(2,1)S(1)} %get-tuple-element.97, bf16[8,1024]{1,0:T(8,128)(2,1)S(1)} %collective-permute-done.1, bf16[8,1024]{1,0:T(8,128)(2,1)S(1)} %collective-permute-done.2, ...), dimensions={0} | concatenate | bytes 655360 | tf_op jit(solution)/shard_map/concatenate | solution.py:335
  62.3 1.2 fusion.5.refs_0_
  63.6 0.6 collective-permute-done.13.refs_5_
  64.2 1.5 shard_map.141
  65.7 1.6 collective-permute-start.15
  67.3 2.4 %collective-permute-start.16 = (bf16[128,512]{1,0:T(8,128)(2,1)S(1)}, bf16[128,512]{1,0:T(8,128)(2,1)S(1)}, u32[]{:S(2)}, u32[]{:S(2)}) collective-permute-start(bf16[128,512]{1,0:T(8,128)(2,1)S(1)} %get-tuple-element.44.refs_2_), channel_id=1, source_target_pairs={{0,2},{1,3},{2,0},{3,1},{4,6},{5,7},{6,4},{7,5},{8,10},{9,11},{10,... | collective-permute-start | bytes 393224 | tf_op jit(solution)/shard_map/ppermute | solution.py:24
  70.3 0.5 fusion.1
  70.8 13.3 %all-gather = f32[512,5]{0,1:T(8,128)S(1)} all-gather(f32[128,5]{0,1:T(8,128)S(1)} %pad_maximum_fusion.6), channel_id=2, replica_groups=mesh['req'=8,'exp'=4] {'exp'}, dimensions={0}, use_global_device_ids=true | all-gather | bytes 12800 | tf_op jit(solution)/shard_map/all_gather | solution.py:392
  84.3 1.3 collective-permute-start.22
  85.7 1.0 collective-permute-start.23
  86.7 2.2 %collective-permute-done.22 = bf16[64,512]{1,0:T(8,128)(2,1)S(1)} collective-permute-done((bf16[64,512]{1,0:T(8,128)(2,1)S(1)}, bf16[64,512]{1,0:T(8,128)(2,1)S(1)}, u32[]{:S(2)}, u32[]{:S(2)}) %collective-permute-start.22) | collective-permute-done | bytes 65568 | tf_op jit(solution)/shard_map/ppermute | solution.py:24
  88.9 1.0 collective-permute-done.23
  89.9 1.6 collective-permute-start.24
  91.7 2.4 %collective-permute-start.25 = (bf16[256,512]{1,0:T(8,128)(2,1)S(1)}, bf16[256,512]{1,0:T(8,128)(2,1)S(1)}, u32[]{:S(2)}, u32[]{:S(2)}) collective-permute-start(bf16[256,512]{1,0:T(8,128)(2,1)S(1)} %constant_dynamic-update-slice_fusion.refs_6_), channel_id=1, source_target_pairs={{0,2},{1,3},{2,0},{3,1},{4,6},{5,7},{6,4},{7,5},{8,10},{9,11},{10,... | collective-permute-start | bytes 786440 | tf_op jit(solution)/shard_map/ppermute | solution.py:24
  95.1 1.3 collective-permute-start.19
  96.3 6.6 %collective-permute-done.24.refs_7_ = bf16[256,512]{1,0:T(8,128)(2,1)S(1)} collective-permute-done((bf16[256,512]{1,0:T(8,128)(2,1)S(1)}, bf16[256,512]{1,0:T(8,128)(2,1)S(1)}, u32[]{:S(2)}, u32[]{:S(2)}) %collective-permute-start.24) | collective-permute-done | bytes 262176 | tf_op jit(solution)/shard_map/ppermute | solution.py:24
  103.1 9.9 %collective-permute-done.25.refs_8_ = bf16[256,512]{1,0:T(8,128)(2,1)S(1)} collective-permute-done((bf16[256,512]{1,0:T(8,128)(2,1)S(1)}, bf16[256,512]{1,0:T(8,128)(2,1)S(1)}, u32[]{:S(2)}, u32[]{:S(2)}) %collective-permute-start.25) | collective-permute-done | bytes 262176 | tf_op jit(solution)/shard_map/ppermute | solution.py:24
  113.1 16.2 %shard_map.143.active = bf16[256,1792]{1,0:T(8,128)(2,1)S(1)} custom-call(s32[1]{0:T(128)} %bitcast.14.refs_0_.place, f32[1,4096]{1,0:T(1,128)S(1)} %bitcast.67, bf16[64,2048]{1,0:T(8,128)(2,1)S(1)} %get-tuple-element.45.refs_2_, bf16[64,2048]{1,0:T(8,128)(2,1)S(1)} %collective-permute-done.18.refs_3_, bf16[64,2048]{1,0:T(8,128)(2,1)S(1)} %collective-permute-done.19.refs_4_, ...), custom_call_target="tpu_custom_call" | custom-call | flops 7516192768 | bytes 29360128 | tf_op jit(solution)/shard_map/pallas_call | solution.py:169
  129.4 3.2 %shard_map.144 = (bf16[64,2048]{1,0:T(8,128)(2,1)S(1)}, bf16[64,2048]{1,0:T(8,128)(2,1)S(1)}, bf16[64,2048]{1,0:T(8,128)(2,1)S(1)}, bf16[64,2048]{1,0:T(8,128)(2,1)S(1)}) custom-call(s32[1]{0:T(128)} %bitcast.14.refs_0_.place, bf16[256,1792]{1,0:T(8,128)(2,1)S(1)} %shard_map.143.active, bf16[1,1792,4096]{2,1,0:T(8,128)(2,1)S(1)} %bitcast.66), custom_call_target="tpu_custom_call" | custom-call | flops 1879048192 | bytes 7340032 | tf_op jit(solution)/shard_map/pallas_call | solution.py:201
  132.6 0.6 collective-permute-start.27
  133.2 1.2 collective-permute-start.28
  134.6 3.3 %shard_map.146 = (bf16[256,512]{1,0:T(8,128)(2,1)S(1)}, bf16[256,512]{1,0:T(8,128)(2,1)S(1)}, bf16[256,512]{1,0:T(8,128)(2,1)S(1)}, bf16[256,512]{1,0:T(8,128)(2,1)S(1)}) custom-call(s32[1]{0:T(128)} %bitcast.14.refs_0_.place, bf16[256,1792]{1,0:T(8,128)(2,1)S(1)} %shard_map.143.active, bf16[1,1792,4096]{2,1,0:T(8,128)(2,1)S(1)} %bitcast.66), custom_call_target="tpu_custom_call" | custom-call | flops 1879048192 | bytes 7340032 | tf_op jit(solution)/shard_map/pallas_call | solution.py:201
  138.0 1.9 %collective-permute-start.35 = (bf16[256,512]{1,0:T(8,128)(2,1)S(1)}, bf16[256,512]{1,0:T(8,128)(2,1)S(1)}, u32[]{:S(2)}, u32[]{:S(2)}) collective-permute-start(bf16[256,512]{1,0:T(8,128)(2,1)S(1)} %get-tuple-element.64), channel_id=1, source_target_pairs={{0,3},{1,2},{2,1},{3,0},{4,7},{5,6},{6,5},{7,4},{8,11},{9,10},{10,... | collective-permute-start | bytes 786440 | tf_op jit(solution)/shard_map/ppermute | solution.py:24
  139.9 1.3 collective-permute-start.40
  141.2 8.7 %collective-permute-done.40 = bf16[8,2,8,512]{3,2,1,0:T(8,128)(2,1)S(1)} collective-permute-done((bf16[8,2,8,512]{3,2,1,0:T(8,128)(2,1)S(1)}, bf16[8,2,8,512]{3,2,1,0:T(8,128)(2,1)S(1)}, u32[]{:S(2)}, u32[]{:S(2)}) %collective-permute-start.40) | collective-permute-done | bytes 131104 | tf_op jit(solution)/shard_map/ppermute | solution.py:24
  149.9 5.6 %collective-permute-start.34 = (bf16[256,512]{1,0:T(8,128)(2,1)S(1)}, bf16[256,512]{1,0:T(8,128)(2,1)S(1)}, u32[]{:S(2)}, u32[]{:S(2)}) collective-permute-start(bf16[256,512]{1,0:T(8,128)(2,1)S(1)} %get-tuple-element.63), channel_id=1, source_target_pairs={{0,2},{1,3},{2,0},{3,1},{4,6},{5,7},{6,4},{7,5},{8,10},{9,11},{10,... | collective-permute-start | bytes 786440 | tf_op jit(solution)/shard_map/ppermute | solution.py:24
  155.6 1.6 collective-permute-start.41
  157.2 1.2 collective-permute-start.42
  158.4 0.5 shard_map.145
  158.9 2.1 %collective-permute-start.30 = (bf16[128,512]{1,0:T(8,128)(2,1)S(1)}, bf16[128,512]{1,0:T(8,128)(2,1)S(1)}, u32[]{:S(2)}, u32[]{:S(2)}) collective-permute-start(bf16[128,512]{1,0:T(8,128)(2,1)S(1)} %get-tuple-element.58), channel_id=1, source_target_pairs={{0,1},{1,0},{2,3},{3,2},{4,5},{5,4},{6,7},{7,6},{8,9},{9,8},{10,11... | collective-permute-start | bytes 393224 | tf_op jit(solution)/shard_map/ppermute | solution.py:24
  161.0 6.4 %collective-permute-done.34 = bf16[256,512]{1,0:T(8,128)(2,1)S(1)} collective-permute-done((bf16[256,512]{1,0:T(8,128)(2,1)S(1)}, bf16[256,512]{1,0:T(8,128)(2,1)S(1)}, u32[]{:S(2)}, u32[]{:S(2)}) %collective-permute-start.34) | collective-permute-done | bytes 262176 | tf_op jit(solution)/shard_map/ppermute | solution.py:24
  167.4 1.3 collective-permute-done.33
  168.7 1.5 collective-permute-start.32
  170.5 1.3 collective-permute-start.37
  171.8 0.9 collective-permute-start.38
  172.7 5.2 %shard_map.149 = bf16[128,2,8,512]{3,2,1,0:T(8,128)(2,1)} custom-call(bf16[256,8,512]{2,1,0:T(8,128)(2,1)S(1)} %copy-done.2, bf16[32,2,8,512]{3,2,1,0:T(8,128)(2,1)S(1)} %constant_dynamic-update-slice_fusion.4.moved, s32[128]{0:T(128)S(1)} %get-tuple-element.98.rows, s32[128]{0:T(128)S(1)} %get-tuple-element.66.slot, s32[256]{0:T(256)S(1)} %reshape.502.table, ...), custom_call_target="tpu_custom_call" | custom-call | bytes 5242880 | tf_op jit(solution)/shard_map/pallas_call | solution.py:40
  177.9 1.6 collective-permute-done.31.refs_5_
  179.6 1.1 shard_map.147
  (152 shorter events, 6.4 us)
Async XLA Ops:
  0.6 69.6 %copy-start = (f32[1024,4]{0,1:T(4,128)S(1)}, f32[1024,4]{0,1:T(4,128)}, u32[]{:S(2)}) copy-start(f32[1024,4]{0,1:T(4,128)} %param.16) | copy-start | bytes 49156
  0.6 2.4 %copy-start.14 = (s32[1024]{0:T(1024)S(1)}, s32[1024]{0:T(1024)}, u32[]{:S(2)}) copy-start(s32[1024]{0:T(1024)} %param.21) | copy-start | bytes 12292
  0.7 2.9 %copy-start.13 = (bf16[128,1024]{1,0:T(8,128)(2,1)S(1)}, bf16[128,1024]{1,0:T(8,128)(2,1)}, u32[]{:S(2)}) copy-start(bf16[128,1024]{1,0:T(8,128)(2,1)} %param.14) | copy-start | bytes 786436
  0.7 9.2 %copy-start.15 = (s32[128,2]{0,1:T(2,128)S(1)}, s32[128,2]{0,1:T(2,128)}, u32[]{:S(2)}) copy-start(s32[128,2]{0,1:T(2,128)} %param.22) | copy-start | bytes 3076
  0.7 9.6 %copy-start.6 = (f32[1024]{0:T(1024)S(1)}, f32[1024]{0:T(1024)}, u32[]{:S(2)}) copy-start(f32[1024]{0:T(1024)} %param.17) | copy-start | bytes 12292
  0.7 23.4 %copy-start.2 = (bf16[256,8,512]{2,1,0:T(8,128)(2,1)S(1)}, bf16[256,8,512]{2,1,0:T(8,128)(2,1)}, u32[]{:S(2)}) copy-start(bf16[256,8,512]{2,1,0:T(8,128)(2,1)} %pool.3) | copy-start | bytes 6291460
  3.5 6.7 %copy-start.17 = (s32[128]{0:T(128)}, s32[128]{0:T(128)S(1)}, u32[]{:S(2)}) copy-start(s32[128]{0:T(128)S(1)} %compare_select_fusion.1) | copy-start | bytes 1540
  4.3 21.9 %collective-permute-start = (bf16[16,1024]{1,0:T(8,128)(2,1)}, bf16[16,1024]{1,0:T(8,128)(2,1)}, u32[]{:S(2)}, u32[]{:S(2)}) collective-permute-start(bf16[16,1024]{1,0:T(8,128)(2,1)} %slice.123), channel_id=1, source_target_pairs={{0,4},{4,0},{8,12},{12,8},{16,20},{20,16},{24,28},{28,24},{1,5},{5... | collective-permute-start | bytes 98312 | tf_op jit(solution)/shard_map/ppermute | solution.py:24
  4.8 40.5 %collective-permute-start.4 = (bf16[512,1024]{1,0:T(8,128)(2,1)}, bf16[512,1024]{1,0:T(8,128)(2,1)}, u32[]{:S(2)}, u32[]{:S(2)}) collective-permute-start(bf16[512,1024]{1,0:T(8,128)(2,1)} %refs_2_.1), channel_id=1, source_target_pairs={{0,4},{4,0},{8,12},{12,8},{16,20},{20,16},{24,28},{28,24},{1,5},{5... | collective-permute-start | bytes 3145736 | tf_op jit(solution)/shard_map/ppermute | solution.py:24
  4.8 37.0 %collective-permute-start.5 = (bf16[128,1024]{1,0:T(8,128)(2,1)}, bf16[128,1024]{1,0:T(8,128)(2,1)S(1)}, u32[]{:S(2)}, u32[]{:S(2)}) collective-permute-start(bf16[128,1024]{1,0:T(8,128)(2,1)} %get-tuple-element.36), channel_id=1, source_target_pairs={{0,8},{4,12},{8,0},{12,4},{16,24},{20,28},{24,16},{28,20},{1,9},{5... | collective-permute-start | bytes 786440 | tf_op jit(solution)/shard_map/ppermute | solution.py:24
  7.8 36.3 %collective-permute-start.6 = (bf16[128,1024]{1,0:T(8,128)(2,1)}, bf16[128,1024]{1,0:T(8,128)(2,1)S(1)}, u32[]{:S(2)}, u32[]{:S(2)}) collective-permute-start(bf16[128,1024]{1,0:T(8,128)(2,1)} %get-tuple-element.37), channel_id=1, source_target_pairs={{0,16},{4,20},{8,24},{12,28},{16,0},{20,4},{24,8},{28,12},{1,17},{... | collective-permute-start | bytes 786440 | tf_op jit(solution)/shard_map/ppermute | solution.py:24
  9.3 36.0 %collective-permute-start.7 = (bf16[128,1024]{1,0:T(8,128)(2,1)}, bf16[128,1024]{1,0:T(8,128)(2,1)}, u32[]{:S(2)}, u32[]{:S(2)}) collective-permute-start(bf16[128,1024]{1,0:T(8,128)(2,1)} %get-tuple-element.38), channel_id=1, source_target_pairs={{0,24},{4,28},{8,16},{12,20},{16,8},{20,12},{24,0},{28,4},{1,25},{... | collective-permute-start | bytes 786440 | tf_op jit(solution)/shard_map/ppermute | solution.py:24
  26.2 1.4 collective-permute-start.8
  27.7 4.0 %collective-permute-start.9 = (bf16[16,1024]{1,0:T(8,128)(2,1)S(1)}, bf16[16,1024]{1,0:T(8,128)(2,1)S(1)}, u32[]{:S(2)}, u32[]{:S(2)}) collective-permute-start(bf16[16,1024]{1,0:T(8,128)(2,1)S(1)} %get-tuple-element.89), channel_id=1, source_target_pairs={{0,8},{4,12},{8,0},{12,4},{16,24},{20,28},{24,16},{28,20},{1,9},{5... | collective-permute-start | bytes 98312 | tf_op jit(solution)/shard_map/ppermute | solution.py:24
  31.6 3.9 %collective-permute-start.10 = (bf16[16,1024]{1,0:T(8,128)(2,1)S(1)}, bf16[16,1024]{1,0:T(8,128)(2,1)S(1)}, u32[]{:S(2)}, u32[]{:S(2)}) collective-permute-start(bf16[16,1024]{1,0:T(8,128)(2,1)S(1)} %get-tuple-element.88), channel_id=1, source_target_pairs={{0,16},{4,20},{8,24},{12,28},{16,0},{20,4},{24,8},{28,12},{1,17},{... | collective-permute-start | bytes 98312 | tf_op jit(solution)/shard_map/ppermute | solution.py:24
  35.6 4.8 %collective-permute-start.11 = (bf16[16,1024]{1,0:T(8,128)(2,1)S(1)}, bf16[16,1024]{1,0:T(8,128)(2,1)S(1)}, u32[]{:S(2)}, u32[]{:S(2)}) collective-permute-start(bf16[16,1024]{1,0:T(8,128)(2,1)S(1)} %get-tuple-element.87), channel_id=1, source_target_pairs={{0,24},{4,28},{8,16},{12,20},{16,8},{20,12},{24,0},{28,4},{1,25},{... | collective-permute-start | bytes 98312 | tf_op jit(solution)/shard_map/ppermute | solution.py:24
  40.4 15.6 %collective-permute-start.1 = (bf16[8,1024]{1,0:T(8,128)(2,1)S(1)}, bf16[8,1024]{1,0:T(8,128)(2,1)S(1)}, u32[]{:S(2)}, u32[]{:S(2)}) collective-permute-start(bf16[8,1024]{1,0:T(8,128)(2,1)S(1)} %pad_maximum_fusion.3), channel_id=1, source_target_pairs={{0,8},{4,12},{8,0},{12,4},{16,24},{20,28},{24,16},{28,20},{1,9},{5... | collective-permute-start | bytes 49160 | tf_op jit(solution)/shard_map/ppermute | solution.py:24
  42.6 15.6 %collective-permute-start.2 = (bf16[8,1024]{1,0:T(8,128)(2,1)S(1)}, bf16[8,1024]{1,0:T(8,128)(2,1)S(1)}, u32[]{:S(2)}, u32[]{:S(2)}) collective-permute-start(bf16[8,1024]{1,0:T(8,128)(2,1)S(1)} %pad_maximum_fusion.4), channel_id=1, source_target_pairs={{0,16},{4,20},{8,24},{12,28},{16,0},{20,4},{24,8},{28,12},{1,17},{... | collective-permute-start | bytes 49160 | tf_op jit(solution)/shard_map/ppermute | solution.py:24
  44.8 13.4 %collective-permute-start.3 = (bf16[8,1024]{1,0:T(8,128)(2,1)S(1)}, bf16[8,1024]{1,0:T(8,128)(2,1)S(1)}, u32[]{:S(2)}, u32[]{:S(2)}) collective-permute-start(bf16[8,1024]{1,0:T(8,128)(2,1)S(1)} %pad_maximum_fusion.5), channel_id=1, source_target_pairs={{0,24},{4,28},{8,16},{12,20},{16,8},{20,12},{24,0},{28,4},{1,25},{... | collective-permute-start | bytes 49160 | tf_op jit(solution)/shard_map/ppermute | solution.py:24
  45.3 1.0 copy-start.5
  48.1 8.3 %copy-start.18 = (s32[128]{0:T(128)S(1)}, s32[128]{0:T(128)}, u32[]{:S(2)}) copy-start(s32[128]{0:T(128)} %copy-done.17) | copy-start | bytes 1540
  48.1 8.4 %copy-start.20 = (s32[128,2]{0,1:T(2,128)S(1)}, s32[128,2]{0,1:T(2,128)}, u32[]{:S(2)}) copy-start(s32[128,2]{0,1:T(2,128)} %param.19) | copy-start | bytes 3076
  48.1 8.7 %copy-start.7 = (s32[128]{0:T(128)S(1)}, s32[128]{0:T(128)}, u32[]{:S(2)}) copy-start(s32[128]{0:T(128)} %length.3) | copy-start | bytes 1540
  52.9 9.4 %copy-start.19 = (s32[128]{0:T(128)S(1)}, s32[128]{0:T(128)}, u32[]{:S(2)}) copy-start(s32[128]{0:T(128)} %get-tuple-element.99) | copy-start | bytes 1540
  52.9 10.6 %collective-permute-start.12 = (bf16[128,1024]{1,0:T(8,128)(2,1)}, bf16[128,1024]{1,0:T(8,128)(2,1)}, u32[]{:S(2)}, u32[]{:S(2)}) collective-permute-start(bf16[128,1024]{1,0:T(8,128)(2,1)} %get-tuple-element.40), channel_id=1, source_target_pairs={{0,8},{4,12},{8,0},{12,4},{16,24},{20,28},{24,16},{28,20},{1,9},{5... | collective-permute-start | bytes 786440 | tf_op jit(solution)/shard_map/ppermute | solution.py:24
  54.4 9.7 %collective-permute-start.13 = (bf16[128,1024]{1,0:T(8,128)(2,1)}, bf16[128,1024]{1,0:T(8,128)(2,1)}, u32[]{:S(2)}, u32[]{:S(2)}) collective-permute-start(bf16[128,1024]{1,0:T(8,128)(2,1)} %get-tuple-element.41), channel_id=1, source_target_pairs={{0,16},{4,20},{8,24},{12,28},{16,0},{20,4},{24,8},{28,12},{1,17},{... | collective-permute-start | bytes 786440 | tf_op jit(solution)/shard_map/ppermute | solution.py:24
  55.9 8.2 %collective-permute-start.14 = (bf16[128,1024]{1,0:T(8,128)(2,1)}, bf16[128,1024]{1,0:T(8,128)(2,1)}, u32[]{:S(2)}, u32[]{:S(2)}) collective-permute-start(bf16[128,1024]{1,0:T(8,128)(2,1)} %get-tuple-element.42), channel_id=1, source_target_pairs={{0,24},{4,28},{8,16},{12,20},{16,8},{20,12},{24,0},{28,4},{1,25},{... | collective-permute-start | bytes 786440 | tf_op jit(solution)/shard_map/ppermute | solution.py:24
  62.3 21.9 %copy-start.16 = (s32[128,2]{0,1:T(2,128)S(1)}, s32[128,2]{0,1:T(2,128)}, u32[]{:S(2)}) copy-start(s32[128,2]{0,1:T(2,128)} %param.22) | copy-start | bytes 3076
  65.6 4.6 %copy-start.3 = (f32[128,1024]{1,0:T(8,128)}, f32[128,1024]{1,0:T(8,128)S(1)}, u32[]{:S(2)}) copy-start(f32[128,1024]{1,0:T(8,128)S(1)} %get-tuple-element.43.refs_2_) | copy-start | bytes 1572868
  65.7 5.1 %copy-start.12 = (bf16[64,512]{1,0:T(8,128)(2,1)}, bf16[64,512]{1,0:T(8,128)(2,1)S(1)}, u32[]{:S(2)}) copy-start(bf16[64,512]{1,0:T(8,128)(2,1)S(1)} %get-tuple-element.50) | copy-start | bytes 196612
  65.7 28.4 %collective-permute-start.15 = (bf16[128,512]{1,0:T(8,128)(2,1)S(1)}, bf16[128,512]{1,0:T(8,128)(2,1)S(1)}, u32[]{:S(2)}, u32[]{:S(2)}) collective-permute-start(bf16[128,512]{1,0:T(8,128)(2,1)S(1)} %get-tuple-element.44.refs_2_), channel_id=1, source_target_pairs={{0,1},{1,0},{2,3},{3,2},{4,5},{5,4},{6,7},{7,6},{8,9},{9,8},{10,11... | collective-permute-start | bytes 393224 | tf_op jit(solution)/shard_map/ppermute | solution.py:24
  67.3 27.2 %collective-permute-start.16 = (bf16[128,512]{1,0:T(8,128)(2,1)S(1)}, bf16[128,512]{1,0:T(8,128)(2,1)S(1)}, u32[]{:S(2)}, u32[]{:S(2)}) collective-permute-start(bf16[128,512]{1,0:T(8,128)(2,1)S(1)} %get-tuple-element.44.refs_2_), channel_id=1, source_target_pairs={{0,2},{1,3},{2,0},{3,1},{4,6},{5,7},{6,4},{7,5},{8,10},{9,11},{10,... | collective-permute-start | bytes 393224 | tf_op jit(solution)/shard_map/ppermute | solution.py:24
  69.7 24.9 %collective-permute-start.17 = (bf16[128,512]{1,0:T(8,128)(2,1)S(1)}, bf16[128,512]{1,0:T(8,128)(2,1)S(1)}, u32[]{:S(2)}, u32[]{:S(2)}) collective-permute-start(bf16[128,512]{1,0:T(8,128)(2,1)S(1)} %get-tuple-element.44.refs_2_), channel_id=1, source_target_pairs={{0,3},{1,2},{2,1},{3,0},{4,7},{5,6},{6,5},{7,4},{8,11},{9,10},{10,... | collective-permute-start | bytes 393224 | tf_op jit(solution)/shard_map/ppermute | solution.py:24
  84.2 1.5 collective-permute-start.21
  84.3 4.6 %collective-permute-start.22 = (bf16[64,512]{1,0:T(8,128)(2,1)S(1)}, bf16[64,512]{1,0:T(8,128)(2,1)S(1)}, u32[]{:S(2)}, u32[]{:S(2)}) collective-permute-start(bf16[64,512]{1,0:T(8,128)(2,1)S(1)} %get-tuple-element.51), channel_id=1, source_target_pairs={{0,8},{4,12},{8,0},{12,4},{16,24},{20,28},{24,16},{28,20},{1,9},{5... | collective-permute-start | bytes 196616 | tf_op jit(solution)/shard_map/ppermute | solution.py:24
  85.7 4.2 %collective-permute-start.23 = (bf16[64,512]{1,0:T(8,128)(2,1)S(1)}, bf16[64,512]{1,0:T(8,128)(2,1)S(1)}, u32[]{:S(2)}, u32[]{:S(2)}) collective-permute-start(bf16[64,512]{1,0:T(8,128)(2,1)S(1)} %get-tuple-element.52), channel_id=1, source_target_pairs={{0,12},{4,8},{8,4},{12,0},{16,28},{20,24},{24,20},{28,16},{1,13},{... | collective-permute-start | bytes 196616 | tf_op jit(solution)/shard_map/ppermute | solution.py:24
  89.9 13.0 %collective-permute-start.24 = (bf16[256,512]{1,0:T(8,128)(2,1)S(1)}, bf16[256,512]{1,0:T(8,128)(2,1)S(1)}, u32[]{:S(2)}, u32[]{:S(2)}) collective-permute-start(bf16[256,512]{1,0:T(8,128)(2,1)S(1)} %constant_dynamic-update-slice_fusion.refs_6_), channel_id=1, source_target_pairs={{0,1},{1,0},{2,3},{3,2},{4,5},{5,4},{6,7},{7,6},{8,9},{9,8},{10,11... | collective-permute-start | bytes 786440 | tf_op jit(solution)/shard_map/ppermute | solution.py:24
  91.7 21.4 %collective-permute-start.25 = (bf16[256,512]{1,0:T(8,128)(2,1)S(1)}, bf16[256,512]{1,0:T(8,128)(2,1)S(1)}, u32[]{:S(2)}, u32[]{:S(2)}) collective-permute-start(bf16[256,512]{1,0:T(8,128)(2,1)S(1)} %constant_dynamic-update-slice_fusion.refs_6_), channel_id=1, source_target_pairs={{0,2},{1,3},{2,0},{3,1},{4,6},{5,7},{6,4},{7,5},{8,10},{9,11},{10,... | collective-permute-start | bytes 786440 | tf_op jit(solution)/shard_map/ppermute | solution.py:24
  94.1 19.0 %collective-permute-start.26 = (bf16[256,512]{1,0:T(8,128)(2,1)S(1)}, bf16[256,512]{1,0:T(8,128)(2,1)S(1)}, u32[]{:S(2)}, u32[]{:S(2)}) collective-permute-start(bf16[256,512]{1,0:T(8,128)(2,1)S(1)} %constant_dynamic-update-slice_fusion.refs_6_), channel_id=1, source_target_pairs={{0,3},{1,2},{2,1},{3,0},{4,7},{5,6},{6,5},{7,4},{8,11},{9,10},{10,... | collective-permute-start | bytes 786440 | tf_op jit(solution)/shard_map/ppermute | solution.py:24
  95.0 18.1 %collective-permute-start.18 = (bf16[64,2048]{1,0:T(8,128)(2,1)S(1)}, bf16[64,2048]{1,0:T(8,128)(2,1)S(1)}, u32[]{:S(2)}, u32[]{:S(2)}) collective-permute-start(bf16[64,2048]{1,0:T(8,128)(2,1)S(1)} %get-tuple-element.46), channel_id=1, source_target_pairs={{0,4},{4,0},{8,12},{12,8},{16,20},{20,16},{24,28},{28,24},{1,5},{5... | collective-permute-start | bytes 786440 | tf_op jit(solution)/shard_map/ppermute | solution.py:24
  95.1 18.0 %collective-permute-start.19 = (bf16[64,2048]{1,0:T(8,128)(2,1)S(1)}, bf16[64,2048]{1,0:T(8,128)(2,1)S(1)}, u32[]{:S(2)}, u32[]{:S(2)}) collective-permute-start(bf16[64,2048]{1,0:T(8,128)(2,1)S(1)} %get-tuple-element.47), channel_id=1, source_target_pairs={{0,8},{4,12},{8,0},{12,4},{16,24},{20,28},{24,16},{28,20},{1,9},{5... | collective-permute-start | bytes 786440 | tf_op jit(solution)/shard_map/ppermute | solution.py:24
  103.0 10.1 %collective-permute-start.20 = (bf16[64,2048]{1,0:T(8,128)(2,1)S(1)}, bf16[64,2048]{1,0:T(8,128)(2,1)S(1)}, u32[]{:S(2)}, u32[]{:S(2)}) collective-permute-start(bf16[64,2048]{1,0:T(8,128)(2,1)S(1)} %get-tuple-element.48), channel_id=1, source_target_pairs={{0,12},{4,8},{8,4},{12,0},{16,28},{20,24},{24,20},{28,16},{1,13},{... | collective-permute-start | bytes 786440 | tf_op jit(solution)/shard_map/ppermute | solution.py:24
  103.1 26.3 %slice-start = ((s8[14680064]{0:T(1024)(128)(4,1)}), s8[4194304]{0:T(1024)(128)(4,1)S(1)}, s32[]{:S(2)}) async-start(s8[14680064]{0:T(1024)(128)(4,1)} %bitcast.65), calls=%async_computation | async-start | bytes 8388608
  113.1 26.8 %collective-permute-start.39 = (bf16[16,2,8,512]{3,2,1,0:T(8,128)(2,1)S(1)}, bf16[16,2,8,512]{3,2,1,0:T(8,128)(2,1)S(1)}, u32[]{:S(2)}, u32[]{:S(2)}) collective-permute-start(bf16[16,2,8,512]{3,2,1,0:T(8,128)(2,1)S(1)} %slice.115), channel_id=1, source_target_pairs={{0,4},{4,0},{8,12},{12,8},{16,20},{20,16},{24,28},{28,24},{1,5},{5... | collective-permute-start | bytes 786440 | tf_op jit(solution)/shard_map/ppermute | solution.py:24
  113.1 16.3 %slice-start.1 = ((s8[14680064]{0:T(1024)(128)(4,1)}), s8[4194304]{0:T(1024)(128)(4,1)S(1)}, s32[]{:S(2)}) async-start(s8[14680064]{0:T(1024)(128)(4,1)} %bitcast.65), calls=%async_computation.1 | async-start | bytes 8388608
  113.1 16.3 %slice-start.2 = ((s8[14680064]{0:T(1024)(128)(4,1)}), s8[4194304]{0:T(1024)(128)(4,1)S(1)}, s32[]{:S(2)}) async-start(s8[14680064]{0:T(1024)(128)(4,1)} %bitcast.65), calls=%async_computation.2 | async-start | bytes 8388608
  113.1 16.3 %slice-start.3 = ((s8[14680064]{0:T(1024)(128)(4,1)}), s8[2097152]{0:T(1024)(128)(4,1)S(1)}, s32[]{:S(2)}) async-start(s8[14680064]{0:T(1024)(128)(4,1)} %bitcast.65), calls=%async_computation.3 | async-start | bytes 4194304
  132.6 22.9 %collective-permute-start.27 = (bf16[64,2048]{1,0:T(8,128)(2,1)S(1)}, bf16[64,2048]{1,0:T(8,128)(2,1)S(1)}, u32[]{:S(2)}, u32[]{:S(2)}) collective-permute-start(bf16[64,2048]{1,0:T(8,128)(2,1)S(1)} %get-tuple-element.54), channel_id=1, source_target_pairs={{0,4},{4,0},{8,12},{12,8},{16,20},{20,16},{24,28},{28,24},{1,5},{5... | collective-permute-start | bytes 786440 | tf_op jit(solution)/shard_map/ppermute | solution.py:24
  133.2 22.4 %collective-permute-start.28 = (bf16[64,2048]{1,0:T(8,128)(2,1)S(1)}, bf16[64,2048]{1,0:T(8,128)(2,1)S(1)}, u32[]{:S(2)}, u32[]{:S(2)}) collective-permute-start(bf16[64,2048]{1,0:T(8,128)(2,1)S(1)} %get-tuple-element.55), channel_id=1, source_target_pairs={{0,8},{4,12},{8,0},{12,4},{16,24},{20,28},{24,16},{28,20},{1,9},{5... | collective-permute-start | bytes 786440 | tf_op jit(solution)/shard_map/ppermute | solution.py:24
  134.4 22.8 %collective-permute-start.29 = (bf16[64,2048]{1,0:T(8,128)(2,1)S(1)}, bf16[64,2048]{1,0:T(8,128)(2,1)S(1)}, u32[]{:S(2)}, u32[]{:S(2)}) collective-permute-start(bf16[64,2048]{1,0:T(8,128)(2,1)S(1)} %get-tuple-element.56), channel_id=1, source_target_pairs={{0,12},{4,8},{8,4},{12,0},{16,28},{20,24},{24,20},{28,16},{1,13},{... | collective-permute-start | bytes 786440 | tf_op jit(solution)/shard_map/ppermute | solution.py:24
  138.0 20.9 %collective-permute-start.35 = (bf16[256,512]{1,0:T(8,128)(2,1)S(1)}, bf16[256,512]{1,0:T(8,128)(2,1)S(1)}, u32[]{:S(2)}, u32[]{:S(2)}) collective-permute-start(bf16[256,512]{1,0:T(8,128)(2,1)S(1)} %get-tuple-element.64), channel_id=1, source_target_pairs={{0,3},{1,2},{2,1},{3,0},{4,7},{5,6},{6,5},{7,4},{8,11},{9,10},{10,... | collective-permute-start | bytes 786440 | tf_op jit(solution)/shard_map/ppermute | solution.py:24
  139.9 10.0 %collective-permute-start.40 = (bf16[8,2,8,512]{3,2,1,0:T(8,128)(2,1)S(1)}, bf16[8,2,8,512]{3,2,1,0:T(8,128)(2,1)S(1)}, u32[]{:S(2)}, u32[]{:S(2)}) collective-permute-start(bf16[8,2,8,512]{3,2,1,0:T(8,128)(2,1)S(1)} %pad_maximum_fusion), channel_id=1, source_target_pairs={{0,8},{4,12},{8,0},{12,4},{16,24},{20,28},{24,16},{28,20},{1,9},{5... | collective-permute-start | bytes 393224 | tf_op jit(solution)/shard_map/ppermute | solution.py:24
  149.9 17.5 %collective-permute-start.34 = (bf16[256,512]{1,0:T(8,128)(2,1)S(1)}, bf16[256,512]{1,0:T(8,128)(2,1)S(1)}, u32[]{:S(2)}, u32[]{:S(2)}) collective-permute-start(bf16[256,512]{1,0:T(8,128)(2,1)S(1)} %get-tuple-element.63), channel_id=1, source_target_pairs={{0,2},{1,3},{2,0},{3,1},{4,6},{5,7},{6,4},{7,5},{8,10},{9,11},{10,... | collective-permute-start | bytes 786440 | tf_op jit(solution)/shard_map/ppermute | solution.py:24
  155.5 13.2 %collective-permute-start.33 = (bf16[256,512]{1,0:T(8,128)(2,1)S(1)}, bf16[256,512]{1,0:T(8,128)(2,1)S(1)}, u32[]{:S(2)}, u32[]{:S(2)}) collective-permute-start(bf16[256,512]{1,0:T(8,128)(2,1)S(1)} %get-tuple-element.62), channel_id=1, source_target_pairs={{0,1},{1,0},{2,3},{3,2},{4,5},{5,4},{6,7},{7,6},{8,9},{9,8},{10,11... | collective-permute-start | bytes 786440 | tf_op jit(solution)/shard_map/ppermute | solution.py:24
  155.6 14.8 %collective-permute-start.41 = (bf16[8,2,8,512]{3,2,1,0:T(8,128)(2,1)S(1)}, bf16[8,2,8,512]{3,2,1,0:T(8,128)(2,1)S(1)}, u32[]{:S(2)}, u32[]{:S(2)}) collective-permute-start(bf16[8,2,8,512]{3,2,1,0:T(8,128)(2,1)S(1)} %pad_maximum_fusion.1), channel_id=1, source_target_pairs={{0,16},{4,20},{8,24},{12,28},{16,0},{20,4},{24,8},{28,12},{1,17},{... | collective-permute-start | bytes 393224 | tf_op jit(solution)/shard_map/ppermute | solution.py:24
  157.2 13.3 %collective-permute-start.42 = (bf16[8,2,8,512]{3,2,1,0:T(8,128)(2,1)S(1)}, bf16[8,2,8,512]{3,2,1,0:T(8,128)(2,1)S(1)}, u32[]{:S(2)}, u32[]{:S(2)}) collective-permute-start(bf16[8,2,8,512]{3,2,1,0:T(8,128)(2,1)S(1)} %pad_maximum_fusion.2), channel_id=1, source_target_pairs={{0,24},{4,28},{8,16},{12,20},{16,8},{20,12},{24,0},{28,4},{1,25},{... | collective-permute-start | bytes 393224 | tf_op jit(solution)/shard_map/ppermute | solution.py:24
  158.9 19.1 %collective-permute-start.30 = (bf16[128,512]{1,0:T(8,128)(2,1)S(1)}, bf16[128,512]{1,0:T(8,128)(2,1)S(1)}, u32[]{:S(2)}, u32[]{:S(2)}) collective-permute-start(bf16[128,512]{1,0:T(8,128)(2,1)S(1)} %get-tuple-element.58), channel_id=1, source_target_pairs={{0,1},{1,0},{2,3},{3,2},{4,5},{5,4},{6,7},{7,6},{8,9},{9,8},{10,11... | collective-permute-start | bytes 393224 | tf_op jit(solution)/shard_map/ppermute | solution.py:24
  167.4 12.2 %collective-permute-start.31 = (bf16[128,512]{1,0:T(8,128)(2,1)S(1)}, bf16[128,512]{1,0:T(8,128)(2,1)S(1)}, u32[]{:S(2)}, u32[]{:S(2)}) collective-permute-start(bf16[128,512]{1,0:T(8,128)(2,1)S(1)} %get-tuple-element.59), channel_id=1, source_target_pairs={{0,2},{1,3},{2,0},{3,1},{4,6},{5,7},{6,4},{7,5},{8,10},{9,11},{10,... | collective-permute-start | bytes 393224 | tf_op jit(solution)/shard_map/ppermute | solution.py:24
  168.7 10.9 %collective-permute-start.32 = (bf16[128,512]{1,0:T(8,128)(2,1)S(1)}, bf16[128,512]{1,0:T(8,128)(2,1)S(1)}, u32[]{:S(2)}, u32[]{:S(2)}) collective-permute-start(bf16[128,512]{1,0:T(8,128)(2,1)S(1)} %get-tuple-element.60), channel_id=1, source_target_pairs={{0,3},{1,2},{2,1},{3,0},{4,7},{5,6},{6,5},{7,4},{8,11},{9,10},{10,... | collective-permute-start | bytes 393224 | tf_op jit(solution)/shard_map/ppermute | solution.py:24
  170.4 1.4 collective-permute-start.36
  170.5 7.4 %collective-permute-start.37 = (bf16[64,512]{1,0:T(8,128)(2,1)S(1)}, bf16[64,512]{1,0:T(8,128)(2,1)S(1)}, u32[]{:S(2)}, u32[]{:S(2)}) collective-permute-start(bf16[64,512]{1,0:T(8,128)(2,1)S(1)} %get-tuple-element.84), channel_id=1, source_target_pairs={{0,8},{4,12},{8,0},{12,4},{16,24},{20,28},{24,16},{28,20},{1,9},{5... | collective-permute-start | bytes 196616 | tf_op jit(solution)/shard_map/ppermute | solution.py:24
  171.8 6.1 %collective-permute-start.38 = (bf16[64,512]{1,0:T(8,128)(2,1)S(1)}, bf16[64,512]{1,0:T(8,128)(2,1)S(1)}, u32[]{:S(2)}, u32[]{:S(2)}) collective-permute-start(bf16[64,512]{1,0:T(8,128)(2,1)S(1)} %get-tuple-element.83), channel_id=1, source_target_pairs={{0,12},{4,8},{8,4},{12,0},{16,28},{20,24},{24,20},{28,16},{1,13},{... | collective-permute-start | bytes 196616 | tf_op jit(solution)/shard_map/ppermute | solution.py:24
  172.7 6.8 %copy-start.4 = (f32[128,1024]{1,0:T(8,128)S(1)}, f32[128,1024]{1,0:T(8,128)}, u32[]{:S(2)}) copy-start(f32[128,1024]{1,0:T(8,128)} %copy-done.3) | copy-start | bytes 1572868
  172.7 7.9 %copy-start.1 = (f32[1024,4]{0,1:T(4,128)S(1)}, f32[1024,4]{0,1:T(4,128)}, u32[]{:S(2)}) copy-start(f32[1024,4]{0,1:T(4,128)} %param.16) | copy-start | bytes 49156
  (4 other events, 3.3 us)

commit v3 on v2

v3 whole, which is shorter than its diff:
```python
import functools

import jax
import jax.numpy as jnp
from jax import lax
from jax.experimental import pallas as pl
from jax.experimental.pallas import tpu as pltpu
from jax.sharding import PartitionSpec as P

D = 4096
SLOTS = 64
MIG = 4
EPSILON = 1e-05
BF = jnp.bfloat16
F32 = jnp.float32
I32 = jnp.int32
MIB = 2**20
VMEM = pl.BlockSpec(memory_space=pltpu.VMEM)
SMEM = pl.BlockSpec(memory_space=pltpu.SMEM)
HBM = pl.BlockSpec(memory_space=pltpu.HBM)


def swap(x, axis, s):
    n = lax.axis_size(axis)
    return lax.ppermute(x, axis, [(i, i ^ s) for i in range(n)])


def hot(index, count):
    return (index[..., None] == jnp.arange(count, dtype=I32)).astype(BF)


def pick(selector, rows):
    return jnp.dot(selector, rows, preferred_element_type=F32)


def lanes(start, width):
    return pl.ds(pl.multiple_of(start, 128), width)


def local_call(kernel, in_specs, args, outs, scratch=(), vmem=16, flops=0, moved=0):
    return pl.pallas_call(
        kernel,
        out_shape=outs,
        in_specs=in_specs,
        out_specs=[VMEM] * len(outs),
        scratch_shapes=list(scratch),
        compiler_params=pltpu.CompilerParams(vmem_limit_bytes=vmem * MIB),
        cost_estimate=pl.CostEstimate(flops=flops, bytes_accessed=moved, transcendentals=0),
    )(*args)


def shape(dims, dtype):
    return jax.ShapeDtypeStruct(dims, dtype)


def page_kernel(pool, moved, rows, slot, table, length, out):
    count, pages, page_len, width = out.shape
    token = lax.broadcasted_iota(I32, (page_len, width), 0)

    @pl.loop(0, count)
    def _(j):
        at = slot[j]

        @pl.when(at >= 0)
        def _():
            for p in range(pages):
                out[j, p] = moved[at, p]

        @pl.when(at < 0)
        def _():
            i = rows[j]
            for p in range(pages):
                page = pool[table[i * pages + p]].astype(F32)
                out[j, p] = jnp.where(token + p * page_len < length[i], page, 0.0).astype(out.dtype)


def take_pages(pool, moved, rows, slot, table, length):
    pages = table.shape[0] // length.shape[0]
    outs = [shape((rows.shape[0], pages) + pool.shape[1:], pool.dtype)]
    args = (pool, moved, rows, slot, table, length)
    return local_call(page_kernel, [VMEM] * 2 + [SMEM] * 4, args, outs, moved=5 * MIB)[0]


def split_kernel(place, x, *outs):
    width = outs[0].shape[1]
    for s, out in enumerate(outs):
        out[...] = x[:, lanes((place[0] ^ s) * width, width)]


def movers_kernel(n_pair, selector, attention, residual, pair, own):
    pair[:, : attention.shape[1]] = pick(selector[:n_pair], attention[...]).astype(BF)
    moving = pick(selector[...], residual[...]).astype(BF)
    pair[:, attention.shape[1] :] = moving[:n_pair]
    own[...] = moving


def handover_kernel(half, place, pair, own, *outs):
    n_pair = half * MIG
    width = own.shape[1]
    for s, out in enumerate(outs):
        first = own[n_pair + (s - 1) * MIG : n_pair + s * MIG] if s else own[:MIG]
        second = pair[s * MIG : (s + 1) * MIG, half * width :]
        blank = jnp.zeros((out.shape[0] - n_pair - 2 * MIG, width), BF)
        columns = pair[:, lanes((place[0] ^ s) * width, width)]
        out[...] = jnp.concatenate([columns, first, second, blank], axis=0)


def project_kernel(half, *refs):
    odd, selector, resid_selector, residual, own, other = refs[:6]
    blocks = refs[6 : 6 + 2 * half]
    outs = refs[6 + 2 * half : 6 + 3 * half]
    buf, weights, sems = refs[6 + 3 * half :]
    rows = residual.shape[0]
    copies = [
        pltpu.make_async_copy(blocks[s], buf.at[pl.ds(s * rows, rows)], sems.at[s])
        for s in range(half)
    ]
    fetches = [
        pltpu.make_async_copy(own, weights.at[odd[0]], sems.at[half]),
        pltpu.make_async_copy(other, weights.at[1 - odd[0]], sems.at[half + 1]),
    ]
    for copy in copies + fetches:
        copy.start()
    at = half * rows
    for block in blocks[half:]:
        buf[at : at + block.shape[0]] = block[...]
        at += block.shape[0]
    resid = pick(resid_selector[:, :rows], residual[...])
    resid = resid + pick(resid_selector[:, rows:], buf[half * rows :])
    for copy in copies:
        copy.wait()
    picked = pick(selector[...], buf[...]).astype(BF)
    for copy in fetches:
        copy.wait()
    depth = own.shape[0]
    product = pick(picked[:, :depth], weights[0]) + pick(picked[:, depth:], weights[1])
    outs[0][...] = resid + product[:rows]
    for t in range(1, half):
        outs[t][...] = product[t * rows : (t + 1) * rows].astype(BF)


def halves(x):
    high = x.astype(BF)
    return high, (x - high.astype(F32)).astype(BF)


def norm_kernel(half, experts, wide, *refs):
    gain, router, selector, pages = refs[:4]
    parts = refs[4 : 4 + half]
    hidden_out, early = refs[4 + half : 6 + half]
    late = refs[6 + half :]
    hidden = parts[0][...]
    for part in parts[1:]:
        hidden = hidden + part[...].astype(F32)
    hidden_out[...] = hidden
    scaled = hidden * gain[...]
    rows = hidden.shape[0]
    lane = lax.broadcasted_iota(I32, (rows, 128), 1)
    stats = jnp.where(lane == 8, jnp.sum(hidden * hidden, axis=1, keepdims=True), 0.0)
    for e in range(experts):
        logit = jnp.sum(scaled * router[e : e + 1], axis=1, keepdims=True)
        stats = jnp.where(lane == e, logit, stats)
    stats = stats.T[: early.shape[0] - rows]
    scaled = scaled.astype(BF)
    early[:rows] = scaled[:, :wide]
    high, low = halves(stats)
    early[rows:] = jnp.zeros((early.shape[0] - rows, wide), BF)
    early[rows:, :rows] = high
    early[rows:, rows : 2 * rows] = low
    chosen = pick(selector[...], scaled[:, wide:]).astype(BF)
    for s in range(experts):
        late[s][:SLOTS] = chosen[s * SLOTS : (s + 1) * SLOTS]
    late[2][SLOTS:] = pages[...]


def dispatch_kernel(ne, experts, *refs):
    place, selector = refs[:2]
    blocks, outs, stats_out = refs[2 : 2 + ne], refs[2 + ne : -1], refs[-1]
    wide = blocks[0].shape[1]
    rows = selector.shape[1]
    stats = jnp.zeros(stats_out.shape, F32)
    for block in blocks:
        stats = stats + block[rows:, :rows].astype(F32) + block[rows:, rows : 2 * rows].astype(F32)
    stats_out[...] = stats
    inverse = lax.rsqrt(stats[stats.shape[0] // 2 :][:1] / D + EPSILON)
    scale = jnp.sum(selector[...].astype(F32) * inverse, axis=1, keepdims=True)
    high, low = halves(scale)
    lane = lax.broadcasted_iota(I32, (scale.shape[0], 128), 1)
    scale = jnp.where(lane == 0, high.astype(F32), jnp.where(lane == 1, low.astype(F32), 0.0)).astype(BF)
    for t in range(experts):
        outs[t][:, ne * wide :] = scale[t * SLOTS : (t + 1) * SLOTS]
    for s in range(ne):
        chosen = pick(selector[...], blocks[s][:rows]).astype(BF)
        columns = lanes((place[0] ^ s) * wide, wide)
        for t in range(experts):
            outs[t][:, columns] = chosen[t * SLOTS : (t + 1) * SLOTS]


def expert_kernel(ne, experts, tiles, place, *refs):
    early, late = refs[:experts], refs[experts : experts + ne]
    gate, up, down = refs[experts + ne : experts + ne + 3]
    refs = refs[experts + ne + 3 :]
    late_out, early_out = refs[:ne], refs[ne : ne + experts]
    rows, scale, active = refs[ne + experts :]
    step = pl.program_id(0)
    rest = late[0].shape[1]
    wide = (early[0].shape[1] - 128) // ne
    feats = wide + rest
    tile = gate.shape[2]

    @pl.when(step == 0)
    def _():
        for t in range(experts):
            at = slice(t * SLOTS, (t + 1) * SLOTS)
            for e in range(ne):
                rows[at, e * feats : e * feats + wide] = early[t][:, e * wide : (e + 1) * wide]
            pieces = early[t][:, ne * wide :].astype(F32)
            scale[at] = pieces[:, :1] + pieces[:, 1:2]
        for s in range(ne):
            rows[:, lanes((place[0] ^ s) * feats + wide, rest)] = late[s][...]

    @pl.when(step < tiles)
    def _():
        gate_h = pick(rows[...], gate[0]) * scale[...]
        up_h = pick(rows[...], up[0]) * scale[...]
        value = gate_h / (1.0 + jnp.exp(-gate_h)) * up_h
        active[:, lanes(step * tile, tile)] = value.astype(BF)

    @pl.when(step >= tiles)
    def _():
        owner = step - tiles
        value = pick(active[...], down[0]).astype(BF)
        for t in range(experts):
            early_out[t][:, lanes(owner * wide, wide)] = value[t * SLOTS : (t + 1) * SLOTS, :wide]
        for s in range(ne):

            @pl.when(owner ^ place[0] == s)
            def _(s=s):
                late_out[s][...] = value[:, wide:]


def expert_call(place, early, late, w_gate, w_up, w_down, ne):
    hidden = w_gate.shape[2]
    slots, rest = late[0].shape
    experts = len(early)
    wide = (early[0].shape[1] - 128) // ne
    tile = 256 if hidden % 256 == 0 else 128
    tiles = hidden // tile
    whole = lambda a: pl.BlockSpec(a.shape, lambda g, place: (0,) * len(a.shape))
    weight = pl.BlockSpec((1, D, tile), lambda g, place: (0, 0, jnp.minimum(g, tiles - 1)))
    down = pl.BlockSpec(
        (1, hidden, wide + rest), lambda g, place: (0, 0, jnp.maximum(g - tiles, 0))
    )
    outs = [shape((slots, rest), BF)] * ne + [shape((SLOTS, ne * wide), BF)] * experts
    values = pl.pallas_call(
        functools.partial(expert_kernel, ne, experts, tiles),
        grid_spec=pltpu.PrefetchScalarGridSpec(
            num_scalar_prefetch=1,
            grid=(tiles + ne,),
            in_specs=[whole(a) for a in (*early, *late)] + [weight] * 2 + [down],
            out_specs=[whole(o) for o in outs],
            scratch_shapes=[
                pltpu.VMEM((slots, D), BF),
                pltpu.VMEM((slots, 1), F32),
                pltpu.VMEM((slots, hidden), BF),
            ],
        ),
        out_shape=outs,
        compiler_params=pltpu.CompilerParams(vmem_limit_bytes=50 * MIB),
        cost_estimate=pl.CostEstimate(
            flops=6 * slots * D * hidden, bytes_accessed=6 * D * hidden, transcendentals=0
        ),
    )(place, *early, *late, w_gate, w_up, w_down)
    return values[:ne], values[ne:]


def weigh_kernel(ne, experts, *refs):
    place, high, low = refs[:3]
    blocks, outs, buf, total = refs[3 : 3 + experts], refs[3 + experts : 3 + experts + ne], *refs[3 + experts + ne :]
    for t in range(experts):
        buf[t * SLOTS : (t + 1) * SLOTS] = blocks[t][...]
    total[...] = pick(high[...], buf[...]) + pick(low[...], buf[...])
    wide = outs[0].shape[1]
    for s in range(ne):
        outs[s][...] = total[:, lanes((place[0] ^ s) * wide, wide)].astype(outs[s].dtype)


def finish_kernel(ne, experts, wide, *refs):
    high, low, hidden = refs[:3]
    early, late = refs[3 : 3 + ne], refs[3 + ne : 3 + ne + experts]
    out, buf = refs[3 + ne + experts :]
    first = hidden[:, :wide]
    for block in early:
        first = first + block[...].astype(F32)
    out[:, :wide] = first
    for t in range(experts):
        buf[t * SLOTS : (t + 1) * SLOTS] = late[t][...]
    out[:, wide:] = hidden[:, wide:] + pick(high[...], buf[...]) + pick(low[...], buf[...])


def body(
    attention_out,
    residual,
    w_out,
    router_w,
    norm_gain,
    page_pool,
    page_table,
    cache_len,
    came_from,
    routes,
    w_gate,
    w_up,
    w_down,
):
    n = lax.axis_size("req")
    ne = lax.axis_size("exp")
    me = lax.axis_index("req")
    ze = lax.axis_index("exp")
    half = n // 2
    q, k = me // 2, me % 2
    rows = attention_out.shape[0]
    feats = residual.shape[1]
    kblock = D // half
    experts = n // 2
    rest = feats // 2
    wide = feats - rest
    place = ze.reshape(1).astype(I32)

    pair_place = q.reshape(1).astype(I32)
    attn_blocks = local_call(
        split_kernel,
        [SMEM, VMEM],
        (pair_place, attention_out),
        [shape((rows, kblock), BF)] * half,
        moved=2 * MIB,
    )
    attn_blocks = [attn_blocks[0]] + [swap(attn_blocks[s], "req", 2 * s) for s in range(1, half)]
    w_other = swap(w_out, "req", 1)
    came_from, _ = lax.optimization_barrier((came_from, attn_blocks[0]))

    local = jnp.arange(rows, dtype=I32)
    in_new = came_from[None, :] == (me * rows + local)[:, None]
    new_ids = jnp.arange(came_from.shape[0], dtype=I32)
    dest = jnp.sum(jnp.where(in_new, new_ids[None, :], 0), axis=1) // rows
    dest_rank = jnp.sum((dest[:, None] == dest[None, :]) & (local[None, :] < local[:, None]), axis=1)
    dest_rel, dest_par = (dest // 2) ^ q, dest % 2
    send_slot = jnp.where(
        dest_par != k,
        dest_rel * MIG + dest_rank,
        jnp.where(dest_rel != 0, (half + dest_rel - 1) * MIG + dest_rank, -1),
    )
    n_pair, n_send = half * MIG, (2 * half - 1) * MIG
    n_hand = -(-(n_pair + 2 * MIG) // 16) * 16
    send_hot = (jnp.arange(n_send, dtype=I32)[:, None] == send_slot[None, :])
    send_row = jnp.sum(jnp.where(send_hot, local[None, :], 0), axis=1)
    send_pick, w_other = lax.optimization_barrier((send_hot.astype(BF), w_other))

    source = jnp.stack(
        [lax.dynamic_slice_in_dim(came_from, (2 * (q ^ t) + k) * rows, rows) for t in range(half)]
    )
    src_group, src_local = source // rows, source % rows
    src_rank = jnp.sum(
        (src_group[:, :, None] == src_group[:, None, :]) & (source[:, None, :] < source[:, :, None]),
        axis=2,
    )
    src_rel, src_par = (src_group // 2) ^ q, src_group % 2
    t_ids = jnp.arange(half, dtype=I32)[:, None]
    attn_at = jnp.where(
        src_par == k,
        src_rel * rows + src_local,
        half * rows + src_rel * n_hand + (t_ids ^ src_rel) * MIG + src_rank,
    ).reshape(-1)
    own_stays = src_group[0] == me
    own_slot = src_rel[0] * 2 * MIG + jnp.where(src_par[0] == k, 0, MIG) + src_rank[0]
    own_hand = src_rel[0] * n_hand + n_pair + jnp.where(src_par[0] == k, 0, MIG) + src_rank[0]
    own_at = jnp.where(own_stays, src_local[0], rows + own_hand)

    pair_rows, own_rows = local_call(
        functools.partial(movers_kernel, n_pair),
        [VMEM] * 3,
        (send_pick, attention_out, residual),
        [shape((n_pair, D + feats), BF), shape((n_send, feats), BF)],
        moved=2 * MIB,
    )
    pair_rows = swap(pair_rows, "req", 1)
    late_blocks = local_call(
        functools.partial(handover_kernel, half),
        [SMEM, VMEM, VMEM],
        (pair_place, pair_rows, own_rows),
        [shape((n_hand, feats), BF)] * half,
        moved=MIB,
    )
    late_blocks = [late_blocks[0]] + [swap(late_blocks[s], "req", 2 * s) for s in range(1, half)]

    expert_ids = jnp.arange(experts, dtype=I32)
    names = routes[:, :, None] == expert_ids[None, None, :]
    named = jnp.any(names, axis=1)
    before = jnp.sum(
        jnp.where((local[None, :] < local[:, None])[:, :, None], named[None, :, :], False), axis=1
    )
    rank = jnp.sum(jnp.where(names, before[:, None, :], 0), axis=2)
    slot_of = ((routes ^ (me % experts)) * SLOTS + rank).astype(I32)
    slot_ids = jnp.arange(experts * SLOTS, dtype=I32)
    slot_pick = jnp.any(slot_ids[:, None, None] == slot_of[None, :, :], axis=2).astype(BF)

    total_rows = half * (rows + n_hand)
    selector = hot(attn_at, total_rows)
    resid_selector = hot(own_at, rows + half * n_hand)
    parts = local_call(
        functools.partial(project_kernel, half),
        [SMEM] + [VMEM] * 3 + [HBM] * (2 + half) + [VMEM] * half,
        (
            k.reshape(1).astype(I32),
            selector,
            resid_selector,
            residual,
            w_out,
            w_other,
            *attn_blocks,
            *late_blocks,
        ),
        [shape((rows, feats), F32)] + [shape((rows, feats), BF)] * (half - 1),
        [
            pltpu.VMEM((total_rows, kblock), BF),
            pltpu.VMEM((2,) + w_out.shape, BF),
            pltpu.SemaphoreType.DMA((half + 2,)),
        ],
        vmem=58,
        flops=2 * half * rows * (total_rows + feats) * kblock,
        moved=6 * MIB,
    )
    parts = [parts[0]] + [swap(parts[s], "req", 2 * s) for s in range(1, half)]

    table = page_table.reshape(-1)
    none = jnp.full((n_send,), -1, I32)
    no_rows = page_pool[:2].reshape((1, 2) + page_pool.shape[1:])
    send_row, _ = lax.optimization_barrier((send_row, parts[0]))
    moving = take_pages(page_pool, no_rows, send_row, none, table, cache_len)
    page = moving.shape[1:]
    pair_pages = swap(moving[:n_pair], "req", 1).reshape((half, MIG) + page)
    own_pages = jnp.concatenate([moving[:MIG], moving[n_pair:]], axis=0).reshape((half, MIG) + page)
    pages = jnp.concatenate([own_pages, pair_pages], axis=1)
    stages = half.bit_length() - 1
    block = pages.shape[1:]
    pages = pages.reshape((half // 2, 2) + block)
    page_rows = pages[:, 1].reshape(-1, page[-1])

    router = jnp.pad(router_w.T, ((0, 8 - experts), (0, 0)))
    late_rows_of = [SLOTS + (page_rows.shape[0] if s == 2 else 0) for s in range(experts)]
    normed = local_call(
        functools.partial(norm_kernel, half, experts, wide),
        [VMEM] * (4 + half),
        (norm_gain[None, :], router, slot_pick, page_rows, *parts),
        [shape((rows, feats), F32), shape((rows + 16, wide), BF)]
        + [shape((count, rest), BF) for count in late_rows_of],
        flops=2 * experts * SLOTS * rows * rest,
        moved=3 * MIB,
    )
    hidden, early = normed[:2]
    late = [normed[2 + s] if s == 0 else swap(normed[2 + s], "req", s) for s in range(experts)]
    early, _ = lax.optimization_barrier((early, late[1]))
    early_blocks = [early] + [swap(early, "exp", s) for s in range(1, ne)]
    came_pages = late[2][SLOTS:].reshape((half // 2,) + block)
    pages = jnp.stack([pages[:, 0], came_pages], axis=1)
    late = jnp.concatenate([x[:SLOTS] for x in late], axis=0)
    late_rows = [late] + [swap(late, "exp", s) for s in range(1, ne)]

    outgoing = local_call(
        functools.partial(dispatch_kernel, ne, experts),
        [SMEM] + [VMEM] * (1 + ne),
        (place, slot_pick, *early_blocks),
        [shape((SLOTS, ne * wide + 128), BF)] * experts + [shape((16, rows), F32)],
        flops=2 * experts * SLOTS * rows * ne * wide,
        moved=3 * MIB,
    )
    stats = outgoing[-1]
    early_rows = [swap(outgoing[s], "req", s) if s else outgoing[s] for s in range(experts)]

    inverse = lax.rsqrt(stats[8] / D + EPSILON)
    logits = (stats[:experts] * inverse[None, :]).T
    chosen = jnp.sum(jnp.where(names, logits[:, None, :], 0.0), axis=2)
    gates = jax.nn.sigmoid(chosen - chosen[:, ::-1])
    gate_slots = jnp.sum(
        jnp.where(slot_of[:, :, None] == slot_ids[None, None, :], gates[:, :, None], 0.0), axis=1
    )
    gate_high, gate_low = halves(gate_slots)

    pages, _ = lax.optimization_barrier((pages, outgoing[0]))
    for bit in range(1, stages):
        pages = pages.reshape((half >> (bit + 1), 2, 1 << bit) + block)
        came_pages = swap(pages[:, 1], "req", 2 << bit)
        pages = jnp.stack([pages[:, 0], came_pages], axis=1)
    moved_pages = pages.reshape((half * 2 * MIG,) + page)

    down_late, down_early = expert_call(place, early_rows, late_rows, w_gate, w_up, w_down, ne)
    late_sum = down_late[0].astype(F32)
    for s in range(1, ne):
        late_sum = late_sum + swap(down_late[s], "exp", s).astype(F32)
    late_sum = late_sum.astype(BF).reshape(experts, SLOTS, rest)
    late_back = [swap(late_sum[s], "req", s) if s else late_sum[s] for s in range(experts)]
    early_back = [swap(down_early[s], "req", s) if s else down_early[s] for s in range(experts)]
    own_slot, _ = lax.optimization_barrier((own_slot, down_early[0]))
    new_pages = take_pages(
        page_pool,
        moved_pages,
        jnp.where(own_stays, src_local[0], 0),
        jnp.where(own_stays, -1, own_slot),
        table,
        cache_len,
    )
    place, new_pages = lax.optimization_barrier((place, new_pages))
    weighted = local_call(
        functools.partial(weigh_kernel, ne, experts),
        [SMEM] + [VMEM] * (2 + experts),
        (place, gate_high, gate_low, *early_back),
        [shape((rows, wide), F32)] + [shape((rows, wide), BF)] * (ne - 1),
        [pltpu.VMEM((experts * SLOTS, ne * wide), BF), pltpu.VMEM((rows, ne * wide), F32)],
        flops=4 * rows * experts * SLOTS * ne * wide,
        moved=3 * MIB,
    )
    early_parts = [weighted[0]] + [swap(weighted[s], "exp", s) for s in range(1, ne)]
    mixed = local_call(
        functools.partial(finish_kernel, ne, experts, wide),
        [VMEM] * (3 + ne + experts),
        (gate_high, gate_low, hidden, *early_parts, *late_back),
        [shape((rows, feats), F32)],
        [pltpu.VMEM((experts * SLOTS, rest), BF)],
        flops=4 * rows * experts * SLOTS * rest,
        moved=2 * MIB,
    )[0]

    return (mixed, new_pages)


def solution(mesh):
    in_specs = (
        P("req", None),
        P("req", "exp"),
        P("req", "exp"),
        P("exp", None),
        P("exp"),
        P("req", None, "exp"),
        P("req", None),
        P("req"),
        P(),
        P("req", None),
        P("req", None, "exp"),
        P("req", None, "exp"),
        P("req", "exp", None),
    )
    out_specs = (P("req", "exp"), P("req", None, None, "exp"))
    return jax.shard_map(body, mesh=mesh, in_specs=in_specs, out_specs=out_specs, check_vma=False)
```

time: 181 us -> 164 us (0.906)
  blocking collectives: 27.1 us -> 0 us
  waiting for transfers between devices: 46.3 us -> 65.9 us
  starting transfers between devices: 49.6 us -> 41.2 us
  other arithmetic: 2.49 us -> 5.98 us
  matrix products: 3.37 us -> 0 us
  local copies, waits for them, and re-layouts: 12.8 us -> 9.78 us
    all_gather x2 -> x0, blocking collectives: 27.1 us -> none  [the longest x1 13.8 us: body(): gain_all = lax.all_gather(norm_gain, 'exp', tiled=True)]
    ppermute x43 -> x37, waiting for transfers between devices: 46.3 us -> 65.9 us  [swap(): return lax.ppermute(x, axis, [(i, i ^ s) for i in range(n)])]
    ppermute x43 -> x37, starting transfers between devices: 49.6 us -> 41.2 us  [swap(): return lax.ppermute(x, axis, [(i, i ^ s) for i in range(n)])]
    concatenate x3 -> x0, local copies, waits for them, and re-layouts: 4.1 us -> none  [the longest x1 4.09 us: body(): jnp.concatenate([residual, moved_resid], axis=0)]
    dot_general x4 -> x0, matrix products: 3.37 us -> none  [the longest x3 2.86 us: pick(): return jnp.dot(selector, rows, preferred_element_type=F32)]
    dynamic_slice x2 -> x0, local copies, waits for them, and re-layouts: 2.34 us -> none  [column_block(): return lax.dynamic_slice_in_dim(x, (q ^ s) * kblock, kblock, axis=1)]
    unnamed x57 -> x59, local copies, waits for them, and re-layouts: 4.53 us -> 6.05 us
    pallas_call x7 -> x10, Pallas kernels: 14.8 us -> 15.8 us  [local_call(): pl.pallas_call(kernel, out_shape=outs, in_specs=in_specs, out_specs=[VMEM...]
  transfers between devices with their start and end apart: 43 -> 37, of which waited for: 14 -> 16; matrix products, arithmetic and copies ran while one was open for 6% -> 6% of each run, Pallas kernels for 19% -> 18%
where the time goes in v3:
time: 164 us; the launch traced here: 163 us
  waiting for transfers between devices  65.9 us (40%)
  starting transfers between devices  41.2 us (25%)
  Pallas kernels  39 us (24%)
  local copies, waits for them, and re-layouts  9.78 us (6%)
  other arithmetic  5.98 us (4%)
    ppermute x37, waiting for transfers between devices, swap(): return lax.ppermute(x, axis, [(i, i ^ s) for i in range(n)])  65.9 us
    ppermute x37, starting transfers between devices, swap(): return lax.ppermute(x, axis, [(i, i ^ s) for i in range(n)])  41.2 us
    pallas_call x1, Pallas kernels, expert_call(): pl.pallas_call(functools.partial(expert_kernel, ne, experts, tiles), grid...  23.3 us
    pallas_call x10, Pallas kernels, local_call(): pl.pallas_call(kernel, out_shape=outs, in_specs=in_specs, out_specs=[VMEM...  15.8 us
    unnamed x59, local copies, waits for them, and re-layouts  6.05 us
  transfers between devices with their start and end apart: 37, of which 16 were waited for; matrix products, arithmetic and copies ran while one was open for 6% of the time, Pallas kernels for 18%

profile of v3, /device:TPU:0, one launch (start us, length us, event | category | flops | bytes accessed | tf_op | source)
XLA Modules:
  0.0 163.1 jit_solution(7462676376833779327)
XLA Ops:
  0.7 1.2 copy-done.1
  2.0 0.7 copy-done.10
  2.7 2.9 %collective-permute-start.1 = (bf16[128,1024]{1,0:T(8,128)(2,1)S(1)}, bf16[128,1024]{1,0:T(8,128)(2,1)S(1)}, u32[]{:S(2)}, u32[]{:S(2)}) collective-permute-start(bf16[128,1024]{1,0:T(8,128)(2,1)S(1)} %get-tuple-element.51), channel_id=1, source_target_pairs={{0,8},{4,12},{8,0},{12,4},{16,24},{20,28},{24,16},{28,20},{1,9},{5... | collective-permute-start | bytes 786440 | tf_op jit(solution)/shard_map/ppermute | solution.py:25
  5.6 1.5 collective-permute-start.2
  7.1 0.9 select_reduce_fusion
  8.3 0.9 dynamic-slice_bitcast_fusion.3
  9.6 0.7 slice_bitcast_fusion.1.moved
  10.4 0.7 fusion.7.refs_2_
  11.1 1.0 fusion.refs_1_
  12.5 0.6 collective-permute-start.4
  13.5 0.6 collective-permute-done.4.pair
  14.1 0.6 copy-done.12
  14.8 2.0 %collective-permute-start.5 = (bf16[32,1024]{1,0:T(8,128)(2,1)S(1)}, bf16[32,1024]{1,0:T(8,128)(2,1)S(1)}, u32[]{:S(2)}, u32[]{:S(2)}) collective-permute-start(bf16[32,1024]{1,0:T(8,128)(2,1)S(1)} %get-tuple-element.58), channel_id=1, source_target_pairs={{0,8},{4,12},{8,0},{12,4},{16,24},{20,28},{24,16},{28,20},{1,9},{5... | collective-permute-start | bytes 196616 | tf_op jit(solution)/shard_map/ppermute | solution.py:25
  16.7 1.5 collective-permute-start.6
  18.3 0.7 collective-permute-done.2.refs_8_
  19.0 0.4 collective-permute-done.5.refs_11_
  19.4 1.7 %collective-permute-done.6.refs_12_ = bf16[32,1024]{1,0:T(8,128)(2,1)S(1)} collective-permute-done((bf16[32,1024]{1,0:T(8,128)(2,1)S(1)}, bf16[32,1024]{1,0:T(8,128)(2,1)S(1)}, u32[]{:S(2)}, u32[]{:S(2)}) %collective-permute-start.6) | collective-permute-done | bytes 65568 | tf_op jit(solution)/shard_map/ppermute | solution.py:25
  21.0 2.4 %collective-permute-done.7.refs_13_ = bf16[32,1024]{1,0:T(8,128)(2,1)S(1)} collective-permute-done((bf16[32,1024]{1,0:T(8,128)(2,1)S(1)}, bf16[32,1024]{1,0:T(8,128)(2,1)S(1)}, u32[]{:S(2)}, u32[]{:S(2)}) %collective-permute-start.7) | collective-permute-done | bytes 65568 | tf_op jit(solution)/shard_map/ppermute | solution.py:25
  23.5 0.6 copy-done.28
  24.1 5.9 %shard_map.143 = (f32[128,1024]{1,0:T(8,128)}, bf16[128,1024]{1,0:T(8,128)(2,1)}, bf16[128,1024]{1,0:T(8,128)(2,1)}, bf16[128,1024]{1,0:T(8,128)(2,1)}) custom-call(s32[1]{0:T(128)} %bitcast.5.refs_0_, bf16[512,640]{1,0:T(8,128)(2,1)} %fusion.refs_1_, bf16[128,256]{1,0:T(8,128)(2,1)} %fusion.7.refs_2_, bf16[128,1024]{1,0:T(8,128)(2,1)} %refs_3_.1, ...), custom_call_target="tpu_custom_call" | custom-call | flops 1744830464 | bytes 6291456 | tf_op jit(solution)/shard_map/pallas_call | solution.py:41
  30.0 1.3 shard_map.144
  31.5 0.6 collective-permute-start.9
  32.1 0.5 collective-permute-start.10
  32.6 2.4 %collective-permute-start.11 = (bf16[128,1024]{1,0:T(8,128)(2,1)S(1)}, bf16[128,1024]{1,0:T(8,128)(2,1)S(1)}, u32[]{:S(2)}, u32[]{:S(2)}) collective-permute-start(bf16[128,1024]{1,0:T(8,128)(2,1)S(1)} %copy-done.23), channel_id=1, source_target_pairs={{0,24},{4,28},{8,16},{12,20},{16,8},{20,12},{24,0},{28,4},{1,25},{... | collective-permute-start | bytes 786440 | tf_op jit(solution)/shard_map/ppermute | solution.py:25
  35.3 5.4 %collective-permute-done.9.refs_5_ = bf16[128,1024]{1,0:T(8,128)(2,1)S(1)} collective-permute-done((bf16[128,1024]{1,0:T(8,128)(2,1)S(1)}, bf16[128,1024]{1,0:T(8,128)(2,1)S(1)}, u32[]{:S(2)}, u32[]{:S(2)}) %collective-permute-start.9) | collective-permute-done | bytes 262176 | tf_op jit(solution)/shard_map/ppermute | solution.py:25
  40.7 5.4 %collective-permute-done.10.refs_6_ = bf16[128,1024]{1,0:T(8,128)(2,1)S(1)} collective-permute-done((bf16[128,1024]{1,0:T(8,128)(2,1)S(1)}, bf16[128,1024]{1,0:T(8,128)(2,1)S(1)}, u32[]{:S(2)}, u32[]{:S(2)}) %collective-permute-start.10) | collective-permute-done | bytes 262176 | tf_op jit(solution)/shard_map/ppermute | solution.py:25
  46.1 1.0 shard_map.145
  47.1 0.6 copy-done.11
  47.7 1.5 collective-permute-done.12
  49.2 3.6 %collective-permute-start.15 = (bf16[144,512]{1,0:T(8,128)(2,1)S(1)}, bf16[144,512]{1,0:T(8,128)(2,1)S(1)}, u32[]{:S(2)}, u32[]{:S(2)}) collective-permute-start(bf16[144,512]{1,0:T(8,128)(2,1)S(1)} %get-tuple-element.68.refs_2_), channel_id=1, source_target_pairs={{0,3},{1,2},{2,1},{3,0},{4,7},{5,6},{6,5},{7,4},{8,11},{9,10},{10,... | collective-permute-start | bytes 442376 | tf_op jit(solution)/shard_map/ppermute | solution.py:25
  52.8 0.8 collective-permute-start.13
  53.6 0.5 collective-permute-start.21
  54.1 1.1 collective-permute-start.16
  55.2 2.6 %collective-permute-done.15.refs_5_ = bf16[144,512]{1,0:T(8,128)(2,1)S(1)} collective-permute-done((bf16[144,512]{1,0:T(8,128)(2,1)S(1)}, bf16[144,512]{1,0:T(8,128)(2,1)S(1)}, u32[]{:S(2)}, u32[]{:S(2)}) %collective-permute-start.15) | collective-permute-done | bytes 147488 | tf_op jit(solution)/shard_map/ppermute | solution.py:25
  57.8 7.8 %collective-permute-done.14.refs_4_ = bf16[144,512]{1,0:T(8,128)(2,1)S(1)} collective-permute-done((bf16[144,512]{1,0:T(8,128)(2,1)S(1)}, bf16[144,512]{1,0:T(8,128)(2,1)S(1)}, u32[]{:S(2)}, u32[]{:S(2)}) %collective-permute-start.14) | collective-permute-done | bytes 147488 | tf_op jit(solution)/shard_map/ppermute | solution.py:25
  65.6 0.4 shard_map.146
  66.1 0.7 copy-done.7
  66.8 0.7 copy-done.8
  67.5 0.7 copy-done.9
  68.5 1.6 collective-permute-start.19
  70.0 0.4 collective-permute-start.20
  70.4 0.8 slice.100
  71.2 0.9 pad_maximum_fusion.2.refs_4_
  72.1 2.5 %collective-permute-start.24 = (bf16[256,512]{1,0:T(8,128)(2,1)S(1)}, bf16[256,512]{1,0:T(8,128)(2,1)S(1)}, u32[]{:S(2)}, u32[]{:S(2)}) collective-permute-start(bf16[256,512]{1,0:T(8,128)(2,1)S(1)} %pad_maximum_fusion.2.refs_4_), channel_id=1, source_target_pairs={{0,3},{1,2},{2,1},{3,0},{4,7},{5,6},{6,5},{7,4},{8,11},{9,10},{10,... | collective-permute-start | bytes 786440 | tf_op jit(solution)/shard_map/ppermute | solution.py:25
  74.7 1.0 slice.97
  75.7 2.0 %collective-permute-start.22 = (bf16[256,512]{1,0:T(8,128)(2,1)S(1)}, bf16[256,512]{1,0:T(8,128)(2,1)S(1)}, u32[]{:S(2)}, u32[]{:S(2)}) collective-permute-start(bf16[256,512]{1,0:T(8,128)(2,1)S(1)} %pad_maximum_fusion.2.refs_4_), channel_id=1, source_target_pairs={{0,1},{1,0},{2,3},{3,2},{4,5},{5,4},{6,7},{7,6},{8,9},{9,8},{10,11... | collective-permute-start | bytes 786440 | tf_op jit(solution)/shard_map/ppermute | solution.py:25
  77.6 1.1 fusion.4
  78.8 1.3 collective-permute-start.17
  80.0 3.4 %collective-permute-done.20.refs_3_ = bf16[64,2176]{1,0:T(8,128)(2,1)S(1)} collective-permute-done((bf16[64,2176]{1,0:T(8,128)(2,1)}, bf16[64,2176]{1,0:T(8,128)(2,1)S(1)}, u32[]{:S(2)}, u32[]{:S(2)}) %collective-permute-start.20) | collective-permute-done | bytes 278560 | tf_op jit(solution)/shard_map/ppermute | solution.py:25
  83.4 13.3 %collective-permute-done.23.refs_6_ = bf16[256,512]{1,0:T(8,128)(2,1)S(1)} collective-permute-done((bf16[256,512]{1,0:T(8,128)(2,1)S(1)}, bf16[256,512]{1,0:T(8,128)(2,1)S(1)}, u32[]{:S(2)}, u32[]{:S(2)}) %collective-permute-start.23) | collective-permute-done | bytes 262176 | tf_op jit(solution)/shard_map/ppermute | solution.py:25
  96.7 23.3 %shard_map.147 = (bf16[256,512]{1,0:T(8,128)(2,1)S(1)}, bf16[256,512]{1,0:T(8,128)(2,1)S(1)}, bf16[256,512]{1,0:T(8,128)(2,1)S(1)}, bf16[256,512]{1,0:T(8,128)(2...) custom-call(s32[1]{0:T(128)} %bitcast.refs_0_.place, ...), custom_call_target="tpu_custom_call" | custom-call | flops 11274289152 | bytes 44040192 | tf_op jit(solution)/shard_map/pallas_call | solution.py:255
  120.0 1.6 collective-permute-start.26
  121.6 1.9 %collective-permute-start.32 = (bf16[256,512]{1,0:T(8,128)(2,1)S(1)}, bf16[256,512]{1,0:T(8,128)(2,1)S(1)}, u32[]{:S(2)}, u32[]{:S(2)}) collective-permute-start(bf16[256,512]{1,0:T(8,128)(2,1)S(1)} %get-tuple-element.91), channel_id=1, source_target_pairs={{0,2},{1,3},{2,0},{3,1},{4,6},{5,7},{6,4},{7,5},{8,10},{9,11},{10,... | collective-permute-start | bytes 786440 | tf_op jit(solution)/shard_map/ppermute | solution.py:25
  123.5 2.5 %collective-permute-start.33 = (bf16[256,512]{1,0:T(8,128)(2,1)S(1)}, bf16[256,512]{1,0:T(8,128)(2,1)S(1)}, u32[]{:S(2)}, u32[]{:S(2)}) collective-permute-start(bf16[256,512]{1,0:T(8,128)(2,1)S(1)} %get-tuple-element.92), channel_id=1, source_target_pairs={{0,3},{1,2},{2,1},{3,0},{4,7},{5,6},{6,5},{7,4},{8,11},{9,10},{10,... | collective-permute-start | bytes 786440 | tf_op jit(solution)/shard_map/ppermute | solution.py:25
  126.0 5.2 %shard_map.148 = bf16[128,2,8,512]{3,2,1,0:T(8,128)(2,1)} custom-call(bf16[256,8,512]{2,1,0:T(8,128)(2,1)S(1)} %copy-done, bf16[32,2,8,512]{3,2,1,0:T(8,128)(2,1)S(1)} %bitcast.71, s32[128]{0:T(128)S(1)} %get-tuple-element.104.rows, s32[128]{0:T(128)S(1)} %bitcast_select_fusion.slot, s32[256]{0:T(256)S(1)} %reshape.524.table, s32[128]{0:T(128)S(1)} %copy-done.6), custom_call_target="tpu_custom_call" | custom-call | bytes 5242880 | tf_op jit(solution)/shard_map/pallas_call | solution.py:41
  131.2 3.1 %collective-permute-done.31 = bf16[256,512]{1,0:T(8,128)(2,1)S(1)} collective-permute-done((bf16[256,512]{1,0:T(8,128)(2,1)S(1)}, bf16[256,512]{1,0:T(8,128)(2,1)S(1)}, u32[]{:S(2)}, u32[]{:S(2)}) %collective-permute-start.31) | collective-permute-done | bytes 262176 | tf_op jit(solution)/shard_map/ppermute | solution.py:25
  134.3 8.6 %collective-permute-done.32 = bf16[256,512]{1,0:T(8,128)(2,1)S(1)} collective-permute-done((bf16[256,512]{1,0:T(8,128)(2,1)S(1)}, bf16[256,512]{1,0:T(8,128)(2,1)S(1)}, u32[]{:S(2)}, u32[]{:S(2)}) %collective-permute-start.32) | collective-permute-done | bytes 262176 | tf_op jit(solution)/shard_map/ppermute | solution.py:25
  143.2 0.5 shard_map.149
  143.7 5.5 %collective-permute-start.28 = (bf16[128,512]{1,0:T(8,128)(2,1)S(1)}, bf16[128,512]{1,0:T(8,128)(2,1)S(1)}, u32[]{:S(2)}, u32[]{:S(2)}) collective-permute-start(bf16[128,512]{1,0:T(8,128)(2,1)S(1)} %get-tuple-element.86), channel_id=1, source_target_pairs={{0,1},{1,0},{2,3},{3,2},{4,5},{5,4},{6,7},{7,6},{8,9},{9,8},{10,11... | collective-permute-start | bytes 393224 | tf_op jit(solution)/shard_map/ppermute | solution.py:25
  149.2 2.4 %collective-permute-start.30 = (bf16[128,512]{1,0:T(8,128)(2,1)S(1)}, bf16[128,512]{1,0:T(8,128)(2,1)S(1)}, u32[]{:S(2)}, u32[]{:S(2)}) collective-permute-start(bf16[128,512]{1,0:T(8,128)(2,1)S(1)} %get-tuple-element.88), channel_id=1, source_target_pairs={{0,3},{1,2},{2,1},{3,0},{4,7},{5,6},{6,5},{7,4},{8,11},{9,10},{10,... | collective-permute-start | bytes 393224 | tf_op jit(solution)/shard_map/ppermute | solution.py:25
  151.6 0.9 collective-permute-start.35
  152.9 3.0 %collective-permute-done.35.refs_9_ = bf16[64,512]{1,0:T(8,128)(2,1)S(1)} collective-permute-done((bf16[64,512]{1,0:T(8,128)(2,1)S(1)}, bf16[64,512]{1,0:T(8,128)(2,1)S(1)}, u32[]{:S(2)}, u32[]{:S(2)}) %collective-permute-start.35) | collective-permute-done | bytes 65568 | tf_op jit(solution)/shard_map/ppermute | solution.py:25
  155.9 6.2 %collective-permute-done.29.refs_5_ = bf16[128,512]{1,0:T(8,128)(2,1)S(1)} collective-permute-done((bf16[128,512]{1,0:T(8,128)(2,1)S(1)}, bf16[128,512]{1,0:T(8,128)(2,1)S(1)}, u32[]{:S(2)}, u32[]{:S(2)}) %collective-permute-start.29) | collective-permute-done | bytes 131104 | tf_op jit(solution)/shard_map/ppermute | solution.py:25
  162.1 1.1 shard_map.150
  (128 shorter events, 3.1 us)
Async XLA Ops:
  0.6 12.4 %copy-start.18 = (s32[128,2]{0,1:T(2,128)S(1)}, s32[128,2]{0,1:T(2,128)}, u32[]{:S(2)}) copy-start(s32[128,2]{0,1:T(2,128)} %param.22) | copy-start | bytes 3076
  0.6 12.5 %copy-start.19 = (s32[128,2]{0,1:T(2,128)S(1)}, s32[128,2]{0,1:T(2,128)}, u32[]{:S(2)}) copy-start(s32[128,2]{0,1:T(2,128)} %param.19) | copy-start | bytes 3076
  0.7 1.2 copy-start.1
  1.9 10.3 %copy-start.2 = (bf16[128,4096]{1,0:T(8,128)(2,1)S(1)}, bf16[128,4096]{1,0:T(8,128)(2,1)}, u32[]{:S(2)}) copy-start(bf16[128,4096]{1,0:T(8,128)(2,1)} %attention.1) | copy-start | bytes 3145732
  1.9 10.3 %copy-start.4 = (bf16[128,1024]{1,0:T(8,128)(2,1)S(1)}, bf16[128,1024]{1,0:T(8,128)(2,1)}, u32[]{:S(2)}) copy-start(bf16[128,1024]{1,0:T(8,128)(2,1)} %refs_3_.1) | copy-start | bytes 786436
  2.0 0.7 copy-start.10
  2.7 15.6 %collective-permute-start.1 = (bf16[128,1024]{1,0:T(8,128)(2,1)S(1)}, bf16[128,1024]{1,0:T(8,128)(2,1)S(1)}, u32[]{:S(2)}, u32[]{:S(2)}) collective-permute-start(bf16[128,1024]{1,0:T(8,128)(2,1)S(1)} %get-tuple-element.51), channel_id=1, source_target_pairs={{0,8},{4,12},{8,0},{12,4},{16,24},{20,28},{24,16},{28,20},{1,9},{5... | collective-permute-start | bytes 786440 | tf_op jit(solution)/shard_map/ppermute | solution.py:25
  5.6 13.4 %collective-permute-start.2 = (bf16[128,1024]{1,0:T(8,128)(2,1)S(1)}, bf16[128,1024]{1,0:T(8,128)(2,1)S(1)}, u32[]{:S(2)}, u32[]{:S(2)}) collective-permute-start(bf16[128,1024]{1,0:T(8,128)(2,1)S(1)} %get-tuple-element.52), channel_id=1, source_target_pairs={{0,16},{4,20},{8,24},{12,28},{16,0},{20,4},{24,8},{28,12},{1,17},{... | collective-permute-start | bytes 786440 | tf_op jit(solution)/shard_map/ppermute | solution.py:25
  7.1 11.9 %collective-permute-start.3 = (bf16[128,1024]{1,0:T(8,128)(2,1)S(1)}, bf16[128,1024]{1,0:T(8,128)(2,1)S(1)}, u32[]{:S(2)}, u32[]{:S(2)}) collective-permute-start(bf16[128,1024]{1,0:T(8,128)(2,1)S(1)} %get-tuple-element.53), channel_id=1, source_target_pairs={{0,24},{4,28},{8,16},{12,20},{16,8},{20,12},{24,0},{28,4},{1,25},{... | collective-permute-start | bytes 786440 | tf_op jit(solution)/shard_map/ppermute | solution.py:25
  7.1 5.1 %collective-permute-start = (bf16[512,1024]{1,0:T(8,128)(2,1)}, bf16[512,1024]{1,0:T(8,128)(2,1)}, u32[]{:S(2)}, u32[]{:S(2)}) collective-permute-start(bf16[512,1024]{1,0:T(8,128)(2,1)} %refs_4_.1), channel_id=1, source_target_pairs={{0,4},{4,0},{8,12},{12,8},{16,20},{20,16},{24,28},{28,24},{1,5},{5... | collective-permute-start | bytes 3145736 | tf_op jit(solution)/shard_map/ppermute | solution.py:25
  12.5 1.6 collective-permute-start.4
  14.1 0.6 copy-start.12
  14.8 4.6 %collective-permute-start.5 = (bf16[32,1024]{1,0:T(8,128)(2,1)S(1)}, bf16[32,1024]{1,0:T(8,128)(2,1)S(1)}, u32[]{:S(2)}, u32[]{:S(2)}) collective-permute-start(bf16[32,1024]{1,0:T(8,128)(2,1)S(1)} %get-tuple-element.58), channel_id=1, source_target_pairs={{0,8},{4,12},{8,0},{12,4},{16,24},{20,28},{24,16},{28,20},{1,9},{5... | collective-permute-start | bytes 196616 | tf_op jit(solution)/shard_map/ppermute | solution.py:25
  16.7 4.3 %collective-permute-start.6 = (bf16[32,1024]{1,0:T(8,128)(2,1)S(1)}, bf16[32,1024]{1,0:T(8,128)(2,1)S(1)}, u32[]{:S(2)}, u32[]{:S(2)}) collective-permute-start(bf16[32,1024]{1,0:T(8,128)(2,1)S(1)} %get-tuple-element.59), channel_id=1, source_target_pairs={{0,16},{4,20},{8,24},{12,28},{16,0},{20,4},{24,8},{28,12},{1,17},{... | collective-permute-start | bytes 196616 | tf_op jit(solution)/shard_map/ppermute | solution.py:25
  18.3 5.2 %copy-start.20 = (bf16[128,1024]{1,0:T(8,128)(2,1)}, bf16[128,1024]{1,0:T(8,128)(2,1)S(1)}, u32[]{:S(2)}) copy-start(bf16[128,1024]{1,0:T(8,128)(2,1)S(1)} %collective-permute-done.1.refs_7_) | copy-start | bytes 786436
  18.3 5.2 %collective-permute-start.7 = (bf16[32,1024]{1,0:T(8,128)(2,1)S(1)}, bf16[32,1024]{1,0:T(8,128)(2,1)S(1)}, u32[]{:S(2)}, u32[]{:S(2)}) collective-permute-start(bf16[32,1024]{1,0:T(8,128)(2,1)S(1)} %get-tuple-element.60), channel_id=1, source_target_pairs={{0,24},{4,28},{8,16},{12,20},{16,8},{20,12},{24,0},{28,4},{1,25},{... | collective-permute-start | bytes 196616 | tf_op jit(solution)/shard_map/ppermute | solution.py:25
  19.0 4.5 %copy-start.21 = (bf16[128,1024]{1,0:T(8,128)(2,1)}, bf16[128,1024]{1,0:T(8,128)(2,1)S(1)}, u32[]{:S(2)}) copy-start(bf16[128,1024]{1,0:T(8,128)(2,1)S(1)} %collective-permute-done.2.refs_8_) | copy-start | bytes 786436
  19.0 4.5 %copy-start.22 = (bf16[128,1024]{1,0:T(8,128)(2,1)}, bf16[128,1024]{1,0:T(8,128)(2,1)S(1)}, u32[]{:S(2)}) copy-start(bf16[128,1024]{1,0:T(8,128)(2,1)S(1)} %collective-permute-done.3.refs_9_) | copy-start | bytes 786436
  19.4 4.1 %copy-start.26 = (bf16[32,1024]{1,0:T(8,128)(2,1)}, bf16[32,1024]{1,0:T(8,128)(2,1)S(1)}, u32[]{:S(2)}) copy-start(bf16[32,1024]{1,0:T(8,128)(2,1)S(1)} %collective-permute-done.5.refs_11_) | copy-start | bytes 196612
  21.0 2.5 %copy-start.27 = (bf16[32,1024]{1,0:T(8,128)(2,1)}, bf16[32,1024]{1,0:T(8,128)(2,1)S(1)}, u32[]{:S(2)}) copy-start(bf16[32,1024]{1,0:T(8,128)(2,1)S(1)} %collective-permute-done.6.refs_12_) | copy-start | bytes 196612
  24.1 5.9 %copy-start = (bf16[256,8,512]{2,1,0:T(8,128)(2,1)S(1)}, bf16[256,8,512]{2,1,0:T(8,128)(2,1)}, u32[]{:S(2)}) copy-start(bf16[256,8,512]{2,1,0:T(8,128)(2,1)} %pool.3) | copy-start | bytes 6291460
  24.1 6.0 %copy-start.6 = (s32[128]{0:T(128)S(1)}, s32[128]{0:T(128)}, u32[]{:S(2)}) copy-start(s32[128]{0:T(128)} %length.3) | copy-start | bytes 1540
  29.9 1.6 copy-start.25
  30.0 2.2 %copy-start.24 = (bf16[128,1024]{1,0:T(8,128)(2,1)S(1)}, bf16[128,1024]{1,0:T(8,128)(2,1)}, u32[]{:S(2)}) copy-start(bf16[128,1024]{1,0:T(8,128)(2,1)} %get-tuple-element.64) | copy-start | bytes 786436
  30.0 2.7 %copy-start.23 = (bf16[128,1024]{1,0:T(8,128)(2,1)S(1)}, bf16[128,1024]{1,0:T(8,128)(2,1)}, u32[]{:S(2)}) copy-start(bf16[128,1024]{1,0:T(8,128)(2,1)} %get-tuple-element.65) | copy-start | bytes 786436
  30.0 5.2 %copy-start.17 = (f32[1024,4]{0,1:T(4,128)S(1)}, f32[1024,4]{0,1:T(4,128)}, u32[]{:S(2)}) copy-start(f32[1024,4]{0,1:T(4,128)} %param.16) | copy-start | bytes 49156
  30.0 16.1 %copy-start.3 = (f32[128,1024]{1,0:T(8,128)S(1)}, f32[128,1024]{1,0:T(8,128)}, u32[]{:S(2)}) copy-start(f32[128,1024]{1,0:T(8,128)} %get-tuple-element.61.refs_4_) | copy-start | bytes 1572868
  30.0 16.1 %copy-start.5 = (f32[1024]{0:T(1024)S(1)}, f32[1024]{0:T(1024)}, u32[]{:S(2)}) copy-start(f32[1024]{0:T(1024)} %param.17) | copy-start | bytes 12292
  31.4 3.8 %collective-permute-start.8 = (bf16[16,2,8,512]{3,2,1,0:T(8,128)(2,1)S(1)}, bf16[16,2,8,512]{3,2,1,0:T(8,128)(2,1)S(1)}, u32[]{:S(2)}, u32[]{:S(2)}) collective-permute-start(bf16[16,2,8,512]{3,2,1,0:T(8,128)(2,1)S(1)} %slice.94), channel_id=1, source_target_pairs={{0,4},{4,0},{8,12},{12,8},{16,20},{20,16},{24,28},{28,24},{1,5},{5... | collective-permute-start | bytes 786440 | tf_op jit(solution)/shard_map/ppermute | solution.py:25
  31.5 9.2 %collective-permute-start.9 = (bf16[128,1024]{1,0:T(8,128)(2,1)S(1)}, bf16[128,1024]{1,0:T(8,128)(2,1)S(1)}, u32[]{:S(2)}, u32[]{:S(2)}) collective-permute-start(bf16[128,1024]{1,0:T(8,128)(2,1)S(1)} %copy-done.25), channel_id=1, source_target_pairs={{0,8},{4,12},{8,0},{12,4},{16,24},{20,28},{24,16},{28,20},{1,9},{5... | collective-permute-start | bytes 786440 | tf_op jit(solution)/shard_map/ppermute | solution.py:25
  32.1 14.0 %collective-permute-start.10 = (bf16[128,1024]{1,0:T(8,128)(2,1)S(1)}, bf16[128,1024]{1,0:T(8,128)(2,1)S(1)}, u32[]{:S(2)}, u32[]{:S(2)}) collective-permute-start(bf16[128,1024]{1,0:T(8,128)(2,1)S(1)} %copy-done.24), channel_id=1, source_target_pairs={{0,16},{4,20},{8,24},{12,28},{16,0},{20,4},{24,8},{28,12},{1,17},{... | collective-permute-start | bytes 786440 | tf_op jit(solution)/shard_map/ppermute | solution.py:25
  32.6 13.5 %collective-permute-start.11 = (bf16[128,1024]{1,0:T(8,128)(2,1)S(1)}, bf16[128,1024]{1,0:T(8,128)(2,1)S(1)}, u32[]{:S(2)}, u32[]{:S(2)}) collective-permute-start(bf16[128,1024]{1,0:T(8,128)(2,1)S(1)} %copy-done.23), channel_id=1, source_target_pairs={{0,24},{4,28},{8,16},{12,20},{16,8},{20,12},{24,0},{28,4},{1,25},{... | collective-permute-start | bytes 786440 | tf_op jit(solution)/shard_map/ppermute | solution.py:25
  35.2 10.9 %copy-start.13 = (bf16[16,2,8,512]{3,2,1,0:T(8,128)(2,1)}, bf16[16,2,8,512]{3,2,1,0:T(8,128)(2,1)S(1)}, u32[]{:S(2)}) copy-start(bf16[16,2,8,512]{3,2,1,0:T(8,128)(2,1)S(1)} %pad_maximum_fusion.1) | copy-start | bytes 786436
  35.3 10.9 %copy-start.14 = (bf16[16,2,8,512]{3,2,1,0:T(8,128)(2,1)}, bf16[16,2,8,512]{3,2,1,0:T(8,128)(2,1)S(1)}, u32[]{:S(2)}) copy-start(bf16[16,2,8,512]{3,2,1,0:T(8,128)(2,1)S(1)} %collective-permute-done.8) | copy-start | bytes 786436
  47.7 1.5 collective-permute-start.12
  49.2 16.4 %copy-start.16 = (bf16[64,512]{1,0:T(8,128)(2,1)}, bf16[64,512]{1,0:T(8,128)(2,1)S(1)}, u32[]{:S(2)}) copy-start(bf16[64,512]{1,0:T(8,128)(2,1)S(1)} %collective-permute-done.12) | copy-start | bytes 196612
  49.2 8.6 %collective-permute-start.15 = (bf16[144,512]{1,0:T(8,128)(2,1)S(1)}, bf16[144,512]{1,0:T(8,128)(2,1)S(1)}, u32[]{:S(2)}, u32[]{:S(2)}) collective-permute-start(bf16[144,512]{1,0:T(8,128)(2,1)S(1)} %get-tuple-element.68.refs_2_), channel_id=1, source_target_pairs={{0,3},{1,2},{2,1},{3,0},{4,7},{5,6},{6,5},{7,4},{8,11},{9,10},{10,... | collective-permute-start | bytes 442376 | tf_op jit(solution)/shard_map/ppermute | solution.py:25
  52.8 12.8 %collective-permute-start.14 = (bf16[144,512]{1,0:T(8,128)(2,1)S(1)}, bf16[144,512]{1,0:T(8,128)(2,1)S(1)}, u32[]{:S(2)}, u32[]{:S(2)}) collective-permute-start(bf16[144,512]{1,0:T(8,128)(2,1)S(1)} %get-tuple-element.68.refs_2_), channel_id=1, source_target_pairs={{0,2},{1,3},{2,0},{3,1},{4,6},{5,7},{6,4},{7,5},{8,10},{9,11},{10,... | collective-permute-start | bytes 442376 | tf_op jit(solution)/shard_map/ppermute | solution.py:25
  52.8 12.8 %collective-permute-start.13 = (bf16[144,512]{1,0:T(8,128)(2,1)S(1)}, bf16[144,512]{1,0:T(8,128)(2,1)S(1)}, u32[]{:S(2)}, u32[]{:S(2)}) collective-permute-start(bf16[144,512]{1,0:T(8,128)(2,1)S(1)} %get-tuple-element.68.refs_2_), channel_id=1, source_target_pairs={{0,1},{1,0},{2,3},{3,2},{4,5},{5,4},{6,7},{7,6},{8,9},{9,8},{10,11... | collective-permute-start | bytes 442376 | tf_op jit(solution)/shard_map/ppermute | solution.py:25
  53.6 17.6 %collective-permute-start.21 = (bf16[64,512]{1,0:T(8,128)(2,1)}, bf16[64,512]{1,0:T(8,128)(2,1)}, u32[]{:S(2)}, u32[]{:S(2)}) collective-permute-start(bf16[64,512]{1,0:T(8,128)(2,1)} %copy-done.11), channel_id=1, source_target_pairs={{0,12},{4,8},{8,4},{12,0},{16,28},{20,24},{24,20},{28,16},{1,13},{... | collective-permute-start | bytes 196616 | tf_op jit(solution)/shard_map/ppermute | solution.py:25
  54.1 16.3 %collective-permute-start.16 = (bf16[320,512]{1,0:T(8,128)(2,1)S(1)}, bf16[320,512]{1,0:T(8,128)(2,1)}, u32[]{:S(2)}, u32[]{:S(2)}) collective-permute-start(bf16[320,512]{1,0:T(8,128)(2,1)S(1)} %get-tuple-element.71), channel_id=1, source_target_pairs={{0,8},{4,12},{8,0},{12,4},{16,24},{20,28},{24,16},{28,20},{1,9},{5... | collective-permute-start | bytes 983048 | tf_op jit(solution)/shard_map/ppermute | solution.py:25
  66.0 0.7 copy-start.7
  66.8 0.7 copy-start.8
  67.5 0.7 copy-start.9
  68.2 7.4 %collective-permute-start.18 = (bf16[64,2176]{1,0:T(8,128)(2,1)}, bf16[64,2176]{1,0:T(8,128)(2,1)S(1)}, u32[]{:S(2)}, u32[]{:S(2)}) collective-permute-start(bf16[64,2176]{1,0:T(8,128)(2,1)} %copy-done.9), channel_id=1, source_target_pairs={{0,4},{4,0},{8,12},{12,8},{16,20},{20,16},{24,28},{28,24},{1,5},{5... | collective-permute-start | bytes 835592 | tf_op jit(solution)/shard_map/ppermute | solution.py:25
  68.5 10.3 %collective-permute-start.19 = (bf16[64,2176]{1,0:T(8,128)(2,1)}, bf16[64,2176]{1,0:T(8,128)(2,1)S(1)}, u32[]{:S(2)}, u32[]{:S(2)}) collective-permute-start(bf16[64,2176]{1,0:T(8,128)(2,1)} %copy-done.8), channel_id=1, source_target_pairs={{0,8},{4,12},{8,0},{12,4},{16,24},{20,28},{24,16},{28,20},{1,9},{5... | collective-permute-start | bytes 835592 | tf_op jit(solution)/shard_map/ppermute | solution.py:25
  70.0 13.3 %collective-permute-start.20 = (bf16[64,2176]{1,0:T(8,128)(2,1)}, bf16[64,2176]{1,0:T(8,128)(2,1)S(1)}, u32[]{:S(2)}, u32[]{:S(2)}) collective-permute-start(bf16[64,2176]{1,0:T(8,128)(2,1)} %copy-done.7), channel_id=1, source_target_pairs={{0,12},{4,8},{8,4},{12,0},{16,28},{20,24},{24,20},{28,16},{1,13},{... | collective-permute-start | bytes 835592 | tf_op jit(solution)/shard_map/ppermute | solution.py:25
  72.1 11.2 %collective-permute-start.24 = (bf16[256,512]{1,0:T(8,128)(2,1)S(1)}, bf16[256,512]{1,0:T(8,128)(2,1)S(1)}, u32[]{:S(2)}, u32[]{:S(2)}) collective-permute-start(bf16[256,512]{1,0:T(8,128)(2,1)S(1)} %pad_maximum_fusion.2.refs_4_), channel_id=1, source_target_pairs={{0,3},{1,2},{2,1},{3,0},{4,7},{5,6},{6,5},{7,4},{8,11},{9,10},{10,... | collective-permute-start | bytes 786440 | tf_op jit(solution)/shard_map/ppermute | solution.py:25
  74.7 22.0 %collective-permute-start.23 = (bf16[256,512]{1,0:T(8,128)(2,1)S(1)}, bf16[256,512]{1,0:T(8,128)(2,1)S(1)}, u32[]{:S(2)}, u32[]{:S(2)}) collective-permute-start(bf16[256,512]{1,0:T(8,128)(2,1)S(1)} %pad_maximum_fusion.2.refs_4_), channel_id=1, source_target_pairs={{0,2},{1,3},{2,0},{3,1},{4,6},{5,7},{6,4},{7,5},{8,10},{9,11},{10,... | collective-permute-start | bytes 786440 | tf_op jit(solution)/shard_map/ppermute | solution.py:25
  75.7 21.0 %collective-permute-start.22 = (bf16[256,512]{1,0:T(8,128)(2,1)S(1)}, bf16[256,512]{1,0:T(8,128)(2,1)S(1)}, u32[]{:S(2)}, u32[]{:S(2)}) collective-permute-start(bf16[256,512]{1,0:T(8,128)(2,1)S(1)} %pad_maximum_fusion.2.refs_4_), channel_id=1, source_target_pairs={{0,1},{1,0},{2,3},{3,2},{4,5},{5,4},{6,7},{7,6},{8,9},{9,8},{10,11... | collective-permute-start | bytes 786440 | tf_op jit(solution)/shard_map/ppermute | solution.py:25
  78.8 44.7 %collective-permute-start.17 = (bf16[1,2,8,2,8,512]{5,4,3,2,1,0:T(8,128)(2,1)S(1)}, bf16[1,2,8,2,8,512]{5,4,3,2,1,0:T(8,128)(2,1)S(1)}, u32[]{:S(2)}, u32[]{:S(2)}) collective-permute-start(bf16[1,2,8,2,8,512]{5,4,3,2,1,0:T(8,128)(2,1)S(1)} %get-tuple-element.99), channel_id=1, source_target_pairs={{0,16},{4,20},{8,24},{12,28},{16,0},{20,4},{24,8},{28,12},{1,17},{... | collective-permute-start | bytes 786440 | tf_op jit(solution)/shard_map/ppermute | solution.py:25
  83.4 13.3 %copy-start.15 = (bf16[64,2176]{1,0:T(8,128)(2,1)}, bf16[64,2176]{1,0:T(8,128)(2,1)S(1)}, u32[]{:S(2)}) copy-start(bf16[64,2176]{1,0:T(8,128)(2,1)S(1)} %collective-permute-done.20.refs_3_) | copy-start | bytes 835588
  119.9 23.2 %collective-permute-start.25 = (bf16[64,2048]{1,0:T(8,128)(2,1)S(1)}, bf16[64,2048]{1,0:T(8,128)(2,1)S(1)}, u32[]{:S(2)}, u32[]{:S(2)}) collective-permute-start(bf16[64,2048]{1,0:T(8,128)(2,1)S(1)} %get-tuple-element.82), channel_id=1, source_target_pairs={{0,4},{4,0},{8,12},{12,8},{16,20},{20,16},{24,28},{28,24},{1,5},{5... | collective-permute-start | bytes 786440 | tf_op jit(solution)/shard_map/ppermute | solution.py:25
  120.0 23.2 %collective-permute-start.26 = (bf16[64,2048]{1,0:T(8,128)(2,1)S(1)}, bf16[64,2048]{1,0:T(8,128)(2,1)S(1)}, u32[]{:S(2)}, u32[]{:S(2)}) collective-permute-start(bf16[64,2048]{1,0:T(8,128)(2,1)S(1)} %get-tuple-element.83), channel_id=1, source_target_pairs={{0,8},{4,12},{8,0},{12,4},{16,24},{20,28},{24,16},{28,20},{1,9},{5... | collective-permute-start | bytes 786440 | tf_op jit(solution)/shard_map/ppermute | solution.py:25
  121.6 12.8 %collective-permute-start.31 = (bf16[256,512]{1,0:T(8,128)(2,1)S(1)}, bf16[256,512]{1,0:T(8,128)(2,1)S(1)}, u32[]{:S(2)}, u32[]{:S(2)}) collective-permute-start(bf16[256,512]{1,0:T(8,128)(2,1)S(1)} %get-tuple-element.90), channel_id=1, source_target_pairs={{0,1},{1,0},{2,3},{3,2},{4,5},{5,4},{6,7},{7,6},{8,9},{9,8},{10,11... | collective-permute-start | bytes 786440 | tf_op jit(solution)/shard_map/ppermute | solution.py:25
  121.6 21.3 %collective-permute-start.32 = (bf16[256,512]{1,0:T(8,128)(2,1)S(1)}, bf16[256,512]{1,0:T(8,128)(2,1)S(1)}, u32[]{:S(2)}, u32[]{:S(2)}) collective-permute-start(bf16[256,512]{1,0:T(8,128)(2,1)S(1)} %get-tuple-element.91), channel_id=1, source_target_pairs={{0,2},{1,3},{2,0},{3,1},{4,6},{5,7},{6,4},{7,5},{8,10},{9,11},{10,... | collective-permute-start | bytes 786440 | tf_op jit(solution)/shard_map/ppermute | solution.py:25
  123.5 19.4 %collective-permute-start.33 = (bf16[256,512]{1,0:T(8,128)(2,1)S(1)}, bf16[256,512]{1,0:T(8,128)(2,1)S(1)}, u32[]{:S(2)}, u32[]{:S(2)}) collective-permute-start(bf16[256,512]{1,0:T(8,128)(2,1)S(1)} %get-tuple-element.92), channel_id=1, source_target_pairs={{0,3},{1,2},{2,1},{3,0},{4,7},{5,6},{6,5},{7,4},{8,11},{9,10},{10,... | collective-permute-start | bytes 786440 | tf_op jit(solution)/shard_map/ppermute | solution.py:25
  134.3 8.8 %collective-permute-start.27 = (bf16[64,2048]{1,0:T(8,128)(2,1)S(1)}, bf16[64,2048]{1,0:T(8,128)(2,1)S(1)}, u32[]{:S(2)}, u32[]{:S(2)}) collective-permute-start(bf16[64,2048]{1,0:T(8,128)(2,1)S(1)} %get-tuple-element.84), channel_id=1, source_target_pairs={{0,12},{4,8},{8,4},{12,0},{16,28},{20,24},{24,20},{28,16},{1,13},{... | collective-permute-start | bytes 786440 | tf_op jit(solution)/shard_map/ppermute | solution.py:25
  143.1 9.5 %collective-permute-start.36 = (bf16[64,512]{1,0:T(8,128)(2,1)S(1)}, bf16[64,512]{1,0:T(8,128)(2,1)S(1)}, u32[]{:S(2)}, u32[]{:S(2)}) collective-permute-start(bf16[64,512]{1,0:T(8,128)(2,1)S(1)} %get-tuple-element.100), channel_id=1, source_target_pairs={{0,12},{4,8},{8,4},{12,0},{16,28},{20,24},{24,20},{28,16},{1,13},{... | collective-permute-start | bytes 196616 | tf_op jit(solution)/shard_map/ppermute | solution.py:25
  143.7 12.2 %collective-permute-start.28 = (bf16[128,512]{1,0:T(8,128)(2,1)S(1)}, bf16[128,512]{1,0:T(8,128)(2,1)S(1)}, u32[]{:S(2)}, u32[]{:S(2)}) collective-permute-start(bf16[128,512]{1,0:T(8,128)(2,1)S(1)} %get-tuple-element.86), channel_id=1, source_target_pairs={{0,1},{1,0},{2,3},{3,2},{4,5},{5,4},{6,7},{7,6},{8,9},{9,8},{10,11... | collective-permute-start | bytes 393224 | tf_op jit(solution)/shard_map/ppermute | solution.py:25
  149.2 12.9 %collective-permute-start.29 = (bf16[128,512]{1,0:T(8,128)(2,1)S(1)}, bf16[128,512]{1,0:T(8,128)(2,1)S(1)}, u32[]{:S(2)}, u32[]{:S(2)}) collective-permute-start(bf16[128,512]{1,0:T(8,128)(2,1)S(1)} %get-tuple-element.87), channel_id=1, source_target_pairs={{0,2},{1,3},{2,0},{3,1},{4,6},{5,7},{6,4},{7,5},{8,10},{9,11},{10,... | collective-permute-start | bytes 393224 | tf_op jit(solution)/shard_map/ppermute | solution.py:25
  149.2 12.8 %collective-permute-start.30 = (bf16[128,512]{1,0:T(8,128)(2,1)S(1)}, bf16[128,512]{1,0:T(8,128)(2,1)S(1)}, u32[]{:S(2)}, u32[]{:S(2)}) collective-permute-start(bf16[128,512]{1,0:T(8,128)(2,1)S(1)} %get-tuple-element.88), channel_id=1, source_target_pairs={{0,3},{1,2},{2,1},{3,0},{4,7},{5,6},{6,5},{7,4},{8,11},{9,10},{10,... | collective-permute-start | bytes 393224 | tf_op jit(solution)/shard_map/ppermute | solution.py:25
  151.6 4.3 %collective-permute-start.35 = (bf16[64,512]{1,0:T(8,128)(2,1)S(1)}, bf16[64,512]{1,0:T(8,128)(2,1)S(1)}, u32[]{:S(2)}, u32[]{:S(2)}) collective-permute-start(bf16[64,512]{1,0:T(8,128)(2,1)S(1)} %get-tuple-element.101), channel_id=1, source_target_pairs={{0,8},{4,12},{8,0},{12,4},{16,24},{20,28},{24,16},{28,20},{1,9},{5... | collective-permute-start | bytes 196616 | tf_op jit(solution)/shard_map/ppermute | solution.py:25
  152.6 3.3 %collective-permute-start.34 = (bf16[64,512]{1,0:T(8,128)(2,1)S(1)}, bf16[64,512]{1,0:T(8,128)(2,1)S(1)}, u32[]{:S(2)}, u32[]{:S(2)}) collective-permute-start(bf16[64,512]{1,0:T(8,128)(2,1)S(1)} %get-tuple-element.102), channel_id=1, source_target_pairs={{0,4},{4,0},{8,12},{12,8},{16,20},{20,16},{24,28},{28,24},{1,5},{5... | collective-permute-start | bytes 196616 | tf_op jit(solution)/shard_map/ppermute | solution.py:25
  (2 other events, 1.2 us)

commit v4 on v3

--- a/solution.py
+++ b/solution.py
@@ -9,6 +9,7 @@
 
 D = 4096
 SLOTS = 64
+PART = 3
 MIG = 4
 EPSILON = 1e-05
 BF = jnp.bfloat16
@@ -37,20 +38,29 @@
     return pl.ds(pl.multiple_of(start, 128), width)
 
 
-def local_call(kernel, in_specs, args, outs, scratch=(), vmem=16, flops=0, moved=0):
+def local_call(kernel, in_specs, args, outs, scratch=(), vmem=16, flops=0, moved=0, after=()):
+    count, waits = len(args), tuple(after)
+
+    def run(*refs):
+        kernel(*refs[:count], *refs[count + len(waits) :])
+
     return pl.pallas_call(
-        kernel,
+        run,
         out_shape=outs,
-        in_specs=in_specs,
+        in_specs=list(in_specs) + [pl.BlockSpec(memory_space=pl.ANY)] * len(waits),
         out_specs=[VMEM] * len(outs),
         scratch_shapes=list(scratch),
         compiler_params=pltpu.CompilerParams(vmem_limit_bytes=vmem * MIB),
         cost_estimate=pl.CostEstimate(flops=flops, bytes_accessed=moved, transcendentals=0),
-    )(*args)
+    )(*args, *waits)
 
 
 def shape(dims, dtype):
     return jax.ShapeDtypeStruct(dims, dtype)
+
+
+def far(dims, dtype):
+    return pltpu.HBM(dims, dtype)
 
 
 def page_kernel(pool, moved, rows, slot, table, length, out):
@@ -74,17 +84,19 @@
                 out[j, p] = jnp.where(token + p * page_len < length[i], page, 0.0).astype(out.dtype)
 
 
-def take_pages(pool, moved, rows, slot, table, length):
+def take_pages(pool, moved, rows, slot, table, length, after=()):
     pages = table.shape[0] // length.shape[0]
     outs = [shape((rows.shape[0], pages) + pool.shape[1:], pool.dtype)]
     args = (pool, moved, rows, slot, table, length)
-    return local_call(page_kernel, [VMEM] * 2 + [SMEM] * 4, args, outs, moved=5 * MIB)[0]
-
-
-def split_kernel(place, x, *outs):
-    width = outs[0].shape[1]
-    for s, out in enumerate(outs):
-        out[...] = x[:, lanes((place[0] ^ s) * width, width)]
+    return local_call(page_kernel, [VMEM] * 2 + [SMEM] * 4, args, outs, moved=5 * MIB, after=after)[0]
+
+
+def split_kernel(place, x, order, *outs):
+    blocks, order_out = outs[:-1], outs[-1]
+    width = blocks[0].shape[1]
+    for s, block in enumerate(blocks):
+        block[...] = x[:, lanes((place[0] ^ s) * width, width)]
+    order_out[...] = order[...]
 
 
 def movers_kernel(n_pair, selector, attention, residual, pair, own):
@@ -169,13 +181,16 @@
     early[rows:, rows : 2 * rows] = low
     chosen = pick(selector[...], scaled[:, wide:]).astype(BF)
     for s in range(experts):
-        late[s][:SLOTS] = chosen[s * SLOTS : (s + 1) * SLOTS]
+        late[s][:SLOTS, : chosen.shape[1]] = chosen[s * SLOTS : (s + 1) * SLOTS]
     late[2][SLOTS:] = pages[...]
 
 
 def dispatch_kernel(ne, experts, *refs):
     place, selector = refs[:2]
-    blocks, outs, stats_out = refs[2 : 2 + ne], refs[2 + ne : -1], refs[-1]
+    blocks, late, refs = refs[2 : 2 + ne], refs[2 + ne : 2 + ne + experts], refs[2 + ne + experts :]
+    outs, stats_out, late_out = refs[:experts], refs[experts], refs[experts + 1]
+    for t in range(experts):
+        late_out[t * SLOTS : (t + 1) * SLOTS] = late[t][:SLOTS, : late_out.shape[1]]
     wide = blocks[0].shape[1]
     rows = selector.shape[1]
     stats = jnp.zeros(stats_out.shape, F32)
@@ -201,8 +216,9 @@
     gate, up, down = refs[experts + ne : experts + ne + 3]
     refs = refs[experts + ne + 3 :]
     late_out, early_out = refs[:ne], refs[ne : ne + experts]
-    rows, scale, active = refs[ne + experts :]
+    done, rows, scale, active = refs[ne + experts :]
     step = pl.program_id(0)
+    done[...] = jnp.zeros(done.shape, I32)
     rest = late[0].shape[1]
     wide = (early[0].shape[1] - 128) // ne
     feats = wide + rest
@@ -252,6 +268,7 @@
         (1, hidden, wide + rest), lambda g, place: (0, 0, jnp.maximum(g - tiles, 0))
     )
     outs = [shape((slots, rest), BF)] * ne + [shape((SLOTS, ne * wide), BF)] * experts
+    outs = outs + [shape((8, 128), I32)]
     values = pl.pallas_call(
         functools.partial(expert_kernel, ne, experts, tiles),
         grid_spec=pltpu.PrefetchScalarGridSpec(
@@ -271,18 +288,25 @@
             flops=6 * slots * D * hidden, bytes_accessed=6 * D * hidden, transcendentals=0
         ),
     )(place, *early, *late, w_gate, w_up, w_down)
-    return values[:ne], values[ne:]
+    return values[:ne], values[ne:-1], values[-1]
 
 
 def weigh_kernel(ne, experts, *refs):
     place, high, low = refs[:3]
-    blocks, outs, buf, total = refs[3 : 3 + experts], refs[3 + experts : 3 + experts + ne], *refs[3 + experts + ne :]
+    blocks, late = refs[3 : 3 + experts], refs[3 + experts : 3 + experts + ne]
+    refs = refs[3 + experts + ne :]
+    outs, late_outs, (buf, total) = refs[:ne], refs[ne : ne + experts], refs[ne + experts :]
     for t in range(experts):
         buf[t * SLOTS : (t + 1) * SLOTS] = blocks[t][...]
     total[...] = pick(high[...], buf[...]) + pick(low[...], buf[...])
     wide = outs[0].shape[1]
     for s in range(ne):
         outs[s][...] = total[:, lanes((place[0] ^ s) * wide, wide)].astype(outs[s].dtype)
+    late_sum = late[0][...].astype(F32)
+    for block in late[1:]:
+        late_sum = late_sum + block[...].astype(F32)
+    for t in range(experts):
+        late_outs[t][...] = late_sum[t * SLOTS : (t + 1) * SLOTS].astype(BF)
 
 
 def finish_kernel(ne, experts, wide, *refs):
@@ -323,21 +347,22 @@
     feats = residual.shape[1]
     kblock = D // half
     experts = n // 2
-    rest = feats // 2
+    rest = max(128, feats * PART // 8 // 128 * 128)
     wide = feats - rest
     place = ze.reshape(1).astype(I32)
 
     pair_place = q.reshape(1).astype(I32)
-    attn_blocks = local_call(
+    *attn_blocks, came_from = local_call(
         split_kernel,
-        [SMEM, VMEM],
-        (pair_place, attention_out),
-        [shape((rows, kblock), BF)] * half,
+        [SMEM, VMEM, VMEM],
+        (pair_place, attention_out, came_from.reshape(n, rows)),
+        [far((rows, kblock), BF)] * half + [shape((n, rows), I32)],
+        vmem=60,
         moved=2 * MIB,
     )
+    came_from = came_from.reshape(-1)
     attn_blocks = [attn_blocks[0]] + [swap(attn_blocks[s], "req", 2 * s) for s in range(1, half)]
     w_other = swap(w_out, "req", 1)
-    came_from, _ = lax.optimization_barrier((came_from, attn_blocks[0]))
 
     local = jnp.arange(rows, dtype=I32)
     in_new = came_from[None, :] == (me * rows + local)[:, None]
@@ -354,7 +379,7 @@
     n_hand = -(-(n_pair + 2 * MIG) // 16) * 16
     send_hot = (jnp.arange(n_send, dtype=I32)[:, None] == send_slot[None, :])
     send_row = jnp.sum(jnp.where(send_hot, local[None, :], 0), axis=1)
-    send_pick, w_other = lax.optimization_barrier((send_hot.astype(BF), w_other))
+    send_pick = send_hot.astype(BF)
 
     source = jnp.stack(
         [lax.dynamic_slice_in_dim(came_from, (2 * (q ^ t) + k) * rows, rows) for t in range(half)]
@@ -382,6 +407,7 @@
         (send_pick, attention_out, residual),
         [shape((n_pair, D + feats), BF), shape((n_send, feats), BF)],
         moved=2 * MIB,
+        after=[w_other],
     )
     pair_rows = swap(pair_rows, "req", 1)
     late_blocks = local_call(
@@ -435,7 +461,6 @@
     table = page_table.reshape(-1)
     none = jnp.full((n_send,), -1, I32)
     no_rows = page_pool[:2].reshape((1, 2) + page_pool.shape[1:])
-    send_row, _ = lax.optimization_barrier((send_row, parts[0]))
     moving = take_pages(page_pool, no_rows, send_row, none, table, cache_len)
     page = moving.shape[1:]
     pair_pages = swap(moving[:n_pair], "req", 1).reshape((half, MIG) + page)
@@ -447,34 +472,36 @@
     page_rows = pages[:, 1].reshape(-1, page[-1])
 
     router = jnp.pad(router_w.T, ((0, 8 - experts), (0, 0)))
-    late_rows_of = [SLOTS + (page_rows.shape[0] if s == 2 else 0) for s in range(experts)]
+    late_shapes = [(SLOTS, rest)] * experts
+    late_shapes[2] = (SLOTS + page_rows.shape[0], page[-1])
     normed = local_call(
         functools.partial(norm_kernel, half, experts, wide),
         [VMEM] * (4 + half),
         (norm_gain[None, :], router, slot_pick, page_rows, *parts),
-        [shape((rows, feats), F32), shape((rows + 16, wide), BF)]
-        + [shape((count, rest), BF) for count in late_rows_of],
+        [shape((rows, feats), F32), far((rows + 16, wide), BF)]
+        + [far(dims, BF) for dims in late_shapes],
         flops=2 * experts * SLOTS * rows * rest,
         moved=3 * MIB,
     )
     hidden, early = normed[:2]
     late = [normed[2 + s] if s == 0 else swap(normed[2 + s], "req", s) for s in range(experts)]
-    early, _ = lax.optimization_barrier((early, late[1]))
     early_blocks = [early] + [swap(early, "exp", s) for s in range(1, ne)]
     came_pages = late[2][SLOTS:].reshape((half // 2,) + block)
     pages = jnp.stack([pages[:, 0], came_pages], axis=1)
-    late = jnp.concatenate([x[:SLOTS] for x in late], axis=0)
-    late_rows = [late] + [swap(late, "exp", s) for s in range(1, ne)]
-
     outgoing = local_call(
         functools.partial(dispatch_kernel, ne, experts),
-        [SMEM] + [VMEM] * (1 + ne),
-        (place, slot_pick, *early_blocks),
-        [shape((SLOTS, ne * wide + 128), BF)] * experts + [shape((16, rows), F32)],
+        [SMEM] + [VMEM] * (1 + ne + experts),
+        (place, slot_pick, *early_blocks, *late),
+        [far((SLOTS, ne * wide + 128), BF)] * experts
+        + [shape((16, rows), F32), far((experts * SLOTS, rest), BF)],
+        vmem=60,
         flops=2 * experts * SLOTS * rows * ne * wide,
         moved=3 * MIB,
     )
-    stats = outgoing[-1]
+    late = outgoing[experts + 1]
+    late_rows = [late] + [swap(late, "exp", s) for s in range(1, ne)]
+
+    stats = outgoing[experts]
     early_rows = [swap(outgoing[s], "req", s) if s else outgoing[s] for s in range(experts)]
 
     inverse = lax.rsqrt(stats[8] / D + EPSILON)
@@ -486,21 +513,15 @@
     )
     gate_high, gate_low = halves(gate_slots)
 
-    pages, _ = lax.optimization_barrier((pages, outgoing[0]))
     for bit in range(1, stages):
         pages = pages.reshape((half >> (bit + 1), 2, 1 << bit) + block)
         came_pages = swap(pages[:, 1], "req", 2 << bit)
         pages = jnp.stack([pages[:, 0], came_pages], axis=1)
     moved_pages = pages.reshape((half * 2 * MIG,) + page)
 
-    down_late, down_early = expert_call(place, early_rows, late_rows, w_gate, w_up, w_down, ne)
-    late_sum = down_late[0].astype(F32)
-    for s in range(1, ne):
-        late_sum = late_sum + swap(down_late[s], "exp", s).astype(F32)
-    late_sum = late_sum.astype(BF).reshape(experts, SLOTS, rest)
-    late_back = [swap(late_sum[s], "req", s) if s else late_sum[s] for s in range(experts)]
+    down_late, down_early, done = expert_call(place, early_rows, late_rows, w_gate, w_up, w_down, ne)
+    late_blocks = [down_late[0]] + [swap(down_late[s], "exp", s) for s in range(1, ne)]
     early_back = [swap(down_early[s], "req", s) if s else down_early[s] for s in range(experts)]
-    own_slot, _ = lax.optimization_barrier((own_slot, down_early[0]))
     new_pages = take_pages(
         page_pool,
         moved_pages,
@@ -508,18 +529,23 @@
         jnp.where(own_stays, -1, own_slot),
         table,
         cache_len,
-    )
-    place, new_pages = lax.optimization_barrier((place, new_pages))
+        [done],
+    )
     weighted = local_call(
         functools.partial(weigh_kernel, ne, experts),
-        [SMEM] + [VMEM] * (2 + experts),
-        (place, gate_high, gate_low, *early_back),
-        [shape((rows, wide), F32)] + [shape((rows, wide), BF)] * (ne - 1),
+        [SMEM] + [VMEM] * (2 + experts + ne),
+        (place, gate_high, gate_low, *early_back, *late_blocks),
+        [shape((rows, wide), F32)]
+        + [shape((rows, wide), BF)] * (ne - 1)
+        + [shape((SLOTS, rest), BF)] * experts,
         [pltpu.VMEM((experts * SLOTS, ne * wide), BF), pltpu.VMEM((rows, ne * wide), F32)],
         flops=4 * rows * experts * SLOTS * ne * wide,
         moved=3 * MIB,
     )
     early_parts = [weighted[0]] + [swap(weighted[s], "exp", s) for s in range(1, ne)]
+    late_back = [
+        swap(weighted[ne + s], "req", s) if s else weighted[ne] for s in range(experts)
+    ]
     mixed = local_call(
         functools.partial(finish_kernel, ne, experts, wide),
         [VMEM] * (3 + ne + experts),

time: 164 us -> 157 us (0.957)
  waiting for transfers between devices: 65.9 us -> 54.5 us
  Pallas kernels: 39 us -> 43.7 us
  local copies, waits for them, and re-layouts: 9.78 us -> 5.82 us
  starting transfers between devices: 41.2 us -> 43.2 us
  other arithmetic: 5.98 us -> 7.69 us
    ppermute x37, waiting for transfers between devices: 65.9 us -> 54.5 us  [swap(): return lax.ppermute(x, axis, [(i, i ^ s) for i in range(n)])]
    pallas_call x10, Pallas kernels: 15.8 us -> 20.9 us  [local_call(): pl.pallas_call(run, out_shape=outs, in_specs=list(in_specs) + [pl.BlockSp...]
    unnamed x59 -> x47, local copies, waits for them, and re-layouts: 6.05 us -> 2.97 us
    ppermute x37, starting transfers between devices: 41.2 us -> 43.2 us  [swap(): return lax.ppermute(x, axis, [(i, i ^ s) for i in range(n)])]
  transfers between devices with their start and end apart: 37 -> 37, of which waited for: 16 -> 16; matrix products, arithmetic and copies ran while one was open for 6% -> 7% of each run, Pallas kernels for 18% -> 9%
where the time goes in v4:
time: 157 us; the launch traced here: 156 us
  waiting for transfers between devices  54.5 us (35%)
  Pallas kernels  43.7 us (28%)
  starting transfers between devices  43.2 us (28%)
  other arithmetic  7.69 us (5%)
  local copies, waits for them, and re-layouts  5.82 us (4%)
    ppermute x37, waiting for transfers between devices, swap(): return lax.ppermute(x, axis, [(i, i ^ s) for i in range(n)])  54.5 us
    ppermute x37, starting transfers between devices, swap(): return lax.ppermute(x, axis, [(i, i ^ s) for i in range(n)])  43.2 us
    pallas_call x1, Pallas kernels, expert_call(): pl.pallas_call(functools.partial(expert_kernel, ne, experts, tiles), grid...  22.8 us
    pallas_call x10, Pallas kernels, local_call(): pl.pallas_call(run, out_shape=outs, in_specs=list(in_specs) + [pl.BlockSp...  20.9 us
  transfers between devices with their start and end apart: 37, of which 16 were waited for; matrix products, arithmetic and copies ran while one was open for 7% of the time, Pallas kernels for 9%

profile of v4, /device:TPU:0, one launch (start us, length us, event | category | flops | bytes accessed | tf_op | source)
XLA Modules:
  0.0 156.1 jit_solution(11768710449483138215)
XLA Ops:
  0.7 2.4 %shard_map.140 = (bf16[128,1024]{1,0:T(8,128)(2,1)}, bf16[128,1024]{1,0:T(8,128)(2,1)}, bf16[128,1024]{1,0:T(8,128)(2,1)}, bf16[128,1024]{1,0:T(8,128)(2,1)}, s32[8,128]{1,0:T(8,128)}) custom-call(s32[1]{0:T(128)} %bitcast.4.refs_0_, bf16[128,4096]{1,0:T(8,128)(2,1)} %refs_1_.3, s32[8,128]{1,0:T(8,128)} %bitcast.81), custom_call_target="tpu_custom_call" | custom-call | bytes 2097152 | tf_op jit(solution)/shard_map/pallas_call | solution.py:47
  3.0 3.0 %collective-permute-start.2 = (bf16[128,1024]{1,0:T(8,128)(2,1)}, bf16[128,1024]{1,0:T(8,128)(2,1)}, u32[]{:S(2)}, u32[]{:S(2)}) collective-permute-start(bf16[128,1024]{1,0:T(8,128)(2,1)} %get-tuple-element.48), channel_id=1, source_target_pairs={{0,8},{4,12},{8,0},{12,4},{16,24},{20,28},{24,16},{28,20},{1,9},{5... | collective-permute-start | bytes 786440 | tf_op jit(solution)/shard_map/ppermute | solution.py:26
  6.0 1.5 collective-permute-start.3
  7.6 0.7 fusion.10
  8.3 0.9 select_reduce_fusion
  9.4 0.9 dynamic-slice_bitcast_fusion.3
  10.9 0.7 slice_bitcast_fusion.1.refs_1_
  11.6 0.7 fusion.8.refs_2_
  12.3 1.0 fusion.refs_1_
  13.4 0.7 select_reduce_fusion.4
  14.1 0.8 copy.26
  15.3 0.6 collective-permute-start.5
  15.9 1.0 collective-permute-done.5.refs_1_
  17.0 2.0 %collective-permute-start.6 = (bf16[32,1024]{1,0:T(8,128)(2,1)S(1)}, bf16[32,1024]{1,0:T(8,128)(2,1)S(1)}, u32[]{:S(2)}, u32[]{:S(2)}) collective-permute-start(bf16[32,1024]{1,0:T(8,128)(2,1)S(1)} %get-tuple-element.54), channel_id=1, source_target_pairs={{0,8},{4,12},{8,0},{12,4},{16,24},{20,28},{24,16},{28,20},{1,9},{5... | collective-permute-start | bytes 196616 | tf_op jit(solution)/shard_map/ppermute | solution.py:26
  19.0 1.5 collective-permute-start.7
  20.7 1.3 shard_map.141
  22.2 1.1 collective-permute-done.7.refs_12_
  23.2 2.4 %collective-permute-done.8.refs_13_ = bf16[32,1024]{1,0:T(8,128)(2,1)S(1)} collective-permute-done((bf16[32,1024]{1,0:T(8,128)(2,1)S(1)}, bf16[32,1024]{1,0:T(8,128)(2,1)S(1)}, u32[]{:S(2)}, u32[]{:S(2)}) %collective-permute-start.8) | collective-permute-done | bytes 65568 | tf_op jit(solution)/shard_map/ppermute | solution.py:26
  25.7 0.6 copy-done.22
  26.3 5.8 %shard_map.144 = (f32[128,1024]{1,0:T(8,128)}, bf16[128,1024]{1,0:T(8,128)(2,1)}, bf16[128,1024]{1,0:T(8,128)(2,1)}, bf16[128,1024]{1,0:T(8,128)(2,1)}) custom-call(s32[1]{0:T(128)} %bitcast.10.refs_0_, bf16[512,640]{1,0:T(8,128)(2,1)} %fusion.refs_1_, bf16[128,256]{1,0:T(8,128)(2,1)} %fusion.8.refs_2_, bf16[128,1024]{1,0:T(8,128)(2,1)} %refs_3_.1, ...), custom_call_target="tpu_custom_call" | custom-call | flops 1744830464 | bytes 6291456 | tf_op jit(solution)/shard_map/pallas_call | solution.py:47
  32.1 0.6 collective-permute-start.9
  32.7 0.5 collective-permute-start.10
  33.2 2.4 %collective-permute-start.11 = (bf16[128,1024]{1,0:T(8,128)(2,1)}, bf16[128,1024]{1,0:T(8,128)(2,1)S(1)}, u32[]{:S(2)}, u32[]{:S(2)}) collective-permute-start(bf16[128,1024]{1,0:T(8,128)(2,1)} %get-tuple-element.60), channel_id=1, source_target_pairs={{0,24},{4,28},{8,16},{12,20},{16,8},{20,12},{24,0},{28,4},{1,25},{... | collective-permute-start | bytes 786440 | tf_op jit(solution)/shard_map/ppermute | solution.py:26
  35.9 5.7 %collective-permute-done.9.refs_5_ = bf16[128,1024]{1,0:T(8,128)(2,1)S(1)} collective-permute-done((bf16[128,1024]{1,0:T(8,128)(2,1)}, bf16[128,1024]{1,0:T(8,128)(2,1)S(1)}, u32[]{:S(2)}, u32[]{:S(2)}) %collective-permute-start.9) | collective-permute-done | bytes 262176 | tf_op jit(solution)/shard_map/ppermute | solution.py:26
  41.6 3.5 %collective-permute-done.10.refs_6_ = bf16[128,1024]{1,0:T(8,128)(2,1)S(1)} collective-permute-done((bf16[128,1024]{1,0:T(8,128)(2,1)}, bf16[128,1024]{1,0:T(8,128)(2,1)S(1)}, u32[]{:S(2)}, u32[]{:S(2)}) %collective-permute-start.10) | collective-permute-done | bytes 262176 | tf_op jit(solution)/shard_map/ppermute | solution.py:26
  45.1 1.2 shard_map.145
  46.3 1.6 collective-permute-start.16
  47.9 3.6 %collective-permute-start.14 = (bf16[144,640]{1,0:T(8,128)(2,1)}, bf16[144,640]{1,0:T(8,128)(2,1)S(1)}, u32[]{:S(2)}, u32[]{:S(2)}) collective-permute-start(bf16[144,640]{1,0:T(8,128)(2,1)} %get-tuple-element.61.refs_2_), channel_id=1, source_target_pairs={{0,3},{1,2},{2,1},{3,0},{4,7},{5,6},{6,5},{7,4},{8,11},{9,10},{10,... | collective-permute-start | bytes 552968 | tf_op jit(solution)/shard_map/ppermute | solution.py:26
  51.5 0.8 collective-permute-start.12
  52.3 1.4 collective-permute-done.15.refs_7_
  54.0 3.6 %collective-permute-done.17.refs_9_ = bf16[64,384]{1,0:T(8,128)(2,1)S(1)} collective-permute-done((bf16[64,384]{1,0:T(8,128)(2,1)}, bf16[64,384]{1,0:T(8,128)(2,1)S(1)}, u32[]{:S(2)}, u32[]{:S(2)}) %collective-permute-start.17) | collective-permute-done | bytes 49184 | tf_op jit(solution)/shard_map/ppermute | solution.py:26
  57.6 7.7 %collective-permute-done.13.refs_4_ = bf16[144,640]{1,0:T(8,128)(2,1)S(1)} collective-permute-done((bf16[144,640]{1,0:T(8,128)(2,1)}, bf16[144,640]{1,0:T(8,128)(2,1)S(1)}, u32[]{:S(2)}, u32[]{:S(2)}) %collective-permute-start.13) | collective-permute-done | bytes 184352 | tf_op jit(solution)/shard_map/ppermute | solution.py:26
  65.4 0.6 copy-done.15
  66.1 2.9 %shard_map.146 = (bf16[64,2688]{1,0:T(8,128)(2,1)}, bf16[64,2688]{1,0:T(8,128)(2,1)}, bf16[64,2688]{1,0:T(8,128)(2,1)}, bf16[64,2688]{1,0:T(8,128)(2,1)}, f32[16,128]{1,0:T(8,128)}, /*index=5*/bf16[256,384]{1,0:T(8,128)(2,1)}) custom-call(s32[1]{0:T(128)} %bitcast.refs_0_.place, bf16[256,128]{1,0:T(8,128)(2,1)} %copy-done.2, ...), custom_call_target="tpu_custom_call" | custom-call | flops 167772160 | bytes 3145728 | tf_op jit(solution)/shard_map/pallas_call | solution.py:47
  69.0 2.6 %collective-permute-start.23 = (bf16[256,384]{1,0:T(8,128)(2,1)}, bf16[256,384]{1,0:T(8,128)(2,1)S(1)}, u32[]{:S(2)}, u32[]{:S(2)}) collective-permute-start(bf16[256,384]{1,0:T(8,128)(2,1)} %get-tuple-element.72.refs_4_), channel_id=1, source_target_pairs={{0,3},{1,2},{2,1},{3,0},{4,7},{5,6},{6,5},{7,4},{8,11},{9,10},{10,... | collective-permute-start | bytes 589832 | tf_op jit(solution)/shard_map/ppermute | solution.py:26
  71.6 0.7 rsqrt_bitcast_fusion
  72.3 0.7 multiply_bitcast_fusion
  73.1 0.4 collective-permute-start.19
  73.5 1.4 collective-permute-start.20
  75.0 1.0 slice.73
  75.9 1.1 fusion.5
  77.0 2.0 %collective-permute-done.23.refs_7_ = bf16[256,384]{1,0:T(8,128)(2,1)S(1)} collective-permute-done((bf16[256,384]{1,0:T(8,128)(2,1)}, bf16[256,384]{1,0:T(8,128)(2,1)S(1)}, u32[]{:S(2)}, u32[]{:S(2)}) %collective-permute-start.23) | collective-permute-done | bytes 196640 | tf_op jit(solution)/shard_map/ppermute | solution.py:26
  79.0 5.7 %collective-permute-start.21 = (bf16[256,384]{1,0:T(8,128)(2,1)}, bf16[256,384]{1,0:T(8,128)(2,1)S(1)}, u32[]{:S(2)}, u32[]{:S(2)}) collective-permute-start(bf16[256,384]{1,0:T(8,128)(2,1)} %get-tuple-element.72.refs_4_), channel_id=1, source_target_pairs={{0,1},{1,0},{2,3},{3,2},{4,5},{5,4},{6,7},{7,6},{8,9},{9,8},{10,11... | collective-permute-start | bytes 589832 | tf_op jit(solution)/shard_map/ppermute | solution.py:26
  84.7 2.3 %collective-permute-done.22.refs_6_ = bf16[256,384]{1,0:T(8,128)(2,1)} collective-permute-done((bf16[256,384]{1,0:T(8,128)(2,1)}, bf16[256,384]{1,0:T(8,128)(2,1)}, u32[]{:S(2)}, u32[]{:S(2)}) %collective-permute-start.22) | collective-permute-done | bytes 196640 | tf_op jit(solution)/shard_map/ppermute | solution.py:26
  87.0 2.0 %collective-permute-done.21.refs_5_ = bf16[256,384]{1,0:T(8,128)(2,1)S(1)} collective-permute-done((bf16[256,384]{1,0:T(8,128)(2,1)}, bf16[256,384]{1,0:T(8,128)(2,1)S(1)}, u32[]{:S(2)}, u32[]{:S(2)}) %collective-permute-start.21) | collective-permute-done | bytes 196640 | tf_op jit(solution)/shard_map/ppermute | solution.py:26
  89.0 1.7 %collective-permute-done.20.refs_3_ = bf16[64,2688]{1,0:T(8,128)(2,1)S(1)} collective-permute-done((bf16[64,2688]{1,0:T(8,128)(2,1)}, bf16[64,2688]{1,0:T(8,128)(2,1)S(1)}, u32[]{:S(2)}, u32[]{:S(2)}) %collective-permute-start.20) | collective-permute-done | bytes 344096 | tf_op jit(solution)/shard_map/ppermute | solution.py:26
  90.7 0.7 copy-done.13
  91.4 22.8 %shard_map.147 = (bf16[256,384]{1,0:T(8,128)(2,1)S(1)}, bf16[256,384]{1,0:T(8,128)(2,1)S(1)}, bf16[256,384]{1,0:T(8,128)(2,1)S(1)}, bf16[256,384]{1,0:T(8,128)(2...) custom-call(s32[1]{0:T(128)} %bitcast.refs_0_.place, ...), custom_call_target="tpu_custom_call" | custom-call | flops 11274289152 | bytes 44040192 | tf_op jit(solution)/shard_map/pallas_call | solution.py:272
  114.2 1.9 %collective-permute-start.27 = (bf16[256,384]{1,0:T(8,128)(2,1)S(1)}, bf16[256,384]{1,0:T(8,128)(2,1)S(1)}, u32[]{:S(2)}, u32[]{:S(2)}) collective-permute-start(bf16[256,384]{1,0:T(8,128)(2,1)S(1)} %get-tuple-element.78), channel_id=1, source_target_pairs={{0,1},{1,0},{2,3},{3,2},{4,5},{5,4},{6,7},{7,6},{8,9},{9,8},{10,11... | collective-permute-start | bytes 589832 | tf_op jit(solution)/shard_map/ppermute | solution.py:26
  116.2 1.1 collective-permute-start.28
  117.3 0.4 collective-permute-start.25
  117.7 1.4 collective-permute-start.26
  119.3 6.3 %collective-permute-done.27.refs_8_ = bf16[256,384]{1,0:T(8,128)(2,1)S(1)} collective-permute-done((bf16[256,384]{1,0:T(8,128)(2,1)S(1)}, bf16[256,384]{1,0:T(8,128)(2,1)S(1)}, u32[]{:S(2)}, u32[]{:S(2)}) %collective-permute-start.27) | collective-permute-done | bytes 196640 | tf_op jit(solution)/shard_map/ppermute | solution.py:26
  125.6 2.5 %collective-permute-done.28.refs_9_ = bf16[256,384]{1,0:T(8,128)(2,1)S(1)} collective-permute-done((bf16[256,384]{1,0:T(8,128)(2,1)S(1)}, bf16[256,384]{1,0:T(8,128)(2,1)S(1)}, u32[]{:S(2)}, u32[]{:S(2)}) %collective-permute-start.28) | collective-permute-done | bytes 196640 | tf_op jit(solution)/shard_map/ppermute | solution.py:26
  128.1 2.5 %collective-permute-start.29 = (bf16[256,384]{1,0:T(8,128)(2,1)S(1)}, bf16[256,384]{1,0:T(8,128)(2,1)S(1)}, u32[]{:S(2)}, u32[]{:S(2)}) collective-permute-start(bf16[256,384]{1,0:T(8,128)(2,1)S(1)} %get-tuple-element.80), channel_id=1, source_target_pairs={{0,3},{1,2},{2,1},{3,0},{4,7},{5,6},{6,5},{7,4},{8,11},{9,10},{10,... | collective-permute-start | bytes 589832 | tf_op jit(solution)/shard_map/ppermute | solution.py:26
  130.6 5.1 %collective-permute-done.29.refs_10_ = bf16[256,384]{1,0:T(8,128)(2,1)S(1)} collective-permute-done((bf16[256,384]{1,0:T(8,128)(2,1)S(1)}, bf16[256,384]{1,0:T(8,128)(2,1)S(1)}, u32[]{:S(2)}, u32[]{:S(2)}) %collective-permute-start.29) | collective-permute-done | bytes 196640 | tf_op jit(solution)/shard_map/ppermute | solution.py:26
  135.7 0.8 shard_map.148
  136.5 3.4 %collective-permute-start.30 = (bf16[128,640]{1,0:T(8,128)(2,1)S(1)}, bf16[128,640]{1,0:T(8,128)(2,1)S(1)}, u32[]{:S(2)}, u32[]{:S(2)}) collective-permute-start(bf16[128,640]{1,0:T(8,128)(2,1)S(1)} %get-tuple-element.82), channel_id=1, source_target_pairs={{0,1},{1,0},{2,3},{3,2},{4,5},{5,4},{6,7},{7,6},{8,9},{9,8},{10,11... | collective-permute-start | bytes 491528 | tf_op jit(solution)/shard_map/ppermute | solution.py:26
  140.0 2.4 %collective-permute-start.32 = (bf16[128,640]{1,0:T(8,128)(2,1)S(1)}, bf16[128,640]{1,0:T(8,128)(2,1)S(1)}, u32[]{:S(2)}, u32[]{:S(2)}) collective-permute-start(bf16[128,640]{1,0:T(8,128)(2,1)S(1)} %get-tuple-element.84), channel_id=1, source_target_pairs={{0,3},{1,2},{2,1},{3,0},{4,7},{5,6},{6,5},{7,4},{8,11},{9,10},{10,... | collective-permute-start | bytes 491528 | tf_op jit(solution)/shard_map/ppermute | solution.py:26
  142.4 0.4 collective-permute-start.34
  142.8 0.8 collective-permute-start.35
  143.6 5.2 %shard_map.150 = bf16[128,2,8,512]{3,2,1,0:T(8,128)(2,1)} custom-call(bf16[256,8,512]{2,1,0:T(8,128)(2,1)S(1)} %copy-done, bf16[32,2,8,512]{3,2,1,0:T(8,128)(2,1)S(1)} %bitcast.69, s32[128]{0:T(128)S(1)} %get-tuple-element.98.refs_2_, s32[128]{0:T(128)S(1)} %get-tuple-element.96.refs_3_, s32[256]{0:T(256)S(1)} %reshape.519.refs_4_, s32[128]{0:T(128)S(1)} %copy-done.8, ...), custom_call_target="tpu_custom_call" | custom-call | bytes 5242880 | tf_op jit(solution)/shard_map/pallas_call | solution.py:47
  148.8 6.2 %collective-permute-done.31.refs_5_ = bf16[128,640]{1,0:T(8,128)(2,1)S(1)} collective-permute-done((bf16[128,640]{1,0:T(8,128)(2,1)S(1)}, bf16[128,640]{1,0:T(8,128)(2,1)S(1)}, u32[]{:S(2)}, u32[]{:S(2)}) %collective-permute-start.31) | collective-permute-done | bytes 163872 | tf_op jit(solution)/shard_map/ppermute | solution.py:26
  155.0 1.1 shard_map.149
  (110 shorter events, 2.7 us)
Async XLA Ops:
  0.6 14.4 %copy-start.1 = (bf16[128,4096]{1,0:T(8,128)(2,1)S(1)}, bf16[128,4096]{1,0:T(8,128)(2,1)}, u32[]{:S(2)}) copy-start(bf16[128,4096]{1,0:T(8,128)(2,1)} %refs_1_.3) | copy-start | bytes 3145732
  0.6 14.4 %copy-start.5 = (bf16[128,1024]{1,0:T(8,128)(2,1)S(1)}, bf16[128,1024]{1,0:T(8,128)(2,1)}, u32[]{:S(2)}) copy-start(bf16[128,1024]{1,0:T(8,128)(2,1)} %refs_3_.1) | copy-start | bytes 786436
  0.7 15.2 %copy-start.19 = (s32[128,2]{0,1:T(2,128)S(1)}, s32[128,2]{0,1:T(2,128)}, u32[]{:S(2)}) copy-start(s32[128,2]{0,1:T(2,128)} %param.22) | copy-start | bytes 3076
  3.0 17.6 %copy-start = (bf16[256,8,512]{2,1,0:T(8,128)(2,1)S(1)}, bf16[256,8,512]{2,1,0:T(8,128)(2,1)}, u32[]{:S(2)}) copy-start(bf16[256,8,512]{2,1,0:T(8,128)(2,1)} %refs_0_.3) | copy-start | bytes 6291460
  3.0 17.6 %copy-start.8 = (s32[128]{0:T(128)S(1)}, s32[128]{0:T(128)}, u32[]{:S(2)}) copy-start(s32[128]{0:T(128)} %refs_5_.3) | copy-start | bytes 1540
  3.0 17.5 %collective-permute-start.2 = (bf16[128,1024]{1,0:T(8,128)(2,1)}, bf16[128,1024]{1,0:T(8,128)(2,1)}, u32[]{:S(2)}, u32[]{:S(2)}) collective-permute-start(bf16[128,1024]{1,0:T(8,128)(2,1)} %get-tuple-element.48), channel_id=1, source_target_pairs={{0,8},{4,12},{8,0},{12,4},{16,24},{20,28},{24,16},{28,20},{1,9},{5... | collective-permute-start | bytes 786440 | tf_op jit(solution)/shard_map/ppermute | solution.py:26
  6.0 16.0 %collective-permute-start.3 = (bf16[128,1024]{1,0:T(8,128)(2,1)}, bf16[128,1024]{1,0:T(8,128)(2,1)}, u32[]{:S(2)}, u32[]{:S(2)}) collective-permute-start(bf16[128,1024]{1,0:T(8,128)(2,1)} %get-tuple-element.49), channel_id=1, source_target_pairs={{0,16},{4,20},{8,24},{12,28},{16,0},{20,4},{24,8},{28,12},{1,17},{... | collective-permute-start | bytes 786440 | tf_op jit(solution)/shard_map/ppermute | solution.py:26
  7.5 14.6 %collective-permute-start.4 = (bf16[128,1024]{1,0:T(8,128)(2,1)}, bf16[128,1024]{1,0:T(8,128)(2,1)}, u32[]{:S(2)}, u32[]{:S(2)}) collective-permute-start(bf16[128,1024]{1,0:T(8,128)(2,1)} %get-tuple-element.50), channel_id=1, source_target_pairs={{0,24},{4,28},{8,16},{12,20},{16,8},{20,12},{24,0},{28,4},{1,25},{... | collective-permute-start | bytes 786440 | tf_op jit(solution)/shard_map/ppermute | solution.py:26
  7.6 7.4 %collective-permute-start.1 = (bf16[512,1024]{1,0:T(8,128)(2,1)}, bf16[512,1024]{1,0:T(8,128)(2,1)}, u32[]{:S(2)}, u32[]{:S(2)}) collective-permute-start(bf16[512,1024]{1,0:T(8,128)(2,1)} %refs_4_.1), channel_id=1, source_target_pairs={{0,4},{4,0},{8,12},{12,8},{16,20},{20,16},{24,28},{28,24},{1,5},{5... | collective-permute-start | bytes 3145736 | tf_op jit(solution)/shard_map/ppermute | solution.py:26
  15.3 1.6 %collective-permute-start.5 = (bf16[16,5120]{1,0:T(8,128)(2,1)S(1)}, bf16[16,5120]{1,0:T(8,128)(2,1)S(1)}, u32[]{:S(2)}, u32[]{:S(2)}) collective-permute-start(bf16[16,5120]{1,0:T(8,128)(2,1)S(1)} %get-tuple-element.51), channel_id=1, source_target_pairs={{0,4},{4,0},{8,12},{12,8},{16,20},{20,16},{24,28},{28,24},{1,5},{5... | collective-permute-start | bytes 491528 | tf_op jit(solution)/shard_map/ppermute | solution.py:26
  16.9 8.7 %copy-start.9 = (bf16[32,1024]{1,0:T(8,128)(2,1)}, bf16[32,1024]{1,0:T(8,128)(2,1)S(1)}, u32[]{:S(2)}) copy-start(bf16[32,1024]{1,0:T(8,128)(2,1)S(1)} %get-tuple-element.53.refs_10_) | copy-start | bytes 196612
  17.0 5.2 %collective-permute-start.6 = (bf16[32,1024]{1,0:T(8,128)(2,1)S(1)}, bf16[32,1024]{1,0:T(8,128)(2,1)S(1)}, u32[]{:S(2)}, u32[]{:S(2)}) collective-permute-start(bf16[32,1024]{1,0:T(8,128)(2,1)S(1)} %get-tuple-element.54), channel_id=1, source_target_pairs={{0,8},{4,12},{8,0},{12,4},{16,24},{20,28},{24,16},{28,20},{1,9},{5... | collective-permute-start | bytes 196616 | tf_op jit(solution)/shard_map/ppermute | solution.py:26
  19.0 4.3 %collective-permute-start.7 = (bf16[32,1024]{1,0:T(8,128)(2,1)S(1)}, bf16[32,1024]{1,0:T(8,128)(2,1)S(1)}, u32[]{:S(2)}, u32[]{:S(2)}) collective-permute-start(bf16[32,1024]{1,0:T(8,128)(2,1)S(1)} %get-tuple-element.55), channel_id=1, source_target_pairs={{0,16},{4,20},{8,24},{12,28},{16,0},{20,4},{24,8},{28,12},{1,17},{... | collective-permute-start | bytes 196616 | tf_op jit(solution)/shard_map/ppermute | solution.py:26
  20.5 5.2 %collective-permute-start.8 = (bf16[32,1024]{1,0:T(8,128)(2,1)S(1)}, bf16[32,1024]{1,0:T(8,128)(2,1)S(1)}, u32[]{:S(2)}, u32[]{:S(2)}) collective-permute-start(bf16[32,1024]{1,0:T(8,128)(2,1)S(1)} %get-tuple-element.56), channel_id=1, source_target_pairs={{0,24},{4,28},{8,16},{12,20},{16,8},{20,12},{24,0},{28,4},{1,25},{... | collective-permute-start | bytes 196616 | tf_op jit(solution)/shard_map/ppermute | solution.py:26
  22.0 13.8 %collective-permute-start = (bf16[16,2,8,512]{3,2,1,0:T(8,128)(2,1)S(1)}, bf16[16,2,8,512]{3,2,1,0:T(8,128)(2,1)S(1)}, u32[]{:S(2)}, u32[]{:S(2)}) collective-permute-start(bf16[16,2,8,512]{3,2,1,0:T(8,128)(2,1)S(1)} %slice.70), channel_id=1, source_target_pairs={{0,4},{4,0},{8,12},{12,8},{16,20},{20,16},{24,28},{28,24},{1,5},{5... | collective-permute-start | bytes 786440 | tf_op jit(solution)/shard_map/ppermute | solution.py:26
  22.1 3.5 %copy-start.20 = (bf16[32,1024]{1,0:T(8,128)(2,1)}, bf16[32,1024]{1,0:T(8,128)(2,1)S(1)}, u32[]{:S(2)}) copy-start(bf16[32,1024]{1,0:T(8,128)(2,1)S(1)} %collective-permute-done.6.refs_11_) | copy-start | bytes 196612
  23.2 2.4 %copy-start.21 = (bf16[32,1024]{1,0:T(8,128)(2,1)}, bf16[32,1024]{1,0:T(8,128)(2,1)S(1)}, u32[]{:S(2)}) copy-start(bf16[32,1024]{1,0:T(8,128)(2,1)S(1)} %collective-permute-done.7.refs_12_) | copy-start | bytes 196612
  25.7 0.6 copy-start.22
  26.3 9.5 %copy-start.18 = (f32[1024,4]{0,1:T(4,128)S(1)}, f32[1024,4]{0,1:T(4,128)}, u32[]{:S(2)}) copy-start(f32[1024,4]{0,1:T(4,128)} %param.16) | copy-start | bytes 49156
  26.3 18.8 %copy-start.7 = (f32[1024]{0:T(1024)S(1)}, f32[1024]{0:T(1024)}, u32[]{:S(2)}) copy-start(f32[1024]{0:T(1024)} %param.17) | copy-start | bytes 12292
  32.1 13.0 %copy-start.3 = (f32[128,1024]{1,0:T(8,128)S(1)}, f32[128,1024]{1,0:T(8,128)}, u32[]{:S(2)}) copy-start(f32[128,1024]{1,0:T(8,128)} %get-tuple-element.57.refs_4_) | copy-start | bytes 1572868
  32.1 9.5 %collective-permute-start.9 = (bf16[128,1024]{1,0:T(8,128)(2,1)}, bf16[128,1024]{1,0:T(8,128)(2,1)S(1)}, u32[]{:S(2)}, u32[]{:S(2)}) collective-permute-start(bf16[128,1024]{1,0:T(8,128)(2,1)} %get-tuple-element.58), channel_id=1, source_target_pairs={{0,8},{4,12},{8,0},{12,4},{16,24},{20,28},{24,16},{28,20},{1,9},{5... | collective-permute-start | bytes 786440 | tf_op jit(solution)/shard_map/ppermute | solution.py:26
  32.7 12.4 %collective-permute-start.10 = (bf16[128,1024]{1,0:T(8,128)(2,1)}, bf16[128,1024]{1,0:T(8,128)(2,1)S(1)}, u32[]{:S(2)}, u32[]{:S(2)}) collective-permute-start(bf16[128,1024]{1,0:T(8,128)(2,1)} %get-tuple-element.59), channel_id=1, source_target_pairs={{0,16},{4,20},{8,24},{12,28},{16,0},{20,4},{24,8},{28,12},{1,17},{... | collective-permute-start | bytes 786440 | tf_op jit(solution)/shard_map/ppermute | solution.py:26
  33.2 11.9 %collective-permute-start.11 = (bf16[128,1024]{1,0:T(8,128)(2,1)}, bf16[128,1024]{1,0:T(8,128)(2,1)S(1)}, u32[]{:S(2)}, u32[]{:S(2)}) collective-permute-start(bf16[128,1024]{1,0:T(8,128)(2,1)} %get-tuple-element.60), channel_id=1, source_target_pairs={{0,24},{4,28},{8,16},{12,20},{16,8},{20,12},{24,0},{28,4},{1,25},{... | collective-permute-start | bytes 786440 | tf_op jit(solution)/shard_map/ppermute | solution.py:26
  35.7 29.6 %copy-start.2 = (bf16[256,128]{1,0:T(8,128)(2,1)}, bf16[256,128]{1,0:T(8,128)(2,1)S(1)}, u32[]{:S(2)}) copy-start(bf16[256,128]{1,0:T(8,128)(2,1)S(1)} %convert_element_type.33.refs_2_.refs_1_) | copy-start | bytes 196612
  35.8 10.5 %copy-start.10 = (bf16[16,2,8,512]{3,2,1,0:T(8,128)(2,1)}, bf16[16,2,8,512]{3,2,1,0:T(8,128)(2,1)S(1)}, u32[]{:S(2)}) copy-start(bf16[16,2,8,512]{3,2,1,0:T(8,128)(2,1)S(1)} %pad_maximum_fusion.1) | copy-start | bytes 786436
  35.8 10.5 %copy-start.12 = (bf16[16,2,8,512]{3,2,1,0:T(8,128)(2,1)}, bf16[16,2,8,512]{3,2,1,0:T(8,128)(2,1)S(1)}, u32[]{:S(2)}) copy-start(bf16[16,2,8,512]{3,2,1,0:T(8,128)(2,1)S(1)} %collective-permute-done) | copy-start | bytes 786436
  46.3 19.0 %collective-permute-start.16 = (bf16[320,512]{1,0:T(8,128)(2,1)}, bf16[320,512]{1,0:T(8,128)(2,1)S(1)}, u32[]{:S(2)}, u32[]{:S(2)}) collective-permute-start(bf16[320,512]{1,0:T(8,128)(2,1)} %get-tuple-element.64), channel_id=1, source_target_pairs={{0,8},{4,12},{8,0},{12,4},{16,24},{20,28},{24,16},{28,20},{1,9},{5... | collective-permute-start | bytes 983048 | tf_op jit(solution)/shard_map/ppermute | solution.py:26
  47.9 9.8 %collective-permute-start.14 = (bf16[144,640]{1,0:T(8,128)(2,1)}, bf16[144,640]{1,0:T(8,128)(2,1)S(1)}, u32[]{:S(2)}, u32[]{:S(2)}) collective-permute-start(bf16[144,640]{1,0:T(8,128)(2,1)} %get-tuple-element.61.refs_2_), channel_id=1, source_target_pairs={{0,3},{1,2},{2,1},{3,0},{4,7},{5,6},{6,5},{7,4},{8,11},{9,10},{10,... | collective-permute-start | bytes 552968 | tf_op jit(solution)/shard_map/ppermute | solution.py:26
  51.5 13.8 %collective-permute-start.13 = (bf16[144,640]{1,0:T(8,128)(2,1)}, bf16[144,640]{1,0:T(8,128)(2,1)S(1)}, u32[]{:S(2)}, u32[]{:S(2)}) collective-permute-start(bf16[144,640]{1,0:T(8,128)(2,1)} %get-tuple-element.61.refs_2_), channel_id=1, source_target_pairs={{0,2},{1,3},{2,0},{3,1},{4,6},{5,7},{6,4},{7,5},{8,10},{9,11},{10,... | collective-permute-start | bytes 552968 | tf_op jit(solution)/shard_map/ppermute | solution.py:26
  51.5 13.8 %collective-permute-start.12 = (bf16[144,640]{1,0:T(8,128)(2,1)}, bf16[144,640]{1,0:T(8,128)(2,1)}, u32[]{:S(2)}, u32[]{:S(2)}) collective-permute-start(bf16[144,640]{1,0:T(8,128)(2,1)} %get-tuple-element.61.refs_2_), channel_id=1, source_target_pairs={{0,1},{1,0},{2,3},{3,2},{4,5},{5,4},{6,7},{7,6},{8,9},{9,8},{10,11... | collective-permute-start | bytes 552968 | tf_op jit(solution)/shard_map/ppermute | solution.py:26
  52.3 1.4 collective-permute-start.15
  53.7 11.6 %copy-start.16 = (bf16[64,384]{1,0:T(8,128)(2,1)}, bf16[64,384]{1,0:T(8,128)(2,1)S(1)}, u32[]{:S(2)}) copy-start(bf16[64,384]{1,0:T(8,128)(2,1)S(1)} %collective-permute-done.15.refs_7_) | copy-start | bytes 147460
  53.7 3.9 %collective-permute-start.17 = (bf16[64,384]{1,0:T(8,128)(2,1)}, bf16[64,384]{1,0:T(8,128)(2,1)S(1)}, u32[]{:S(2)}, u32[]{:S(2)}) collective-permute-start(bf16[64,384]{1,0:T(8,128)(2,1)} %get-tuple-element.65), channel_id=1, source_target_pairs={{0,12},{4,8},{8,4},{12,0},{16,28},{20,24},{24,20},{28,16},{1,13},{... | collective-permute-start | bytes 147464 | tf_op jit(solution)/shard_map/ppermute | solution.py:26
  57.6 7.7 %copy-start.17 = (bf16[64,384]{1,0:T(8,128)(2,1)}, bf16[64,384]{1,0:T(8,128)(2,1)S(1)}, u32[]{:S(2)}) copy-start(bf16[64,384]{1,0:T(8,128)(2,1)S(1)} %collective-permute-done.17.refs_9_) | copy-start | bytes 147460
  57.6 7.7 %copy-start.14 = (bf16[144,640]{1,0:T(8,128)(2,1)}, bf16[144,640]{1,0:T(8,128)(2,1)S(1)}, u32[]{:S(2)}) copy-start(bf16[144,640]{1,0:T(8,128)(2,1)S(1)} %collective-permute-done.14.refs_5_) | copy-start | bytes 552964
  65.3 0.7 copy-start.15
  65.3 0.8 copy-start.11
  69.0 22.4 %copy-start.4 = (bf16[64,2688]{1,0:T(8,128)(2,1)S(1)}, bf16[64,2688]{1,0:T(8,128)(2,1)}, u32[]{:S(2)}) copy-start(bf16[64,2688]{1,0:T(8,128)(2,1)} %get-tuple-element.68.refs_0_) | copy-start | bytes 1032196
  69.0 22.4 %copy-start.6 = (bf16[256,384]{1,0:T(8,128)(2,1)S(1)}, bf16[256,384]{1,0:T(8,128)(2,1)}, u32[]{:S(2)}) copy-start(bf16[256,384]{1,0:T(8,128)(2,1)} %get-tuple-element.72.refs_4_) | copy-start | bytes 589828
  69.0 10.0 %collective-permute-start.23 = (bf16[256,384]{1,0:T(8,128)(2,1)}, bf16[256,384]{1,0:T(8,128)(2,1)S(1)}, u32[]{:S(2)}, u32[]{:S(2)}) collective-permute-start(bf16[256,384]{1,0:T(8,128)(2,1)} %get-tuple-element.72.refs_4_), channel_id=1, source_target_pairs={{0,3},{1,2},{2,1},{3,0},{4,7},{5,6},{6,5},{7,4},{8,11},{9,10},{10,... | collective-permute-start | bytes 589832 | tf_op jit(solution)/shard_map/ppermute | solution.py:26
  71.6 15.4 %collective-permute-start.22 = (bf16[256,384]{1,0:T(8,128)(2,1)}, bf16[256,384]{1,0:T(8,128)(2,1)}, u32[]{:S(2)}, u32[]{:S(2)}) collective-permute-start(bf16[256,384]{1,0:T(8,128)(2,1)} %get-tuple-element.72.refs_4_), channel_id=1, source_target_pairs={{0,2},{1,3},{2,0},{3,1},{4,6},{5,7},{6,4},{7,5},{8,10},{9,11},{10,... | collective-permute-start | bytes 589832 | tf_op jit(solution)/shard_map/ppermute | solution.py:26
  73.0 15.9 %collective-permute-start.18 = (bf16[64,2688]{1,0:T(8,128)(2,1)}, bf16[64,2688]{1,0:T(8,128)(2,1)S(1)}, u32[]{:S(2)}, u32[]{:S(2)}) collective-permute-start(bf16[64,2688]{1,0:T(8,128)(2,1)} %get-tuple-element.69), channel_id=1, source_target_pairs={{0,4},{4,0},{8,12},{12,8},{16,20},{20,16},{24,28},{28,24},{1,5},{5... | collective-permute-start | bytes 1032200 | tf_op jit(solution)/shard_map/ppermute | solution.py:26
  73.1 15.9 %collective-permute-start.19 = (bf16[64,2688]{1,0:T(8,128)(2,1)}, bf16[64,2688]{1,0:T(8,128)(2,1)S(1)}, u32[]{:S(2)}, u32[]{:S(2)}) collective-permute-start(bf16[64,2688]{1,0:T(8,128)(2,1)} %get-tuple-element.70), channel_id=1, source_target_pairs={{0,8},{4,12},{8,0},{12,4},{16,24},{20,28},{24,16},{28,20},{1,9},{5... | collective-permute-start | bytes 1032200 | tf_op jit(solution)/shard_map/ppermute | solution.py:26
  73.5 17.2 %collective-permute-start.20 = (bf16[64,2688]{1,0:T(8,128)(2,1)}, bf16[64,2688]{1,0:T(8,128)(2,1)S(1)}, u32[]{:S(2)}, u32[]{:S(2)}) collective-permute-start(bf16[64,2688]{1,0:T(8,128)(2,1)} %get-tuple-element.71), channel_id=1, source_target_pairs={{0,12},{4,8},{8,4},{12,0},{16,28},{20,24},{24,20},{28,16},{1,13},{... | collective-permute-start | bytes 1032200 | tf_op jit(solution)/shard_map/ppermute | solution.py:26
  79.0 10.0 %collective-permute-start.21 = (bf16[256,384]{1,0:T(8,128)(2,1)}, bf16[256,384]{1,0:T(8,128)(2,1)S(1)}, u32[]{:S(2)}, u32[]{:S(2)}) collective-permute-start(bf16[256,384]{1,0:T(8,128)(2,1)} %get-tuple-element.72.refs_4_), channel_id=1, source_target_pairs={{0,1},{1,0},{2,3},{3,2},{4,5},{5,4},{6,7},{7,6},{8,9},{9,8},{10,11... | collective-permute-start | bytes 589832 | tf_op jit(solution)/shard_map/ppermute | solution.py:26
  90.7 0.7 copy-start.13
  114.2 11.4 %collective-permute-start.27 = (bf16[256,384]{1,0:T(8,128)(2,1)S(1)}, bf16[256,384]{1,0:T(8,128)(2,1)S(1)}, u32[]{:S(2)}, u32[]{:S(2)}) collective-permute-start(bf16[256,384]{1,0:T(8,128)(2,1)S(1)} %get-tuple-element.78), channel_id=1, source_target_pairs={{0,1},{1,0},{2,3},{3,2},{4,5},{5,4},{6,7},{7,6},{8,9},{9,8},{10,11... | collective-permute-start | bytes 589832 | tf_op jit(solution)/shard_map/ppermute | solution.py:26
  116.2 12.0 %collective-permute-start.28 = (bf16[256,384]{1,0:T(8,128)(2,1)S(1)}, bf16[256,384]{1,0:T(8,128)(2,1)S(1)}, u32[]{:S(2)}, u32[]{:S(2)}) collective-permute-start(bf16[256,384]{1,0:T(8,128)(2,1)S(1)} %get-tuple-element.79), channel_id=1, source_target_pairs={{0,2},{1,3},{2,0},{3,1},{4,6},{5,7},{6,4},{7,5},{8,10},{9,11},{10,... | collective-permute-start | bytes 589832 | tf_op jit(solution)/shard_map/ppermute | solution.py:26
  117.3 18.4 %collective-permute-start.24 = (bf16[64,2560]{1,0:T(8,128)(2,1)S(1)}, bf16[64,2560]{1,0:T(8,128)(2,1)S(1)}, u32[]{:S(2)}, u32[]{:S(2)}) collective-permute-start(bf16[64,2560]{1,0:T(8,128)(2,1)S(1)} %get-tuple-element.74), channel_id=1, source_target_pairs={{0,4},{4,0},{8,12},{12,8},{16,20},{20,16},{24,28},{28,24},{1,5},{5... | collective-permute-start | bytes 983048 | tf_op jit(solution)/shard_map/ppermute | solution.py:26
  117.3 18.4 %collective-permute-start.25 = (bf16[64,2560]{1,0:T(8,128)(2,1)S(1)}, bf16[64,2560]{1,0:T(8,128)(2,1)S(1)}, u32[]{:S(2)}, u32[]{:S(2)}) collective-permute-start(bf16[64,2560]{1,0:T(8,128)(2,1)S(1)} %get-tuple-element.75), channel_id=1, source_target_pairs={{0,8},{4,12},{8,0},{12,4},{16,24},{20,28},{24,16},{28,20},{1,9},{5... | collective-permute-start | bytes 983048 | tf_op jit(solution)/shard_map/ppermute | solution.py:26
  117.7 18.0 %collective-permute-start.26 = (bf16[64,2560]{1,0:T(8,128)(2,1)S(1)}, bf16[64,2560]{1,0:T(8,128)(2,1)S(1)}, u32[]{:S(2)}, u32[]{:S(2)}) collective-permute-start(bf16[64,2560]{1,0:T(8,128)(2,1)S(1)} %get-tuple-element.76), channel_id=1, source_target_pairs={{0,12},{4,8},{8,4},{12,0},{16,28},{20,24},{24,20},{28,16},{1,13},{... | collective-permute-start | bytes 983048 | tf_op jit(solution)/shard_map/ppermute | solution.py:26
  125.6 16.8 %collective-permute-start.36 = (bf16[1,2,8,2,8,512]{5,4,3,2,1,0:T(8,128)(2,1)S(1)}, bf16[1,2,8,2,8,512]{5,4,3,2,1,0:T(8,128)(2,1)S(1)}, u32[]{:S(2)}, u32[]{:S(2)}) collective-permute-start(bf16[1,2,8,2,8,512]{5,4,3,2,1,0:T(8,128)(2,1)S(1)} %get-tuple-element.95), channel_id=1, source_target_pairs={{0,16},{4,20},{8,24},{12,28},{16,0},{20,4},{24,8},{28,12},{1,17},{... | collective-permute-start | bytes 786440 | tf_op jit(solution)/shard_map/ppermute | solution.py:26
  128.1 7.6 %collective-permute-start.29 = (bf16[256,384]{1,0:T(8,128)(2,1)S(1)}, bf16[256,384]{1,0:T(8,128)(2,1)S(1)}, u32[]{:S(2)}, u32[]{:S(2)}) collective-permute-start(bf16[256,384]{1,0:T(8,128)(2,1)S(1)} %get-tuple-element.80), channel_id=1, source_target_pairs={{0,3},{1,2},{2,1},{3,0},{4,7},{5,6},{6,5},{7,4},{8,11},{9,10},{10,... | collective-permute-start | bytes 589832 | tf_op jit(solution)/shard_map/ppermute | solution.py:26
  136.5 6.3 %collective-permute-start.33 = (bf16[64,384]{1,0:T(8,128)(2,1)S(1)}, bf16[64,384]{1,0:T(8,128)(2,1)S(1)}, u32[]{:S(2)}, u32[]{:S(2)}) collective-permute-start(bf16[64,384]{1,0:T(8,128)(2,1)S(1)} %get-tuple-element.86), channel_id=1, source_target_pairs={{0,4},{4,0},{8,12},{12,8},{16,20},{20,16},{24,28},{28,24},{1,5},{5... | collective-permute-start | bytes 147464 | tf_op jit(solution)/shard_map/ppermute | solution.py:26
  136.5 12.2 %collective-permute-start.30 = (bf16[128,640]{1,0:T(8,128)(2,1)S(1)}, bf16[128,640]{1,0:T(8,128)(2,1)S(1)}, u32[]{:S(2)}, u32[]{:S(2)}) collective-permute-start(bf16[128,640]{1,0:T(8,128)(2,1)S(1)} %get-tuple-element.82), channel_id=1, source_target_pairs={{0,1},{1,0},{2,3},{3,2},{4,5},{5,4},{6,7},{7,6},{8,9},{9,8},{10,11... | collective-permute-start | bytes 491528 | tf_op jit(solution)/shard_map/ppermute | solution.py:26
  139.9 15.0 %collective-permute-start.31 = (bf16[128,640]{1,0:T(8,128)(2,1)S(1)}, bf16[128,640]{1,0:T(8,128)(2,1)S(1)}, u32[]{:S(2)}, u32[]{:S(2)}) collective-permute-start(bf16[128,640]{1,0:T(8,128)(2,1)S(1)} %get-tuple-element.83), channel_id=1, source_target_pairs={{0,2},{1,3},{2,0},{3,1},{4,6},{5,7},{6,4},{7,5},{8,10},{9,11},{10,... | collective-permute-start | bytes 491528 | tf_op jit(solution)/shard_map/ppermute | solution.py:26
  140.0 15.0 %collective-permute-start.32 = (bf16[128,640]{1,0:T(8,128)(2,1)S(1)}, bf16[128,640]{1,0:T(8,128)(2,1)S(1)}, u32[]{:S(2)}, u32[]{:S(2)}) collective-permute-start(bf16[128,640]{1,0:T(8,128)(2,1)S(1)} %get-tuple-element.84), channel_id=1, source_target_pairs={{0,3},{1,2},{2,1},{3,0},{4,7},{5,6},{6,5},{7,4},{8,11},{9,10},{10,... | collective-permute-start | bytes 491528 | tf_op jit(solution)/shard_map/ppermute | solution.py:26
  142.4 6.4 %collective-permute-start.34 = (bf16[64,384]{1,0:T(8,128)(2,1)S(1)}, bf16[64,384]{1,0:T(8,128)(2,1)S(1)}, u32[]{:S(2)}, u32[]{:S(2)}) collective-permute-start(bf16[64,384]{1,0:T(8,128)(2,1)S(1)} %get-tuple-element.87), channel_id=1, source_target_pairs={{0,8},{4,12},{8,0},{12,4},{16,24},{20,28},{24,16},{28,20},{1,9},{5... | collective-permute-start | bytes 147464 | tf_op jit(solution)/shard_map/ppermute | solution.py:26
  142.8 6.0 %collective-permute-start.35 = (bf16[64,384]{1,0:T(8,128)(2,1)S(1)}, bf16[64,384]{1,0:T(8,128)(2,1)S(1)}, u32[]{:S(2)}, u32[]{:S(2)}) collective-permute-start(bf16[64,384]{1,0:T(8,128)(2,1)S(1)} %get-tuple-element.88), channel_id=1, source_target_pairs={{0,12},{4,8},{8,4},{12,0},{16,28},{20,24},{24,20},{28,16},{1,13},{... | collective-permute-start | bytes 147464 | tf_op jit(solution)/shard_map/ppermute | solution.py:26

commit v5 on v4

--- a/solution.py
+++ b/solution.py
@@ -10,6 +10,7 @@
 D = 4096
 SLOTS = 64
 PART = 3
+AHEAD = 3
 MIG = 4
 EPSILON = 1e-05
 BF = jnp.bfloat16
@@ -38,7 +39,7 @@
     return pl.ds(pl.multiple_of(start, 128), width)
 
 
-def local_call(kernel, in_specs, args, outs, scratch=(), vmem=16, flops=0, moved=0, after=()):
+def local_call(kernel, in_specs, args, outs, scratch=(), vmem=16, flops=0, moved=0, after=(), out_specs=None):
     count, waits = len(args), tuple(after)
 
     def run(*refs):
@@ -48,7 +49,7 @@
         run,
         out_shape=outs,
         in_specs=list(in_specs) + [pl.BlockSpec(memory_space=pl.ANY)] * len(waits),
-        out_specs=[VMEM] * len(outs),
+        out_specs=out_specs or [VMEM] * len(outs),
         scratch_shapes=list(scratch),
         compiler_params=pltpu.CompilerParams(vmem_limit_bytes=vmem * MIB),
         cost_estimate=pl.CostEstimate(flops=flops, bytes_accessed=moved, transcendentals=0),
@@ -99,14 +100,37 @@
     order_out[...] = order[...]
 
 
-def movers_kernel(n_pair, selector, attention, residual, pair, own):
+def movers_kernel(half, spot, order, attention, residual, pair, own, row_out):
+    n, rows = order.shape
+    down, across = (lax.broadcasted_iota(I32, (rows, rows), d) for d in (0, 1))
+    mine = (2 * spot[0] + spot[1]) * rows + down
+    found = jnp.zeros((rows, rows), F32)
+    for g in range(1, n):
+        found = found + jnp.where(order[g : g + 1] == mine, float(g), 0.0)
+    dest = jnp.broadcast_to(jnp.sum(found, axis=1, keepdims=True), (rows, rows))
+    dest_row = dest.T
+    rank = jnp.sum(jnp.where((dest == dest_row) & (down < across), 1.0, 0.0), axis=0, keepdims=True)
+    rank = rank.astype(I32)
+    to = dest_row[:1].astype(I32)
+    far_off, core = (to >> 1) ^ spot[0], to & 1
+    kept = jnp.where(far_off != 0, (half + far_off - 1) * MIG + rank, -1)
+    slot = jnp.where(core != spot[1], far_off * MIG + rank, kept)
+    chosen = lax.broadcasted_iota(I32, (own.shape[0], rows), 0) == slot
+    selector = jnp.where(chosen, 1.0, 0.0)
+    numbers = lax.broadcasted_iota(I32, selector.shape, 1).astype(F32)
+    number = jnp.sum(selector * numbers, axis=1, keepdims=True)
+    row_out[...] = jnp.broadcast_to(number, row_out.shape).astype(I32)
+    selector = selector.astype(BF)
+    n_pair = pair.shape[0]
     pair[:, : attention.shape[1]] = pick(selector[:n_pair], attention[...]).astype(BF)
-    moving = pick(selector[...], residual[...]).astype(BF)
+    moving = pick(selector, residual[...]).astype(BF)
     pair[:, attention.shape[1] :] = moving[:n_pair]
     own[...] = moving
 
 
-def handover_kernel(half, place, pair, own, *outs):
+def handover_kernel(half, place, pair, own, order, *outs):
+    outs[-1][...] = order[...]
+    outs = outs[:-1]
     n_pair = half * MIG
     width = own.shape[1]
     for s, out in enumerate(outs):
@@ -115,6 +139,23 @@
         blank = jnp.zeros((out.shape[0] - n_pair - 2 * MIG, width), BF)
         columns = pair[:, lanes((place[0] ^ s) * width, width)]
         out[...] = jnp.concatenate([columns, first, second, blank], axis=0)
+
+
+def slots_kernel(experts, spot, routes, picked, slots):
+    rows = routes.shape[1]
+    ids = lax.broadcasted_iota(I32, (8, rows), 0)
+    named = jnp.where((ids == routes[0:1]) | (ids == routes[1:2]), 1.0, 0.0)
+    down, across = (lax.broadcasted_iota(I32, (rows, rows), d) for d in (0, 1))
+    before = pick(named.astype(BF), jnp.where(down < across, 1.0, 0.0).astype(BF))
+    at = lax.broadcasted_iota(I32, picked.shape, 0)
+    chosen = jnp.zeros(picked.shape, F32)
+    for top in range(2):
+        route = routes[top : top + 1]
+        rank = jnp.sum(jnp.where(ids == route, before, 0.0), axis=0, keepdims=True).astype(I32)
+        slot = (route ^ spot[0]) * SLOTS + rank
+        slots[top : top + 1] = slot
+        chosen = chosen + jnp.where(at == slot, 1.0, 0.0)
+    picked[...] = chosen.astype(BF)
 
 
 def project_kernel(half, *refs):
@@ -185,6 +226,14 @@
     late[2][SLOTS:] = pages[...]
 
 
+def hold_kernel(x, out):
+    out[...] = x[...]
+
+
+def hold(x, after):
+    return local_call(hold_kernel, [VMEM], (x,), [far(x.shape, x.dtype)], after=[after])[0]
+
+
 def dispatch_kernel(ne, experts, *refs):
     place, selector = refs[:2]
     blocks, late, refs = refs[2 : 2 + ne], refs[2 + ne : 2 + ne + experts], refs[2 + ne + experts :]
@@ -211,91 +260,155 @@
             outs[t][:, columns] = chosen[t * SLOTS : (t + 1) * SLOTS]
 
 
-def expert_kernel(ne, experts, tiles, place, *refs):
+def expert_kernel(ne, experts, tile, spot, *refs):
     early, late = refs[:experts], refs[experts : experts + ne]
-    gate, up, down = refs[experts + ne : experts + ne + 3]
-    refs = refs[experts + ne + 3 :]
+    gate, up, down, stats = refs[experts + ne : experts + ne + 4]
+    refs = refs[experts + ne + 4 :]
     late_out, early_out = refs[:ne], refs[ne : ne + experts]
-    done, rows, scale, active = refs[ne + experts :]
-    step = pl.program_id(0)
-    done[...] = jnp.zeros(done.shape, I32)
+    stats_out = refs[ne + experts]
+    rows, pieces, active, gate_buf, up_buf, down_buf, late_buf, early_buf = refs[ne + experts + 1 : -3]
+    sems, load_sems, out_sems = refs[-3:]
+    place = spot[0]
     rest = late[0].shape[1]
     wide = (early[0].shape[1] - 128) // ne
     feats = wide + rest
-    tile = gate.shape[2]
-
-    @pl.when(step == 0)
-    def _():
+    tiles = gate.shape[2] // tile
+
+    def copies(f):
+        columns = lanes(f * tile, tile)
+        return [
+            pltpu.make_async_copy(gate.at[0, :, columns], gate_buf.at[:, columns], sems.at[0, f]),
+            pltpu.make_async_copy(up.at[0, :, columns], up_buf.at[:, columns], sems.at[1, f]),
+        ]
+
+    def down_copy(e):
+        return pltpu.make_async_copy(down.at[0, :, lanes(e * feats, feats)], down_buf.at[e], sems.at[2, e])
+
+    def early_copy(e, t):
+        columns = lanes(e * wide, wide)
+        return pltpu.make_async_copy(
+            early_buf.at[t, :, columns], early_out[t].at[:, columns], out_sems.at[e, t]
+        )
+
+    def late_copy(e, s):
+        return pltpu.make_async_copy(late_buf.at[e], late_out[s], out_sems.at[e, experts])
+
+    def start(unit):
+        @pl.when(unit < tiles)
+        def _():
+            for copy in copies(unit):
+                copy.start()
+
+        @pl.when((unit >= tiles) & (unit < tiles + ne))
+        def _():
+            down_copy(unit - tiles).start()
+
+    loads = []
+
+    def load(source, target):
+        loads.append(pltpu.make_async_copy(source, target, load_sems.at[len(loads)]))
+
+    for t in range(experts):
+        at = pl.ds(t * SLOTS, SLOTS)
+        load(early[t].at[:, pl.ds(ne * wide, 128)], pieces.at[at])
+        for e in range(ne):
+            load(early[t].at[:, pl.ds(e * wide, wide)], rows.at[at, pl.ds(e * feats, wide)])
+    for s in range(ne):
+        load(late[s], rows.at[:, lanes((place ^ s) * feats + wide, rest)])
+    for copy in loads:
+        copy.start()
+    start(jnp.int32(0))
+    stats_out[...] = stats[...]
+    for copy in loads:
+        copy.wait()
+    for unit in range(1, AHEAD):
+        start(jnp.int32(unit))
+    scale = pieces[:, :1].astype(F32) + pieces[:, 1:2].astype(F32)
+
+    @pl.loop(0, tiles)
+    def _(f):
+        for copy in copies(f):
+            copy.wait()
+        start(f + AHEAD)
+        columns = lanes(f * tile, tile)
+        gate_h = pick(rows[...], gate_buf[:, columns]) * scale
+        up_h = pick(rows[...], up_buf[:, columns]) * scale
+        active[:, columns] = (gate_h / (1.0 + jnp.exp(-gate_h)) * up_h).astype(BF)
+
+    @pl.loop(0, ne)
+    def _(e):
+        down_copy(e).wait()
+        start(e + tiles + AHEAD)
+        value = pick(active[...], down_buf[e]).astype(BF)
+        late_buf[e] = value[:, wide:]
         for t in range(experts):
-            at = slice(t * SLOTS, (t + 1) * SLOTS)
-            for e in range(ne):
-                rows[at, e * feats : e * feats + wide] = early[t][:, e * wide : (e + 1) * wide]
-            pieces = early[t][:, ne * wide :].astype(F32)
-            scale[at] = pieces[:, :1] + pieces[:, 1:2]
+            early_buf[t, :, lanes(e * wide, wide)] = value[t * SLOTS : (t + 1) * SLOTS, :wide]
+            early_copy(e, t).start()
         for s in range(ne):
-            rows[:, lanes((place[0] ^ s) * feats + wide, rest)] = late[s][...]
-
-    @pl.when(step < tiles)
-    def _():
-        gate_h = pick(rows[...], gate[0]) * scale[...]
-        up_h = pick(rows[...], up[0]) * scale[...]
-        value = gate_h / (1.0 + jnp.exp(-gate_h)) * up_h
-        active[:, lanes(step * tile, tile)] = value.astype(BF)
-
-    @pl.when(step >= tiles)
-    def _():
-        owner = step - tiles
-        value = pick(active[...], down[0]).astype(BF)
+
+            @pl.when(e ^ place == s)
+            def _():
+                late_copy(e, s).start()
+
+    @pl.loop(0, ne)
+    def _(e):
+        late_copy(e, 0).wait()
         for t in range(experts):
-            early_out[t][:, lanes(owner * wide, wide)] = value[t * SLOTS : (t + 1) * SLOTS, :wide]
-        for s in range(ne):
-
-            @pl.when(owner ^ place[0] == s)
-            def _(s=s):
-                late_out[s][...] = value[:, wide:]
-
-
-def expert_call(place, early, late, w_gate, w_up, w_down, ne):
+            early_copy(e, t).wait()
+
+
+def expert_call(place, early, late, w_gate, w_up, w_down, stats, ne):
     hidden = w_gate.shape[2]
     slots, rest = late[0].shape
     experts = len(early)
     wide = (early[0].shape[1] - 128) // ne
     tile = 256 if hidden % 256 == 0 else 128
-    tiles = hidden // tile
-    whole = lambda a: pl.BlockSpec(a.shape, lambda g, place: (0,) * len(a.shape))
-    weight = pl.BlockSpec((1, D, tile), lambda g, place: (0, 0, jnp.minimum(g, tiles - 1)))
-    down = pl.BlockSpec(
-        (1, hidden, wide + rest), lambda g, place: (0, 0, jnp.maximum(g - tiles, 0))
-    )
-    outs = [shape((slots, rest), BF)] * ne + [shape((SLOTS, ne * wide), BF)] * experts
-    outs = outs + [shape((8, 128), I32)]
-    values = pl.pallas_call(
-        functools.partial(expert_kernel, ne, experts, tiles),
-        grid_spec=pltpu.PrefetchScalarGridSpec(
-            num_scalar_prefetch=1,
-            grid=(tiles + ne,),
-            in_specs=[whole(a) for a in (*early, *late)] + [weight] * 2 + [down],
-            out_specs=[whole(o) for o in outs],
-            scratch_shapes=[
-                pltpu.VMEM((slots, D), BF),
-                pltpu.VMEM((slots, 1), F32),
-                pltpu.VMEM((slots, hidden), BF),
-            ],
-        ),
-        out_shape=outs,
-        compiler_params=pltpu.CompilerParams(vmem_limit_bytes=50 * MIB),
-        cost_estimate=pl.CostEstimate(
-            flops=6 * slots * D * hidden, bytes_accessed=6 * D * hidden, transcendentals=0
-        ),
-    )(place, *early, *late, w_gate, w_up, w_down)
+    values = local_call(
+        functools.partial(expert_kernel, ne, experts, tile),
+        [SMEM] + [HBM] * (experts + ne + 3) + [VMEM],
+        (place, *early, *late, w_gate, w_up, w_down, stats),
+        [far((slots, rest), BF)] * ne
+        + [far((SLOTS, ne * wide), BF)] * experts
+        + [shape(stats.shape, F32)],
+        [
+            pltpu.VMEM((slots, D), BF),
+            pltpu.VMEM((slots, 128), BF),
+            pltpu.VMEM((slots, hidden), BF),
+            pltpu.VMEM((D, hidden), BF),
+            pltpu.VMEM((D, hidden), BF),
+            pltpu.VMEM((ne, hidden, wide + rest), BF),
+            pltpu.VMEM((ne, slots, rest), BF),
+            pltpu.VMEM((experts, SLOTS, ne * wide), BF),
+            pltpu.SemaphoreType.DMA((3, max(hidden // tile, ne))),
+            pltpu.SemaphoreType.DMA((experts * (ne + 1) + ne,)),
+            pltpu.SemaphoreType.DMA((ne, experts + 1)),
+        ],
+        vmem=60,
+        out_specs=[HBM] * (ne + experts) + [VMEM],
+        flops=6 * slots * D * hidden,
+        moved=6 * D * hidden,
+    )
     return values[:ne], values[ne:-1], values[-1]
 
 
 def weigh_kernel(ne, experts, *refs):
-    place, high, low = refs[:3]
-    blocks, late = refs[3 : 3 + experts], refs[3 + experts : 3 + experts + ne]
-    refs = refs[3 + experts + ne :]
-    outs, late_outs, (buf, total) = refs[:ne], refs[ne : ne + experts], refs[ne + experts :]
+    place, stats, routes, slots = refs[:4]
+    blocks, late = refs[4 : 4 + experts], refs[4 + experts : 4 + experts + ne]
+    refs = refs[4 + experts + ne :]
+    outs, late_outs, (high, low, buf, total) = refs[:ne], refs[ne : ne + experts], refs[ne + experts :]
+    rows = routes.shape[1]
+    logits = stats[:8] * lax.rsqrt(stats[8:9] / D + EPSILON)
+    ids = lax.broadcasted_iota(I32, (8, rows), 0)
+    chosen = [
+        jnp.sum(jnp.where(ids == routes[top : top + 1], logits, 0.0), axis=0, keepdims=True)
+        for top in range(2)
+    ]
+    at = lax.broadcasted_iota(I32, (experts * SLOTS, rows), 0)
+    gates = jnp.zeros(at.shape, F32)
+    for top in range(2):
+        gate = 1.0 / (1.0 + jnp.exp(chosen[1 - top] - chosen[top]))
+        gates = gates + jnp.where(at == slots[top : top + 1], gate, 0.0)
+    high[...], low[...] = halves(gates.T)
     for t in range(experts):
         buf[t * SLOTS : (t + 1) * SLOTS] = blocks[t][...]
     total[...] = pick(high[...], buf[...]) + pick(low[...], buf[...])
@@ -364,22 +477,32 @@
     attn_blocks = [attn_blocks[0]] + [swap(attn_blocks[s], "req", 2 * s) for s in range(1, half)]
     w_other = swap(w_out, "req", 1)
 
-    local = jnp.arange(rows, dtype=I32)
-    in_new = came_from[None, :] == (me * rows + local)[:, None]
-    new_ids = jnp.arange(came_from.shape[0], dtype=I32)
-    dest = jnp.sum(jnp.where(in_new, new_ids[None, :], 0), axis=1) // rows
-    dest_rank = jnp.sum((dest[:, None] == dest[None, :]) & (local[None, :] < local[:, None]), axis=1)
-    dest_rel, dest_par = (dest // 2) ^ q, dest % 2
-    send_slot = jnp.where(
-        dest_par != k,
-        dest_rel * MIG + dest_rank,
-        jnp.where(dest_rel != 0, (half + dest_rel - 1) * MIG + dest_rank, -1),
-    )
     n_pair, n_send = half * MIG, (2 * half - 1) * MIG
     n_hand = -(-(n_pair + 2 * MIG) // 16) * 16
-    send_hot = (jnp.arange(n_send, dtype=I32)[:, None] == send_slot[None, :])
-    send_row = jnp.sum(jnp.where(send_hot, local[None, :], 0), axis=1)
-    send_pick = send_hot.astype(BF)
+    pair_rows, own_rows, send_row = local_call(
+        functools.partial(movers_kernel, half),
+        [SMEM] + [VMEM] * 3,
+        (jnp.stack([q, k]).astype(I32), came_from.reshape(n, rows), attention_out, residual),
+        [
+            shape((n_pair, D + feats), BF),
+            shape((2 * n_pair, feats), BF),
+            shape((2 * n_pair, 128), I32),
+        ],
+        vmem=60,
+        moved=2 * MIB,
+        after=[w_other],
+    )
+    send_row = send_row[:n_send, 0]
+    pair_rows = swap(pair_rows, "req", 1)
+    *late_blocks, order = local_call(
+        functools.partial(handover_kernel, half),
+        [SMEM, VMEM, VMEM, VMEM],
+        (pair_place, pair_rows, own_rows, came_from.reshape(n, rows)),
+        [shape((n_hand, feats), BF)] * half + [shape((n, rows), I32)],
+        moved=MIB,
+    )
+    late_blocks = [late_blocks[0]] + [swap(late_blocks[s], "req", 2 * s) for s in range(1, half)]
+    came_from = order.reshape(-1)
 
     source = jnp.stack(
         [lax.dynamic_slice_in_dim(came_from, (2 * (q ^ t) + k) * rows, rows) for t in range(half)]
@@ -401,34 +524,13 @@
     own_hand = src_rel[0] * n_hand + n_pair + jnp.where(src_par[0] == k, 0, MIG) + src_rank[0]
     own_at = jnp.where(own_stays, src_local[0], rows + own_hand)
 
-    pair_rows, own_rows = local_call(
-        functools.partial(movers_kernel, n_pair),
-        [VMEM] * 3,
-        (send_pick, attention_out, residual),
-        [shape((n_pair, D + feats), BF), shape((n_send, feats), BF)],
-        moved=2 * MIB,
-        after=[w_other],
-    )
-    pair_rows = swap(pair_rows, "req", 1)
-    late_blocks = local_call(
-        functools.partial(handover_kernel, half),
-        [SMEM, VMEM, VMEM],
-        (pair_place, pair_rows, own_rows),
-        [shape((n_hand, feats), BF)] * half,
-        moved=MIB,
-    )
-    late_blocks = [late_blocks[0]] + [swap(late_blocks[s], "req", 2 * s) for s in range(1, half)]
-
-    expert_ids = jnp.arange(experts, dtype=I32)
-    names = routes[:, :, None] == expert_ids[None, None, :]
-    named = jnp.any(names, axis=1)
-    before = jnp.sum(
-        jnp.where((local[None, :] < local[:, None])[:, :, None], named[None, :, :], False), axis=1
-    )
-    rank = jnp.sum(jnp.where(names, before[:, None, :], 0), axis=2)
-    slot_of = ((routes ^ (me % experts)) * SLOTS + rank).astype(I32)
-    slot_ids = jnp.arange(experts * SLOTS, dtype=I32)
-    slot_pick = jnp.any(slot_ids[:, None, None] == slot_of[None, :, :], axis=2).astype(BF)
+    slot_pick, slot_of = local_call(
+        functools.partial(slots_kernel, experts),
+        [SMEM, VMEM],
+        ((me % experts).reshape(1).astype(I32), routes.T),
+        [shape((experts * SLOTS, rows), BF), shape((2, rows), I32)],
+        after=[order],
+    )
 
     total_rows = half * (rows + n_hand)
     selector = hot(attn_at, total_rows)
@@ -461,7 +563,7 @@
     table = page_table.reshape(-1)
     none = jnp.full((n_send,), -1, I32)
     no_rows = page_pool[:2].reshape((1, 2) + page_pool.shape[1:])
-    moving = take_pages(page_pool, no_rows, send_row, none, table, cache_len)
+    moving = take_pages(page_pool, no_rows, send_row, none, table, cache_len, [order])
     page = moving.shape[1:]
     pair_pages = swap(moving[:n_pair], "req", 1).reshape((half, MIG) + page)
     own_pages = jnp.concatenate([moving[:MIG], moving[n_pair:]], axis=0).reshape((half, MIG) + page)
@@ -501,17 +603,7 @@
     late = outgoing[experts + 1]
     late_rows = [late] + [swap(late, "exp", s) for s in range(1, ne)]
 
-    stats = outgoing[experts]
     early_rows = [swap(outgoing[s], "req", s) if s else outgoing[s] for s in range(experts)]
-
-    inverse = lax.rsqrt(stats[8] / D + EPSILON)
-    logits = (stats[:experts] * inverse[None, :]).T
-    chosen = jnp.sum(jnp.where(names, logits[:, None, :], 0.0), axis=2)
-    gates = jax.nn.sigmoid(chosen - chosen[:, ::-1])
-    gate_slots = jnp.sum(
-        jnp.where(slot_of[:, :, None] == slot_ids[None, None, :], gates[:, :, None], 0.0), axis=1
-    )
-    gate_high, gate_low = halves(gate_slots)
 
     for bit in range(1, stages):
         pages = pages.reshape((half >> (bit + 1), 2, 1 << bit) + block)
@@ -519,9 +611,15 @@
         pages = jnp.stack([pages[:, 0], came_pages], axis=1)
     moved_pages = pages.reshape((half * 2 * MIG,) + page)
 
-    down_late, down_early, done = expert_call(place, early_rows, late_rows, w_gate, w_up, w_down, ne)
+    down_late, down_early, stats = expert_call(
+        place, early_rows, late_rows, w_gate, w_up, w_down, outgoing[experts], ne
+    )
     late_blocks = [down_late[0]] + [swap(down_late[s], "exp", s) for s in range(1, ne)]
-    early_back = [swap(down_early[s], "req", s) if s else down_early[s] for s in range(experts)]
+    near_back = hold(down_early[1], late_blocks[1])
+    early_back = [
+        swap(down_early[s] if s > 1 else near_back, "req", s) if s else down_early[s]
+        for s in range(experts)
+    ]
     new_pages = take_pages(
         page_pool,
         moved_pages,
@@ -529,15 +627,16 @@
         jnp.where(own_stays, -1, own_slot),
         table,
         cache_len,
-        [done],
+        [stats],
     )
     weighted = local_call(
         functools.partial(weigh_kernel, ne, experts),
-        [SMEM] + [VMEM] * (2 + experts + ne),
-        (place, gate_high, gate_low, *early_back, *late_blocks),
+        [SMEM] + [VMEM] * (3 + experts + ne),
+        (place, stats, routes.T, slot_of, *early_back, *late_blocks),
         [shape((rows, wide), F32)]
         + [shape((rows, wide), BF)] * (ne - 1)
-        + [shape((SLOTS, rest), BF)] * experts,
+        + [shape((SLOTS, rest), BF)] * experts
+        + [shape((rows, experts * SLOTS), BF)] * 2,
         [pltpu.VMEM((experts * SLOTS, ne * wide), BF), pltpu.VMEM((rows, ne * wide), F32)],
         flops=4 * rows * experts * SLOTS * ne * wide,
         moved=3 * MIB,
@@ -549,7 +648,7 @@
     mixed = local_call(
         functools.partial(finish_kernel, ne, experts, wide),
         [VMEM] * (3 + ne + experts),
-        (gate_high, gate_low, hidden, *early_parts, *late_back),
+        (*weighted[-2:], hidden, *early_parts, *late_back),
         [shape((rows, feats), F32)],
         [pltpu.VMEM((experts * SLOTS, rest), BF)],
         flops=4 * rows * experts * SLOTS * rest,

time: 157 us -> 153 us (0.975)
  other arithmetic: 7.69 us -> 4.69 us
  starting transfers between devices: 43.2 us -> 40.8 us
  local copies, waits for them, and re-layouts: 5.82 us -> 7.82 us
    pallas_call x10 -> x13, Pallas kernels: 20.9 us -> 44.9 us  [local_call(): pl.pallas_call(run, out_shape=outs, in_specs=list(in_specs) + [pl.BlockSp...]
    pallas_call x1 -> x0, Pallas kernels: 22.8 us -> none  [expert_call(): pl.pallas_call(functools.partial(expert_kernel, ne, experts, tiles), grid...]
    unnamed x47 -> x67, local copies, waits for them, and re-layouts: 2.97 us -> 5.97 us
    ppermute x37, starting transfers between devices: 43.2 us -> 40.8 us  [swap(): return lax.ppermute(x, axis, [(i, i ^ s) for i in range(n)])]
    reduce_sum x7 -> x0, other arithmetic: 2.16 us -> none  [the longest x1 0.88 us: body(): dest = jnp.sum(jnp.where(in_new, new_ids[None, :], 0), axis=1) // rows]
  transfers between devices with their start and end apart: 37 -> 37, of which waited for: 16 -> 15; matrix products, arithmetic and copies ran while one was open for 7% -> 4% of each run, Pallas kernels for 9% -> 12%
where the time goes in v5:
time: 153 us; the launch traced here: 152 us
  waiting for transfers between devices  53.2 us (35%)
  Pallas kernels  44.9 us (29%)
  starting transfers between devices  40.8 us (27%)
  local copies, waits for them, and re-layouts  7.82 us (5%)
  other arithmetic  4.69 us (3%)
    ppermute x37, waiting for transfers between devices, swap(): return lax.ppermute(x, axis, [(i, i ^ s) for i in range(n)])  53.2 us
    pallas_call x13, Pallas kernels, local_call(): pl.pallas_call(run, out_shape=outs, in_specs=list(in_specs) + [pl.BlockSp...  44.9 us
    ppermute x37, starting transfers between devices, swap(): return lax.ppermute(x, axis, [(i, i ^ s) for i in range(n)])  40.8 us
    unnamed x67, local copies, waits for them, and re-layouts  5.97 us
  transfers between devices with their start and end apart: 37, of which 15 were waited for; matrix products, arithmetic and copies ran while one was open for 4% of the time, Pallas kernels for 12%

profile of v5, /device:TPU:0, one launch (start us, length us, event | category | flops | bytes accessed | tf_op | source)
XLA Modules:
  0.0 152.4 jit_solution(1499815818039949141)
XLA Ops:
  0.7 0.5 collective-permute-start
  1.2 2.4 %shard_map.140 = (bf16[128,1024]{1,0:T(8,128)(2,1)}, bf16[128,1024]{1,0:T(8,128)(2,1)}, bf16[128,1024]{1,0:T(8,128)(2,1)}, bf16[128,1024]{1,0:T(8,128)(2,1)}, s32[8,128]{1,0:T(8,128)}) custom-call(s32[1]{0:T(128)} %bitcast.3.refs_0_, bf16[128,4096]{1,0:T(8,128)(2,1)} %refs_2_.1, s32[8,128]{1,0:T(8,128)} %bitcast.78), custom_call_target="tpu_custom_call" | custom-call | bytes 2097152 | tf_op jit(solution)/shard_map/pallas_call | solution.py:48
  3.5 2.5 %collective-permute-start.3 = (bf16[128,1024]{1,0:T(8,128)(2,1)}, bf16[128,1024]{1,0:T(8,128)(2,1)}, u32[]{:S(2)}, u32[]{:S(2)}) collective-permute-start(bf16[128,1024]{1,0:T(8,128)(2,1)} %get-tuple-element.59), channel_id=1, source_target_pairs={{0,8},{4,12},{8,0},{12,4},{16,24},{20,28},{24,16},{28,20},{1,9},{5... | collective-permute-start | bytes 786440 | tf_op jit(solution)/shard_map/ppermute | solution.py:27
  6.1 1.5 collective-permute-start.4
  7.6 0.6 pad_add_fusion.1.refs_0_
  8.2 1.0 copy-done.16
  9.1 2.5 %shard_map.141 = (bf16[16,5120]{1,0:T(8,128)(2,1)}, bf16[32,1024]{1,0:T(8,128)(2,1)}, s32[32,128]{1,0:T(8,128)}) custom-call(s32[2]{0:T(128)} %pad_add_fusion.1.refs_0_, s32[8,128]{1,0:T(8,128)} %get-tuple-element.52.refs_1_.refs_3_, bf16[128,4096]{1,0:T(8,128)(2,1)} %refs_2_.1, bf16[128,1024]{1,0:T(8,128)(2,1)} %refs_3_.3, bf16[512,1024]{1,0:T(8,128)(2,1)} %copy-done.16), custom_call_target="tpu_custom_call" | custom-call | bytes 2097152 | tf_op jit(solution)/shard_map/pallas_call | solution.py:48
  11.9 0.8 slice_reduce_fusion.refs_2_
  12.8 0.4 collective-permute-done.1.refs_1_
  13.2 0.8 copy-done.8
  14.6 2.0 %collective-permute-start.6 = (bf16[32,1024]{1,0:T(8,128)(2,1)S(1)}, bf16[32,1024]{1,0:T(8,128)(2,1)S(1)}, u32[]{:S(2)}, u32[]{:S(2)}) collective-permute-start(bf16[32,1024]{1,0:T(8,128)(2,1)S(1)} %get-tuple-element.63), channel_id=1, source_target_pairs={{0,8},{4,12},{8,0},{12,4},{16,24},{20,28},{24,16},{28,20},{1,9},{5... | collective-permute-start | bytes 196616 | tf_op jit(solution)/shard_map/ppermute | solution.py:27
  16.6 1.5 collective-permute-start.7
  18.1 1.0 fusion.refs_1_
  19.3 0.7 fusion.7.refs_2_
  20.0 1.3 shard_map.144
  21.3 0.7 slice.66
  22.1 2.3 %collective-permute-done.8.refs_13_ = bf16[32,1024]{1,0:T(8,128)(2,1)S(1)} collective-permute-done((bf16[32,1024]{1,0:T(8,128)(2,1)S(1)}, bf16[32,1024]{1,0:T(8,128)(2,1)S(1)}, u32[]{:S(2)}, u32[]{:S(2)}) %collective-permute-start.8) | collective-permute-done | bytes 65568 | tf_op jit(solution)/shard_map/ppermute | solution.py:27
  24.4 0.6 copy-done.32
  25.1 5.8 %shard_map.145 = (f32[128,1024]{1,0:T(8,128)}, bf16[128,1024]{1,0:T(8,128)(2,1)}, bf16[128,1024]{1,0:T(8,128)(2,1)}, bf16[128,1024]{1,0:T(8,128)(2,1)}) custom-call(s32[1]{0:T(128)} %bitcast.4.refs_0_, bf16[512,640]{1,0:T(8,128)(2,1)} %fusion.refs_1_, bf16[128,256]{1,0:T(8,128)(2,1)} %fusion.7.refs_2_, bf16[128,1024]{1,0:T(8,128)(2,1)} %refs_3_.3, ...), custom_call_target="tpu_custom_call" | custom-call | flops 1744830464 | bytes 6291456 | tf_op jit(solution)/shard_map/pallas_call | solution.py:48
  30.8 0.6 collective-permute-start.9
  31.4 0.7 collective-permute-start.10
  32.1 2.3 %collective-permute-start.11 = (bf16[128,1024]{1,0:T(8,128)(2,1)}, bf16[128,1024]{1,0:T(8,128)(2,1)}, u32[]{:S(2)}, u32[]{:S(2)}) collective-permute-start(bf16[128,1024]{1,0:T(8,128)(2,1)} %get-tuple-element.69), channel_id=1, source_target_pairs={{0,24},{4,28},{8,16},{12,20},{16,8},{20,12},{24,0},{28,4},{1,25},{... | collective-permute-start | bytes 786440 | tf_op jit(solution)/shard_map/ppermute | solution.py:27
  34.7 0.9 fusion.6
  35.6 4.7 %collective-permute-done.9.refs_5_ = bf16[128,1024]{1,0:T(8,128)(2,1)S(1)} collective-permute-done((bf16[128,1024]{1,0:T(8,128)(2,1)}, bf16[128,1024]{1,0:T(8,128)(2,1)S(1)}, u32[]{:S(2)}, u32[]{:S(2)}) %collective-permute-start.9) | collective-permute-done | bytes 262176 | tf_op jit(solution)/shard_map/ppermute | solution.py:27
  40.4 4.6 %collective-permute-done.10.refs_6_ = bf16[128,1024]{1,0:T(8,128)(2,1)} collective-permute-done((bf16[128,1024]{1,0:T(8,128)(2,1)}, bf16[128,1024]{1,0:T(8,128)(2,1)}, u32[]{:S(2)}, u32[]{:S(2)}) %collective-permute-start.10) | collective-permute-done | bytes 262176 | tf_op jit(solution)/shard_map/ppermute | solution.py:27
  44.9 2.3 %shard_map.146 = (f32[128,1024]{1,0:T(8,128)S(1)}, bf16[144,640]{1,0:T(8,128)(2,1)}, bf16[64,384]{1,0:T(8,128)(2,1)}, bf16[64,384]{1,0:T(8,128)(2,1)}, bf16[320,...) custom-call(f32[1,1024]{1,0:T(1,128)S(1)} %bitcast.70, f32[8,1024]{1,0:T(8,128)S(1)} %pad.4.refs_1_, ...), custom_call_target="tpu_custom_call" | custom-call | flops 25165824 | bytes 3145728 | tf_op jit(solution)/shard_map/pallas_call | solution.py:48
  47.2 0.8 copy-done.2
  48.0 1.2 collective-permute-start.16
  49.2 3.6 %collective-permute-start.14 = (bf16[144,640]{1,0:T(8,128)(2,1)}, bf16[144,640]{1,0:T(8,128)(2,1)S(1)}, u32[]{:S(2)}, u32[]{:S(2)}) collective-permute-start(bf16[144,640]{1,0:T(8,128)(2,1)} %get-tuple-element.70.refs_2_), channel_id=1, source_target_pairs={{0,3},{1,2},{2,1},{3,0},{4,7},{5,6},{6,5},{7,4},{8,11},{9,10},{10,... | collective-permute-start | bytes 552968 | tf_op jit(solution)/shard_map/ppermute | solution.py:27
  52.8 0.8 collective-permute-start.12
  53.6 1.4 collective-permute-done.15.refs_7_
  55.0 0.6 collective-permute-start.17
  55.6 3.3 %collective-permute-done.17.refs_9_ = bf16[64,384]{1,0:T(8,128)(2,1)S(1)} collective-permute-done((bf16[64,384]{1,0:T(8,128)(2,1)}, bf16[64,384]{1,0:T(8,128)(2,1)S(1)}, u32[]{:S(2)}, u32[]{:S(2)}) %collective-permute-start.17) | collective-permute-done | bytes 49184 | tf_op jit(solution)/shard_map/ppermute | solution.py:27
  59.0 9.3 %collective-permute-done.13.refs_4_ = bf16[144,640]{1,0:T(8,128)(2,1)S(1)} collective-permute-done((bf16[144,640]{1,0:T(8,128)(2,1)}, bf16[144,640]{1,0:T(8,128)(2,1)S(1)}, u32[]{:S(2)}, u32[]{:S(2)}) %collective-permute-start.13) | collective-permute-done | bytes 184352 | tf_op jit(solution)/shard_map/ppermute | solution.py:27
  68.3 0.6 copy-done.24
  69.1 2.9 %shard_map.147 = (bf16[64,2688]{1,0:T(8,128)(2,1)}, bf16[64,2688]{1,0:T(8,128)(2,1)}, bf16[64,2688]{1,0:T(8,128)(2,1)}, bf16[64,2688]{1,0:T(8,128)(2,1)}, f32[16,128]{1,0:T(8,128)}, /*index=5*/bf16[256,384]{1,0:T(8,128)(2,1)}) custom-call(s32[1]{0:T(128)} %bitcast.refs_0_, bf16[256,128]{1,0:T(8,128)(2,1)} %copy-done.6, ...), custom_call_target="tpu_custom_call" | custom-call | flops 167772160 | bytes 3145728 | tf_op jit(solution)/shard_map/pallas_call | solution.py:48
  72.0 2.5 %collective-permute-start.23 = (bf16[256,384]{1,0:T(8,128)(2,1)}, bf16[256,384]{1,0:T(8,128)(2,1)S(1)}, u32[]{:S(2)}, u32[]{:S(2)}) collective-permute-start(bf16[256,384]{1,0:T(8,128)(2,1)} %get-tuple-element.79.refs_5_), channel_id=1, source_target_pairs={{0,3},{1,2},{2,1},{3,0},{4,7},{5,6},{6,5},{7,4},{8,11},{9,10},{10,... | collective-permute-start | bytes 589832 | tf_op jit(solution)/shard_map/ppermute | solution.py:27
  74.8 1.5 %collective-permute-start.20 = (bf16[64,2688]{1,0:T(8,128)(2,1)}, bf16[64,2688]{1,0:T(8,128)(2,1)S(1)}, u32[]{:S(2)}, u32[]{:S(2)}) collective-permute-start(bf16[64,2688]{1,0:T(8,128)(2,1)} %get-tuple-element.78), channel_id=1, source_target_pairs={{0,12},{4,8},{8,4},{12,0},{16,28},{20,24},{24,20},{28,16},{1,13},{... | collective-permute-start | bytes 1032200 | tf_op jit(solution)/shard_map/ppermute | solution.py:27
  76.3 4.5 %collective-permute-done.23.refs_8_ = bf16[256,384]{1,0:T(8,128)(2,1)S(1)} collective-permute-done((bf16[256,384]{1,0:T(8,128)(2,1)}, bf16[256,384]{1,0:T(8,128)(2,1)S(1)}, u32[]{:S(2)}, u32[]{:S(2)}) %collective-permute-start.23) | collective-permute-done | bytes 196640 | tf_op jit(solution)/shard_map/ppermute | solution.py:27
  80.9 6.4 %collective-permute-start.21 = (bf16[256,384]{1,0:T(8,128)(2,1)}, bf16[256,384]{1,0:T(8,128)(2,1)S(1)}, u32[]{:S(2)}, u32[]{:S(2)}) collective-permute-start(bf16[256,384]{1,0:T(8,128)(2,1)} %get-tuple-element.79.refs_5_), channel_id=1, source_target_pairs={{0,1},{1,0},{2,3},{3,2},{4,5},{5,4},{6,7},{7,6},{8,9},{9,8},{10,11... | collective-permute-start | bytes 589832 | tf_op jit(solution)/shard_map/ppermute | solution.py:27
  87.3 2.5 %collective-permute-done.22.refs_7_ = bf16[256,384]{1,0:T(8,128)(2,1)S(1)} collective-permute-done((bf16[256,384]{1,0:T(8,128)(2,1)}, bf16[256,384]{1,0:T(8,128)(2,1)S(1)}, u32[]{:S(2)}, u32[]{:S(2)}) %collective-permute-start.22) | collective-permute-done | bytes 196640 | tf_op jit(solution)/shard_map/ppermute | solution.py:27
  89.8 2.0 %collective-permute-done.21.refs_6_ = bf16[256,384]{1,0:T(8,128)(2,1)S(1)} collective-permute-done((bf16[256,384]{1,0:T(8,128)(2,1)}, bf16[256,384]{1,0:T(8,128)(2,1)S(1)}, u32[]{:S(2)}, u32[]{:S(2)}) %collective-permute-start.21) | collective-permute-done | bytes 196640 | tf_op jit(solution)/shard_map/ppermute | solution.py:27
  92.2 0.4 copy-done.22
  92.5 0.4 copy-done.19
  92.9 19.7 %shard_map.148 = (bf16[256,384]{1,0:T(8,128)(2,1)}, bf16[256,384]{1,0:T(8,128)(2,1)}, bf16[256,384]{1,0:T(8,128)(2,1)}, bf16[256,384]{1,0:T(8,128)(2,1)}, bf16[6...) custom-call(s32[1]{0:T(128)} %bitcast.refs_0_, ...), custom_call_target="tpu_custom_call" | custom-call | flops 11274289152 | bytes 44040192 | tf_op jit(solution)/shard_map/pallas_call | solution.py:48
  112.7 1.4 collective-permute-start.24
  114.1 1.0 fusion.5
  115.1 0.9 collective-permute-start.28
  115.9 2.3 %collective-permute-start.29 = (bf16[256,384]{1,0:T(8,128)(2,1)}, bf16[256,384]{1,0:T(8,128)(2,1)S(1)}, u32[]{:S(2)}, u32[]{:S(2)}) collective-permute-start(bf16[256,384]{1,0:T(8,128)(2,1)} %get-tuple-element.90), channel_id=1, source_target_pairs={{0,3},{1,2},{2,1},{3,0},{4,7},{5,6},{6,5},{7,4},{8,11},{9,10},{10,... | collective-permute-start | bytes 589832 | tf_op jit(solution)/shard_map/ppermute | solution.py:27
  118.2 0.3 collective-permute-start.26
  118.5 0.4 collective-permute-start.27
  118.9 2.9 %collective-permute-done.24.refs_1_.refs_9_ = bf16[256,384]{1,0:T(8,128)(2,1)S(1)} collective-permute-done((bf16[256,384]{1,0:T(8,128)(2,1)}, bf16[256,384]{1,0:T(8,128)(2,1)S(1)}, u32[]{:S(2)}, u32[]{:S(2)}) %collective-permute-start.24) | collective-permute-done | bytes 196640 | tf_op jit(solution)/shard_map/ppermute | solution.py:27
  121.8 1.0 copy-done.4
  122.8 0.7 shard_map.149
  123.6 8.5 %collective-permute-done.28.refs_10_ = bf16[256,384]{1,0:T(8,128)(2,1)S(1)} collective-permute-done((bf16[256,384]{1,0:T(8,128)(2,1)}, bf16[256,384]{1,0:T(8,128)(2,1)S(1)}, u32[]{:S(2)}, u32[]{:S(2)}) %collective-permute-start.28) | collective-permute-done | bytes 196640 | tf_op jit(solution)/shard_map/ppermute | solution.py:27
  132.7 0.8 shard_map.150
  133.6 1.6 %collective-permute-start.33 = (bf16[64,384]{1,0:T(8,128)(2,1)S(1)}, bf16[64,384]{1,0:T(8,128)(2,1)S(1)}, u32[]{:S(2)}, u32[]{:S(2)}) collective-permute-start(bf16[64,384]{1,0:T(8,128)(2,1)S(1)} %get-tuple-element.99), channel_id=1, source_target_pairs={{0,4},{4,0},{8,12},{12,8},{16,20},{20,16},{24,28},{28,24},{1,5},{5... | collective-permute-start | bytes 147464 | tf_op jit(solution)/shard_map/ppermute | solution.py:27
  135.1 1.2 collective-permute-start.30
  136.3 0.7 collective-permute-start.31
  137.1 2.5 %collective-permute-start.32 = (bf16[128,640]{1,0:T(8,128)(2,1)S(1)}, bf16[128,640]{1,0:T(8,128)(2,1)S(1)}, u32[]{:S(2)}, u32[]{:S(2)}) collective-permute-start(bf16[128,640]{1,0:T(8,128)(2,1)S(1)} %get-tuple-element.97), channel_id=1, source_target_pairs={{0,3},{1,2},{2,1},{3,0},{4,7},{5,6},{6,5},{7,4},{8,11},{9,10},{10,... | collective-permute-start | bytes 491528 | tf_op jit(solution)/shard_map/ppermute | solution.py:27
  139.5 0.3 collective-permute-start.34
  140.2 5.2 %shard_map.152 = bf16[128,2,8,512]{3,2,1,0:T(8,128)(2,1)} custom-call(bf16[256,8,512]{2,1,0:T(8,128)(2,1)S(1)} %copy-done, bf16[32,2,8,512]{3,2,1,0:T(8,128)(2,1)S(1)} %bitcast.67, s32[128]{0:T(128)S(1)} %get-tuple-element.108.refs_2_, s32[128]{0:T(128)S(1)} %get-tuple-element.106.refs_3_, s32[256]{0:T(256)S(1)} %reshape.425.refs_4_, s32[128]{0:T(128)S(1)} %copy-done.13, ...), custom_call_target="tpu_custom_call" | custom-call | bytes 5242880 | tf_op jit(solution)/shard_map/pallas_call | solution.py:48
  145.4 5.9 %collective-permute-done.31.refs_5_ = bf16[128,640]{1,0:T(8,128)(2,1)S(1)} collective-permute-done((bf16[128,640]{1,0:T(8,128)(2,1)S(1)}, bf16[128,640]{1,0:T(8,128)(2,1)S(1)}, u32[]{:S(2)}, u32[]{:S(2)}) %collective-permute-start.31) | collective-permute-done | bytes 163872 | tf_op jit(solution)/shard_map/ppermute | solution.py:27
  151.3 1.1 shard_map.151
  (114 shorter events, 3.1 us)
Async XLA Ops:
  0.6 11.0 %copy-start = (bf16[256,8,512]{2,1,0:T(8,128)(2,1)S(1)}, bf16[256,8,512]{2,1,0:T(8,128)(2,1)}, u32[]{:S(2)}) copy-start(bf16[256,8,512]{2,1,0:T(8,128)(2,1)} %refs_0_.3) | copy-start | bytes 6291460
  0.6 11.0 %copy-start.29 = (s32[128,2]{0,1:T(2,128)S(1)}, s32[128,2]{0,1:T(2,128)}, u32[]{:S(2)}) copy-start(s32[128,2]{0,1:T(2,128)} %param.19) | copy-start | bytes 3076
  0.7 7.5 %collective-permute-start = (bf16[512,1024]{1,0:T(8,128)(2,1)}, bf16[512,1024]{1,0:T(8,128)(2,1)S(1)}, u32[]{:S(2)}, u32[]{:S(2)}) collective-permute-start(bf16[512,1024]{1,0:T(8,128)(2,1)} %refs_4_.1), channel_id=1, source_target_pairs={{0,4},{4,0},{8,12},{12,8},{16,20},{20,16},{24,28},{28,24},{1,5},{5... | collective-permute-start | bytes 3145736 | tf_op jit(solution)/shard_map/ppermute | solution.py:27
  1.2 18.8 %copy-start.13 = (s32[128]{0:T(128)S(1)}, s32[128]{0:T(128)}, u32[]{:S(2)}) copy-start(s32[128]{0:T(128)} %refs_5_.3) | copy-start | bytes 1540
  3.5 9.7 %copy-start.10 = (s32[8,128]{1,0:T(8,128)S(1)}, s32[8,128]{1,0:T(8,128)}, u32[]{:S(2)}) copy-start(s32[8,128]{1,0:T(8,128)} %get-tuple-element.52.refs_1_.refs_3_) | copy-start | bytes 12292
  3.5 15.6 %collective-permute-start.3 = (bf16[128,1024]{1,0:T(8,128)(2,1)}, bf16[128,1024]{1,0:T(8,128)(2,1)}, u32[]{:S(2)}, u32[]{:S(2)}) collective-permute-start(bf16[128,1024]{1,0:T(8,128)(2,1)} %get-tuple-element.59), channel_id=1, source_target_pairs={{0,8},{4,12},{8,0},{12,4},{16,24},{20,28},{24,16},{28,20},{1,9},{5... | collective-permute-start | bytes 786440 | tf_op jit(solution)/shard_map/ppermute | solution.py:27
  6.1 16.0 %collective-permute-start.4 = (bf16[128,1024]{1,0:T(8,128)(2,1)}, bf16[128,1024]{1,0:T(8,128)(2,1)}, u32[]{:S(2)}, u32[]{:S(2)}) collective-permute-start(bf16[128,1024]{1,0:T(8,128)(2,1)} %get-tuple-element.60), channel_id=1, source_target_pairs={{0,16},{4,20},{8,24},{12,28},{16,0},{20,4},{24,8},{28,12},{1,17},{... | collective-permute-start | bytes 786440 | tf_op jit(solution)/shard_map/ppermute | solution.py:27
  7.6 14.5 %collective-permute-start.5 = (bf16[128,1024]{1,0:T(8,128)(2,1)}, bf16[128,1024]{1,0:T(8,128)(2,1)}, u32[]{:S(2)}, u32[]{:S(2)}) collective-permute-start(bf16[128,1024]{1,0:T(8,128)(2,1)} %get-tuple-element.61), channel_id=1, source_target_pairs={{0,24},{4,28},{8,16},{12,20},{16,8},{20,12},{24,0},{28,4},{1,25},{... | collective-permute-start | bytes 786440 | tf_op jit(solution)/shard_map/ppermute | solution.py:27
  8.2 1.0 copy-start.16
  11.6 1.6 %collective-permute-start.1 = (bf16[16,5120]{1,0:T(8,128)(2,1)}, bf16[16,5120]{1,0:T(8,128)(2,1)S(1)}, u32[]{:S(2)}, u32[]{:S(2)}) collective-permute-start(bf16[16,5120]{1,0:T(8,128)(2,1)} %get-tuple-element.53), channel_id=1, source_target_pairs={{0,4},{4,0},{8,12},{12,8},{16,20},{20,16},{24,28},{28,24},{1,5},{5... | collective-permute-start | bytes 491528 | tf_op jit(solution)/shard_map/ppermute | solution.py:27
  14.1 10.3 %copy-start.14 = (bf16[32,1024]{1,0:T(8,128)(2,1)}, bf16[32,1024]{1,0:T(8,128)(2,1)S(1)}, u32[]{:S(2)}) copy-start(bf16[32,1024]{1,0:T(8,128)(2,1)S(1)} %get-tuple-element.62.refs_10_) | copy-start | bytes 196612
  14.6 7.5 %collective-permute-start.6 = (bf16[32,1024]{1,0:T(8,128)(2,1)S(1)}, bf16[32,1024]{1,0:T(8,128)(2,1)S(1)}, u32[]{:S(2)}, u32[]{:S(2)}) collective-permute-start(bf16[32,1024]{1,0:T(8,128)(2,1)S(1)} %get-tuple-element.63), channel_id=1, source_target_pairs={{0,8},{4,12},{8,0},{12,4},{16,24},{20,28},{24,16},{28,20},{1,9},{5... | collective-permute-start | bytes 196616 | tf_op jit(solution)/shard_map/ppermute | solution.py:27
  16.6 5.5 %collective-permute-start.7 = (bf16[32,1024]{1,0:T(8,128)(2,1)S(1)}, bf16[32,1024]{1,0:T(8,128)(2,1)S(1)}, u32[]{:S(2)}, u32[]{:S(2)}) collective-permute-start(bf16[32,1024]{1,0:T(8,128)(2,1)S(1)} %get-tuple-element.64), channel_id=1, source_target_pairs={{0,16},{4,20},{8,24},{12,28},{16,0},{20,4},{24,8},{28,12},{1,17},{... | collective-permute-start | bytes 196616 | tf_op jit(solution)/shard_map/ppermute | solution.py:27
  19.2 5.2 %collective-permute-start.8 = (bf16[32,1024]{1,0:T(8,128)(2,1)S(1)}, bf16[32,1024]{1,0:T(8,128)(2,1)S(1)}, u32[]{:S(2)}, u32[]{:S(2)}) collective-permute-start(bf16[32,1024]{1,0:T(8,128)(2,1)S(1)} %get-tuple-element.65), channel_id=1, source_target_pairs={{0,24},{4,28},{8,16},{12,20},{16,8},{20,12},{24,0},{28,4},{1,25},{... | collective-permute-start | bytes 196616 | tf_op jit(solution)/shard_map/ppermute | solution.py:27
  22.1 12.6 %collective-permute-start.2 = (bf16[16,2,8,512]{3,2,1,0:T(8,128)(2,1)}, bf16[16,2,8,512]{3,2,1,0:T(8,128)(2,1)}, u32[]{:S(2)}, u32[]{:S(2)}) collective-permute-start(bf16[16,2,8,512]{3,2,1,0:T(8,128)(2,1)} %slice.66), channel_id=1, source_target_pairs={{0,4},{4,0},{8,12},{12,8},{16,20},{20,16},{24,28},{28,24},{1,5},{5... | collective-permute-start | bytes 786440 | tf_op jit(solution)/shard_map/ppermute | solution.py:27
  22.1 2.3 %copy-start.30 = (bf16[32,1024]{1,0:T(8,128)(2,1)}, bf16[32,1024]{1,0:T(8,128)(2,1)S(1)}, u32[]{:S(2)}) copy-start(bf16[32,1024]{1,0:T(8,128)(2,1)S(1)} %collective-permute-done.6.refs_11_) | copy-start | bytes 196612
  22.1 2.3 %copy-start.31 = (bf16[32,1024]{1,0:T(8,128)(2,1)}, bf16[32,1024]{1,0:T(8,128)(2,1)S(1)}, u32[]{:S(2)}) copy-start(bf16[32,1024]{1,0:T(8,128)(2,1)S(1)} %collective-permute-done.7.refs_12_) | copy-start | bytes 196612
  25.0 9.3 %copy-start.28 = (f32[1024,4]{0,1:T(4,128)S(1)}, f32[1024,4]{0,1:T(4,128)}, u32[]{:S(2)}) copy-start(f32[1024,4]{0,1:T(4,128)} %param.16) | copy-start | bytes 49156
  25.1 9.4 %copy-start.12 = (s32[128,2]{0,1:T(2,128)S(1)}, s32[128,2]{0,1:T(2,128)}, u32[]{:S(2)}) copy-start(s32[128,2]{0,1:T(2,128)} %param.22) | copy-start | bytes 3076
  25.1 19.9 %copy-start.11 = (f32[1024]{0:T(1024)S(1)}, f32[1024]{0:T(1024)}, u32[]{:S(2)}) copy-start(f32[1024]{0:T(1024)} %param.17) | copy-start | bytes 12292
  30.8 14.1 %copy-start.1 = (f32[128,1024]{1,0:T(8,128)S(1)}, f32[128,1024]{1,0:T(8,128)}, u32[]{:S(2)}) copy-start(f32[128,1024]{1,0:T(8,128)} %get-tuple-element.66.refs_4_) | copy-start | bytes 1572868
  30.8 9.5 %collective-permute-start.9 = (bf16[128,1024]{1,0:T(8,128)(2,1)}, bf16[128,1024]{1,0:T(8,128)(2,1)S(1)}, u32[]{:S(2)}, u32[]{:S(2)}) collective-permute-start(bf16[128,1024]{1,0:T(8,128)(2,1)} %get-tuple-element.67), channel_id=1, source_target_pairs={{0,8},{4,12},{8,0},{12,4},{16,24},{20,28},{24,16},{28,20},{1,9},{5... | collective-permute-start | bytes 786440 | tf_op jit(solution)/shard_map/ppermute | solution.py:27
  31.4 13.5 %collective-permute-start.10 = (bf16[128,1024]{1,0:T(8,128)(2,1)}, bf16[128,1024]{1,0:T(8,128)(2,1)}, u32[]{:S(2)}, u32[]{:S(2)}) collective-permute-start(bf16[128,1024]{1,0:T(8,128)(2,1)} %get-tuple-element.68), channel_id=1, source_target_pairs={{0,16},{4,20},{8,24},{12,28},{16,0},{20,4},{24,8},{28,12},{1,17},{... | collective-permute-start | bytes 786440 | tf_op jit(solution)/shard_map/ppermute | solution.py:27
  32.1 12.8 %collective-permute-start.11 = (bf16[128,1024]{1,0:T(8,128)(2,1)}, bf16[128,1024]{1,0:T(8,128)(2,1)}, u32[]{:S(2)}, u32[]{:S(2)}) collective-permute-start(bf16[128,1024]{1,0:T(8,128)(2,1)} %get-tuple-element.69), channel_id=1, source_target_pairs={{0,24},{4,28},{8,16},{12,20},{16,8},{20,12},{24,0},{28,4},{1,25},{... | collective-permute-start | bytes 786440 | tf_op jit(solution)/shard_map/ppermute | solution.py:27
  34.6 33.6 %copy-start.6 = (bf16[256,128]{1,0:T(8,128)(2,1)}, bf16[256,128]{1,0:T(8,128)(2,1)S(1)}, u32[]{:S(2)}) copy-start(bf16[256,128]{1,0:T(8,128)(2,1)S(1)} %get-tuple-element.56.refs_2_.refs_1_) | copy-start | bytes 196612
  48.0 20.3 %collective-permute-start.16 = (bf16[320,512]{1,0:T(8,128)(2,1)}, bf16[320,512]{1,0:T(8,128)(2,1)S(1)}, u32[]{:S(2)}, u32[]{:S(2)}) collective-permute-start(bf16[320,512]{1,0:T(8,128)(2,1)} %get-tuple-element.73), channel_id=1, source_target_pairs={{0,8},{4,12},{8,0},{12,4},{16,24},{20,28},{24,16},{28,20},{1,9},{5... | collective-permute-start | bytes 983048 | tf_op jit(solution)/shard_map/ppermute | solution.py:27
  49.2 9.8 %collective-permute-start.14 = (bf16[144,640]{1,0:T(8,128)(2,1)}, bf16[144,640]{1,0:T(8,128)(2,1)S(1)}, u32[]{:S(2)}, u32[]{:S(2)}) collective-permute-start(bf16[144,640]{1,0:T(8,128)(2,1)} %get-tuple-element.70.refs_2_), channel_id=1, source_target_pairs={{0,3},{1,2},{2,1},{3,0},{4,7},{5,6},{6,5},{7,4},{8,11},{9,10},{10,... | collective-permute-start | bytes 552968 | tf_op jit(solution)/shard_map/ppermute | solution.py:27
  52.8 15.4 %collective-permute-start.13 = (bf16[144,640]{1,0:T(8,128)(2,1)}, bf16[144,640]{1,0:T(8,128)(2,1)S(1)}, u32[]{:S(2)}, u32[]{:S(2)}) collective-permute-start(bf16[144,640]{1,0:T(8,128)(2,1)} %get-tuple-element.70.refs_2_), channel_id=1, source_target_pairs={{0,2},{1,3},{2,0},{3,1},{4,6},{5,7},{6,4},{7,5},{8,10},{9,11},{10,... | collective-permute-start | bytes 552968 | tf_op jit(solution)/shard_map/ppermute | solution.py:27
  52.8 15.4 %collective-permute-start.12 = (bf16[144,640]{1,0:T(8,128)(2,1)}, bf16[144,640]{1,0:T(8,128)(2,1)S(1)}, u32[]{:S(2)}, u32[]{:S(2)}) collective-permute-start(bf16[144,640]{1,0:T(8,128)(2,1)} %get-tuple-element.70.refs_2_), channel_id=1, source_target_pairs={{0,1},{1,0},{2,3},{3,2},{4,5},{5,4},{6,7},{7,6},{8,9},{9,8},{10,11... | collective-permute-start | bytes 552968 | tf_op jit(solution)/shard_map/ppermute | solution.py:27
  53.6 1.4 collective-permute-start.15
  55.0 13.3 %copy-start.26 = (bf16[64,384]{1,0:T(8,128)(2,1)}, bf16[64,384]{1,0:T(8,128)(2,1)S(1)}, u32[]{:S(2)}) copy-start(bf16[64,384]{1,0:T(8,128)(2,1)S(1)} %collective-permute-done.15.refs_7_) | copy-start | bytes 147460
  55.0 3.9 %collective-permute-start.17 = (bf16[64,384]{1,0:T(8,128)(2,1)}, bf16[64,384]{1,0:T(8,128)(2,1)S(1)}, u32[]{:S(2)}, u32[]{:S(2)}) collective-permute-start(bf16[64,384]{1,0:T(8,128)(2,1)} %get-tuple-element.74), channel_id=1, source_target_pairs={{0,12},{4,8},{8,4},{12,0},{16,28},{20,24},{24,20},{28,16},{1,13},{... | collective-permute-start | bytes 147464 | tf_op jit(solution)/shard_map/ppermute | solution.py:27
  58.9 9.4 %copy-start.27 = (bf16[64,384]{1,0:T(8,128)(2,1)}, bf16[64,384]{1,0:T(8,128)(2,1)S(1)}, u32[]{:S(2)}) copy-start(bf16[64,384]{1,0:T(8,128)(2,1)S(1)} %collective-permute-done.17.refs_9_) | copy-start | bytes 147460
  59.0 9.4 %copy-start.23 = (bf16[144,640]{1,0:T(8,128)(2,1)}, bf16[144,640]{1,0:T(8,128)(2,1)S(1)}, u32[]{:S(2)}) copy-start(bf16[144,640]{1,0:T(8,128)(2,1)S(1)} %collective-permute-done.14.refs_5_) | copy-start | bytes 552964
  68.3 0.9 copy-start.15
  72.0 8.9 %collective-permute-start.23 = (bf16[256,384]{1,0:T(8,128)(2,1)}, bf16[256,384]{1,0:T(8,128)(2,1)S(1)}, u32[]{:S(2)}, u32[]{:S(2)}) collective-permute-start(bf16[256,384]{1,0:T(8,128)(2,1)} %get-tuple-element.79.refs_5_), channel_id=1, source_target_pairs={{0,3},{1,2},{2,1},{3,0},{4,7},{5,6},{6,5},{7,4},{8,11},{9,10},{10,... | collective-permute-start | bytes 589832 | tf_op jit(solution)/shard_map/ppermute | solution.py:27
  74.5 17.4 %collective-permute-start.18 = (bf16[64,2688]{1,0:T(8,128)(2,1)}, bf16[64,2688]{1,0:T(8,128)(2,1)S(1)}, u32[]{:S(2)}, u32[]{:S(2)}) collective-permute-start(bf16[64,2688]{1,0:T(8,128)(2,1)} %get-tuple-element.76), channel_id=1, source_target_pairs={{0,4},{4,0},{8,12},{12,8},{16,20},{20,16},{24,28},{28,24},{1,5},{5... | collective-permute-start | bytes 1032200 | tf_op jit(solution)/shard_map/ppermute | solution.py:27
  74.5 17.4 %collective-permute-start.19 = (bf16[64,2688]{1,0:T(8,128)(2,1)}, bf16[64,2688]{1,0:T(8,128)(2,1)S(1)}, u32[]{:S(2)}, u32[]{:S(2)}) collective-permute-start(bf16[64,2688]{1,0:T(8,128)(2,1)} %get-tuple-element.77), channel_id=1, source_target_pairs={{0,8},{4,12},{8,0},{12,4},{16,24},{20,28},{24,16},{28,20},{1,9},{5... | collective-permute-start | bytes 1032200 | tf_op jit(solution)/shard_map/ppermute | solution.py:27
  74.8 17.4 %collective-permute-start.20 = (bf16[64,2688]{1,0:T(8,128)(2,1)}, bf16[64,2688]{1,0:T(8,128)(2,1)S(1)}, u32[]{:S(2)}, u32[]{:S(2)}) collective-permute-start(bf16[64,2688]{1,0:T(8,128)(2,1)} %get-tuple-element.78), channel_id=1, source_target_pairs={{0,12},{4,8},{8,4},{12,0},{16,28},{20,24},{24,20},{28,16},{1,13},{... | collective-permute-start | bytes 1032200 | tf_op jit(solution)/shard_map/ppermute | solution.py:27
  76.3 13.5 %collective-permute-start.22 = (bf16[256,384]{1,0:T(8,128)(2,1)}, bf16[256,384]{1,0:T(8,128)(2,1)S(1)}, u32[]{:S(2)}, u32[]{:S(2)}) collective-permute-start(bf16[256,384]{1,0:T(8,128)(2,1)} %get-tuple-element.79.refs_5_), channel_id=1, source_target_pairs={{0,2},{1,3},{2,0},{3,1},{4,6},{5,7},{6,4},{7,5},{8,10},{9,11},{10,... | collective-permute-start | bytes 589832 | tf_op jit(solution)/shard_map/ppermute | solution.py:27
  80.9 12.0 %copy-start.20 = (bf16[256,384]{1,0:T(8,128)(2,1)}, bf16[256,384]{1,0:T(8,128)(2,1)S(1)}, u32[]{:S(2)}) copy-start(bf16[256,384]{1,0:T(8,128)(2,1)S(1)} %collective-permute-done.23.refs_8_) | copy-start | bytes 589828
  80.9 10.9 %collective-permute-start.21 = (bf16[256,384]{1,0:T(8,128)(2,1)}, bf16[256,384]{1,0:T(8,128)(2,1)S(1)}, u32[]{:S(2)}, u32[]{:S(2)}) collective-permute-start(bf16[256,384]{1,0:T(8,128)(2,1)} %get-tuple-element.79.refs_5_), channel_id=1, source_target_pairs={{0,1},{1,0},{2,3},{3,2},{4,5},{5,4},{6,7},{7,6},{8,9},{9,8},{10,11... | collective-permute-start | bytes 589832 | tf_op jit(solution)/shard_map/ppermute | solution.py:27
  89.8 3.1 %copy-start.21 = (bf16[256,384]{1,0:T(8,128)(2,1)}, bf16[256,384]{1,0:T(8,128)(2,1)S(1)}, u32[]{:S(2)}) copy-start(bf16[256,384]{1,0:T(8,128)(2,1)S(1)} %collective-permute-done.22.refs_7_) | copy-start | bytes 589828
  91.8 1.1 copy-start.17
  91.8 1.1 copy-start.18
  92.9 21.2 %slice-start = ((bf16[320,512]{1,0:T(8,128)(2,1)}), bf16[256,512]{1,0:T(8,128)(2,1)S(1)}, s32[]{:S(2)}) async-start(bf16[320,512]{1,0:T(8,128)(2,1)} %copy-done.15), calls=%async_computation | async-start | bytes 524288 | tf_op jit(solution)/shard_map/slice | solution.py:591
  112.7 20.1 %copy-start.5 = (bf16[64,2560]{1,0:T(8,128)(2,1)S(1)}, bf16[64,2560]{1,0:T(8,128)(2,1)}, u32[]{:S(2)}) copy-start(bf16[64,2560]{1,0:T(8,128)(2,1)} %get-tuple-element.83.refs_4_) | copy-start | bytes 983044
  112.7 20.0 %copy-start.7 = (bf16[256,384]{1,0:T(8,128)(2,1)S(1)}, bf16[256,384]{1,0:T(8,128)(2,1)}, u32[]{:S(2)}) copy-start(bf16[256,384]{1,0:T(8,128)(2,1)} %get-tuple-element.88.refs_8_) | copy-start | bytes 589828
  112.7 20.0 %copy-start.9 = (f32[16,128]{1,0:T(8,128)S(1)}, f32[16,128]{1,0:T(8,128)}, u32[]{:S(2)}) copy-start(f32[16,128]{1,0:T(8,128)} %get-tuple-element.81.refs_1_.refs_6_) | copy-start | bytes 24580
  112.7 9.1 %collective-permute-start.24 = (bf16[256,384]{1,0:T(8,128)(2,1)}, bf16[256,384]{1,0:T(8,128)(2,1)S(1)}, u32[]{:S(2)}, u32[]{:S(2)}) collective-permute-start(bf16[256,384]{1,0:T(8,128)(2,1)} %get-tuple-element.85), channel_id=1, source_target_pairs={{0,1},{1,0},{2,3},{3,2},{4,5},{5,4},{6,7},{7,6},{8,9},{9,8},{10,11... | collective-permute-start | bytes 589832 | tf_op jit(solution)/shard_map/ppermute | solution.py:27
  115.1 17.0 %collective-permute-start.28 = (bf16[256,384]{1,0:T(8,128)(2,1)}, bf16[256,384]{1,0:T(8,128)(2,1)S(1)}, u32[]{:S(2)}, u32[]{:S(2)}) collective-permute-start(bf16[256,384]{1,0:T(8,128)(2,1)} %get-tuple-element.89), channel_id=1, source_target_pairs={{0,2},{1,3},{2,0},{3,1},{4,6},{5,7},{6,4},{7,5},{8,10},{9,11},{10,... | collective-permute-start | bytes 589832 | tf_op jit(solution)/shard_map/ppermute | solution.py:27
  115.9 16.4 %collective-permute-start.29 = (bf16[256,384]{1,0:T(8,128)(2,1)}, bf16[256,384]{1,0:T(8,128)(2,1)S(1)}, u32[]{:S(2)}, u32[]{:S(2)}) collective-permute-start(bf16[256,384]{1,0:T(8,128)(2,1)} %get-tuple-element.90), channel_id=1, source_target_pairs={{0,3},{1,2},{2,1},{3,0},{4,7},{5,6},{6,5},{7,4},{8,11},{9,10},{10,... | collective-permute-start | bytes 589832 | tf_op jit(solution)/shard_map/ppermute | solution.py:27
  118.2 14.2 %collective-permute-start.26 = (bf16[64,2560]{1,0:T(8,128)(2,1)}, bf16[64,2560]{1,0:T(8,128)(2,1)S(1)}, u32[]{:S(2)}, u32[]{:S(2)}) collective-permute-start(bf16[64,2560]{1,0:T(8,128)(2,1)} %get-tuple-element.86), channel_id=1, source_target_pairs={{0,8},{4,12},{8,0},{12,4},{16,24},{20,28},{24,16},{28,20},{1,9},{5... | collective-permute-start | bytes 983048 | tf_op jit(solution)/shard_map/ppermute | solution.py:27
  118.5 14.2 %collective-permute-start.27 = (bf16[64,2560]{1,0:T(8,128)(2,1)}, bf16[64,2560]{1,0:T(8,128)(2,1)S(1)}, u32[]{:S(2)}, u32[]{:S(2)}) collective-permute-start(bf16[64,2560]{1,0:T(8,128)(2,1)} %get-tuple-element.87), channel_id=1, source_target_pairs={{0,12},{4,8},{8,4},{12,0},{16,28},{20,24},{24,20},{28,16},{1,13},{... | collective-permute-start | bytes 983048 | tf_op jit(solution)/shard_map/ppermute | solution.py:27
  121.8 1.0 copy-start.4
  123.5 9.2 %collective-permute-start.25 = (bf16[64,2560]{1,0:T(8,128)(2,1)}, bf16[64,2560]{1,0:T(8,128)(2,1)S(1)}, u32[]{:S(2)}, u32[]{:S(2)}) collective-permute-start(bf16[64,2560]{1,0:T(8,128)(2,1)} %shard_map.149), channel_id=1, source_target_pairs={{0,4},{4,0},{8,12},{12,8},{16,20},{20,16},{24,28},{28,24},{1,5},{5... | collective-permute-start | bytes 983048 | tf_op jit(solution)/shard_map/ppermute | solution.py:27
  132.1 7.4 %collective-permute-start.36 = (bf16[1,2,8,2,8,512]{5,4,3,2,1,0:T(8,128)(2,1)S(1)}, bf16[1,2,8,2,8,512]{5,4,3,2,1,0:T(8,128)(2,1)S(1)}, u32[]{:S(2)}, u32[]{:S(2)}) collective-permute-start(bf16[1,2,8,2,8,512]{5,4,3,2,1,0:T(8,128)(2,1)S(1)} %get-tuple-element.105), channel_id=1, source_target_pairs={{0,16},{4,20},{8,24},{12,28},{16,0},{20,4},{24,8},{28,12},{1,17},{... | collective-permute-start | bytes 786440 | tf_op jit(solution)/shard_map/ppermute | solution.py:27
  133.6 6.3 %collective-permute-start.33 = (bf16[64,384]{1,0:T(8,128)(2,1)S(1)}, bf16[64,384]{1,0:T(8,128)(2,1)S(1)}, u32[]{:S(2)}, u32[]{:S(2)}) collective-permute-start(bf16[64,384]{1,0:T(8,128)(2,1)S(1)} %get-tuple-element.99), channel_id=1, source_target_pairs={{0,4},{4,0},{8,12},{12,8},{16,20},{20,16},{24,28},{28,24},{1,5},{5... | collective-permute-start | bytes 147464 | tf_op jit(solution)/shard_map/ppermute | solution.py:27
  135.1 10.3 %collective-permute-start.30 = (bf16[128,640]{1,0:T(8,128)(2,1)S(1)}, bf16[128,640]{1,0:T(8,128)(2,1)S(1)}, u32[]{:S(2)}, u32[]{:S(2)}) collective-permute-start(bf16[128,640]{1,0:T(8,128)(2,1)S(1)} %get-tuple-element.95), channel_id=1, source_target_pairs={{0,1},{1,0},{2,3},{3,2},{4,5},{5,4},{6,7},{7,6},{8,9},{9,8},{10,11... | collective-permute-start | bytes 491528 | tf_op jit(solution)/shard_map/ppermute | solution.py:27
  136.3 15.0 %collective-permute-start.31 = (bf16[128,640]{1,0:T(8,128)(2,1)S(1)}, bf16[128,640]{1,0:T(8,128)(2,1)S(1)}, u32[]{:S(2)}, u32[]{:S(2)}) collective-permute-start(bf16[128,640]{1,0:T(8,128)(2,1)S(1)} %get-tuple-element.96), channel_id=1, source_target_pairs={{0,2},{1,3},{2,0},{3,1},{4,6},{5,7},{6,4},{7,5},{8,10},{9,11},{10,... | collective-permute-start | bytes 491528 | tf_op jit(solution)/shard_map/ppermute | solution.py:27
  137.1 14.3 %collective-permute-start.32 = (bf16[128,640]{1,0:T(8,128)(2,1)S(1)}, bf16[128,640]{1,0:T(8,128)(2,1)S(1)}, u32[]{:S(2)}, u32[]{:S(2)}) collective-permute-start(bf16[128,640]{1,0:T(8,128)(2,1)S(1)} %get-tuple-element.97), channel_id=1, source_target_pairs={{0,3},{1,2},{2,1},{3,0},{4,7},{5,6},{6,5},{7,4},{8,11},{9,10},{10,... | collective-permute-start | bytes 491528 | tf_op jit(solution)/shard_map/ppermute | solution.py:27
  139.5 5.9 %collective-permute-start.34 = (bf16[64,384]{1,0:T(8,128)(2,1)S(1)}, bf16[64,384]{1,0:T(8,128)(2,1)S(1)}, u32[]{:S(2)}, u32[]{:S(2)}) collective-permute-start(bf16[64,384]{1,0:T(8,128)(2,1)S(1)} %get-tuple-element.100), channel_id=1, source_target_pairs={{0,8},{4,12},{8,0},{12,4},{16,24},{20,28},{24,16},{28,20},{1,9},{5... | collective-permute-start | bytes 147464 | tf_op jit(solution)/shard_map/ppermute | solution.py:27
  139.9 5.5 %collective-permute-start.35 = (bf16[64,384]{1,0:T(8,128)(2,1)S(1)}, bf16[64,384]{1,0:T(8,128)(2,1)S(1)}, u32[]{:S(2)}, u32[]{:S(2)}) collective-permute-start(bf16[64,384]{1,0:T(8,128)(2,1)S(1)} %get-tuple-element.101), channel_id=1, source_target_pairs={{0,12},{4,8},{8,4},{12,0},{16,28},{20,24},{24,20},{28,16},{1,13},{... | collective-permute-start | bytes 147464 | tf_op jit(solution)/shard_map/ppermute | solution.py:27
  140.2 11.2 %copy-start.3 = (f32[128,1024]{1,0:T(8,128)S(1)}, f32[128,1024]{1,0:T(8,128)}, u32[]{:S(2)}) copy-start(f32[128,1024]{1,0:T(8,128)} %copy-done.2) | copy-start | bytes 1572868
  (7 other events, 5.1 us)

commit v6 on v5

--- a/solution.py
+++ b/solution.py
@@ -20,6 +20,7 @@
 VMEM = pl.BlockSpec(memory_space=pltpu.VMEM)
 SMEM = pl.BlockSpec(memory_space=pltpu.SMEM)
 HBM = pl.BlockSpec(memory_space=pltpu.HBM)
+ANY = pl.BlockSpec(memory_space=pl.ANY)
 
 
 def swap(x, axis, s):
@@ -60,6 +61,10 @@
     return jax.ShapeDtypeStruct(dims, dtype)
 
 
+def near(dims, dtype):
+    return pltpu.VMEM(dims, dtype)
+
+
 def far(dims, dtype):
     return pltpu.HBM(dims, dtype)
 
@@ -81,29 +86,37 @@
         def _():
             i = rows[j]
             for p in range(pages):
-                page = pool[table[i * pages + p]].astype(F32)
+                page = pool[table[p, i]].astype(F32)
                 out[j, p] = jnp.where(token + p * page_len < length[i], page, 0.0).astype(out.dtype)
 
 
+def send_pages_kernel(pool, rows, table, length, out):
+    count, pages, page_len, width = out.shape
+    position = lax.broadcasted_iota(I32, (page_len, width), 0)
+
+    @pl.loop(0, count)
+    def _(j):
+        i = rows[j, 0]
+        for p in range(pages):
+            page = pool[table[p, i]].astype(F32)
+            out[j, p] = jnp.where(position + p * page_len < length[i], page, 0.0).astype(out.dtype)
+
+
 def take_pages(pool, moved, rows, slot, table, length, after=()):
-    pages = table.shape[0] // length.shape[0]
-    outs = [shape((rows.shape[0], pages) + pool.shape[1:], pool.dtype)]
+    outs = [shape(slot.shape + table.shape[:1] + pool.shape[1:], pool.dtype)]
     args = (pool, moved, rows, slot, table, length)
     return local_call(page_kernel, [VMEM] * 2 + [SMEM] * 4, args, outs, moved=5 * MIB, after=after)[0]
 
 
-def split_kernel(place, x, order, *outs):
-    blocks, order_out = outs[:-1], outs[-1]
-    width = blocks[0].shape[1]
-    for s, block in enumerate(blocks):
-        block[...] = x[:, lanes((place[0] ^ s) * width, width)]
-    order_out[...] = order[...]
-
-
-def movers_kernel(half, spot, order, attention, residual, pair, own, row_out):
+def movers_kernel(half, spot, order, attention, residual, *outs):
+    chip, side = spot[0] // 2, spot[0] % 2
+    pair, own, row_out = outs[half:]
+    for s, block in enumerate(outs[:half]):
+        width = block.shape[1]
+        block[...] = attention[:, lanes((chip ^ s) * width, width)]
     n, rows = order.shape
     down, across = (lax.broadcasted_iota(I32, (rows, rows), d) for d in (0, 1))
-    mine = (2 * spot[0] + spot[1]) * rows + down
+    mine = spot[0] * rows + down
     found = jnp.zeros((rows, rows), F32)
     for g in range(1, n):
         found = found + jnp.where(order[g : g + 1] == mine, float(g), 0.0)
@@ -112,9 +125,9 @@
     rank = jnp.sum(jnp.where((dest == dest_row) & (down < across), 1.0, 0.0), axis=0, keepdims=True)
     rank = rank.astype(I32)
     to = dest_row[:1].astype(I32)
-    far_off, core = (to >> 1) ^ spot[0], to & 1
+    far_off, core = (to >> 1) ^ chip, to & 1
     kept = jnp.where(far_off != 0, (half + far_off - 1) * MIG + rank, -1)
-    slot = jnp.where(core != spot[1], far_off * MIG + rank, kept)
+    slot = jnp.where(core != side, far_off * MIG + rank, kept)
     chosen = lax.broadcasted_iota(I32, (own.shape[0], rows), 0) == slot
     selector = jnp.where(chosen, 1.0, 0.0)
     numbers = lax.broadcasted_iota(I32, selector.shape, 1).astype(F32)
@@ -159,15 +172,16 @@
 
 
 def project_kernel(half, *refs):
-    odd, selector, resid_selector, residual, own, other = refs[:6]
+    odd, selector_far, resid_selector, residual, own, other = refs[:6]
     blocks = refs[6 : 6 + 2 * half]
     outs = refs[6 + 2 * half : 6 + 3 * half]
-    buf, weights, sems = refs[6 + 3 * half :]
+    buf, weights, selector, sems = refs[6 + 3 * half :]
     rows = residual.shape[0]
     copies = [
         pltpu.make_async_copy(blocks[s], buf.at[pl.ds(s * rows, rows)], sems.at[s])
         for s in range(half)
     ]
+    copies.append(pltpu.make_async_copy(selector_far, selector, sems.at[half + 2]))
     fetches = [
         pltpu.make_async_copy(own, weights.at[odd[0]], sems.at[half]),
         pltpu.make_async_copy(other, weights.at[1 - odd[0]], sems.at[half + 1]),
@@ -357,7 +371,7 @@
             early_copy(e, t).wait()
 
 
-def expert_call(place, early, late, w_gate, w_up, w_down, stats, ne):
+def expert_call(place, early, late, w_gate, w_up, w_down, stats, ne, after):
     hidden = w_gate.shape[2]
     slots, rest = late[0].shape
     experts = len(early)
@@ -367,9 +381,11 @@
         functools.partial(expert_kernel, ne, experts, tile),
         [SMEM] + [HBM] * (experts + ne + 3) + [VMEM],
         (place, *early, *late, w_gate, w_up, w_down, stats),
-        [far((slots, rest), BF)] * ne
-        + [far((SLOTS, ne * wide), BF)] * experts
-        + [shape(stats.shape, F32)],
+        [near((slots, rest), BF)]
+        + [far((slots, rest), BF)] * (ne - 1)
+        + [near((SLOTS, ne * wide), BF)]
+        + [far((SLOTS, ne * wide), BF)] * (experts - 1)
+        + [near(stats.shape, F32)],
         [
             pltpu.VMEM((slots, D), BF),
             pltpu.VMEM((slots, 128), BF),
@@ -384,7 +400,8 @@
             pltpu.SemaphoreType.DMA((ne, experts + 1)),
         ],
         vmem=60,
-        out_specs=[HBM] * (ne + experts) + [VMEM],
+        out_specs=[ANY] + [HBM] * (ne - 1) + [ANY] + [HBM] * (experts - 1) + [VMEM],
+        after=[after],
         flops=6 * slots * D * hidden,
         moved=6 * D * hidden,
     )
@@ -465,41 +482,32 @@
     place = ze.reshape(1).astype(I32)
 
     pair_place = q.reshape(1).astype(I32)
-    *attn_blocks, came_from = local_call(
-        split_kernel,
-        [SMEM, VMEM, VMEM],
-        (pair_place, attention_out, came_from.reshape(n, rows)),
-        [far((rows, kblock), BF)] * half + [shape((n, rows), I32)],
-        vmem=60,
-        moved=2 * MIB,
-    )
-    came_from = came_from.reshape(-1)
-    attn_blocks = [attn_blocks[0]] + [swap(attn_blocks[s], "req", 2 * s) for s in range(1, half)]
-    w_other = swap(w_out, "req", 1)
-
     n_pair, n_send = half * MIG, (2 * half - 1) * MIG
     n_hand = -(-(n_pair + 2 * MIG) // 16) * 16
-    pair_rows, own_rows, send_row = local_call(
+    *attn_blocks, pair_rows, own_rows, send_row = local_call(
         functools.partial(movers_kernel, half),
         [SMEM] + [VMEM] * 3,
-        (jnp.stack([q, k]).astype(I32), came_from.reshape(n, rows), attention_out, residual),
-        [
-            shape((n_pair, D + feats), BF),
-            shape((2 * n_pair, feats), BF),
+        (me.reshape(1).astype(I32), came_from.reshape(n, rows), attention_out, residual),
+        [far((rows, kblock), BF)] * half
+        + [
+            far((n_pair, D + feats), BF),
+            far((2 * n_pair, feats), BF),
             shape((2 * n_pair, 128), I32),
         ],
         vmem=60,
         moved=2 * MIB,
-        after=[w_other],
-    )
-    send_row = send_row[:n_send, 0]
+    )
+    attn_blocks = [attn_blocks[0]] + [swap(attn_blocks[s], "req", 2 * s) for s in range(1, half)]
+    w_other = swap(w_out, "req", 1)
     pair_rows = swap(pair_rows, "req", 1)
     *late_blocks, order = local_call(
         functools.partial(handover_kernel, half),
         [SMEM, VMEM, VMEM, VMEM],
         (pair_place, pair_rows, own_rows, came_from.reshape(n, rows)),
-        [shape((n_hand, feats), BF)] * half + [shape((n, rows), I32)],
+        [far((n_hand, feats), BF)] * half + [shape((n, rows), I32)],
+        vmem=60,
         moved=MIB,
+        after=[w_other],
     )
     late_blocks = [late_blocks[0]] + [swap(late_blocks[s], "req", 2 * s) for s in range(1, half)]
     came_from = order.reshape(-1)
@@ -537,7 +545,7 @@
     resid_selector = hot(own_at, rows + half * n_hand)
     parts = local_call(
         functools.partial(project_kernel, half),
-        [SMEM] + [VMEM] * 3 + [HBM] * (2 + half) + [VMEM] * half,
+        [SMEM, HBM] + [VMEM] * 2 + [HBM] * (2 + half) + [VMEM] * half,
         (
             k.reshape(1).astype(I32),
             selector,
@@ -552,7 +560,8 @@
         [
             pltpu.VMEM((total_rows, kblock), BF),
             pltpu.VMEM((2,) + w_out.shape, BF),
-            pltpu.SemaphoreType.DMA((half + 2,)),
+            pltpu.VMEM(selector.shape, BF),
+            pltpu.SemaphoreType.DMA((half + 3,)),
         ],
         vmem=58,
         flops=2 * half * rows * (total_rows + feats) * kblock,
@@ -560,10 +569,15 @@
     )
     parts = [parts[0]] + [swap(parts[s], "req", 2 * s) for s in range(1, half)]
 
-    table = page_table.reshape(-1)
-    none = jnp.full((n_send,), -1, I32)
-    no_rows = page_pool[:2].reshape((1, 2) + page_pool.shape[1:])
-    moving = take_pages(page_pool, no_rows, send_row, none, table, cache_len, [order])
+    table = page_table.T
+    moving = local_call(
+        send_pages_kernel,
+        [VMEM] + [SMEM] * 3,
+        (page_pool, send_row, table, cache_len),
+        [shape((n_send,) + table.shape[:1] + page_pool.shape[1:], BF)],
+        moved=3 * MIB,
+        after=[order],
+    )[0]
     page = moving.shape[1:]
     pair_pages = swap(moving[:n_pair], "req", 1).reshape((half, MIG) + page)
     own_pages = jnp.concatenate([moving[:MIG], moving[n_pair:]], axis=0).reshape((half, MIG) + page)
@@ -580,7 +594,7 @@
         functools.partial(norm_kernel, half, experts, wide),
         [VMEM] * (4 + half),
         (norm_gain[None, :], router, slot_pick, page_rows, *parts),
-        [shape((rows, feats), F32), far((rows + 16, wide), BF)]
+        [far((rows, feats), F32), far((rows + 16, wide), BF)]
         + [far(dims, BF) for dims in late_shapes],
         flops=2 * experts * SLOTS * rows * rest,
         moved=3 * MIB,
@@ -594,8 +608,9 @@
         functools.partial(dispatch_kernel, ne, experts),
         [SMEM] + [VMEM] * (1 + ne + experts),
         (place, slot_pick, *early_blocks, *late),
-        [far((SLOTS, ne * wide + 128), BF)] * experts
-        + [shape((16, rows), F32), far((experts * SLOTS, rest), BF)],
+        [far((SLOTS, ne * wide + 128), BF)]
+        + [near((SLOTS, ne * wide + 128), BF)] * (experts - 1)
+        + [near((16, rows), F32), far((experts * SLOTS, rest), BF)],
         vmem=60,
         flops=2 * experts * SLOTS * rows * ne * wide,
         moved=3 * MIB,
@@ -605,6 +620,7 @@
 
     early_rows = [swap(outgoing[s], "req", s) if s else outgoing[s] for s in range(experts)]
 
+    crossing = pages
     for bit in range(1, stages):
         pages = pages.reshape((half >> (bit + 1), 2, 1 << bit) + block)
         came_pages = swap(pages[:, 1], "req", 2 << bit)
@@ -612,10 +628,10 @@
     moved_pages = pages.reshape((half * 2 * MIG,) + page)
 
     down_late, down_early, stats = expert_call(
-        place, early_rows, late_rows, w_gate, w_up, w_down, outgoing[experts], ne
+        place, early_rows, late_rows, w_gate, w_up, w_down, outgoing[experts], ne, crossing
     )
     late_blocks = [down_late[0]] + [swap(down_late[s], "exp", s) for s in range(1, ne)]
-    near_back = hold(down_early[1], late_blocks[1])
+    near_back = hold(down_early[1], late_blocks[-1])
     early_back = [
         swap(down_early[s] if s > 1 else near_back, "req", s) if s else down_early[s]
         for s in range(experts)
@@ -641,7 +657,8 @@
         flops=4 * rows * experts * SLOTS * ne * wide,
         moved=3 * MIB,
     )
-    early_parts = [weighted[0]] + [swap(weighted[s], "exp", s) for s in range(1, ne)]
+    early_parts = [swap(weighted[s], "exp", s) for s in range(ne - 1, 0, -1)]
+    early_parts = [weighted[0]] + early_parts[::-1]
     late_back = [
         swap(weighted[ne + s], "req", s) if s else weighted[ne] for s in range(experts)
     ]

time: 153 us -> 149 us (0.974)
  waiting for transfers between devices: 53.2 us -> 48.1 us
  starting transfers between devices: 40.8 us -> 42.6 us
    ppermute x37, waiting for transfers between devices: 53.2 us -> 48.1 us  [swap(): return lax.ppermute(x, axis, [(i, i ^ s) for i in range(n)])]
    ppermute x37, starting transfers between devices: 40.8 us -> 42.6 us  [swap(): return lax.ppermute(x, axis, [(i, i ^ s) for i in range(n)])]
    another operation x1 -> x2, other arithmetic: 0.05 us -> 1.83 us  [body(): pages = jnp.stack([pages[:, 0], came_pages], axis=1)]
    unnamed x67 -> x60, local copies, waits for them, and re-layouts: 5.97 us -> 5.04 us
    pallas_call x13 -> x12, Pallas kernels: 44.9 us -> 44 us  [local_call(): pl.pallas_call(run, out_shape=outs, in_specs=list(in_specs) + [pl.BlockSp...]
  transfers between devices with their start and end apart: 37 -> 37, of which waited for: 15 -> 15; matrix products, arithmetic and copies ran while one was open for 4% -> 5% of each run, Pallas kernels for 12% -> 12%
where the time goes in v6:
time: 149 us; the launch traced here: 148 us
  waiting for transfers between devices  48.1 us (32%)
  Pallas kernels  44 us (30%)
  starting transfers between devices  42.6 us (29%)
  local copies, waits for them, and re-layouts  7.68 us (5%)
  other arithmetic  4.93 us (3%)
    ppermute x37, waiting for transfers between devices, swap(): return lax.ppermute(x, axis, [(i, i ^ s) for i in range(n)])  48.1 us
    pallas_call x12, Pallas kernels, local_call(): pl.pallas_call(run, out_shape=outs, in_specs=list(in_specs) + [pl.BlockSp...  44 us
    ppermute x37, starting transfers between devices, swap(): return lax.ppermute(x, axis, [(i, i ^ s) for i in range(n)])  42.6 us
    unnamed x60, local copies, waits for them, and re-layouts  5.04 us
  transfers between devices with their start and end apart: 37, of which 15 were waited for; matrix products, arithmetic and copies ran while one was open for 5% of the time, Pallas kernels for 12%

profile of v6, /device:TPU:0, one launch (start us, length us, event | category | flops | bytes accessed | tf_op | source)
XLA Modules:
  0.0 148.2 jit_solution(8000796038053908281)
XLA Ops:
  0.7 0.5 collective-permute-start.1
  1.2 2.8 %shard_map.140 = (bf16[128,1024]{1,0:T(8,128)(2,1)}, bf16[128,1024]{1,0:T(8,128)(2,1)}, bf16[128,1024]{1,0:T(8,128)(2,1)}, bf16[128,1024]{1,0:T(8,128)(2,1)}, bf...) custom-call(s32[1]{0:T(128)} %bitcast.4.refs_0_, s32[8,128]{1,0:T(8,128)} %bitcast.77, ...), custom_call_target="tpu_custom_call" | custom-call | bytes 2097152 | tf_op jit(solution)/shard_map/pallas_call | solution.py:49
  4.1 2.8 %collective-permute-start.3 = (bf16[128,1024]{1,0:T(8,128)(2,1)}, bf16[128,1024]{1,0:T(8,128)(2,1)}, u32[]{:S(2)}, u32[]{:S(2)}) collective-permute-start(bf16[128,1024]{1,0:T(8,128)(2,1)} %get-tuple-element.57), channel_id=1, source_target_pairs={{0,8},{4,12},{8,0},{12,4},{16,24},{20,28},{24,16},{28,20},{1,9},{5... | collective-permute-start | bytes 786440 | tf_op jit(solution)/shard_map/ppermute | solution.py:28
  6.9 1.5 %collective-permute-start.4 = (bf16[128,1024]{1,0:T(8,128)(2,1)}, bf16[128,1024]{1,0:T(8,128)(2,1)}, u32[]{:S(2)}, u32[]{:S(2)}) collective-permute-start(bf16[128,1024]{1,0:T(8,128)(2,1)} %get-tuple-element.58), channel_id=1, source_target_pairs={{0,16},{4,20},{8,24},{12,28},{16,0},{20,4},{24,8},{28,12},{1,17},{... | collective-permute-start | bytes 786440 | tf_op jit(solution)/shard_map/ppermute | solution.py:28
  8.4 0.6 copy-done.23
  9.1 0.4 copy-done.13
  9.4 1.7 %shard_map.141 = (bf16[32,1024]{1,0:T(8,128)(2,1)}, bf16[32,1024]{1,0:T(8,128)(2,1)}, bf16[32,1024]{1,0:T(8,128)(2,1)}, bf16[32,1024]{1,0:T(8,128)(2,1)}, s32[8,128]{1,0:T(8,128)}) custom-call(s32[1]{0:T(128)} %bitcast.3.refs_0_, bf16[16,5120]{1,0:T(8,128)(2,1)} %copy-done.23, bf16[32,1024]{1,0:T(8,128)(2,1)} %get-tuple-element.52.refs_2_, ...), custom_call_target="tpu_custom_call" | custom-call | bytes 1048576 | tf_op jit(solution)/shard_map/pallas_call | solution.py:49
  11.1 0.9 dynamic-slice_bitcast_fusion.3
  12.0 0.3 convert_reduce_fusion
  12.4 2.0 %collective-permute-start.6 = (bf16[32,1024]{1,0:T(8,128)(2,1)}, bf16[32,1024]{1,0:T(8,128)(2,1)S(1)}, u32[]{:S(2)}, u32[]{:S(2)}) collective-permute-start(bf16[32,1024]{1,0:T(8,128)(2,1)} %get-tuple-element.61), channel_id=1, source_target_pairs={{0,8},{4,12},{8,0},{12,4},{16,24},{20,28},{24,16},{28,20},{1,9},{5... | collective-permute-start | bytes 196616 | tf_op jit(solution)/shard_map/ppermute | solution.py:28
  14.4 1.5 %collective-permute-start.7 = (bf16[32,1024]{1,0:T(8,128)(2,1)}, bf16[32,1024]{1,0:T(8,128)(2,1)S(1)}, u32[]{:S(2)}, u32[]{:S(2)}) collective-permute-start(bf16[32,1024]{1,0:T(8,128)(2,1)} %get-tuple-element.62), channel_id=1, source_target_pairs={{0,16},{4,20},{8,24},{12,28},{16,0},{20,4},{24,8},{28,12},{1,17},{... | collective-permute-start | bytes 196616 | tf_op jit(solution)/shard_map/ppermute | solution.py:28
  15.9 1.0 fusion.refs_1_
  17.3 0.7 fusion.6.refs_2_
  18.0 0.7 copy-done.5
  18.7 1.2 shard_map.143
  19.9 0.7 slice.58
  20.6 1.4 collective-permute-done.4.refs_8_
  22.1 1.5 %collective-permute-done.7.refs_12_ = bf16[32,1024]{1,0:T(8,128)(2,1)S(1)} collective-permute-done((bf16[32,1024]{1,0:T(8,128)(2,1)}, bf16[32,1024]{1,0:T(8,128)(2,1)S(1)}, u32[]{:S(2)}, u32[]{:S(2)}) %collective-permute-start.7) | collective-permute-done | bytes 65568 | tf_op jit(solution)/shard_map/ppermute | solution.py:28
  23.6 0.6 copy-done.28
  24.3 5.7 %shard_map.144 = (f32[128,1024]{1,0:T(8,128)}, bf16[128,1024]{1,0:T(8,128)(2,1)}, bf16[128,1024]{1,0:T(8,128)(2,1)}, bf16[128,1024]{1,0:T(8,128)(2,1)}) custom-call(s32[1]{0:T(128)} %bitcast.12.refs_0_, bf16[512,640]{1,0:T(8,128)(2,1)} %fusion.refs_1_, bf16[128,256]{1,0:T(8,128)(2,1)} %fusion.6.refs_2_, bf16[128,1024]{1,0:T(8,128)(2,1)} %refs_3_.5, ...), custom_call_target="tpu_custom_call" | custom-call | flops 1744830464 | bytes 6291456 | tf_op jit(solution)/shard_map/pallas_call | solution.py:49
  30.0 1.3 collective-permute-start.9
  31.3 0.8 collective-permute-start.10
  32.1 1.4 collective-permute-start.11
  33.9 0.9 fusion.5
  34.8 4.6 %collective-permute-done.9.refs_5_ = bf16[128,1024]{1,0:T(8,128)(2,1)S(1)} collective-permute-done((bf16[128,1024]{1,0:T(8,128)(2,1)}, bf16[128,1024]{1,0:T(8,128)(2,1)S(1)}, u32[]{:S(2)}, u32[]{:S(2)}) %collective-permute-start.9) | collective-permute-done | bytes 262176 | tf_op jit(solution)/shard_map/ppermute | solution.py:28
  39.5 5.7 %collective-permute-done.11.refs_7_ = bf16[128,1024]{1,0:T(8,128)(2,1)} collective-permute-done((bf16[128,1024]{1,0:T(8,128)(2,1)}, bf16[128,1024]{1,0:T(8,128)(2,1)}, u32[]{:S(2)}, u32[]{:S(2)}) %collective-permute-start.11) | collective-permute-done | bytes 262176 | tf_op jit(solution)/shard_map/ppermute | solution.py:28
  45.1 2.3 %shard_map.145 = (f32[128,1024]{1,0:T(8,128)}, bf16[144,640]{1,0:T(8,128)(2,1)}, bf16[64,384]{1,0:T(8,128)(2,1)}, bf16[64,384]{1,0:T(8,128)(2,1)}, bf16[320,512]{1,0:T(8,128)(2,1)}, /*index=5*/bf16[64,384]{1,0:T(8,128)(2,1)}) custom-call(f32[1,1024]{1,0:T(1,128)S(1)} %bitcast.67, f32[8,1024]{1,0:T(8,128)S(1)} %pad.4.refs_1_, ...), custom_call_target="tpu_custom_call" | custom-call | flops 25165824 | bytes 3145728 | tf_op jit(solution)/shard_map/pallas_call | solution.py:49
  47.5 0.9 collective-permute-start.16
  48.3 3.6 %collective-permute-start.14 = (bf16[144,640]{1,0:T(8,128)(2,1)}, bf16[144,640]{1,0:T(8,128)(2,1)S(1)}, u32[]{:S(2)}, u32[]{:S(2)}) collective-permute-start(bf16[144,640]{1,0:T(8,128)(2,1)} %get-tuple-element.68.refs_2_), channel_id=1, source_target_pairs={{0,3},{1,2},{2,1},{3,0},{4,7},{5,6},{6,5},{7,4},{8,11},{9,10},{10,... | collective-permute-start | bytes 552968 | tf_op jit(solution)/shard_map/ppermute | solution.py:28
  51.9 0.8 collective-permute-start.12
  52.7 1.4 collective-permute-done.15.refs_7_
  54.2 0.9 collective-permute-start.17
  55.1 3.0 %collective-permute-done.17.refs_9_ = bf16[64,384]{1,0:T(8,128)(2,1)S(1)} collective-permute-done((bf16[64,384]{1,0:T(8,128)(2,1)}, bf16[64,384]{1,0:T(8,128)(2,1)S(1)}, u32[]{:S(2)}, u32[]{:S(2)}) %collective-permute-start.17) | collective-permute-done | bytes 49184 | tf_op jit(solution)/shard_map/ppermute | solution.py:28
  58.1 8.4 %collective-permute-done.13.refs_4_ = bf16[144,640]{1,0:T(8,128)(2,1)S(1)} collective-permute-done((bf16[144,640]{1,0:T(8,128)(2,1)}, bf16[144,640]{1,0:T(8,128)(2,1)S(1)}, u32[]{:S(2)}, u32[]{:S(2)}) %collective-permute-start.13) | collective-permute-done | bytes 184352 | tf_op jit(solution)/shard_map/ppermute | solution.py:28
  66.5 0.6 copy-done.21
  67.3 2.6 %shard_map.146 = (bf16[64,2688]{1,0:T(8,128)(2,1)}, bf16[64,2688]{1,0:T(8,128)(2,1)S(1)}, bf16[64,2688]{1,0:T(8,128)(2,1)S(1)}, bf16[64,2688]{1,0:T(8,128)(2,1)S...) custom-call(s32[1]{0:T(128)} %bitcast.refs_0_, bf16[256,128]{1,0:T(8,128)(2,1)} %copy-done.4, ...), custom_call_target="tpu_custom_call" | custom-call | flops 167772160 | bytes 3145728 | tf_op jit(solution)/shard_map/pallas_call | solution.py:49
  69.8 2.5 %collective-permute-start.23 = (bf16[256,384]{1,0:T(8,128)(2,1)}, bf16[256,384]{1,0:T(8,128)(2,1)S(1)}, u32[]{:S(2)}, u32[]{:S(2)}) collective-permute-start(bf16[256,384]{1,0:T(8,128)(2,1)} %get-tuple-element.77.refs_5_), channel_id=1, source_target_pairs={{0,3},{1,2},{2,1},{3,0},{4,7},{5,6},{6,5},{7,4},{8,11},{9,10},{10,... | collective-permute-start | bytes 589832 | tf_op jit(solution)/shard_map/ppermute | solution.py:28
  72.3 1.4 collective-permute-start.19
  73.8 0.4 collective-permute-start.20
  74.2 4.5 %collective-permute-done.23.refs_8_ = bf16[256,384]{1,0:T(8,128)(2,1)S(1)} collective-permute-done((bf16[256,384]{1,0:T(8,128)(2,1)}, bf16[256,384]{1,0:T(8,128)(2,1)S(1)}, u32[]{:S(2)}, u32[]{:S(2)}) %collective-permute-start.23) | collective-permute-done | bytes 196640 | tf_op jit(solution)/shard_map/ppermute | solution.py:28
  78.7 6.5 %collective-permute-start.21 = (bf16[256,384]{1,0:T(8,128)(2,1)}, bf16[256,384]{1,0:T(8,128)(2,1)S(1)}, u32[]{:S(2)}, u32[]{:S(2)}) collective-permute-start(bf16[256,384]{1,0:T(8,128)(2,1)} %get-tuple-element.77.refs_5_), channel_id=1, source_target_pairs={{0,1},{1,0},{2,3},{3,2},{4,5},{5,4},{6,7},{7,6},{8,9},{9,8},{10,11... | collective-permute-start | bytes 589832 | tf_op jit(solution)/shard_map/ppermute | solution.py:28
  85.2 1.0 slice.61
  86.2 1.8 %fusion.4.refs_13_ = bf16[2,2,8,2,8,512]{5,4,3,2,1,0:T(8,128)(2,1)} fusion(bf16[2,2,4,2,8,512]{5,4,3,2,1,0:T(8,128)(2,1)S(1)} %bitcast.74, bf16[2,2,4,2,8,512]{5,4,3,2,1,0:T(8,128)(2,1)} %bitcast.10, bf16[2,1,8,2,8,512]{5,4,3,2,1,0:T(8,128)(2,1)S(1)} %bitcast.75), kind=kLoop, calls=%fused_computation.8 | loop fusion | flops 2359296 | bytes 1310720 | tf_op jit(solution)/shard_map/stack | solution.py:606
  88.0 1.7 %collective-permute-done.21.refs_6_ = bf16[256,384]{1,0:T(8,128)(2,1)S(1)} collective-permute-done((bf16[256,384]{1,0:T(8,128)(2,1)}, bf16[256,384]{1,0:T(8,128)(2,1)S(1)}, u32[]{:S(2)}, u32[]{:S(2)}) %collective-permute-start.21) | collective-permute-done | bytes 196640 | tf_op jit(solution)/shard_map/ppermute | solution.py:28
  89.8 0.6 copy-done.19
  90.8 19.6 %shard_map.147 = (bf16[256,384]{1,0:T(8,128)(2,1)S(1)}, bf16[256,384]{1,0:T(8,128)(2,1)}, bf16[256,384]{1,0:T(8,128)(2,1)}, bf16[256,384]{1,0:T(8,128)(2,1)}, bf...) custom-call(s32[1]{0:T(128)} %bitcast.refs_0_, ...), custom_call_target="tpu_custom_call" | custom-call | flops 11274289152 | bytes 44040192 | tf_op jit(solution)/shard_map/pallas_call | solution.py:49
  110.4 1.2 collective-permute-start.24
  111.6 0.3 collective-permute-start.28
  111.9 2.9 %collective-permute-start.29 = (bf16[256,384]{1,0:T(8,128)(2,1)}, bf16[256,384]{1,0:T(8,128)(2,1)S(1)}, u32[]{:S(2)}, u32[]{:S(2)}) collective-permute-start(bf16[256,384]{1,0:T(8,128)(2,1)} %get-tuple-element.88), channel_id=1, source_target_pairs={{0,2},{1,3},{2,0},{3,1},{4,6},{5,7},{6,4},{7,5},{8,10},{9,11},{10,... | collective-permute-start | bytes 589832 | tf_op jit(solution)/shard_map/ppermute | solution.py:28
  114.8 1.4 collective-permute-start.26
  116.2 4.0 %collective-permute-done.24.refs_1_.refs_11_ = bf16[256,384]{1,0:T(8,128)(2,1)S(1)} collective-permute-done((bf16[256,384]{1,0:T(8,128)(2,1)}, bf16[256,384]{1,0:T(8,128)(2,1)S(1)}, u32[]{:S(2)}, u32[]{:S(2)}) %collective-permute-start.24) | collective-permute-done | bytes 196640 | tf_op jit(solution)/shard_map/ppermute | solution.py:28
  120.3 1.0 copy-done.3
  121.2 0.8 shard_map.148
  122.0 2.6 %collective-permute-done.28.refs_9_ = bf16[256,384]{1,0:T(8,128)(2,1)S(1)} collective-permute-done((bf16[256,384]{1,0:T(8,128)(2,1)}, bf16[256,384]{1,0:T(8,128)(2,1)S(1)}, u32[]{:S(2)}, u32[]{:S(2)}) %collective-permute-start.28) | collective-permute-done | bytes 196640 | tf_op jit(solution)/shard_map/ppermute | solution.py:28
  124.6 0.5 collective-permute-start.36
  125.1 4.7 %collective-permute-done.29.refs_10_ = bf16[256,384]{1,0:T(8,128)(2,1)S(1)} collective-permute-done((bf16[256,384]{1,0:T(8,128)(2,1)}, bf16[256,384]{1,0:T(8,128)(2,1)S(1)}, u32[]{:S(2)}, u32[]{:S(2)}) %collective-permute-start.29) | collective-permute-done | bytes 196640 | tf_op jit(solution)/shard_map/ppermute | solution.py:28
  129.9 0.8 shard_map.149
  130.7 1.2 collective-permute-start.33
  132.1 1.3 collective-permute-start.31
  133.4 2.9 %collective-permute-start.32 = (bf16[128,640]{1,0:T(8,128)(2,1)S(1)}, bf16[128,640]{1,0:T(8,128)(2,1)S(1)}, u32[]{:S(2)}, u32[]{:S(2)}) collective-permute-start(bf16[128,640]{1,0:T(8,128)(2,1)S(1)} %get-tuple-element.95), channel_id=1, source_target_pairs={{0,3},{1,2},{2,1},{3,0},{4,7},{5,6},{6,5},{7,4},{8,11},{9,10},{10,... | collective-permute-start | bytes 491528 | tf_op jit(solution)/shard_map/ppermute | solution.py:28
  136.2 1.4 collective-permute-start.34
  137.7 5.2 %shard_map.151 = bf16[128,2,8,512]{3,2,1,0:T(8,128)(2,1)} custom-call(bf16[256,8,512]{2,1,0:T(8,128)(2,1)S(1)} %copy-done, bf16[32,2,8,512]{3,2,1,0:T(8,128)(2,1)S(1)} %bitcast.64, s32[128]{0:T(128)S(1)} %get-tuple-element.106.refs_2_, s32[128]{0:T(128)S(1)} %get-tuple-element.104.refs_3_, s32[2,128]{1,0:T(2,128)S(1)} %bitcast.69, s32[128]{0:T(128)S(1)} %copy-done.11, ...), custom_call_target="tpu_custom_call" | custom-call | bytes 5242880 | tf_op jit(solution)/shard_map/pallas_call | solution.py:49
  142.9 4.2 %collective-permute-done.31.refs_5_ = bf16[128,640]{1,0:T(8,128)(2,1)S(1)} collective-permute-done((bf16[128,640]{1,0:T(8,128)(2,1)S(1)}, bf16[128,640]{1,0:T(8,128)(2,1)S(1)}, u32[]{:S(2)}, u32[]{:S(2)}) %collective-permute-start.31) | collective-permute-done | bytes 163872 | tf_op jit(solution)/shard_map/ppermute | solution.py:28
  147.1 1.1 shard_map.150
  (100 shorter events, 1.9 us)
Async XLA Ops:
  0.6 17.4 %copy-start.11 = (s32[128]{0:T(128)S(1)}, s32[128]{0:T(128)}, u32[]{:S(2)}) copy-start(s32[128]{0:T(128)} %refs_5_.1) | copy-start | bytes 1540
  0.6 17.4 %copy-start = (bf16[256,8,512]{2,1,0:T(8,128)(2,1)S(1)}, bf16[256,8,512]{2,1,0:T(8,128)(2,1)}, u32[]{:S(2)}) copy-start(bf16[256,8,512]{2,1,0:T(8,128)(2,1)} %refs_0_.3) | copy-start | bytes 6291460
  0.7 17.4 %copy-start.9 = (s32[128,2]{0,1:T(2,128)S(1)}, s32[128,2]{0,1:T(2,128)}, u32[]{:S(2)}) copy-start(s32[128,2]{0,1:T(2,128)} %param.19) | copy-start | bytes 3076
  0.7 7.8 %collective-permute-start.1 = (bf16[512,1024]{1,0:T(8,128)(2,1)}, bf16[512,1024]{1,0:T(8,128)(2,1)S(1)}, u32[]{:S(2)}, u32[]{:S(2)}) collective-permute-start(bf16[512,1024]{1,0:T(8,128)(2,1)} %refs_4_.1), channel_id=1, source_target_pairs={{0,4},{4,0},{8,12},{12,8},{16,20},{20,16},{24,28},{28,24},{1,5},{5... | collective-permute-start | bytes 3145736 | tf_op jit(solution)/shard_map/ppermute | solution.py:28
  4.0 14.0 %copy-start.6 = (s32[32,128]{1,0:T(8,128)S(1)}, s32[32,128]{1,0:T(8,128)}, u32[]{:S(2)}) copy-start(s32[32,128]{1,0:T(8,128)} %get-tuple-element.55.refs_1_) | copy-start | bytes 49156
  4.0 4.4 %collective-permute-start = (bf16[16,5120]{1,0:T(8,128)(2,1)}, bf16[16,5120]{1,0:T(8,128)(2,1)S(1)}, u32[]{:S(2)}, u32[]{:S(2)}) collective-permute-start(bf16[16,5120]{1,0:T(8,128)(2,1)} %get-tuple-element.51), channel_id=1, source_target_pairs={{0,4},{4,0},{8,12},{12,8},{16,20},{20,16},{24,28},{28,24},{1,5},{5... | collective-permute-start | bytes 491528 | tf_op jit(solution)/shard_map/ppermute | solution.py:28
  4.1 13.0 %collective-permute-start.3 = (bf16[128,1024]{1,0:T(8,128)(2,1)}, bf16[128,1024]{1,0:T(8,128)(2,1)}, u32[]{:S(2)}, u32[]{:S(2)}) collective-permute-start(bf16[128,1024]{1,0:T(8,128)(2,1)} %get-tuple-element.57), channel_id=1, source_target_pairs={{0,8},{4,12},{8,0},{12,4},{16,24},{20,28},{24,16},{28,20},{1,9},{5... | collective-permute-start | bytes 786440 | tf_op jit(solution)/shard_map/ppermute | solution.py:28
  6.9 15.2 %collective-permute-start.4 = (bf16[128,1024]{1,0:T(8,128)(2,1)}, bf16[128,1024]{1,0:T(8,128)(2,1)}, u32[]{:S(2)}, u32[]{:S(2)}) collective-permute-start(bf16[128,1024]{1,0:T(8,128)(2,1)} %get-tuple-element.58), channel_id=1, source_target_pairs={{0,16},{4,20},{8,24},{12,28},{16,0},{20,4},{24,8},{28,12},{1,17},{... | collective-permute-start | bytes 786440 | tf_op jit(solution)/shard_map/ppermute | solution.py:28
  8.4 13.7 %collective-permute-start.5 = (bf16[128,1024]{1,0:T(8,128)(2,1)}, bf16[128,1024]{1,0:T(8,128)(2,1)}, u32[]{:S(2)}, u32[]{:S(2)}) collective-permute-start(bf16[128,1024]{1,0:T(8,128)(2,1)} %get-tuple-element.59), channel_id=1, source_target_pairs={{0,24},{4,28},{8,16},{12,20},{16,8},{20,12},{24,0},{28,4},{1,25},{... | collective-permute-start | bytes 786440 | tf_op jit(solution)/shard_map/ppermute | solution.py:28
  8.4 0.7 copy-start.23
  8.4 1.0 copy-start.13
  12.4 9.7 %collective-permute-start.6 = (bf16[32,1024]{1,0:T(8,128)(2,1)}, bf16[32,1024]{1,0:T(8,128)(2,1)S(1)}, u32[]{:S(2)}, u32[]{:S(2)}) collective-permute-start(bf16[32,1024]{1,0:T(8,128)(2,1)} %get-tuple-element.61), channel_id=1, source_target_pairs={{0,8},{4,12},{8,0},{12,4},{16,24},{20,28},{24,16},{28,20},{1,9},{5... | collective-permute-start | bytes 196616 | tf_op jit(solution)/shard_map/ppermute | solution.py:28
  14.4 9.2 %collective-permute-start.7 = (bf16[32,1024]{1,0:T(8,128)(2,1)}, bf16[32,1024]{1,0:T(8,128)(2,1)S(1)}, u32[]{:S(2)}, u32[]{:S(2)}) collective-permute-start(bf16[32,1024]{1,0:T(8,128)(2,1)} %get-tuple-element.62), channel_id=1, source_target_pairs={{0,16},{4,20},{8,24},{12,28},{16,0},{20,4},{24,8},{28,12},{1,17},{... | collective-permute-start | bytes 196616 | tf_op jit(solution)/shard_map/ppermute | solution.py:28
  17.0 6.6 %collective-permute-start.8 = (bf16[32,1024]{1,0:T(8,128)(2,1)}, bf16[32,1024]{1,0:T(8,128)(2,1)S(1)}, u32[]{:S(2)}, u32[]{:S(2)}) collective-permute-start(bf16[32,1024]{1,0:T(8,128)(2,1)} %get-tuple-element.63), channel_id=1, source_target_pairs={{0,24},{4,28},{8,16},{12,20},{16,8},{20,12},{24,0},{28,4},{1,25},{... | collective-permute-start | bytes 196616 | tf_op jit(solution)/shard_map/ppermute | solution.py:28
  18.0 0.7 copy-start.5
  22.1 11.8 %collective-permute-start.2 = (bf16[16,2,8,512]{3,2,1,0:T(8,128)(2,1)}, bf16[16,2,8,512]{3,2,1,0:T(8,128)(2,1)}, u32[]{:S(2)}, u32[]{:S(2)}) collective-permute-start(bf16[16,2,8,512]{3,2,1,0:T(8,128)(2,1)} %slice.58), channel_id=1, source_target_pairs={{0,4},{4,0},{8,12},{12,8},{16,20},{20,16},{24,28},{28,24},{1,5},{5... | collective-permute-start | bytes 786440 | tf_op jit(solution)/shard_map/ppermute | solution.py:28
  22.1 1.6 %copy-start.27 = (bf16[32,1024]{1,0:T(8,128)(2,1)}, bf16[32,1024]{1,0:T(8,128)(2,1)S(1)}, u32[]{:S(2)}) copy-start(bf16[32,1024]{1,0:T(8,128)(2,1)S(1)} %collective-permute-done.6.refs_11_) | copy-start | bytes 196612
  24.3 9.3 %copy-start.26 = (f32[1024,4]{0,1:T(4,128)S(1)}, f32[1024,4]{0,1:T(4,128)}, u32[]{:S(2)}) copy-start(f32[1024,4]{0,1:T(4,128)} %param.16) | copy-start | bytes 49156
  24.3 9.4 %copy-start.10 = (s32[128,2]{0,1:T(2,128)S(1)}, s32[128,2]{0,1:T(2,128)}, u32[]{:S(2)}) copy-start(s32[128,2]{0,1:T(2,128)} %param.22) | copy-start | bytes 3076
  24.3 20.9 %copy-start.8 = (f32[1024]{0:T(1024)S(1)}, f32[1024]{0:T(1024)}, u32[]{:S(2)}) copy-start(f32[1024]{0:T(1024)} %param.17) | copy-start | bytes 12292
  30.0 15.1 %copy-start.1 = (f32[128,1024]{1,0:T(8,128)S(1)}, f32[128,1024]{1,0:T(8,128)}, u32[]{:S(2)}) copy-start(f32[128,1024]{1,0:T(8,128)} %get-tuple-element.64.refs_4_) | copy-start | bytes 1572868
  30.0 9.4 %collective-permute-start.9 = (bf16[128,1024]{1,0:T(8,128)(2,1)}, bf16[128,1024]{1,0:T(8,128)(2,1)S(1)}, u32[]{:S(2)}, u32[]{:S(2)}) collective-permute-start(bf16[128,1024]{1,0:T(8,128)(2,1)} %get-tuple-element.65), channel_id=1, source_target_pairs={{0,8},{4,12},{8,0},{12,4},{16,24},{20,28},{24,16},{28,20},{1,9},{5... | collective-permute-start | bytes 786440 | tf_op jit(solution)/shard_map/ppermute | solution.py:28
  31.3 8.1 %collective-permute-start.10 = (bf16[128,1024]{1,0:T(8,128)(2,1)}, bf16[128,1024]{1,0:T(8,128)(2,1)}, u32[]{:S(2)}, u32[]{:S(2)}) collective-permute-start(bf16[128,1024]{1,0:T(8,128)(2,1)} %get-tuple-element.66), channel_id=1, source_target_pairs={{0,16},{4,20},{8,24},{12,28},{16,0},{20,4},{24,8},{28,12},{1,17},{... | collective-permute-start | bytes 786440 | tf_op jit(solution)/shard_map/ppermute | solution.py:28
  32.1 13.0 %collective-permute-start.11 = (bf16[128,1024]{1,0:T(8,128)(2,1)}, bf16[128,1024]{1,0:T(8,128)(2,1)}, u32[]{:S(2)}, u32[]{:S(2)}) collective-permute-start(bf16[128,1024]{1,0:T(8,128)(2,1)} %get-tuple-element.67), channel_id=1, source_target_pairs={{0,24},{4,28},{8,16},{12,20},{16,8},{20,12},{24,0},{28,4},{1,25},{... | collective-permute-start | bytes 786440 | tf_op jit(solution)/shard_map/ppermute | solution.py:28
  33.8 33.4 %copy-start.4 = (bf16[256,128]{1,0:T(8,128)(2,1)}, bf16[256,128]{1,0:T(8,128)(2,1)S(1)}, u32[]{:S(2)}) copy-start(bf16[256,128]{1,0:T(8,128)(2,1)S(1)} %get-tuple-element.54.refs_2_.refs_1_) | copy-start | bytes 196612
  47.5 19.1 %collective-permute-start.16 = (bf16[320,512]{1,0:T(8,128)(2,1)}, bf16[320,512]{1,0:T(8,128)(2,1)}, u32[]{:S(2)}, u32[]{:S(2)}) collective-permute-start(bf16[320,512]{1,0:T(8,128)(2,1)} %get-tuple-element.71), channel_id=1, source_target_pairs={{0,8},{4,12},{8,0},{12,4},{16,24},{20,28},{24,16},{28,20},{1,9},{5... | collective-permute-start | bytes 983048 | tf_op jit(solution)/shard_map/ppermute | solution.py:28
  48.3 9.8 %collective-permute-start.14 = (bf16[144,640]{1,0:T(8,128)(2,1)}, bf16[144,640]{1,0:T(8,128)(2,1)S(1)}, u32[]{:S(2)}, u32[]{:S(2)}) collective-permute-start(bf16[144,640]{1,0:T(8,128)(2,1)} %get-tuple-element.68.refs_2_), channel_id=1, source_target_pairs={{0,3},{1,2},{2,1},{3,0},{4,7},{5,6},{6,5},{7,4},{8,11},{9,10},{10,... | collective-permute-start | bytes 552968 | tf_op jit(solution)/shard_map/ppermute | solution.py:28
  51.9 14.6 %collective-permute-start.13 = (bf16[144,640]{1,0:T(8,128)(2,1)}, bf16[144,640]{1,0:T(8,128)(2,1)S(1)}, u32[]{:S(2)}, u32[]{:S(2)}) collective-permute-start(bf16[144,640]{1,0:T(8,128)(2,1)} %get-tuple-element.68.refs_2_), channel_id=1, source_target_pairs={{0,2},{1,3},{2,0},{3,1},{4,6},{5,7},{6,4},{7,5},{8,10},{9,11},{10,... | collective-permute-start | bytes 552968 | tf_op jit(solution)/shard_map/ppermute | solution.py:28
  51.9 14.6 %collective-permute-start.12 = (bf16[144,640]{1,0:T(8,128)(2,1)}, bf16[144,640]{1,0:T(8,128)(2,1)S(1)}, u32[]{:S(2)}, u32[]{:S(2)}) collective-permute-start(bf16[144,640]{1,0:T(8,128)(2,1)} %get-tuple-element.68.refs_2_), channel_id=1, source_target_pairs={{0,1},{1,0},{2,3},{3,2},{4,5},{5,4},{6,7},{7,6},{8,9},{9,8},{10,11... | collective-permute-start | bytes 552968 | tf_op jit(solution)/shard_map/ppermute | solution.py:28
  52.7 1.4 collective-permute-start.15
  54.2 13.1 %copy-start.24 = (bf16[64,384]{1,0:T(8,128)(2,1)}, bf16[64,384]{1,0:T(8,128)(2,1)S(1)}, u32[]{:S(2)}) copy-start(bf16[64,384]{1,0:T(8,128)(2,1)S(1)} %collective-permute-done.15.refs_7_) | copy-start | bytes 147460
  54.2 3.9 %collective-permute-start.17 = (bf16[64,384]{1,0:T(8,128)(2,1)}, bf16[64,384]{1,0:T(8,128)(2,1)S(1)}, u32[]{:S(2)}, u32[]{:S(2)}) collective-permute-start(bf16[64,384]{1,0:T(8,128)(2,1)} %get-tuple-element.72), channel_id=1, source_target_pairs={{0,12},{4,8},{8,4},{12,0},{16,28},{20,24},{24,20},{28,16},{1,13},{... | collective-permute-start | bytes 147464 | tf_op jit(solution)/shard_map/ppermute | solution.py:28
  58.1 9.2 %copy-start.25 = (bf16[64,384]{1,0:T(8,128)(2,1)}, bf16[64,384]{1,0:T(8,128)(2,1)S(1)}, u32[]{:S(2)}) copy-start(bf16[64,384]{1,0:T(8,128)(2,1)S(1)} %collective-permute-done.17.refs_9_) | copy-start | bytes 147460
  58.1 9.2 %copy-start.20 = (bf16[144,640]{1,0:T(8,128)(2,1)}, bf16[144,640]{1,0:T(8,128)(2,1)S(1)}, u32[]{:S(2)}) copy-start(bf16[144,640]{1,0:T(8,128)(2,1)S(1)} %collective-permute-done.14.refs_5_) | copy-start | bytes 552964
  66.5 0.7 copy-start.22
  69.8 20.9 %copy-start.7 = (f32[16,128]{1,0:T(8,128)}, f32[16,128]{1,0:T(8,128)S(1)}, u32[]{:S(2)}) copy-start(f32[16,128]{1,0:T(8,128)S(1)} %get-tuple-element.78.refs_12_) | copy-start | bytes 24580
  69.8 8.9 %collective-permute-start.23 = (bf16[256,384]{1,0:T(8,128)(2,1)}, bf16[256,384]{1,0:T(8,128)(2,1)S(1)}, u32[]{:S(2)}, u32[]{:S(2)}) collective-permute-start(bf16[256,384]{1,0:T(8,128)(2,1)} %get-tuple-element.77.refs_5_), channel_id=1, source_target_pairs={{0,3},{1,2},{2,1},{3,0},{4,7},{5,6},{6,5},{7,4},{8,11},{9,10},{10,... | collective-permute-start | bytes 589832 | tf_op jit(solution)/shard_map/ppermute | solution.py:28
  72.3 17.4 %collective-permute-start.18 = (bf16[64,2688]{1,0:T(8,128)(2,1)S(1)}, bf16[64,2688]{1,0:T(8,128)(2,1)S(1)}, u32[]{:S(2)}, u32[]{:S(2)}) collective-permute-start(bf16[64,2688]{1,0:T(8,128)(2,1)S(1)} %get-tuple-element.74), channel_id=1, source_target_pairs={{0,4},{4,0},{8,12},{12,8},{16,20},{20,16},{24,28},{28,24},{1,5},{5... | collective-permute-start | bytes 1032200 | tf_op jit(solution)/shard_map/ppermute | solution.py:28
  72.3 17.4 %collective-permute-start.19 = (bf16[64,2688]{1,0:T(8,128)(2,1)S(1)}, bf16[64,2688]{1,0:T(8,128)(2,1)S(1)}, u32[]{:S(2)}, u32[]{:S(2)}) collective-permute-start(bf16[64,2688]{1,0:T(8,128)(2,1)S(1)} %get-tuple-element.75), channel_id=1, source_target_pairs={{0,8},{4,12},{8,0},{12,4},{16,24},{20,28},{24,16},{28,20},{1,9},{5... | collective-permute-start | bytes 1032200 | tf_op jit(solution)/shard_map/ppermute | solution.py:28
  73.8 16.0 %collective-permute-start.20 = (bf16[64,2688]{1,0:T(8,128)(2,1)S(1)}, bf16[64,2688]{1,0:T(8,128)(2,1)S(1)}, u32[]{:S(2)}, u32[]{:S(2)}) collective-permute-start(bf16[64,2688]{1,0:T(8,128)(2,1)S(1)} %get-tuple-element.76), channel_id=1, source_target_pairs={{0,12},{4,8},{8,4},{12,0},{16,28},{20,24},{24,20},{28,16},{1,13},{... | collective-permute-start | bytes 1032200 | tf_op jit(solution)/shard_map/ppermute | solution.py:28
  74.2 13.7 %collective-permute-start.22 = (bf16[256,384]{1,0:T(8,128)(2,1)}, bf16[256,384]{1,0:T(8,128)(2,1)S(1)}, u32[]{:S(2)}, u32[]{:S(2)}) collective-permute-start(bf16[256,384]{1,0:T(8,128)(2,1)} %get-tuple-element.77.refs_5_), channel_id=1, source_target_pairs={{0,2},{1,3},{2,0},{3,1},{4,6},{5,7},{6,4},{7,5},{8,10},{9,11},{10,... | collective-permute-start | bytes 589832 | tf_op jit(solution)/shard_map/ppermute | solution.py:28
  78.7 12.0 %copy-start.17 = (bf16[256,384]{1,0:T(8,128)(2,1)}, bf16[256,384]{1,0:T(8,128)(2,1)S(1)}, u32[]{:S(2)}) copy-start(bf16[256,384]{1,0:T(8,128)(2,1)S(1)} %collective-permute-done.23.refs_8_) | copy-start | bytes 589828
  78.7 11.0 %collective-permute-start.21 = (bf16[256,384]{1,0:T(8,128)(2,1)}, bf16[256,384]{1,0:T(8,128)(2,1)S(1)}, u32[]{:S(2)}, u32[]{:S(2)}) collective-permute-start(bf16[256,384]{1,0:T(8,128)(2,1)} %get-tuple-element.77.refs_5_), channel_id=1, source_target_pairs={{0,1},{1,0},{2,3},{3,2},{4,5},{5,4},{6,7},{7,6},{8,9},{9,8},{10,11... | collective-permute-start | bytes 589832 | tf_op jit(solution)/shard_map/ppermute | solution.py:28
  87.9 1.9 %copy-start.18 = (bf16[256,384]{1,0:T(8,128)(2,1)}, bf16[256,384]{1,0:T(8,128)(2,1)S(1)}, u32[]{:S(2)}) copy-start(bf16[256,384]{1,0:T(8,128)(2,1)S(1)} %collective-permute-done.22.refs_7_) | copy-start | bytes 589828
  89.7 0.7 copy-start.19
  89.7 0.8 copy-start.14
  89.7 0.9 copy-start.15
  89.8 0.9 copy-start.16
  90.8 31.2 %copy-start.12 = (bf16[2,2,8,2,8,512]{5,4,3,2,1,0:T(8,128)(2,1)S(1)}, bf16[2,2,8,2,8,512]{5,4,3,2,1,0:T(8,128)(2,1)}, u32[]{:S(2)}) copy-start(bf16[2,2,8,2,8,512]{5,4,3,2,1,0:T(8,128)(2,1)} %fusion.4.refs_13_) | copy-start | bytes 1572868
  110.4 9.9 %collective-permute-start.24 = (bf16[256,384]{1,0:T(8,128)(2,1)}, bf16[256,384]{1,0:T(8,128)(2,1)S(1)}, u32[]{:S(2)}, u32[]{:S(2)}) collective-permute-start(bf16[256,384]{1,0:T(8,128)(2,1)} %get-tuple-element.83), channel_id=1, source_target_pairs={{0,3},{1,2},{2,1},{3,0},{4,7},{5,6},{6,5},{7,4},{8,11},{9,10},{10,... | collective-permute-start | bytes 589832 | tf_op jit(solution)/shard_map/ppermute | solution.py:28
  111.6 13.0 %collective-permute-start.28 = (bf16[256,384]{1,0:T(8,128)(2,1)}, bf16[256,384]{1,0:T(8,128)(2,1)S(1)}, u32[]{:S(2)}, u32[]{:S(2)}) collective-permute-start(bf16[256,384]{1,0:T(8,128)(2,1)} %get-tuple-element.87), channel_id=1, source_target_pairs={{0,1},{1,0},{2,3},{3,2},{4,5},{5,4},{6,7},{7,6},{8,9},{9,8},{10,11... | collective-permute-start | bytes 589832 | tf_op jit(solution)/shard_map/ppermute | solution.py:28
  111.9 17.9 %collective-permute-start.29 = (bf16[256,384]{1,0:T(8,128)(2,1)}, bf16[256,384]{1,0:T(8,128)(2,1)S(1)}, u32[]{:S(2)}, u32[]{:S(2)}) collective-permute-start(bf16[256,384]{1,0:T(8,128)(2,1)} %get-tuple-element.88), channel_id=1, source_target_pairs={{0,2},{1,3},{2,0},{3,1},{4,6},{5,7},{6,4},{7,5},{8,10},{9,11},{10,... | collective-permute-start | bytes 589832 | tf_op jit(solution)/shard_map/ppermute | solution.py:28
  114.8 14.9 %collective-permute-start.26 = (bf16[64,2560]{1,0:T(8,128)(2,1)}, bf16[64,2560]{1,0:T(8,128)(2,1)S(1)}, u32[]{:S(2)}, u32[]{:S(2)}) collective-permute-start(bf16[64,2560]{1,0:T(8,128)(2,1)} %get-tuple-element.84), channel_id=1, source_target_pairs={{0,8},{4,12},{8,0},{12,4},{16,24},{20,28},{24,16},{28,20},{1,9},{5... | collective-permute-start | bytes 983048 | tf_op jit(solution)/shard_map/ppermute | solution.py:28
  116.2 13.6 %collective-permute-start.27 = (bf16[64,2560]{1,0:T(8,128)(2,1)}, bf16[64,2560]{1,0:T(8,128)(2,1)S(1)}, u32[]{:S(2)}, u32[]{:S(2)}) collective-permute-start(bf16[64,2560]{1,0:T(8,128)(2,1)} %get-tuple-element.85), channel_id=1, source_target_pairs={{0,12},{4,8},{8,4},{12,0},{16,28},{20,24},{24,20},{28,16},{1,13},{... | collective-permute-start | bytes 983048 | tf_op jit(solution)/shard_map/ppermute | solution.py:28
  120.3 1.0 copy-start.3
  122.0 7.9 %collective-permute-start.25 = (bf16[64,2560]{1,0:T(8,128)(2,1)}, bf16[64,2560]{1,0:T(8,128)(2,1)S(1)}, u32[]{:S(2)}, u32[]{:S(2)}) collective-permute-start(bf16[64,2560]{1,0:T(8,128)(2,1)} %shard_map.148), channel_id=1, source_target_pairs={{0,4},{4,0},{8,12},{12,8},{16,20},{20,16},{24,28},{28,24},{1,5},{5... | collective-permute-start | bytes 983048 | tf_op jit(solution)/shard_map/ppermute | solution.py:28
  124.6 11.6 %collective-permute-start.36 = (bf16[1,2,8,2,8,512]{5,4,3,2,1,0:T(8,128)(2,1)S(1)}, bf16[1,2,8,2,8,512]{5,4,3,2,1,0:T(8,128)(2,1)S(1)}, u32[]{:S(2)}, u32[]{:S(2)}) collective-permute-start(bf16[1,2,8,2,8,512]{5,4,3,2,1,0:T(8,128)(2,1)S(1)} %get-tuple-element.103), channel_id=1, source_target_pairs={{0,16},{4,20},{8,24},{12,28},{16,0},{20,4},{24,8},{28,12},{1,17},{... | collective-permute-start | bytes 786440 | tf_op jit(solution)/shard_map/ppermute | solution.py:28
  130.7 6.9 %collective-permute-start.33 = (bf16[64,384]{1,0:T(8,128)(2,1)S(1)}, bf16[64,384]{1,0:T(8,128)(2,1)S(1)}, u32[]{:S(2)}, u32[]{:S(2)}) collective-permute-start(bf16[64,384]{1,0:T(8,128)(2,1)S(1)} %get-tuple-element.97), channel_id=1, source_target_pairs={{0,4},{4,0},{8,12},{12,8},{16,20},{20,16},{24,28},{28,24},{1,5},{5... | collective-permute-start | bytes 147464 | tf_op jit(solution)/shard_map/ppermute | solution.py:28
  131.8 11.1 %collective-permute-start.30 = (bf16[128,640]{1,0:T(8,128)(2,1)S(1)}, bf16[128,640]{1,0:T(8,128)(2,1)S(1)}, u32[]{:S(2)}, u32[]{:S(2)}) collective-permute-start(bf16[128,640]{1,0:T(8,128)(2,1)S(1)} %get-tuple-element.93), channel_id=1, source_target_pairs={{0,1},{1,0},{2,3},{3,2},{4,5},{5,4},{6,7},{7,6},{8,9},{9,8},{10,11... | collective-permute-start | bytes 491528 | tf_op jit(solution)/shard_map/ppermute | solution.py:28
  132.1 15.0 %collective-permute-start.31 = (bf16[128,640]{1,0:T(8,128)(2,1)S(1)}, bf16[128,640]{1,0:T(8,128)(2,1)S(1)}, u32[]{:S(2)}, u32[]{:S(2)}) collective-permute-start(bf16[128,640]{1,0:T(8,128)(2,1)S(1)} %get-tuple-element.94), channel_id=1, source_target_pairs={{0,2},{1,3},{2,0},{3,1},{4,6},{5,7},{6,4},{7,5},{8,10},{9,11},{10,... | collective-permute-start | bytes 491528 | tf_op jit(solution)/shard_map/ppermute | solution.py:28
  133.4 13.7 %collective-permute-start.32 = (bf16[128,640]{1,0:T(8,128)(2,1)S(1)}, bf16[128,640]{1,0:T(8,128)(2,1)S(1)}, u32[]{:S(2)}, u32[]{:S(2)}) collective-permute-start(bf16[128,640]{1,0:T(8,128)(2,1)S(1)} %get-tuple-element.95), channel_id=1, source_target_pairs={{0,3},{1,2},{2,1},{3,0},{4,7},{5,6},{6,5},{7,4},{8,11},{9,10},{10,... | collective-permute-start | bytes 491528 | tf_op jit(solution)/shard_map/ppermute | solution.py:28
  136.2 6.7 %collective-permute-start.34 = (bf16[64,384]{1,0:T(8,128)(2,1)S(1)}, bf16[64,384]{1,0:T(8,128)(2,1)S(1)}, u32[]{:S(2)}, u32[]{:S(2)}) collective-permute-start(bf16[64,384]{1,0:T(8,128)(2,1)S(1)} %get-tuple-element.98), channel_id=1, source_target_pairs={{0,8},{4,12},{8,0},{12,4},{16,24},{20,28},{24,16},{28,20},{1,9},{5... | collective-permute-start | bytes 147464 | tf_op jit(solution)/shard_map/ppermute | solution.py:28
  137.6 5.3 %collective-permute-start.35 = (bf16[64,384]{1,0:T(8,128)(2,1)S(1)}, bf16[64,384]{1,0:T(8,128)(2,1)S(1)}, u32[]{:S(2)}, u32[]{:S(2)}) collective-permute-start(bf16[64,384]{1,0:T(8,128)(2,1)S(1)} %get-tuple-element.99), channel_id=1, source_target_pairs={{0,12},{4,8},{8,4},{12,0},{16,28},{20,24},{24,20},{28,16},{1,13},{... | collective-permute-start | bytes 147464 | tf_op jit(solution)/shard_map/ppermute | solution.py:28
  137.7 9.4 %copy-start.2 = (f32[128,1024]{1,0:T(8,128)S(1)}, f32[128,1024]{1,0:T(8,128)}, u32[]{:S(2)}) copy-start(f32[128,1024]{1,0:T(8,128)} %get-tuple-element.91.refs_2_) | copy-start | bytes 1572868
  (3 other events, 1.9 us)

commit v7 on v6

--- a/solution.py
+++ b/solution.py
@@ -172,31 +172,29 @@
 
 
 def project_kernel(half, *refs):
-    odd, selector_far, resid_selector, residual, own, other = refs[:6]
+    odd, selector_far, resid_selector_far, residual_far, own, other = refs[:6]
     blocks = refs[6 : 6 + 2 * half]
     outs = refs[6 + 2 * half : 6 + 3 * half]
-    buf, weights, selector, sems = refs[6 + 3 * half :]
+    buf, weights, selector, resid_selector, residual, sems = refs[6 + 3 * half :]
     rows = residual.shape[0]
+    pairs = [(selector_far, selector), (resid_selector_far, resid_selector), (residual_far, residual)]
+    at = 0
+    for block in blocks:
+        pairs.append((block, buf.at[pl.ds(at, block.shape[0])]))
+        at += block.shape[0]
+    pairs += [(own, weights.at[odd[0]]), (other, weights.at[1 - odd[0]])]
     copies = [
-        pltpu.make_async_copy(blocks[s], buf.at[pl.ds(s * rows, rows)], sems.at[s])
-        for s in range(half)
+        pltpu.make_async_copy(source, target, sems.at[c])
+        for c, (source, target) in enumerate(pairs)
     ]
-    copies.append(pltpu.make_async_copy(selector_far, selector, sems.at[half + 2]))
-    fetches = [
-        pltpu.make_async_copy(own, weights.at[odd[0]], sems.at[half]),
-        pltpu.make_async_copy(other, weights.at[1 - odd[0]], sems.at[half + 1]),
-    ]
-    for copy in copies + fetches:
+    for copy in copies:
         copy.start()
-    at = half * rows
-    for block in blocks[half:]:
-        buf[at : at + block.shape[0]] = block[...]
-        at += block.shape[0]
-    resid = pick(resid_selector[:, :rows], residual[...])
-    resid = resid + pick(resid_selector[:, rows:], buf[half * rows :])
+    copies, fetches = copies[:-2], copies[-2:]
     for copy in copies:
         copy.wait()
     picked = pick(selector[...], buf[...]).astype(BF)
+    resid = pick(resid_selector[:, :rows], residual[...])
+    resid = resid + pick(resid_selector[:, rows:], buf[half * rows :])
     for copy in fetches:
         copy.wait()
     depth = own.shape[0]
@@ -488,7 +486,7 @@
         functools.partial(movers_kernel, half),
         [SMEM] + [VMEM] * 3,
         (me.reshape(1).astype(I32), came_from.reshape(n, rows), attention_out, residual),
-        [far((rows, kblock), BF)] * half
+        [far((rows, kblock), BF)] + [near((rows, kblock), BF)] * (half - 1)
         + [
             far((n_pair, D + feats), BF),
             far((2 * n_pair, feats), BF),
@@ -545,7 +543,7 @@
     resid_selector = hot(own_at, rows + half * n_hand)
     parts = local_call(
         functools.partial(project_kernel, half),
-        [SMEM, HBM] + [VMEM] * 2 + [HBM] * (2 + half) + [VMEM] * half,
+        [SMEM] + [HBM] * (5 + 2 * half),
         (
             k.reshape(1).astype(I32),
             selector,
@@ -556,12 +554,14 @@
             *attn_blocks,
             *late_blocks,
         ),
-        [shape((rows, feats), F32)] + [shape((rows, feats), BF)] * (half - 1),
+        [near((rows, feats), F32)] + [near((rows, feats), BF)] * (half - 1),
         [
             pltpu.VMEM((total_rows, kblock), BF),
             pltpu.VMEM((2,) + w_out.shape, BF),
             pltpu.VMEM(selector.shape, BF),
-            pltpu.SemaphoreType.DMA((half + 3,)),
+            pltpu.VMEM(resid_selector.shape, BF),
+            pltpu.VMEM(residual.shape, BF),
+            pltpu.SemaphoreType.DMA((2 * half + 5,)),
         ],
         vmem=58,
         flops=2 * half * rows * (total_rows + feats) * kblock,

time: 149 us -> 147 us (0.987)
    unnamed x60 -> x58, local copies, waits for them, and re-layouts: 5.04 us -> 4.67 us
where the time goes in v7:
time: 147 us
  waiting for transfers between devices  48.3 us (33%)
  Pallas kernels  42.8 us (29%)
  starting transfers between devices  42.6 us (29%)
  local copies, waits for them, and re-layouts  7.33 us (5%)
  other arithmetic  4.9 us (3%)
    ppermute x37, waiting for transfers between devices, swap(): return lax.ppermute(x, axis, [(i, i ^ s) for i in range(n)])  48.3 us
    pallas_call x12, Pallas kernels, local_call(): pl.pallas_call(run, out_shape=outs, in_specs=list(in_specs) + [pl.BlockSp...  42.8 us
    ppermute x37, starting transfers between devices, swap(): return lax.ppermute(x, axis, [(i, i ^ s) for i in range(n)])  42.6 us
    unnamed x58, local copies, waits for them, and re-layouts  4.67 us
  transfers between devices with their start and end apart: 37, of which 15 were waited for; matrix products, arithmetic and copies ran while one was open for 5% of the time, Pallas kernels for 12%

profile of v7, /device:TPU:0, one launch (start us, length us, event | category | flops | bytes accessed | tf_op | source)
XLA Modules:
  0.0 146.8 jit_solution(14254337166522995833)
XLA Ops:
  0.7 0.5 collective-permute-start.1
  1.2 2.6 %shard_map.140 = (bf16[128,1024]{1,0:T(8,128)(2,1)}, bf16[128,1024]{1,0:T(8,128)(2,1)S(1)}, bf16[128,1024]{1,0:T(8,128)(2,1)S(1)}, bf16[128,1024]{1,0:T(8,128)(2...) custom-call(s32[1]{0:T(128)} %bitcast.4.refs_0_, s32[8,128]{1,0:T(8,128)} %bitcast.77, ...), custom_call_target="tpu_custom_call" | custom-call | bytes 2097152 | tf_op jit(solution)/shard_map/pallas_call | solution.py:49
  3.8 2.8 %collective-permute-start.3 = (bf16[128,1024]{1,0:T(8,128)(2,1)S(1)}, bf16[128,1024]{1,0:T(8,128)(2,1)S(1)}, u32[]{:S(2)}, u32[]{:S(2)}) collective-permute-start(bf16[128,1024]{1,0:T(8,128)(2,1)S(1)} %get-tuple-element.57), channel_id=1, source_target_pairs={{0,8},{4,12},{8,0},{12,4},{16,24},{20,28},{24,16},{28,20},{1,9},{5... | collective-permute-start | bytes 786440 | tf_op jit(solution)/shard_map/ppermute | solution.py:28
  6.6 1.5 %collective-permute-start.4 = (bf16[128,1024]{1,0:T(8,128)(2,1)S(1)}, bf16[128,1024]{1,0:T(8,128)(2,1)}, u32[]{:S(2)}, u32[]{:S(2)}) collective-permute-start(bf16[128,1024]{1,0:T(8,128)(2,1)S(1)} %get-tuple-element.58), channel_id=1, source_target_pairs={{0,16},{4,20},{8,24},{12,28},{16,0},{20,4},{24,8},{28,12},{1,17},{... | collective-permute-start | bytes 786440 | tf_op jit(solution)/shard_map/ppermute | solution.py:28
  8.2 0.7 copy-done.21
  8.8 1.7 %shard_map.141 = (bf16[32,1024]{1,0:T(8,128)(2,1)}, bf16[32,1024]{1,0:T(8,128)(2,1)}, bf16[32,1024]{1,0:T(8,128)(2,1)}, bf16[32,1024]{1,0:T(8,128)(2,1)}, s32[8,128]{1,0:T(8,128)}) custom-call(s32[1]{0:T(128)} %bitcast.3.refs_0_, bf16[16,5120]{1,0:T(8,128)(2,1)} %copy-done.21, bf16[32,1024]{1,0:T(8,128)(2,1)} %get-tuple-element.52.refs_2_, ...), custom_call_target="tpu_custom_call" | custom-call | bytes 1048576 | tf_op jit(solution)/shard_map/pallas_call | solution.py:49
  10.5 0.9 dynamic-slice_bitcast_fusion.3
  11.4 0.3 convert_reduce_fusion
  11.8 2.0 %collective-permute-start.6 = (bf16[32,1024]{1,0:T(8,128)(2,1)}, bf16[32,1024]{1,0:T(8,128)(2,1)S(1)}, u32[]{:S(2)}, u32[]{:S(2)}) collective-permute-start(bf16[32,1024]{1,0:T(8,128)(2,1)} %get-tuple-element.61), channel_id=1, source_target_pairs={{0,8},{4,12},{8,0},{12,4},{16,24},{20,28},{24,16},{28,20},{1,9},{5... | collective-permute-start | bytes 196616 | tf_op jit(solution)/shard_map/ppermute | solution.py:28
  13.8 1.5 %collective-permute-start.7 = (bf16[32,1024]{1,0:T(8,128)(2,1)}, bf16[32,1024]{1,0:T(8,128)(2,1)S(1)}, u32[]{:S(2)}, u32[]{:S(2)}) collective-permute-start(bf16[32,1024]{1,0:T(8,128)(2,1)} %get-tuple-element.62), channel_id=1, source_target_pairs={{0,16},{4,20},{8,24},{12,28},{16,0},{20,4},{24,8},{28,12},{1,17},{... | collective-permute-start | bytes 196616 | tf_op jit(solution)/shard_map/ppermute | solution.py:28
  15.3 1.0 fusion.refs_1_
  16.4 0.4 collective-permute-start.8
  16.7 0.7 fusion.6.refs_2_
  17.5 0.7 copy-done.4
  18.1 1.2 shard_map.143
  19.4 0.7 slice.58
  20.1 1.4 collective-permute-done.4.refs_8_
  21.5 1.6 %collective-permute-done.7.refs_12_ = bf16[32,1024]{1,0:T(8,128)(2,1)S(1)} collective-permute-done((bf16[32,1024]{1,0:T(8,128)(2,1)}, bf16[32,1024]{1,0:T(8,128)(2,1)S(1)}, u32[]{:S(2)}, u32[]{:S(2)}) %collective-permute-start.7) | collective-permute-done | bytes 65568 | tf_op jit(solution)/shard_map/ppermute | solution.py:28
  23.2 0.6 copy-done.27
  23.8 4.8 %shard_map.144 = (f32[128,1024]{1,0:T(8,128)S(1)}, bf16[128,1024]{1,0:T(8,128)(2,1)}, bf16[128,1024]{1,0:T(8,128)(2,1)}, bf16[128,1024]{1,0:T(8,128)(2,1)}) custom-call(s32[1]{0:T(128)} %bitcast.12.refs_0_, bf16[512,640]{1,0:T(8,128)(2,1)} %fusion.refs_1_, bf16[128,256]{1,0:T(8,128)(2,1)} %fusion.6.refs_2_, bf16[128,1024]{1,0:T(8,128)(2,1)} %refs_3_.5, ...), custom_call_target="tpu_custom_call" | custom-call | flops 1744830464 | bytes 6291456 | tf_op jit(solution)/shard_map/pallas_call | solution.py:49
  28.6 1.3 collective-permute-start.9
  29.9 0.8 collective-permute-start.10
  30.7 1.4 collective-permute-start.11
  32.4 0.9 fusion.5
  33.4 4.6 %collective-permute-done.9.refs_5_ = bf16[128,1024]{1,0:T(8,128)(2,1)S(1)} collective-permute-done((bf16[128,1024]{1,0:T(8,128)(2,1)}, bf16[128,1024]{1,0:T(8,128)(2,1)S(1)}, u32[]{:S(2)}, u32[]{:S(2)}) %collective-permute-start.9) | collective-permute-done | bytes 262176 | tf_op jit(solution)/shard_map/ppermute | solution.py:28
  38.0 5.7 %collective-permute-done.11.refs_7_ = bf16[128,1024]{1,0:T(8,128)(2,1)} collective-permute-done((bf16[128,1024]{1,0:T(8,128)(2,1)}, bf16[128,1024]{1,0:T(8,128)(2,1)}, u32[]{:S(2)}, u32[]{:S(2)}) %collective-permute-start.11) | collective-permute-done | bytes 262176 | tf_op jit(solution)/shard_map/ppermute | solution.py:28
  43.7 2.3 %shard_map.145 = (f32[128,1024]{1,0:T(8,128)}, bf16[144,640]{1,0:T(8,128)(2,1)}, bf16[64,384]{1,0:T(8,128)(2,1)}, bf16[64,384]{1,0:T(8,128)(2,1)}, bf16[320,512]{1,0:T(8,128)(2,1)}, /*index=5*/bf16[64,384]{1,0:T(8,128)(2,1)}) custom-call(f32[1,1024]{1,0:T(1,128)S(1)} %bitcast.67, f32[8,1024]{1,0:T(8,128)S(1)} %pad.4.refs_1_, ...), custom_call_target="tpu_custom_call" | custom-call | flops 25165824 | bytes 3145728 | tf_op jit(solution)/shard_map/pallas_call | solution.py:49
  46.0 0.9 collective-permute-start.16
  46.9 3.6 %collective-permute-start.14 = (bf16[144,640]{1,0:T(8,128)(2,1)}, bf16[144,640]{1,0:T(8,128)(2,1)S(1)}, u32[]{:S(2)}, u32[]{:S(2)}) collective-permute-start(bf16[144,640]{1,0:T(8,128)(2,1)} %get-tuple-element.68.refs_2_), channel_id=1, source_target_pairs={{0,3},{1,2},{2,1},{3,0},{4,7},{5,6},{6,5},{7,4},{8,11},{9,10},{10,... | collective-permute-start | bytes 552968 | tf_op jit(solution)/shard_map/ppermute | solution.py:28
  50.5 0.8 collective-permute-start.12
  51.3 1.4 collective-permute-done.15.refs_7_
  52.7 0.9 collective-permute-start.17
  53.6 3.0 %collective-permute-done.17.refs_9_ = bf16[64,384]{1,0:T(8,128)(2,1)S(1)} collective-permute-done((bf16[64,384]{1,0:T(8,128)(2,1)}, bf16[64,384]{1,0:T(8,128)(2,1)S(1)}, u32[]{:S(2)}, u32[]{:S(2)}) %collective-permute-start.17) | collective-permute-done | bytes 49184 | tf_op jit(solution)/shard_map/ppermute | solution.py:28
  56.6 8.4 %collective-permute-done.13.refs_4_ = bf16[144,640]{1,0:T(8,128)(2,1)S(1)} collective-permute-done((bf16[144,640]{1,0:T(8,128)(2,1)}, bf16[144,640]{1,0:T(8,128)(2,1)S(1)}, u32[]{:S(2)}, u32[]{:S(2)}) %collective-permute-start.13) | collective-permute-done | bytes 184352 | tf_op jit(solution)/shard_map/ppermute | solution.py:28
  65.1 0.7 copy-done.19
  65.8 2.6 %shard_map.146 = (bf16[64,2688]{1,0:T(8,128)(2,1)}, bf16[64,2688]{1,0:T(8,128)(2,1)S(1)}, bf16[64,2688]{1,0:T(8,128)(2,1)S(1)}, bf16[64,2688]{1,0:T(8,128)(2,1)S...) custom-call(s32[1]{0:T(128)} %bitcast.refs_0_, bf16[256,128]{1,0:T(8,128)(2,1)} %copy-done.3, ...), custom_call_target="tpu_custom_call" | custom-call | flops 167772160 | bytes 3145728 | tf_op jit(solution)/shard_map/pallas_call | solution.py:49
  68.4 2.5 %collective-permute-start.23 = (bf16[256,384]{1,0:T(8,128)(2,1)}, bf16[256,384]{1,0:T(8,128)(2,1)S(1)}, u32[]{:S(2)}, u32[]{:S(2)}) collective-permute-start(bf16[256,384]{1,0:T(8,128)(2,1)} %get-tuple-element.77.refs_5_), channel_id=1, source_target_pairs={{0,3},{1,2},{2,1},{3,0},{4,7},{5,6},{6,5},{7,4},{8,11},{9,10},{10,... | collective-permute-start | bytes 589832 | tf_op jit(solution)/shard_map/ppermute | solution.py:28
  70.9 1.4 collective-permute-start.19
  72.3 0.5 collective-permute-start.20
  72.7 4.5 %collective-permute-done.23.refs_8_ = bf16[256,384]{1,0:T(8,128)(2,1)S(1)} collective-permute-done((bf16[256,384]{1,0:T(8,128)(2,1)}, bf16[256,384]{1,0:T(8,128)(2,1)S(1)}, u32[]{:S(2)}, u32[]{:S(2)}) %collective-permute-start.23) | collective-permute-done | bytes 196640 | tf_op jit(solution)/shard_map/ppermute | solution.py:28
  77.3 6.5 %collective-permute-start.21 = (bf16[256,384]{1,0:T(8,128)(2,1)}, bf16[256,384]{1,0:T(8,128)(2,1)S(1)}, u32[]{:S(2)}, u32[]{:S(2)}) collective-permute-start(bf16[256,384]{1,0:T(8,128)(2,1)} %get-tuple-element.77.refs_5_), channel_id=1, source_target_pairs={{0,1},{1,0},{2,3},{3,2},{4,5},{5,4},{6,7},{7,6},{8,9},{9,8},{10,11... | collective-permute-start | bytes 589832 | tf_op jit(solution)/shard_map/ppermute | solution.py:28
  83.7 1.0 slice.61
  84.7 1.8 %fusion.4.refs_13_ = bf16[2,2,8,2,8,512]{5,4,3,2,1,0:T(8,128)(2,1)} fusion(bf16[2,2,4,2,8,512]{5,4,3,2,1,0:T(8,128)(2,1)S(1)} %bitcast.74, bf16[2,2,4,2,8,512]{5,4,3,2,1,0:T(8,128)(2,1)} %bitcast.10, bf16[2,1,8,2,8,512]{5,4,3,2,1,0:T(8,128)(2,1)S(1)} %bitcast.75), kind=kLoop, calls=%fused_computation.8 | loop fusion | flops 2359296 | bytes 1310720 | tf_op jit(solution)/shard_map/stack | solution.py:606
  86.5 1.8 %collective-permute-done.21.refs_6_ = bf16[256,384]{1,0:T(8,128)(2,1)S(1)} collective-permute-done((bf16[256,384]{1,0:T(8,128)(2,1)}, bf16[256,384]{1,0:T(8,128)(2,1)S(1)}, u32[]{:S(2)}, u32[]{:S(2)}) %collective-permute-start.21) | collective-permute-done | bytes 196640 | tf_op jit(solution)/shard_map/ppermute | solution.py:28
  88.3 0.6 copy-done.17
  89.3 19.7 %shard_map.147 = (bf16[256,384]{1,0:T(8,128)(2,1)S(1)}, bf16[256,384]{1,0:T(8,128)(2,1)}, bf16[256,384]{1,0:T(8,128)(2,1)}, bf16[256,384]{1,0:T(8,128)(2,1)}, bf...) custom-call(s32[1]{0:T(128)} %bitcast.refs_0_, ...), custom_call_target="tpu_custom_call" | custom-call | flops 11274289152 | bytes 44040192 | tf_op jit(solution)/shard_map/pallas_call | solution.py:49
  108.9 1.2 collective-permute-start.24
  110.2 0.3 collective-permute-start.28
  110.4 2.9 %collective-permute-start.29 = (bf16[256,384]{1,0:T(8,128)(2,1)}, bf16[256,384]{1,0:T(8,128)(2,1)S(1)}, u32[]{:S(2)}, u32[]{:S(2)}) collective-permute-start(bf16[256,384]{1,0:T(8,128)(2,1)} %get-tuple-element.88), channel_id=1, source_target_pairs={{0,2},{1,3},{2,0},{3,1},{4,6},{5,7},{6,4},{7,5},{8,10},{9,11},{10,... | collective-permute-start | bytes 589832 | tf_op jit(solution)/shard_map/ppermute | solution.py:28
  113.4 1.4 collective-permute-start.26
  114.8 4.0 %collective-permute-done.24.refs_1_.refs_11_ = bf16[256,384]{1,0:T(8,128)(2,1)S(1)} collective-permute-done((bf16[256,384]{1,0:T(8,128)(2,1)}, bf16[256,384]{1,0:T(8,128)(2,1)S(1)}, u32[]{:S(2)}, u32[]{:S(2)}) %collective-permute-start.24) | collective-permute-done | bytes 196640 | tf_op jit(solution)/shard_map/ppermute | solution.py:28
  118.8 1.0 copy-done.2
  119.8 0.8 shard_map.148
  120.6 2.6 %collective-permute-done.28.refs_9_ = bf16[256,384]{1,0:T(8,128)(2,1)S(1)} collective-permute-done((bf16[256,384]{1,0:T(8,128)(2,1)}, bf16[256,384]{1,0:T(8,128)(2,1)S(1)}, u32[]{:S(2)}, u32[]{:S(2)}) %collective-permute-start.28) | collective-permute-done | bytes 196640 | tf_op jit(solution)/shard_map/ppermute | solution.py:28
  123.2 0.4 collective-permute-start.36
  123.6 4.7 %collective-permute-done.29.refs_10_ = bf16[256,384]{1,0:T(8,128)(2,1)S(1)} collective-permute-done((bf16[256,384]{1,0:T(8,128)(2,1)}, bf16[256,384]{1,0:T(8,128)(2,1)S(1)}, u32[]{:S(2)}, u32[]{:S(2)}) %collective-permute-start.29) | collective-permute-done | bytes 196640 | tf_op jit(solution)/shard_map/ppermute | solution.py:28
  128.4 0.8 shard_map.149
  129.3 1.2 collective-permute-start.33
  130.7 1.2 collective-permute-start.31
  131.9 2.9 %collective-permute-start.32 = (bf16[128,640]{1,0:T(8,128)(2,1)S(1)}, bf16[128,640]{1,0:T(8,128)(2,1)S(1)}, u32[]{:S(2)}, u32[]{:S(2)}) collective-permute-start(bf16[128,640]{1,0:T(8,128)(2,1)S(1)} %get-tuple-element.95), channel_id=1, source_target_pairs={{0,3},{1,2},{2,1},{3,0},{4,7},{5,6},{6,5},{7,4},{8,11},{9,10},{10,... | collective-permute-start | bytes 491528 | tf_op jit(solution)/shard_map/ppermute | solution.py:28
  134.8 1.4 collective-permute-start.34
  136.3 5.2 %shard_map.151 = bf16[128,2,8,512]{3,2,1,0:T(8,128)(2,1)} custom-call(bf16[256,8,512]{2,1,0:T(8,128)(2,1)S(1)} %copy-done, bf16[32,2,8,512]{3,2,1,0:T(8,128)(2,1)S(1)} %bitcast.64, s32[128]{0:T(128)S(1)} %get-tuple-element.106.refs_2_, s32[128]{0:T(128)S(1)} %get-tuple-element.104.refs_3_, s32[2,128]{1,0:T(2,128)S(1)} %bitcast.69, s32[128]{0:T(128)S(1)} %copy-done.10, ...), custom_call_target="tpu_custom_call" | custom-call | bytes 5242880 | tf_op jit(solution)/shard_map/pallas_call | solution.py:49
  141.5 4.2 %collective-permute-done.31.refs_5_ = bf16[128,640]{1,0:T(8,128)(2,1)S(1)} collective-permute-done((bf16[128,640]{1,0:T(8,128)(2,1)S(1)}, bf16[128,640]{1,0:T(8,128)(2,1)S(1)}, u32[]{:S(2)}, u32[]{:S(2)}) %collective-permute-start.31) | collective-permute-done | bytes 163872 | tf_op jit(solution)/shard_map/ppermute | solution.py:28
  145.7 1.1 shard_map.150
  (98 shorter events, 1.6 us)
Async XLA Ops:
  0.6 16.8 %copy-start.10 = (s32[128]{0:T(128)S(1)}, s32[128]{0:T(128)}, u32[]{:S(2)}) copy-start(s32[128]{0:T(128)} %refs_5_.1) | copy-start | bytes 1540
  0.6 16.8 %copy-start = (bf16[256,8,512]{2,1,0:T(8,128)(2,1)S(1)}, bf16[256,8,512]{2,1,0:T(8,128)(2,1)}, u32[]{:S(2)}) copy-start(bf16[256,8,512]{2,1,0:T(8,128)(2,1)} %refs_0_.3) | copy-start | bytes 6291460
  0.7 16.8 %copy-start.8 = (s32[128,2]{0,1:T(2,128)S(1)}, s32[128,2]{0,1:T(2,128)}, u32[]{:S(2)}) copy-start(s32[128,2]{0,1:T(2,128)} %param.19) | copy-start | bytes 3076
  0.7 7.5 %collective-permute-start.1 = (bf16[512,1024]{1,0:T(8,128)(2,1)}, bf16[512,1024]{1,0:T(8,128)(2,1)}, u32[]{:S(2)}, u32[]{:S(2)}) collective-permute-start(bf16[512,1024]{1,0:T(8,128)(2,1)} %refs_4_.1), channel_id=1, source_target_pairs={{0,4},{4,0},{8,12},{12,8},{16,20},{20,16},{24,28},{28,24},{1,5},{5... | collective-permute-start | bytes 3145736 | tf_op jit(solution)/shard_map/ppermute | solution.py:28
  3.7 13.7 %copy-start.5 = (s32[32,128]{1,0:T(8,128)S(1)}, s32[32,128]{1,0:T(8,128)}, u32[]{:S(2)}) copy-start(s32[32,128]{1,0:T(8,128)} %get-tuple-element.55.refs_1_) | copy-start | bytes 49156
  3.7 4.4 %collective-permute-start = (bf16[16,5120]{1,0:T(8,128)(2,1)}, bf16[16,5120]{1,0:T(8,128)(2,1)S(1)}, u32[]{:S(2)}, u32[]{:S(2)}) collective-permute-start(bf16[16,5120]{1,0:T(8,128)(2,1)} %get-tuple-element.51), channel_id=1, source_target_pairs={{0,4},{4,0},{8,12},{12,8},{16,20},{20,16},{24,28},{28,24},{1,5},{5... | collective-permute-start | bytes 491528 | tf_op jit(solution)/shard_map/ppermute | solution.py:28
  3.8 12.5 %collective-permute-start.3 = (bf16[128,1024]{1,0:T(8,128)(2,1)S(1)}, bf16[128,1024]{1,0:T(8,128)(2,1)S(1)}, u32[]{:S(2)}, u32[]{:S(2)}) collective-permute-start(bf16[128,1024]{1,0:T(8,128)(2,1)S(1)} %get-tuple-element.57), channel_id=1, source_target_pairs={{0,8},{4,12},{8,0},{12,4},{16,24},{20,28},{24,16},{28,20},{1,9},{5... | collective-permute-start | bytes 786440 | tf_op jit(solution)/shard_map/ppermute | solution.py:28
  6.6 14.8 %collective-permute-start.4 = (bf16[128,1024]{1,0:T(8,128)(2,1)S(1)}, bf16[128,1024]{1,0:T(8,128)(2,1)}, u32[]{:S(2)}, u32[]{:S(2)}) collective-permute-start(bf16[128,1024]{1,0:T(8,128)(2,1)S(1)} %get-tuple-element.58), channel_id=1, source_target_pairs={{0,16},{4,20},{8,24},{12,28},{16,0},{20,4},{24,8},{28,12},{1,17},{... | collective-permute-start | bytes 786440 | tf_op jit(solution)/shard_map/ppermute | solution.py:28
  8.2 13.3 %collective-permute-start.5 = (bf16[128,1024]{1,0:T(8,128)(2,1)S(1)}, bf16[128,1024]{1,0:T(8,128)(2,1)}, u32[]{:S(2)}, u32[]{:S(2)}) collective-permute-start(bf16[128,1024]{1,0:T(8,128)(2,1)S(1)} %get-tuple-element.59), channel_id=1, source_target_pairs={{0,24},{4,28},{8,16},{12,20},{16,8},{20,12},{24,0},{28,4},{1,25},{... | collective-permute-start | bytes 786440 | tf_op jit(solution)/shard_map/ppermute | solution.py:28
  8.2 0.7 copy-start.21
  11.8 9.7 %collective-permute-start.6 = (bf16[32,1024]{1,0:T(8,128)(2,1)}, bf16[32,1024]{1,0:T(8,128)(2,1)S(1)}, u32[]{:S(2)}, u32[]{:S(2)}) collective-permute-start(bf16[32,1024]{1,0:T(8,128)(2,1)} %get-tuple-element.61), channel_id=1, source_target_pairs={{0,8},{4,12},{8,0},{12,4},{16,24},{20,28},{24,16},{28,20},{1,9},{5... | collective-permute-start | bytes 196616 | tf_op jit(solution)/shard_map/ppermute | solution.py:28
  13.8 9.3 %collective-permute-start.7 = (bf16[32,1024]{1,0:T(8,128)(2,1)}, bf16[32,1024]{1,0:T(8,128)(2,1)S(1)}, u32[]{:S(2)}, u32[]{:S(2)}) collective-permute-start(bf16[32,1024]{1,0:T(8,128)(2,1)} %get-tuple-element.62), channel_id=1, source_target_pairs={{0,16},{4,20},{8,24},{12,28},{16,0},{20,4},{24,8},{28,12},{1,17},{... | collective-permute-start | bytes 196616 | tf_op jit(solution)/shard_map/ppermute | solution.py:28
  16.4 1.1 copy-start.25
  16.4 6.8 %collective-permute-start.8 = (bf16[32,1024]{1,0:T(8,128)(2,1)}, bf16[32,1024]{1,0:T(8,128)(2,1)S(1)}, u32[]{:S(2)}, u32[]{:S(2)}) collective-permute-start(bf16[32,1024]{1,0:T(8,128)(2,1)} %get-tuple-element.63), channel_id=1, source_target_pairs={{0,24},{4,28},{8,16},{12,20},{16,8},{20,12},{24,0},{28,4},{1,25},{... | collective-permute-start | bytes 196616 | tf_op jit(solution)/shard_map/ppermute | solution.py:28
  17.5 0.7 copy-start.4
  21.5 10.9 %collective-permute-start.2 = (bf16[16,2,8,512]{3,2,1,0:T(8,128)(2,1)}, bf16[16,2,8,512]{3,2,1,0:T(8,128)(2,1)}, u32[]{:S(2)}, u32[]{:S(2)}) collective-permute-start(bf16[16,2,8,512]{3,2,1,0:T(8,128)(2,1)} %slice.58), channel_id=1, source_target_pairs={{0,4},{4,0},{8,12},{12,8},{16,20},{20,16},{24,28},{28,24},{1,5},{5... | collective-permute-start | bytes 786440 | tf_op jit(solution)/shard_map/ppermute | solution.py:28
  21.5 1.7 %copy-start.26 = (bf16[32,1024]{1,0:T(8,128)(2,1)}, bf16[32,1024]{1,0:T(8,128)(2,1)S(1)}, u32[]{:S(2)}) copy-start(bf16[32,1024]{1,0:T(8,128)(2,1)S(1)} %collective-permute-done.6.refs_11_) | copy-start | bytes 196612
  23.8 8.3 %copy-start.24 = (f32[1024,4]{0,1:T(4,128)S(1)}, f32[1024,4]{0,1:T(4,128)}, u32[]{:S(2)}) copy-start(f32[1024,4]{0,1:T(4,128)} %param.16) | copy-start | bytes 49156
  23.8 8.4 %copy-start.9 = (s32[128,2]{0,1:T(2,128)S(1)}, s32[128,2]{0,1:T(2,128)}, u32[]{:S(2)}) copy-start(s32[128,2]{0,1:T(2,128)} %param.22) | copy-start | bytes 3076
  23.8 19.9 %copy-start.7 = (f32[1024]{0:T(1024)S(1)}, f32[1024]{0:T(1024)}, u32[]{:S(2)}) copy-start(f32[1024]{0:T(1024)} %param.17) | copy-start | bytes 12292
  28.6 9.4 %collective-permute-start.9 = (bf16[128,1024]{1,0:T(8,128)(2,1)}, bf16[128,1024]{1,0:T(8,128)(2,1)S(1)}, u32[]{:S(2)}, u32[]{:S(2)}) collective-permute-start(bf16[128,1024]{1,0:T(8,128)(2,1)} %get-tuple-element.65), channel_id=1, source_target_pairs={{0,8},{4,12},{8,0},{12,4},{16,24},{20,28},{24,16},{28,20},{1,9},{5... | collective-permute-start | bytes 786440 | tf_op jit(solution)/shard_map/ppermute | solution.py:28
  29.9 8.1 %collective-permute-start.10 = (bf16[128,1024]{1,0:T(8,128)(2,1)}, bf16[128,1024]{1,0:T(8,128)(2,1)}, u32[]{:S(2)}, u32[]{:S(2)}) collective-permute-start(bf16[128,1024]{1,0:T(8,128)(2,1)} %get-tuple-element.66), channel_id=1, source_target_pairs={{0,16},{4,20},{8,24},{12,28},{16,0},{20,4},{24,8},{28,12},{1,17},{... | collective-permute-start | bytes 786440 | tf_op jit(solution)/shard_map/ppermute | solution.py:28
  30.7 13.0 %collective-permute-start.11 = (bf16[128,1024]{1,0:T(8,128)(2,1)}, bf16[128,1024]{1,0:T(8,128)(2,1)}, u32[]{:S(2)}, u32[]{:S(2)}) collective-permute-start(bf16[128,1024]{1,0:T(8,128)(2,1)} %get-tuple-element.67), channel_id=1, source_target_pairs={{0,24},{4,28},{8,16},{12,20},{16,8},{20,12},{24,0},{28,4},{1,25},{... | collective-permute-start | bytes 786440 | tf_op jit(solution)/shard_map/ppermute | solution.py:28
  32.4 33.4 %copy-start.3 = (bf16[256,128]{1,0:T(8,128)(2,1)}, bf16[256,128]{1,0:T(8,128)(2,1)S(1)}, u32[]{:S(2)}) copy-start(bf16[256,128]{1,0:T(8,128)(2,1)S(1)} %get-tuple-element.54.refs_2_.refs_1_) | copy-start | bytes 196612
  46.0 19.1 %collective-permute-start.16 = (bf16[320,512]{1,0:T(8,128)(2,1)}, bf16[320,512]{1,0:T(8,128)(2,1)}, u32[]{:S(2)}, u32[]{:S(2)}) collective-permute-start(bf16[320,512]{1,0:T(8,128)(2,1)} %get-tuple-element.71), channel_id=1, source_target_pairs={{0,8},{4,12},{8,0},{12,4},{16,24},{20,28},{24,16},{28,20},{1,9},{5... | collective-permute-start | bytes 983048 | tf_op jit(solution)/shard_map/ppermute | solution.py:28
  46.9 9.8 %collective-permute-start.14 = (bf16[144,640]{1,0:T(8,128)(2,1)}, bf16[144,640]{1,0:T(8,128)(2,1)S(1)}, u32[]{:S(2)}, u32[]{:S(2)}) collective-permute-start(bf16[144,640]{1,0:T(8,128)(2,1)} %get-tuple-element.68.refs_2_), channel_id=1, source_target_pairs={{0,3},{1,2},{2,1},{3,0},{4,7},{5,6},{6,5},{7,4},{8,11},{9,10},{10,... | collective-permute-start | bytes 552968 | tf_op jit(solution)/shard_map/ppermute | solution.py:28
  50.5 14.6 %collective-permute-start.13 = (bf16[144,640]{1,0:T(8,128)(2,1)}, bf16[144,640]{1,0:T(8,128)(2,1)S(1)}, u32[]{:S(2)}, u32[]{:S(2)}) collective-permute-start(bf16[144,640]{1,0:T(8,128)(2,1)} %get-tuple-element.68.refs_2_), channel_id=1, source_target_pairs={{0,2},{1,3},{2,0},{3,1},{4,6},{5,7},{6,4},{7,5},{8,10},{9,11},{10,... | collective-permute-start | bytes 552968 | tf_op jit(solution)/shard_map/ppermute | solution.py:28
  50.5 14.6 %collective-permute-start.12 = (bf16[144,640]{1,0:T(8,128)(2,1)}, bf16[144,640]{1,0:T(8,128)(2,1)S(1)}, u32[]{:S(2)}, u32[]{:S(2)}) collective-permute-start(bf16[144,640]{1,0:T(8,128)(2,1)} %get-tuple-element.68.refs_2_), channel_id=1, source_target_pairs={{0,1},{1,0},{2,3},{3,2},{4,5},{5,4},{6,7},{7,6},{8,9},{9,8},{10,11... | collective-permute-start | bytes 552968 | tf_op jit(solution)/shard_map/ppermute | solution.py:28
  51.3 1.4 collective-permute-start.15
  52.7 13.1 %copy-start.22 = (bf16[64,384]{1,0:T(8,128)(2,1)}, bf16[64,384]{1,0:T(8,128)(2,1)S(1)}, u32[]{:S(2)}) copy-start(bf16[64,384]{1,0:T(8,128)(2,1)S(1)} %collective-permute-done.15.refs_7_) | copy-start | bytes 147460
  52.7 3.9 %collective-permute-start.17 = (bf16[64,384]{1,0:T(8,128)(2,1)}, bf16[64,384]{1,0:T(8,128)(2,1)S(1)}, u32[]{:S(2)}, u32[]{:S(2)}) collective-permute-start(bf16[64,384]{1,0:T(8,128)(2,1)} %get-tuple-element.72), channel_id=1, source_target_pairs={{0,12},{4,8},{8,4},{12,0},{16,28},{20,24},{24,20},{28,16},{1,13},{... | collective-permute-start | bytes 147464 | tf_op jit(solution)/shard_map/ppermute | solution.py:28
  56.6 9.2 %copy-start.23 = (bf16[64,384]{1,0:T(8,128)(2,1)}, bf16[64,384]{1,0:T(8,128)(2,1)S(1)}, u32[]{:S(2)}) copy-start(bf16[64,384]{1,0:T(8,128)(2,1)S(1)} %collective-permute-done.17.refs_9_) | copy-start | bytes 147460
  56.6 9.2 %copy-start.18 = (bf16[144,640]{1,0:T(8,128)(2,1)}, bf16[144,640]{1,0:T(8,128)(2,1)S(1)}, u32[]{:S(2)}) copy-start(bf16[144,640]{1,0:T(8,128)(2,1)S(1)} %collective-permute-done.14.refs_5_) | copy-start | bytes 552964
  65.0 0.7 copy-start.19
  65.1 0.7 copy-start.20
  68.4 20.9 %copy-start.6 = (f32[16,128]{1,0:T(8,128)}, f32[16,128]{1,0:T(8,128)S(1)}, u32[]{:S(2)}) copy-start(f32[16,128]{1,0:T(8,128)S(1)} %get-tuple-element.78.refs_12_) | copy-start | bytes 24580
  68.4 8.9 %collective-permute-start.23 = (bf16[256,384]{1,0:T(8,128)(2,1)}, bf16[256,384]{1,0:T(8,128)(2,1)S(1)}, u32[]{:S(2)}, u32[]{:S(2)}) collective-permute-start(bf16[256,384]{1,0:T(8,128)(2,1)} %get-tuple-element.77.refs_5_), channel_id=1, source_target_pairs={{0,3},{1,2},{2,1},{3,0},{4,7},{5,6},{6,5},{7,4},{8,11},{9,10},{10,... | collective-permute-start | bytes 589832 | tf_op jit(solution)/shard_map/ppermute | solution.py:28
  70.9 17.4 %collective-permute-start.18 = (bf16[64,2688]{1,0:T(8,128)(2,1)S(1)}, bf16[64,2688]{1,0:T(8,128)(2,1)S(1)}, u32[]{:S(2)}, u32[]{:S(2)}) collective-permute-start(bf16[64,2688]{1,0:T(8,128)(2,1)S(1)} %get-tuple-element.74), channel_id=1, source_target_pairs={{0,4},{4,0},{8,12},{12,8},{16,20},{20,16},{24,28},{28,24},{1,5},{5... | collective-permute-start | bytes 1032200 | tf_op jit(solution)/shard_map/ppermute | solution.py:28
  70.9 17.4 %collective-permute-start.19 = (bf16[64,2688]{1,0:T(8,128)(2,1)S(1)}, bf16[64,2688]{1,0:T(8,128)(2,1)S(1)}, u32[]{:S(2)}, u32[]{:S(2)}) collective-permute-start(bf16[64,2688]{1,0:T(8,128)(2,1)S(1)} %get-tuple-element.75), channel_id=1, source_target_pairs={{0,8},{4,12},{8,0},{12,4},{16,24},{20,28},{24,16},{28,20},{1,9},{5... | collective-permute-start | bytes 1032200 | tf_op jit(solution)/shard_map/ppermute | solution.py:28
  72.3 16.1 %collective-permute-start.20 = (bf16[64,2688]{1,0:T(8,128)(2,1)S(1)}, bf16[64,2688]{1,0:T(8,128)(2,1)S(1)}, u32[]{:S(2)}, u32[]{:S(2)}) collective-permute-start(bf16[64,2688]{1,0:T(8,128)(2,1)S(1)} %get-tuple-element.76), channel_id=1, source_target_pairs={{0,12},{4,8},{8,4},{12,0},{16,28},{20,24},{24,20},{28,16},{1,13},{... | collective-permute-start | bytes 1032200 | tf_op jit(solution)/shard_map/ppermute | solution.py:28
  72.7 13.7 %collective-permute-start.22 = (bf16[256,384]{1,0:T(8,128)(2,1)}, bf16[256,384]{1,0:T(8,128)(2,1)S(1)}, u32[]{:S(2)}, u32[]{:S(2)}) collective-permute-start(bf16[256,384]{1,0:T(8,128)(2,1)} %get-tuple-element.77.refs_5_), channel_id=1, source_target_pairs={{0,2},{1,3},{2,0},{3,1},{4,6},{5,7},{6,4},{7,5},{8,10},{9,11},{10,... | collective-permute-start | bytes 589832 | tf_op jit(solution)/shard_map/ppermute | solution.py:28
  77.3 12.0 %copy-start.15 = (bf16[256,384]{1,0:T(8,128)(2,1)}, bf16[256,384]{1,0:T(8,128)(2,1)S(1)}, u32[]{:S(2)}) copy-start(bf16[256,384]{1,0:T(8,128)(2,1)S(1)} %collective-permute-done.23.refs_8_) | copy-start | bytes 589828
  77.3 11.0 %collective-permute-start.21 = (bf16[256,384]{1,0:T(8,128)(2,1)}, bf16[256,384]{1,0:T(8,128)(2,1)S(1)}, u32[]{:S(2)}, u32[]{:S(2)}) collective-permute-start(bf16[256,384]{1,0:T(8,128)(2,1)} %get-tuple-element.77.refs_5_), channel_id=1, source_target_pairs={{0,1},{1,0},{2,3},{3,2},{4,5},{5,4},{6,7},{7,6},{8,9},{9,8},{10,11... | collective-permute-start | bytes 589832 | tf_op jit(solution)/shard_map/ppermute | solution.py:28
  86.5 1.9 %copy-start.16 = (bf16[256,384]{1,0:T(8,128)(2,1)}, bf16[256,384]{1,0:T(8,128)(2,1)S(1)}, u32[]{:S(2)}) copy-start(bf16[256,384]{1,0:T(8,128)(2,1)S(1)} %collective-permute-done.22.refs_7_) | copy-start | bytes 589828
  88.2 0.7 copy-start.17
  88.2 0.8 copy-start.12
  88.2 0.9 copy-start.13
  88.3 0.9 copy-start.14
  89.3 31.3 %copy-start.11 = (bf16[2,2,8,2,8,512]{5,4,3,2,1,0:T(8,128)(2,1)S(1)}, bf16[2,2,8,2,8,512]{5,4,3,2,1,0:T(8,128)(2,1)}, u32[]{:S(2)}) copy-start(bf16[2,2,8,2,8,512]{5,4,3,2,1,0:T(8,128)(2,1)} %fusion.4.refs_13_) | copy-start | bytes 1572868
  108.9 9.9 %collective-permute-start.24 = (bf16[256,384]{1,0:T(8,128)(2,1)}, bf16[256,384]{1,0:T(8,128)(2,1)S(1)}, u32[]{:S(2)}, u32[]{:S(2)}) collective-permute-start(bf16[256,384]{1,0:T(8,128)(2,1)} %get-tuple-element.83), channel_id=1, source_target_pairs={{0,3},{1,2},{2,1},{3,0},{4,7},{5,6},{6,5},{7,4},{8,11},{9,10},{10,... | collective-permute-start | bytes 589832 | tf_op jit(solution)/shard_map/ppermute | solution.py:28
  110.2 13.0 %collective-permute-start.28 = (bf16[256,384]{1,0:T(8,128)(2,1)}, bf16[256,384]{1,0:T(8,128)(2,1)S(1)}, u32[]{:S(2)}, u32[]{:S(2)}) collective-permute-start(bf16[256,384]{1,0:T(8,128)(2,1)} %get-tuple-element.87), channel_id=1, source_target_pairs={{0,1},{1,0},{2,3},{3,2},{4,5},{5,4},{6,7},{7,6},{8,9},{9,8},{10,11... | collective-permute-start | bytes 589832 | tf_op jit(solution)/shard_map/ppermute | solution.py:28
  110.4 17.9 %collective-permute-start.29 = (bf16[256,384]{1,0:T(8,128)(2,1)}, bf16[256,384]{1,0:T(8,128)(2,1)S(1)}, u32[]{:S(2)}, u32[]{:S(2)}) collective-permute-start(bf16[256,384]{1,0:T(8,128)(2,1)} %get-tuple-element.88), channel_id=1, source_target_pairs={{0,2},{1,3},{2,0},{3,1},{4,6},{5,7},{6,4},{7,5},{8,10},{9,11},{10,... | collective-permute-start | bytes 589832 | tf_op jit(solution)/shard_map/ppermute | solution.py:28
  113.4 14.9 %collective-permute-start.26 = (bf16[64,2560]{1,0:T(8,128)(2,1)}, bf16[64,2560]{1,0:T(8,128)(2,1)S(1)}, u32[]{:S(2)}, u32[]{:S(2)}) collective-permute-start(bf16[64,2560]{1,0:T(8,128)(2,1)} %get-tuple-element.84), channel_id=1, source_target_pairs={{0,8},{4,12},{8,0},{12,4},{16,24},{20,28},{24,16},{28,20},{1,9},{5... | collective-permute-start | bytes 983048 | tf_op jit(solution)/shard_map/ppermute | solution.py:28
  114.8 13.6 %collective-permute-start.27 = (bf16[64,2560]{1,0:T(8,128)(2,1)}, bf16[64,2560]{1,0:T(8,128)(2,1)S(1)}, u32[]{:S(2)}, u32[]{:S(2)}) collective-permute-start(bf16[64,2560]{1,0:T(8,128)(2,1)} %get-tuple-element.85), channel_id=1, source_target_pairs={{0,12},{4,8},{8,4},{12,0},{16,28},{20,24},{24,20},{28,16},{1,13},{... | collective-permute-start | bytes 983048 | tf_op jit(solution)/shard_map/ppermute | solution.py:28
  118.8 1.0 copy-start.2
  120.6 7.9 %collective-permute-start.25 = (bf16[64,2560]{1,0:T(8,128)(2,1)}, bf16[64,2560]{1,0:T(8,128)(2,1)S(1)}, u32[]{:S(2)}, u32[]{:S(2)}) collective-permute-start(bf16[64,2560]{1,0:T(8,128)(2,1)} %shard_map.148), channel_id=1, source_target_pairs={{0,4},{4,0},{8,12},{12,8},{16,20},{20,16},{24,28},{28,24},{1,5},{5... | collective-permute-start | bytes 983048 | tf_op jit(solution)/shard_map/ppermute | solution.py:28
  123.2 11.6 %collective-permute-start.36 = (bf16[1,2,8,2,8,512]{5,4,3,2,1,0:T(8,128)(2,1)S(1)}, bf16[1,2,8,2,8,512]{5,4,3,2,1,0:T(8,128)(2,1)S(1)}, u32[]{:S(2)}, u32[]{:S(2)}) collective-permute-start(bf16[1,2,8,2,8,512]{5,4,3,2,1,0:T(8,128)(2,1)S(1)} %get-tuple-element.103), channel_id=1, source_target_pairs={{0,16},{4,20},{8,24},{12,28},{16,0},{20,4},{24,8},{28,12},{1,17},{... | collective-permute-start | bytes 786440 | tf_op jit(solution)/shard_map/ppermute | solution.py:28
  129.3 7.0 %collective-permute-start.33 = (bf16[64,384]{1,0:T(8,128)(2,1)S(1)}, bf16[64,384]{1,0:T(8,128)(2,1)S(1)}, u32[]{:S(2)}, u32[]{:S(2)}) collective-permute-start(bf16[64,384]{1,0:T(8,128)(2,1)S(1)} %get-tuple-element.97), channel_id=1, source_target_pairs={{0,4},{4,0},{8,12},{12,8},{16,20},{20,16},{24,28},{28,24},{1,5},{5... | collective-permute-start | bytes 147464 | tf_op jit(solution)/shard_map/ppermute | solution.py:28
  130.4 11.1 %collective-permute-start.30 = (bf16[128,640]{1,0:T(8,128)(2,1)S(1)}, bf16[128,640]{1,0:T(8,128)(2,1)S(1)}, u32[]{:S(2)}, u32[]{:S(2)}) collective-permute-start(bf16[128,640]{1,0:T(8,128)(2,1)S(1)} %get-tuple-element.93), channel_id=1, source_target_pairs={{0,1},{1,0},{2,3},{3,2},{4,5},{5,4},{6,7},{7,6},{8,9},{9,8},{10,11... | collective-permute-start | bytes 491528 | tf_op jit(solution)/shard_map/ppermute | solution.py:28
  130.7 15.0 %collective-permute-start.31 = (bf16[128,640]{1,0:T(8,128)(2,1)S(1)}, bf16[128,640]{1,0:T(8,128)(2,1)S(1)}, u32[]{:S(2)}, u32[]{:S(2)}) collective-permute-start(bf16[128,640]{1,0:T(8,128)(2,1)S(1)} %get-tuple-element.94), channel_id=1, source_target_pairs={{0,2},{1,3},{2,0},{3,1},{4,6},{5,7},{6,4},{7,5},{8,10},{9,11},{10,... | collective-permute-start | bytes 491528 | tf_op jit(solution)/shard_map/ppermute | solution.py:28
  131.9 13.8 %collective-permute-start.32 = (bf16[128,640]{1,0:T(8,128)(2,1)S(1)}, bf16[128,640]{1,0:T(8,128)(2,1)S(1)}, u32[]{:S(2)}, u32[]{:S(2)}) collective-permute-start(bf16[128,640]{1,0:T(8,128)(2,1)S(1)} %get-tuple-element.95), channel_id=1, source_target_pairs={{0,3},{1,2},{2,1},{3,0},{4,7},{5,6},{6,5},{7,4},{8,11},{9,10},{10,... | collective-permute-start | bytes 491528 | tf_op jit(solution)/shard_map/ppermute | solution.py:28
  134.8 6.7 %collective-permute-start.34 = (bf16[64,384]{1,0:T(8,128)(2,1)S(1)}, bf16[64,384]{1,0:T(8,128)(2,1)S(1)}, u32[]{:S(2)}, u32[]{:S(2)}) collective-permute-start(bf16[64,384]{1,0:T(8,128)(2,1)S(1)} %get-tuple-element.98), channel_id=1, source_target_pairs={{0,8},{4,12},{8,0},{12,4},{16,24},{20,28},{24,16},{28,20},{1,9},{5... | collective-permute-start | bytes 147464 | tf_op jit(solution)/shard_map/ppermute | solution.py:28
  136.2 5.3 %collective-permute-start.35 = (bf16[64,384]{1,0:T(8,128)(2,1)S(1)}, bf16[64,384]{1,0:T(8,128)(2,1)S(1)}, u32[]{:S(2)}, u32[]{:S(2)}) collective-permute-start(bf16[64,384]{1,0:T(8,128)(2,1)S(1)} %get-tuple-element.99), channel_id=1, source_target_pairs={{0,12},{4,8},{8,4},{12,0},{16,28},{20,24},{24,20},{28,16},{1,13},{... | collective-permute-start | bytes 147464 | tf_op jit(solution)/shard_map/ppermute | solution.py:28
  136.3 9.4 %copy-start.1 = (f32[128,1024]{1,0:T(8,128)S(1)}, f32[128,1024]{1,0:T(8,128)}, u32[]{:S(2)}) copy-start(f32[128,1024]{1,0:T(8,128)} %get-tuple-element.91.refs_2_) | copy-start | bytes 1572868
  (2 other events, 1.3 us)

commit v8 on v7

--- a/solution.py
+++ b/solution.py
@@ -488,8 +488,8 @@
         (me.reshape(1).astype(I32), came_from.reshape(n, rows), attention_out, residual),
         [far((rows, kblock), BF)] + [near((rows, kblock), BF)] * (half - 1)
         + [
-            far((n_pair, D + feats), BF),
-            far((2 * n_pair, feats), BF),
+            near((n_pair, D + feats), BF),
+            near((2 * n_pair, feats), BF),
             shape((2 * n_pair, 128), I32),
         ],
         vmem=60,
@@ -502,8 +502,8 @@
         functools.partial(handover_kernel, half),
         [SMEM, VMEM, VMEM, VMEM],
         (pair_place, pair_rows, own_rows, came_from.reshape(n, rows)),
-        [far((n_hand, feats), BF)] * half + [shape((n, rows), I32)],
-        vmem=60,
+        [near((n_hand, feats), BF)] * half + [near((n, rows), I32)],
+        vmem=30,
         moved=MIB,
         after=[w_other],
     )
@@ -649,9 +649,9 @@
         functools.partial(weigh_kernel, ne, experts),
         [SMEM] + [VMEM] * (3 + experts + ne),
         (place, stats, routes.T, slot_of, *early_back, *late_blocks),
-        [shape((rows, wide), F32)]
-        + [shape((rows, wide), BF)] * (ne - 1)
-        + [shape((SLOTS, rest), BF)] * experts
+        [near((rows, wide), F32)]
+        + [near((rows, wide), BF)] * (ne - 1)
+        + [near((SLOTS, rest), BF)] * experts
         + [shape((rows, experts * SLOTS), BF)] * 2,
         [pltpu.VMEM((experts * SLOTS, ne * wide), BF), pltpu.VMEM((rows, ne * wide), F32)],
         flops=4 * rows * experts * SLOTS * ne * wide,

time: 147 us -> 147 us (level)
  starting transfers between devices: 42.6 us -> 46.7 us
  waiting for transfers between devices: 48.3 us -> 45.5 us
  Pallas kernels: 42.8 us -> 41 us
    ppermute x37, starting transfers between devices: 42.6 us -> 46.7 us  [swap(): return lax.ppermute(x, axis, [(i, i ^ s) for i in range(n)])]
    ppermute x37, waiting for transfers between devices: 48.3 us -> 45.5 us  [swap(): return lax.ppermute(x, axis, [(i, i ^ s) for i in range(n)])]
    pallas_call x12, Pallas kernels: 42.8 us -> 41 us  [local_call(): pl.pallas_call(run, out_shape=outs, in_specs=list(in_specs) + [pl.BlockSp...]
    unnamed x58 -> x64, local copies, waits for them, and re-layouts: 4.67 us -> 5.44 us
  transfers between devices with their start and end apart: 37 -> 37, of which waited for: 15 -> 16; matrix products, arithmetic and copies ran while one was open for 5% -> 5% of each run, Pallas kernels for 12% -> 11%
where the time goes in v8:
time: 147 us
  starting transfers between devices  46.7 us (32%)
  waiting for transfers between devices  45.5 us (31%)
  Pallas kernels  41 us (28%)
  local copies, waits for them, and re-layouts  7.28 us (5%)
  other arithmetic  5.09 us (3%)
    ppermute x37, starting transfers between devices, swap(): return lax.ppermute(x, axis, [(i, i ^ s) for i in range(n)])  46.7 us
    ppermute x37, waiting for transfers between devices, swap(): return lax.ppermute(x, axis, [(i, i ^ s) for i in range(n)])  45.5 us
    pallas_call x12, Pallas kernels, local_call(): pl.pallas_call(run, out_shape=outs, in_specs=list(in_specs) + [pl.BlockSp...  41 us
    unnamed x64, local copies, waits for them, and re-layouts  5.44 us
  transfers between devices with their start and end apart: 37, of which 16 were waited for; matrix products, arithmetic and copies ran while one was open for 5% of the time, Pallas kernels for 11%

profile of v8, /device:TPU:0, one launch (start us, length us, event | category | flops | bytes accessed | tf_op | source)
XLA Modules:
  0.0 146.5 jit_solution(650117513071130727)
XLA Ops:
  0.6 0.5 collective-permute-start.1
  1.2 2.5 %shard_map.140 = (bf16[128,1024]{1,0:T(8,128)(2,1)}, bf16[128,1024]{1,0:T(8,128)(2,1)S(1)}, bf16[128,1024]{1,0:T(8,128)(2,1)S(1)}, bf16[128,1024]{1,0:T(8,128)(2...) custom-call(s32[1]{0:T(128)} %bitcast.4.refs_0_, s32[8,128]{1,0:T(8,128)} %bitcast.67, ...), custom_call_target="tpu_custom_call" | custom-call | bytes 2097152 | tf_op jit(solution)/shard_map/pallas_call | solution.py:49
  3.7 2.8 %collective-permute-start.3 = (bf16[128,1024]{1,0:T(8,128)(2,1)S(1)}, bf16[128,1024]{1,0:T(8,128)(2,1)}, u32[]{:S(2)}, u32[]{:S(2)}) collective-permute-start(bf16[128,1024]{1,0:T(8,128)(2,1)S(1)} %get-tuple-element.57), channel_id=1, source_target_pairs={{0,8},{4,12},{8,0},{12,4},{16,24},{20,28},{24,16},{28,20},{1,9},{5... | collective-permute-start | bytes 786440 | tf_op jit(solution)/shard_map/ppermute | solution.py:28
  6.6 1.5 %collective-permute-start.4 = (bf16[128,1024]{1,0:T(8,128)(2,1)S(1)}, bf16[128,1024]{1,0:T(8,128)(2,1)}, u32[]{:S(2)}, u32[]{:S(2)}) collective-permute-start(bf16[128,1024]{1,0:T(8,128)(2,1)S(1)} %get-tuple-element.58), channel_id=1, source_target_pairs={{0,16},{4,20},{8,24},{12,28},{16,0},{20,4},{24,8},{28,12},{1,17},{... | collective-permute-start | bytes 786440 | tf_op jit(solution)/shard_map/ppermute | solution.py:28
  8.1 0.7 copy-done.5
  8.9 0.3 convert_reduce_fusion
  9.3 2.0 %collective-permute-start.6 = (bf16[32,1024]{1,0:T(8,128)(2,1)S(1)}, bf16[32,1024]{1,0:T(8,128)(2,1)S(1)}, u32[]{:S(2)}, u32[]{:S(2)}) collective-permute-start(bf16[32,1024]{1,0:T(8,128)(2,1)S(1)} %get-tuple-element.61), channel_id=1, source_target_pairs={{0,8},{4,12},{8,0},{12,4},{16,24},{20,28},{24,16},{28,20},{1,9},{5... | collective-permute-start | bytes 196616 | tf_op jit(solution)/shard_map/ppermute | solution.py:28
  11.3 1.5 %collective-permute-start.7 = (bf16[32,1024]{1,0:T(8,128)(2,1)S(1)}, bf16[32,1024]{1,0:T(8,128)(2,1)S(1)}, u32[]{:S(2)}, u32[]{:S(2)}) collective-permute-start(bf16[32,1024]{1,0:T(8,128)(2,1)S(1)} %get-tuple-element.62), channel_id=1, source_target_pairs={{0,16},{4,20},{8,24},{12,28},{16,0},{20,4},{24,8},{28,12},{1,17},{... | collective-permute-start | bytes 196616 | tf_op jit(solution)/shard_map/ppermute | solution.py:28
  12.8 1.0 fusion.refs_1_
  13.9 2.9 %collective-permute-start.8 = (bf16[32,1024]{1,0:T(8,128)(2,1)S(1)}, bf16[32,1024]{1,0:T(8,128)(2,1)S(1)}, u32[]{:S(2)}, u32[]{:S(2)}) collective-permute-start(bf16[32,1024]{1,0:T(8,128)(2,1)S(1)} %get-tuple-element.63), channel_id=1, source_target_pairs={{0,24},{4,28},{8,16},{12,20},{16,8},{20,12},{24,0},{28,4},{1,25},{... | collective-permute-start | bytes 196616 | tf_op jit(solution)/shard_map/ppermute | solution.py:28
  16.8 0.7 fusion.6.refs_2_
  17.5 0.7 copy-done.8
  18.2 0.7 copy-done.11
  18.8 1.2 shard_map.143
  20.1 0.7 slice.58
  20.8 0.6 collective-permute-done.4.refs_8_
  21.4 1.6 %collective-permute-done.7.refs_12_ = bf16[32,1024]{1,0:T(8,128)(2,1)S(1)} collective-permute-done((bf16[32,1024]{1,0:T(8,128)(2,1)S(1)}, bf16[32,1024]{1,0:T(8,128)(2,1)S(1)}, u32[]{:S(2)}, u32[]{:S(2)}) %collective-permute-start.7) | collective-permute-done | bytes 65568 | tf_op jit(solution)/shard_map/ppermute | solution.py:28
  23.1 0.6 copy-done.30
  23.7 4.7 %shard_map.144 = (f32[128,1024]{1,0:T(8,128)S(1)}, bf16[128,1024]{1,0:T(8,128)(2,1)}, bf16[128,1024]{1,0:T(8,128)(2,1)}, bf16[128,1024]{1,0:T(8,128)(2,1)}) custom-call(s32[1]{0:T(128)} %bitcast.12.refs_0_, bf16[512,640]{1,0:T(8,128)(2,1)} %fusion.refs_1_, bf16[128,256]{1,0:T(8,128)(2,1)} %fusion.6.refs_2_, bf16[128,1024]{1,0:T(8,128)(2,1)} %refs_3_.5, ...), custom_call_target="tpu_custom_call" | custom-call | flops 1744830464 | bytes 6291456 | tf_op jit(solution)/shard_map/pallas_call | solution.py:49
  28.5 1.3 collective-permute-start.9
  29.8 0.8 collective-permute-start.10
  30.6 1.4 collective-permute-start.11
  32.3 1.0 fusion.5
  33.4 4.6 %collective-permute-done.9.refs_5_ = bf16[128,1024]{1,0:T(8,128)(2,1)S(1)} collective-permute-done((bf16[128,1024]{1,0:T(8,128)(2,1)}, bf16[128,1024]{1,0:T(8,128)(2,1)S(1)}, u32[]{:S(2)}, u32[]{:S(2)}) %collective-permute-start.9) | collective-permute-done | bytes 262176 | tf_op jit(solution)/shard_map/ppermute | solution.py:28
  38.0 3.8 %collective-permute-done.10.refs_6_ = bf16[128,1024]{1,0:T(8,128)(2,1)} collective-permute-done((bf16[128,1024]{1,0:T(8,128)(2,1)}, bf16[128,1024]{1,0:T(8,128)(2,1)}, u32[]{:S(2)}, u32[]{:S(2)}) %collective-permute-start.10) | collective-permute-done | bytes 262176 | tf_op jit(solution)/shard_map/ppermute | solution.py:28
  41.7 1.8 %collective-permute-done.11.refs_7_ = bf16[128,1024]{1,0:T(8,128)(2,1)} collective-permute-done((bf16[128,1024]{1,0:T(8,128)(2,1)}, bf16[128,1024]{1,0:T(8,128)(2,1)}, u32[]{:S(2)}, u32[]{:S(2)}) %collective-permute-start.11) | collective-permute-done | bytes 262176 | tf_op jit(solution)/shard_map/ppermute | solution.py:28
  43.6 2.3 %shard_map.145 = (f32[128,1024]{1,0:T(8,128)}, bf16[144,640]{1,0:T(8,128)(2,1)}, bf16[64,384]{1,0:T(8,128)(2,1)}, bf16[64,384]{1,0:T(8,128)(2,1)}, bf16[320,512]{1,0:T(8,128)(2,1)}, /*index=5*/bf16[64,384]{1,0:T(8,128)(2,1)}) custom-call(f32[1,1024]{1,0:T(1,128)S(1)} %bitcast.69, f32[8,1024]{1,0:T(8,128)S(1)} %pad.4.refs_1_, ...), custom_call_target="tpu_custom_call" | custom-call | flops 25165824 | bytes 3145728 | tf_op jit(solution)/shard_map/pallas_call | solution.py:49
  45.9 0.6 collective-permute-start.16
  46.5 3.6 %collective-permute-start.14 = (bf16[144,640]{1,0:T(8,128)(2,1)}, bf16[144,640]{1,0:T(8,128)(2,1)S(1)}, u32[]{:S(2)}, u32[]{:S(2)}) collective-permute-start(bf16[144,640]{1,0:T(8,128)(2,1)} %get-tuple-element.68.refs_2_), channel_id=1, source_target_pairs={{0,3},{1,2},{2,1},{3,0},{4,7},{5,6},{6,5},{7,4},{8,11},{9,10},{10,... | collective-permute-start | bytes 552968 | tf_op jit(solution)/shard_map/ppermute | solution.py:28
  50.1 0.8 collective-permute-start.12
  50.9 1.4 collective-permute-done.15.refs_7_
  52.3 1.2 collective-permute-start.17
  53.5 2.7 %collective-permute-done.17.refs_9_ = bf16[64,384]{1,0:T(8,128)(2,1)S(1)} collective-permute-done((bf16[64,384]{1,0:T(8,128)(2,1)}, bf16[64,384]{1,0:T(8,128)(2,1)S(1)}, u32[]{:S(2)}, u32[]{:S(2)}) %collective-permute-start.17) | collective-permute-done | bytes 49184 | tf_op jit(solution)/shard_map/ppermute | solution.py:28
  56.2 8.4 %collective-permute-done.13.refs_4_ = bf16[144,640]{1,0:T(8,128)(2,1)S(1)} collective-permute-done((bf16[144,640]{1,0:T(8,128)(2,1)}, bf16[144,640]{1,0:T(8,128)(2,1)S(1)}, u32[]{:S(2)}, u32[]{:S(2)}) %collective-permute-start.13) | collective-permute-done | bytes 184352 | tf_op jit(solution)/shard_map/ppermute | solution.py:28
  64.7 0.7 copy-done.25
  65.5 2.6 %shard_map.146 = (bf16[64,2688]{1,0:T(8,128)(2,1)}, bf16[64,2688]{1,0:T(8,128)(2,1)S(1)}, bf16[64,2688]{1,0:T(8,128)(2,1)S(1)}, bf16[64,2688]{1,0:T(8,128)(2,1)S...) custom-call(s32[1]{0:T(128)} %bitcast.refs_0_, bf16[256,128]{1,0:T(8,128)(2,1)} %copy-done.3, ...), custom_call_target="tpu_custom_call" | custom-call | flops 167772160 | bytes 3145728 | tf_op jit(solution)/shard_map/pallas_call | solution.py:49
  68.1 2.5 %collective-permute-start.23 = (bf16[256,384]{1,0:T(8,128)(2,1)}, bf16[256,384]{1,0:T(8,128)(2,1)S(1)}, u32[]{:S(2)}, u32[]{:S(2)}) collective-permute-start(bf16[256,384]{1,0:T(8,128)(2,1)} %get-tuple-element.77.refs_5_), channel_id=1, source_target_pairs={{0,3},{1,2},{2,1},{3,0},{4,7},{5,6},{6,5},{7,4},{8,11},{9,10},{10,... | collective-permute-start | bytes 589832 | tf_op jit(solution)/shard_map/ppermute | solution.py:28
  70.6 1.7 %collective-permute-start.19 = (bf16[64,2688]{1,0:T(8,128)(2,1)S(1)}, bf16[64,2688]{1,0:T(8,128)(2,1)S(1)}, u32[]{:S(2)}, u32[]{:S(2)}) collective-permute-start(bf16[64,2688]{1,0:T(8,128)(2,1)S(1)} %get-tuple-element.75), channel_id=1, source_target_pairs={{0,8},{4,12},{8,0},{12,4},{16,24},{20,28},{24,16},{28,20},{1,9},{5... | collective-permute-start | bytes 1032200 | tf_op jit(solution)/shard_map/ppermute | solution.py:28
  72.5 4.5 %collective-permute-done.23.refs_8_ = bf16[256,384]{1,0:T(8,128)(2,1)S(1)} collective-permute-done((bf16[256,384]{1,0:T(8,128)(2,1)}, bf16[256,384]{1,0:T(8,128)(2,1)S(1)}, u32[]{:S(2)}, u32[]{:S(2)}) %collective-permute-start.23) | collective-permute-done | bytes 196640 | tf_op jit(solution)/shard_map/ppermute | solution.py:28
  77.0 6.5 %collective-permute-start.21 = (bf16[256,384]{1,0:T(8,128)(2,1)}, bf16[256,384]{1,0:T(8,128)(2,1)S(1)}, u32[]{:S(2)}, u32[]{:S(2)}) collective-permute-start(bf16[256,384]{1,0:T(8,128)(2,1)} %get-tuple-element.77.refs_5_), channel_id=1, source_target_pairs={{0,1},{1,0},{2,3},{3,2},{4,5},{5,4},{6,7},{7,6},{8,9},{9,8},{10,11... | collective-permute-start | bytes 589832 | tf_op jit(solution)/shard_map/ppermute | solution.py:28
  83.4 1.0 slice.61
  84.4 1.9 %fusion.4.refs_13_ = bf16[2,2,8,2,8,512]{5,4,3,2,1,0:T(8,128)(2,1)} fusion(bf16[2,2,4,2,8,512]{5,4,3,2,1,0:T(8,128)(2,1)} %bitcast.76, bf16[2,2,4,2,8,512]{5,4,3,2,1,0:T(8,128)(2,1)} %bitcast.10, bf16[2,1,8,2,8,512]{5,4,3,2,1,0:T(8,128)(2,1)S(1)} %bitcast.77), kind=kLoop, calls=%fused_computation.8 | loop fusion | flops 2359296 | bytes 1310720 | tf_op jit(solution)/shard_map/stack | solution.py:606
  86.3 1.7 %collective-permute-done.21.refs_6_ = bf16[256,384]{1,0:T(8,128)(2,1)S(1)} collective-permute-done((bf16[256,384]{1,0:T(8,128)(2,1)}, bf16[256,384]{1,0:T(8,128)(2,1)S(1)}, u32[]{:S(2)}, u32[]{:S(2)}) %collective-permute-start.21) | collective-permute-done | bytes 196640 | tf_op jit(solution)/shard_map/ppermute | solution.py:28
  88.1 0.6 copy-done.22
  89.0 19.6 %shard_map.147 = (bf16[256,384]{1,0:T(8,128)(2,1)S(1)}, bf16[256,384]{1,0:T(8,128)(2,1)}, bf16[256,384]{1,0:T(8,128)(2,1)}, bf16[256,384]{1,0:T(8,128)(2,1)}, bf...) custom-call(s32[1]{0:T(128)} %bitcast.refs_0_, ...), custom_call_target="tpu_custom_call" | custom-call | flops 11274289152 | bytes 44040192 | tf_op jit(solution)/shard_map/pallas_call | solution.py:49
  108.6 1.3 collective-permute-start.24
  110.2 2.9 %collective-permute-start.29 = (bf16[256,384]{1,0:T(8,128)(2,1)}, bf16[256,384]{1,0:T(8,128)(2,1)S(1)}, u32[]{:S(2)}, u32[]{:S(2)}) collective-permute-start(bf16[256,384]{1,0:T(8,128)(2,1)} %get-tuple-element.88), channel_id=1, source_target_pairs={{0,2},{1,3},{2,0},{3,1},{4,6},{5,7},{6,4},{7,5},{8,10},{9,11},{10,... | collective-permute-start | bytes 589832 | tf_op jit(solution)/shard_map/ppermute | solution.py:28
  113.1 1.7 %collective-permute-start.26 = (bf16[64,2560]{1,0:T(8,128)(2,1)}, bf16[64,2560]{1,0:T(8,128)(2,1)S(1)}, u32[]{:S(2)}, u32[]{:S(2)}) collective-permute-start(bf16[64,2560]{1,0:T(8,128)(2,1)} %get-tuple-element.84), channel_id=1, source_target_pairs={{0,8},{4,12},{8,0},{12,4},{16,24},{20,28},{24,16},{28,20},{1,9},{5... | collective-permute-start | bytes 983048 | tf_op jit(solution)/shard_map/ppermute | solution.py:28
  114.8 3.7 %collective-permute-done.24.refs_1_.refs_11_ = bf16[256,384]{1,0:T(8,128)(2,1)S(1)} collective-permute-done((bf16[256,384]{1,0:T(8,128)(2,1)}, bf16[256,384]{1,0:T(8,128)(2,1)S(1)}, u32[]{:S(2)}, u32[]{:S(2)}) %collective-permute-start.24) | collective-permute-done | bytes 196640 | tf_op jit(solution)/shard_map/ppermute | solution.py:28
  118.5 1.0 copy-done.2
  119.5 0.8 shard_map.148
  120.3 2.6 %collective-permute-done.28.refs_9_ = bf16[256,384]{1,0:T(8,128)(2,1)S(1)} collective-permute-done((bf16[256,384]{1,0:T(8,128)(2,1)}, bf16[256,384]{1,0:T(8,128)(2,1)S(1)}, u32[]{:S(2)}, u32[]{:S(2)}) %collective-permute-start.28) | collective-permute-done | bytes 196640 | tf_op jit(solution)/shard_map/ppermute | solution.py:28
  122.9 1.7 %collective-permute-start.36 = (bf16[1,2,8,2,8,512]{5,4,3,2,1,0:T(8,128)(2,1)S(1)}, bf16[1,2,8,2,8,512]{5,4,3,2,1,0:T(8,128)(2,1)S(1)}, u32[]{:S(2)}, u32[]{:S(2)}) collective-permute-start(bf16[1,2,8,2,8,512]{5,4,3,2,1,0:T(8,128)(2,1)S(1)} %get-tuple-element.103), channel_id=1, source_target_pairs={{0,16},{4,20},{8,24},{12,28},{16,0},{20,4},{24,8},{28,12},{1,17},{... | collective-permute-start | bytes 786440 | tf_op jit(solution)/shard_map/ppermute | solution.py:28
  124.5 3.5 %collective-permute-done.29.refs_10_ = bf16[256,384]{1,0:T(8,128)(2,1)S(1)} collective-permute-done((bf16[256,384]{1,0:T(8,128)(2,1)}, bf16[256,384]{1,0:T(8,128)(2,1)S(1)}, u32[]{:S(2)}, u32[]{:S(2)}) %collective-permute-start.29) | collective-permute-done | bytes 196640 | tf_op jit(solution)/shard_map/ppermute | solution.py:28
  128.0 0.4 collective-permute-done.27.refs_7_
  128.4 0.8 shard_map.149
  129.2 0.9 collective-permute-start.33
  130.1 0.3 collective-permute-start.30
  130.4 1.2 collective-permute-start.31
  131.6 2.8 %collective-permute-start.32 = (bf16[128,640]{1,0:T(8,128)(2,1)S(1)}, bf16[128,640]{1,0:T(8,128)(2,1)S(1)}, u32[]{:S(2)}, u32[]{:S(2)}) collective-permute-start(bf16[128,640]{1,0:T(8,128)(2,1)S(1)} %get-tuple-element.95), channel_id=1, source_target_pairs={{0,3},{1,2},{2,1},{3,0},{4,7},{5,6},{6,5},{7,4},{8,11},{9,10},{10,... | collective-permute-start | bytes 491528 | tf_op jit(solution)/shard_map/ppermute | solution.py:28
  134.5 1.7 %collective-permute-start.34 = (bf16[64,384]{1,0:T(8,128)(2,1)S(1)}, bf16[64,384]{1,0:T(8,128)(2,1)S(1)}, u32[]{:S(2)}, u32[]{:S(2)}) collective-permute-start(bf16[64,384]{1,0:T(8,128)(2,1)S(1)} %get-tuple-element.98), channel_id=1, source_target_pairs={{0,8},{4,12},{8,0},{12,4},{16,24},{20,28},{24,16},{28,20},{1,9},{5... | collective-permute-start | bytes 147464 | tf_op jit(solution)/shard_map/ppermute | solution.py:28
  136.3 5.2 %shard_map.151 = bf16[128,2,8,512]{3,2,1,0:T(8,128)(2,1)} custom-call(bf16[256,8,512]{2,1,0:T(8,128)(2,1)S(1)} %copy-done, bf16[32,2,8,512]{3,2,1,0:T(8,128)(2,1)S(1)} %bitcast.64, s32[128]{0:T(128)S(1)} %get-tuple-element.106.refs_2_, s32[128]{0:T(128)S(1)} %get-tuple-element.104.refs_3_, s32[2,128]{1,0:T(2,128)S(1)} %bitcast.71, s32[128]{0:T(128)S(1)} %copy-done.12, ...), custom_call_target="tpu_custom_call" | custom-call | bytes 5242880 | tf_op jit(solution)/shard_map/pallas_call | solution.py:49
  141.5 3.9 %collective-permute-done.31.refs_5_ = bf16[128,640]{1,0:T(8,128)(2,1)S(1)} collective-permute-done((bf16[128,640]{1,0:T(8,128)(2,1)S(1)}, bf16[128,640]{1,0:T(8,128)(2,1)S(1)}, u32[]{:S(2)}, u32[]{:S(2)}) %collective-permute-start.31) | collective-permute-done | bytes 163872 | tf_op jit(solution)/shard_map/ppermute | solution.py:28
  145.4 1.1 shard_map.150
  (104 shorter events, 1.8 us)
Async XLA Ops:
  0.6 16.9 %copy-start = (bf16[256,8,512]{2,1,0:T(8,128)(2,1)S(1)}, bf16[256,8,512]{2,1,0:T(8,128)(2,1)}, u32[]{:S(2)}) copy-start(bf16[256,8,512]{2,1,0:T(8,128)(2,1)} %refs_0_.3) | copy-start | bytes 6291460
  0.6 7.4 %collective-permute-start.1 = (bf16[512,1024]{1,0:T(8,128)(2,1)}, bf16[512,1024]{1,0:T(8,128)(2,1)}, u32[]{:S(2)}, u32[]{:S(2)}) collective-permute-start(bf16[512,1024]{1,0:T(8,128)(2,1)} %refs_4_.1), channel_id=1, source_target_pairs={{0,4},{4,0},{8,12},{12,8},{16,20},{20,16},{24,28},{28,24},{1,5},{5... | collective-permute-start | bytes 3145736 | tf_op jit(solution)/shard_map/ppermute | solution.py:28
  3.7 13.8 %copy-start.4 = (s32[32,128]{1,0:T(8,128)S(1)}, s32[32,128]{1,0:T(8,128)}, u32[]{:S(2)}) copy-start(s32[32,128]{1,0:T(8,128)} %get-tuple-element.55.refs_1_) | copy-start | bytes 49156
  3.7 4.4 %collective-permute-start = (bf16[16,5120]{1,0:T(8,128)(2,1)S(1)}, bf16[16,5120]{1,0:T(8,128)(2,1)S(1)}, u32[]{:S(2)}, u32[]{:S(2)}) collective-permute-start(bf16[16,5120]{1,0:T(8,128)(2,1)S(1)} %get-tuple-element.51), channel_id=1, source_target_pairs={{0,4},{4,0},{8,12},{12,8},{16,20},{20,16},{24,28},{28,24},{1,5},{5... | collective-permute-start | bytes 491528 | tf_op jit(solution)/shard_map/ppermute | solution.py:28
  3.7 10.1 %collective-permute-start.3 = (bf16[128,1024]{1,0:T(8,128)(2,1)S(1)}, bf16[128,1024]{1,0:T(8,128)(2,1)}, u32[]{:S(2)}, u32[]{:S(2)}) collective-permute-start(bf16[128,1024]{1,0:T(8,128)(2,1)S(1)} %get-tuple-element.57), channel_id=1, source_target_pairs={{0,8},{4,12},{8,0},{12,4},{16,24},{20,28},{24,16},{28,20},{1,9},{5... | collective-permute-start | bytes 786440 | tf_op jit(solution)/shard_map/ppermute | solution.py:28
  6.6 14.8 %collective-permute-start.4 = (bf16[128,1024]{1,0:T(8,128)(2,1)S(1)}, bf16[128,1024]{1,0:T(8,128)(2,1)}, u32[]{:S(2)}, u32[]{:S(2)}) collective-permute-start(bf16[128,1024]{1,0:T(8,128)(2,1)S(1)} %get-tuple-element.58), channel_id=1, source_target_pairs={{0,16},{4,20},{8,24},{12,28},{16,0},{20,4},{24,8},{28,12},{1,17},{... | collective-permute-start | bytes 786440 | tf_op jit(solution)/shard_map/ppermute | solution.py:28
  8.1 13.3 %collective-permute-start.5 = (bf16[128,1024]{1,0:T(8,128)(2,1)S(1)}, bf16[128,1024]{1,0:T(8,128)(2,1)}, u32[]{:S(2)}, u32[]{:S(2)}) collective-permute-start(bf16[128,1024]{1,0:T(8,128)(2,1)S(1)} %get-tuple-element.59), channel_id=1, source_target_pairs={{0,24},{4,28},{8,16},{12,20},{16,8},{20,12},{24,0},{28,4},{1,25},{... | collective-permute-start | bytes 786440 | tf_op jit(solution)/shard_map/ppermute | solution.py:28
  8.1 0.7 copy-start.5
  8.8 14.3 %copy-start.13 = (bf16[32,1024]{1,0:T(8,128)(2,1)}, bf16[32,1024]{1,0:T(8,128)(2,1)S(1)}, u32[]{:S(2)}) copy-start(bf16[32,1024]{1,0:T(8,128)(2,1)S(1)} %get-tuple-element.60.refs_10_) | copy-start | bytes 196612
  9.3 12.1 %collective-permute-start.6 = (bf16[32,1024]{1,0:T(8,128)(2,1)S(1)}, bf16[32,1024]{1,0:T(8,128)(2,1)S(1)}, u32[]{:S(2)}, u32[]{:S(2)}) collective-permute-start(bf16[32,1024]{1,0:T(8,128)(2,1)S(1)} %get-tuple-element.61), channel_id=1, source_target_pairs={{0,8},{4,12},{8,0},{12,4},{16,24},{20,28},{24,16},{28,20},{1,9},{5... | collective-permute-start | bytes 196616 | tf_op jit(solution)/shard_map/ppermute | solution.py:28
  11.3 11.8 %collective-permute-start.7 = (bf16[32,1024]{1,0:T(8,128)(2,1)S(1)}, bf16[32,1024]{1,0:T(8,128)(2,1)S(1)}, u32[]{:S(2)}, u32[]{:S(2)}) collective-permute-start(bf16[32,1024]{1,0:T(8,128)(2,1)S(1)} %get-tuple-element.62), channel_id=1, source_target_pairs={{0,16},{4,20},{8,24},{12,28},{16,0},{20,4},{24,8},{28,12},{1,17},{... | collective-permute-start | bytes 196616 | tf_op jit(solution)/shard_map/ppermute | solution.py:28
  13.9 9.2 %collective-permute-start.8 = (bf16[32,1024]{1,0:T(8,128)(2,1)S(1)}, bf16[32,1024]{1,0:T(8,128)(2,1)S(1)}, u32[]{:S(2)}, u32[]{:S(2)}) collective-permute-start(bf16[32,1024]{1,0:T(8,128)(2,1)S(1)} %get-tuple-element.63), channel_id=1, source_target_pairs={{0,24},{4,28},{8,16},{12,20},{16,8},{20,12},{24,0},{28,4},{1,25},{... | collective-permute-start | bytes 196616 | tf_op jit(solution)/shard_map/ppermute | solution.py:28
  21.4 10.9 %collective-permute-start.2 = (bf16[16,2,8,512]{3,2,1,0:T(8,128)(2,1)}, bf16[16,2,8,512]{3,2,1,0:T(8,128)(2,1)}, u32[]{:S(2)}, u32[]{:S(2)}) collective-permute-start(bf16[16,2,8,512]{3,2,1,0:T(8,128)(2,1)} %slice.58), channel_id=1, source_target_pairs={{0,4},{4,0},{8,12},{12,8},{16,20},{20,16},{24,28},{28,24},{1,5},{5... | collective-permute-start | bytes 786440 | tf_op jit(solution)/shard_map/ppermute | solution.py:28
  21.4 1.7 %copy-start.29 = (bf16[32,1024]{1,0:T(8,128)(2,1)}, bf16[32,1024]{1,0:T(8,128)(2,1)S(1)}, u32[]{:S(2)}) copy-start(bf16[32,1024]{1,0:T(8,128)(2,1)S(1)} %collective-permute-done.6.refs_11_) | copy-start | bytes 196612
  23.7 8.3 %copy-start.28 = (f32[1024,4]{0,1:T(4,128)S(1)}, f32[1024,4]{0,1:T(4,128)}, u32[]{:S(2)}) copy-start(f32[1024,4]{0,1:T(4,128)} %param.16) | copy-start | bytes 49156
  23.7 8.3 %copy-start.10 = (s32[128,2]{0,1:T(2,128)S(1)}, s32[128,2]{0,1:T(2,128)}, u32[]{:S(2)}) copy-start(s32[128,2]{0,1:T(2,128)} %param.22) | copy-start | bytes 3076
  23.7 19.9 %copy-start.7 = (f32[1024]{0:T(1024)S(1)}, f32[1024]{0:T(1024)}, u32[]{:S(2)}) copy-start(f32[1024]{0:T(1024)} %param.17) | copy-start | bytes 12292
  28.5 9.5 %collective-permute-start.9 = (bf16[128,1024]{1,0:T(8,128)(2,1)}, bf16[128,1024]{1,0:T(8,128)(2,1)S(1)}, u32[]{:S(2)}, u32[]{:S(2)}) collective-permute-start(bf16[128,1024]{1,0:T(8,128)(2,1)} %get-tuple-element.65), channel_id=1, source_target_pairs={{0,8},{4,12},{8,0},{12,4},{16,24},{20,28},{24,16},{28,20},{1,9},{5... | collective-permute-start | bytes 786440 | tf_op jit(solution)/shard_map/ppermute | solution.py:28
  29.8 12.0 %collective-permute-start.10 = (bf16[128,1024]{1,0:T(8,128)(2,1)}, bf16[128,1024]{1,0:T(8,128)(2,1)}, u32[]{:S(2)}, u32[]{:S(2)}) collective-permute-start(bf16[128,1024]{1,0:T(8,128)(2,1)} %get-tuple-element.66), channel_id=1, source_target_pairs={{0,16},{4,20},{8,24},{12,28},{16,0},{20,4},{24,8},{28,12},{1,17},{... | collective-permute-start | bytes 786440 | tf_op jit(solution)/shard_map/ppermute | solution.py:28
  30.6 13.0 %collective-permute-start.11 = (bf16[128,1024]{1,0:T(8,128)(2,1)}, bf16[128,1024]{1,0:T(8,128)(2,1)}, u32[]{:S(2)}, u32[]{:S(2)}) collective-permute-start(bf16[128,1024]{1,0:T(8,128)(2,1)} %get-tuple-element.67), channel_id=1, source_target_pairs={{0,24},{4,28},{8,16},{12,20},{16,8},{20,12},{24,0},{28,4},{1,25},{... | collective-permute-start | bytes 786440 | tf_op jit(solution)/shard_map/ppermute | solution.py:28
  32.3 33.1 %copy-start.3 = (bf16[256,128]{1,0:T(8,128)(2,1)}, bf16[256,128]{1,0:T(8,128)(2,1)S(1)}, u32[]{:S(2)}) copy-start(bf16[256,128]{1,0:T(8,128)(2,1)S(1)} %get-tuple-element.54.refs_2_.refs_1_) | copy-start | bytes 196612
  32.3 5.7 %copy-start.15 = (bf16[16,2,8,512]{3,2,1,0:T(8,128)(2,1)}, bf16[16,2,8,512]{3,2,1,0:T(8,128)(2,1)S(1)}, u32[]{:S(2)}) copy-start(bf16[16,2,8,512]{3,2,1,0:T(8,128)(2,1)S(1)} %pad_maximum_fusion.1) | copy-start | bytes 786436
  45.9 18.8 %collective-permute-start.16 = (bf16[320,512]{1,0:T(8,128)(2,1)}, bf16[320,512]{1,0:T(8,128)(2,1)S(1)}, u32[]{:S(2)}, u32[]{:S(2)}) collective-permute-start(bf16[320,512]{1,0:T(8,128)(2,1)} %get-tuple-element.71), channel_id=1, source_target_pairs={{0,8},{4,12},{8,0},{12,4},{16,24},{20,28},{24,16},{28,20},{1,9},{5... | collective-permute-start | bytes 983048 | tf_op jit(solution)/shard_map/ppermute | solution.py:28
  46.5 9.8 %collective-permute-start.14 = (bf16[144,640]{1,0:T(8,128)(2,1)}, bf16[144,640]{1,0:T(8,128)(2,1)S(1)}, u32[]{:S(2)}, u32[]{:S(2)}) collective-permute-start(bf16[144,640]{1,0:T(8,128)(2,1)} %get-tuple-element.68.refs_2_), channel_id=1, source_target_pairs={{0,3},{1,2},{2,1},{3,0},{4,7},{5,6},{6,5},{7,4},{8,11},{9,10},{10,... | collective-permute-start | bytes 552968 | tf_op jit(solution)/shard_map/ppermute | solution.py:28
  50.1 14.6 %collective-permute-start.13 = (bf16[144,640]{1,0:T(8,128)(2,1)}, bf16[144,640]{1,0:T(8,128)(2,1)S(1)}, u32[]{:S(2)}, u32[]{:S(2)}) collective-permute-start(bf16[144,640]{1,0:T(8,128)(2,1)} %get-tuple-element.68.refs_2_), channel_id=1, source_target_pairs={{0,2},{1,3},{2,0},{3,1},{4,6},{5,7},{6,4},{7,5},{8,10},{9,11},{10,... | collective-permute-start | bytes 552968 | tf_op jit(solution)/shard_map/ppermute | solution.py:28
  50.1 14.6 %collective-permute-start.12 = (bf16[144,640]{1,0:T(8,128)(2,1)}, bf16[144,640]{1,0:T(8,128)(2,1)S(1)}, u32[]{:S(2)}, u32[]{:S(2)}) collective-permute-start(bf16[144,640]{1,0:T(8,128)(2,1)} %get-tuple-element.68.refs_2_), channel_id=1, source_target_pairs={{0,1},{1,0},{2,3},{3,2},{4,5},{5,4},{6,7},{7,6},{8,9},{9,8},{10,11... | collective-permute-start | bytes 552968 | tf_op jit(solution)/shard_map/ppermute | solution.py:28
  50.9 1.4 collective-permute-start.15
  52.3 13.1 %copy-start.26 = (bf16[64,384]{1,0:T(8,128)(2,1)}, bf16[64,384]{1,0:T(8,128)(2,1)S(1)}, u32[]{:S(2)}) copy-start(bf16[64,384]{1,0:T(8,128)(2,1)S(1)} %collective-permute-done.15.refs_7_) | copy-start | bytes 147460
  52.3 3.9 %collective-permute-start.17 = (bf16[64,384]{1,0:T(8,128)(2,1)}, bf16[64,384]{1,0:T(8,128)(2,1)S(1)}, u32[]{:S(2)}, u32[]{:S(2)}) collective-permute-start(bf16[64,384]{1,0:T(8,128)(2,1)} %get-tuple-element.72), channel_id=1, source_target_pairs={{0,12},{4,8},{8,4},{12,0},{16,28},{20,24},{24,20},{28,16},{1,13},{... | collective-permute-start | bytes 147464 | tf_op jit(solution)/shard_map/ppermute | solution.py:28
  56.2 9.2 %copy-start.27 = (bf16[64,384]{1,0:T(8,128)(2,1)}, bf16[64,384]{1,0:T(8,128)(2,1)S(1)}, u32[]{:S(2)}) copy-start(bf16[64,384]{1,0:T(8,128)(2,1)S(1)} %collective-permute-done.17.refs_9_) | copy-start | bytes 147460
  56.2 9.2 %copy-start.23 = (bf16[144,640]{1,0:T(8,128)(2,1)}, bf16[144,640]{1,0:T(8,128)(2,1)S(1)}, u32[]{:S(2)}) copy-start(bf16[144,640]{1,0:T(8,128)(2,1)S(1)} %collective-permute-done.14.refs_5_) | copy-start | bytes 552964
  64.7 0.8 copy-start.24
  64.7 0.7 copy-start.25
  64.7 0.8 copy-start.16
  68.1 20.9 %copy-start.6 = (f32[16,128]{1,0:T(8,128)}, f32[16,128]{1,0:T(8,128)S(1)}, u32[]{:S(2)}) copy-start(f32[16,128]{1,0:T(8,128)S(1)} %get-tuple-element.78.refs_12_) | copy-start | bytes 24580
  68.1 8.9 %collective-permute-start.23 = (bf16[256,384]{1,0:T(8,128)(2,1)}, bf16[256,384]{1,0:T(8,128)(2,1)S(1)}, u32[]{:S(2)}, u32[]{:S(2)}) collective-permute-start(bf16[256,384]{1,0:T(8,128)(2,1)} %get-tuple-element.77.refs_5_), channel_id=1, source_target_pairs={{0,3},{1,2},{2,1},{3,0},{4,7},{5,6},{6,5},{7,4},{8,11},{9,10},{10,... | collective-permute-start | bytes 589832 | tf_op jit(solution)/shard_map/ppermute | solution.py:28
  70.6 17.4 %collective-permute-start.18 = (bf16[64,2688]{1,0:T(8,128)(2,1)S(1)}, bf16[64,2688]{1,0:T(8,128)(2,1)S(1)}, u32[]{:S(2)}, u32[]{:S(2)}) collective-permute-start(bf16[64,2688]{1,0:T(8,128)(2,1)S(1)} %get-tuple-element.74), channel_id=1, source_target_pairs={{0,4},{4,0},{8,12},{12,8},{16,20},{20,16},{24,28},{28,24},{1,5},{5... | collective-permute-start | bytes 1032200 | tf_op jit(solution)/shard_map/ppermute | solution.py:28
  70.6 17.4 %collective-permute-start.19 = (bf16[64,2688]{1,0:T(8,128)(2,1)S(1)}, bf16[64,2688]{1,0:T(8,128)(2,1)S(1)}, u32[]{:S(2)}, u32[]{:S(2)}) collective-permute-start(bf16[64,2688]{1,0:T(8,128)(2,1)S(1)} %get-tuple-element.75), channel_id=1, source_target_pairs={{0,8},{4,12},{8,0},{12,4},{16,24},{20,28},{24,16},{28,20},{1,9},{5... | collective-permute-start | bytes 1032200 | tf_op jit(solution)/shard_map/ppermute | solution.py:28
  72.3 15.8 %collective-permute-start.20 = (bf16[64,2688]{1,0:T(8,128)(2,1)S(1)}, bf16[64,2688]{1,0:T(8,128)(2,1)S(1)}, u32[]{:S(2)}, u32[]{:S(2)}) collective-permute-start(bf16[64,2688]{1,0:T(8,128)(2,1)S(1)} %get-tuple-element.76), channel_id=1, source_target_pairs={{0,12},{4,8},{8,4},{12,0},{16,28},{20,24},{24,20},{28,16},{1,13},{... | collective-permute-start | bytes 1032200 | tf_op jit(solution)/shard_map/ppermute | solution.py:28
  72.5 13.8 %collective-permute-start.22 = (bf16[256,384]{1,0:T(8,128)(2,1)}, bf16[256,384]{1,0:T(8,128)(2,1)S(1)}, u32[]{:S(2)}, u32[]{:S(2)}) collective-permute-start(bf16[256,384]{1,0:T(8,128)(2,1)} %get-tuple-element.77.refs_5_), channel_id=1, source_target_pairs={{0,2},{1,3},{2,0},{3,1},{4,6},{5,7},{6,4},{7,5},{8,10},{9,11},{10,... | collective-permute-start | bytes 589832 | tf_op jit(solution)/shard_map/ppermute | solution.py:28
  77.0 12.0 %copy-start.20 = (bf16[256,384]{1,0:T(8,128)(2,1)}, bf16[256,384]{1,0:T(8,128)(2,1)S(1)}, u32[]{:S(2)}) copy-start(bf16[256,384]{1,0:T(8,128)(2,1)S(1)} %collective-permute-done.23.refs_8_) | copy-start | bytes 589828
  77.0 11.0 %collective-permute-start.21 = (bf16[256,384]{1,0:T(8,128)(2,1)}, bf16[256,384]{1,0:T(8,128)(2,1)S(1)}, u32[]{:S(2)}, u32[]{:S(2)}) collective-permute-start(bf16[256,384]{1,0:T(8,128)(2,1)} %get-tuple-element.77.refs_5_), channel_id=1, source_target_pairs={{0,1},{1,0},{2,3},{3,2},{4,5},{5,4},{6,7},{7,6},{8,9},{9,8},{10,11... | collective-permute-start | bytes 589832 | tf_op jit(solution)/shard_map/ppermute | solution.py:28
  86.3 1.8 %copy-start.21 = (bf16[256,384]{1,0:T(8,128)(2,1)}, bf16[256,384]{1,0:T(8,128)(2,1)S(1)}, u32[]{:S(2)}) copy-start(bf16[256,384]{1,0:T(8,128)(2,1)S(1)} %collective-permute-done.22.refs_7_) | copy-start | bytes 589828
  88.0 0.8 copy-start.17
  88.0 0.9 copy-start.18
  88.1 0.9 copy-start.19
  89.0 31.3 %copy-start.14 = (bf16[2,2,8,2,8,512]{5,4,3,2,1,0:T(8,128)(2,1)S(1)}, bf16[2,2,8,2,8,512]{5,4,3,2,1,0:T(8,128)(2,1)}, u32[]{:S(2)}) copy-start(bf16[2,2,8,2,8,512]{5,4,3,2,1,0:T(8,128)(2,1)} %fusion.4.refs_13_) | copy-start | bytes 1572868
  108.6 9.9 %collective-permute-start.24 = (bf16[256,384]{1,0:T(8,128)(2,1)}, bf16[256,384]{1,0:T(8,128)(2,1)S(1)}, u32[]{:S(2)}, u32[]{:S(2)}) collective-permute-start(bf16[256,384]{1,0:T(8,128)(2,1)} %get-tuple-element.83), channel_id=1, source_target_pairs={{0,3},{1,2},{2,1},{3,0},{4,7},{5,6},{6,5},{7,4},{8,11},{9,10},{10,... | collective-permute-start | bytes 589832 | tf_op jit(solution)/shard_map/ppermute | solution.py:28
  109.9 13.0 %collective-permute-start.28 = (bf16[256,384]{1,0:T(8,128)(2,1)}, bf16[256,384]{1,0:T(8,128)(2,1)S(1)}, u32[]{:S(2)}, u32[]{:S(2)}) collective-permute-start(bf16[256,384]{1,0:T(8,128)(2,1)} %get-tuple-element.87), channel_id=1, source_target_pairs={{0,1},{1,0},{2,3},{3,2},{4,5},{5,4},{6,7},{7,6},{8,9},{9,8},{10,11... | collective-permute-start | bytes 589832 | tf_op jit(solution)/shard_map/ppermute | solution.py:28
  110.2 17.9 %collective-permute-start.29 = (bf16[256,384]{1,0:T(8,128)(2,1)}, bf16[256,384]{1,0:T(8,128)(2,1)S(1)}, u32[]{:S(2)}, u32[]{:S(2)}) collective-permute-start(bf16[256,384]{1,0:T(8,128)(2,1)} %get-tuple-element.88), channel_id=1, source_target_pairs={{0,2},{1,3},{2,0},{3,1},{4,6},{5,7},{6,4},{7,5},{8,10},{9,11},{10,... | collective-permute-start | bytes 589832 | tf_op jit(solution)/shard_map/ppermute | solution.py:28
  113.1 15.0 %collective-permute-start.26 = (bf16[64,2560]{1,0:T(8,128)(2,1)}, bf16[64,2560]{1,0:T(8,128)(2,1)S(1)}, u32[]{:S(2)}, u32[]{:S(2)}) collective-permute-start(bf16[64,2560]{1,0:T(8,128)(2,1)} %get-tuple-element.84), channel_id=1, source_target_pairs={{0,8},{4,12},{8,0},{12,4},{16,24},{20,28},{24,16},{28,20},{1,9},{5... | collective-permute-start | bytes 983048 | tf_op jit(solution)/shard_map/ppermute | solution.py:28
  114.8 13.6 %collective-permute-start.27 = (bf16[64,2560]{1,0:T(8,128)(2,1)}, bf16[64,2560]{1,0:T(8,128)(2,1)S(1)}, u32[]{:S(2)}, u32[]{:S(2)}) collective-permute-start(bf16[64,2560]{1,0:T(8,128)(2,1)} %get-tuple-element.85), channel_id=1, source_target_pairs={{0,12},{4,8},{8,4},{12,0},{16,28},{20,24},{24,20},{28,16},{1,13},{... | collective-permute-start | bytes 983048 | tf_op jit(solution)/shard_map/ppermute | solution.py:28
  118.5 1.0 copy-start.2
  120.2 8.2 %collective-permute-start.25 = (bf16[64,2560]{1,0:T(8,128)(2,1)}, bf16[64,2560]{1,0:T(8,128)(2,1)S(1)}, u32[]{:S(2)}, u32[]{:S(2)}) collective-permute-start(bf16[64,2560]{1,0:T(8,128)(2,1)} %shard_map.148), channel_id=1, source_target_pairs={{0,4},{4,0},{8,12},{12,8},{16,20},{20,16},{24,28},{28,24},{1,5},{5... | collective-permute-start | bytes 983048 | tf_op jit(solution)/shard_map/ppermute | solution.py:28
  120.2 16.0 %copy-start.9 = (s32[128,2]{0,1:T(2,128)S(1)}, s32[128,2]{0,1:T(2,128)}, u32[]{:S(2)}) copy-start(s32[128,2]{0,1:T(2,128)} %param.19) | copy-start | bytes 3076
  120.3 16.0 %copy-start.12 = (s32[128]{0:T(128)S(1)}, s32[128]{0:T(128)}, u32[]{:S(2)}) copy-start(s32[128]{0:T(128)} %refs_5_.1) | copy-start | bytes 1540
  122.9 11.6 %collective-permute-start.36 = (bf16[1,2,8,2,8,512]{5,4,3,2,1,0:T(8,128)(2,1)S(1)}, bf16[1,2,8,2,8,512]{5,4,3,2,1,0:T(8,128)(2,1)S(1)}, u32[]{:S(2)}, u32[]{:S(2)}) collective-permute-start(bf16[1,2,8,2,8,512]{5,4,3,2,1,0:T(8,128)(2,1)S(1)} %get-tuple-element.103), channel_id=1, source_target_pairs={{0,16},{4,20},{8,24},{12,28},{16,0},{20,4},{24,8},{28,12},{1,17},{... | collective-permute-start | bytes 786440 | tf_op jit(solution)/shard_map/ppermute | solution.py:28
  129.2 7.0 %collective-permute-start.33 = (bf16[64,384]{1,0:T(8,128)(2,1)S(1)}, bf16[64,384]{1,0:T(8,128)(2,1)S(1)}, u32[]{:S(2)}, u32[]{:S(2)}) collective-permute-start(bf16[64,384]{1,0:T(8,128)(2,1)S(1)} %get-tuple-element.97), channel_id=1, source_target_pairs={{0,4},{4,0},{8,12},{12,8},{16,20},{20,16},{24,28},{28,24},{1,5},{5... | collective-permute-start | bytes 147464 | tf_op jit(solution)/shard_map/ppermute | solution.py:28
  130.1 11.4 %collective-permute-start.30 = (bf16[128,640]{1,0:T(8,128)(2,1)S(1)}, bf16[128,640]{1,0:T(8,128)(2,1)S(1)}, u32[]{:S(2)}, u32[]{:S(2)}) collective-permute-start(bf16[128,640]{1,0:T(8,128)(2,1)S(1)} %get-tuple-element.93), channel_id=1, source_target_pairs={{0,1},{1,0},{2,3},{3,2},{4,5},{5,4},{6,7},{7,6},{8,9},{9,8},{10,11... | collective-permute-start | bytes 491528 | tf_op jit(solution)/shard_map/ppermute | solution.py:28
  130.4 15.0 %collective-permute-start.31 = (bf16[128,640]{1,0:T(8,128)(2,1)S(1)}, bf16[128,640]{1,0:T(8,128)(2,1)S(1)}, u32[]{:S(2)}, u32[]{:S(2)}) collective-permute-start(bf16[128,640]{1,0:T(8,128)(2,1)S(1)} %get-tuple-element.94), channel_id=1, source_target_pairs={{0,2},{1,3},{2,0},{3,1},{4,6},{5,7},{6,4},{7,5},{8,10},{9,11},{10,... | collective-permute-start | bytes 491528 | tf_op jit(solution)/shard_map/ppermute | solution.py:28
  131.6 13.8 %collective-permute-start.32 = (bf16[128,640]{1,0:T(8,128)(2,1)S(1)}, bf16[128,640]{1,0:T(8,128)(2,1)S(1)}, u32[]{:S(2)}, u32[]{:S(2)}) collective-permute-start(bf16[128,640]{1,0:T(8,128)(2,1)S(1)} %get-tuple-element.95), channel_id=1, source_target_pairs={{0,3},{1,2},{2,1},{3,0},{4,7},{5,6},{6,5},{7,4},{8,11},{9,10},{10,... | collective-permute-start | bytes 491528 | tf_op jit(solution)/shard_map/ppermute | solution.py:28
  134.5 7.0 %collective-permute-start.34 = (bf16[64,384]{1,0:T(8,128)(2,1)S(1)}, bf16[64,384]{1,0:T(8,128)(2,1)S(1)}, u32[]{:S(2)}, u32[]{:S(2)}) collective-permute-start(bf16[64,384]{1,0:T(8,128)(2,1)S(1)} %get-tuple-element.98), channel_id=1, source_target_pairs={{0,8},{4,12},{8,0},{12,4},{16,24},{20,28},{24,16},{28,20},{1,9},{5... | collective-permute-start | bytes 147464 | tf_op jit(solution)/shard_map/ppermute | solution.py:28
  136.2 5.3 %collective-permute-start.35 = (bf16[64,384]{1,0:T(8,128)(2,1)S(1)}, bf16[64,384]{1,0:T(8,128)(2,1)S(1)}, u32[]{:S(2)}, u32[]{:S(2)}) collective-permute-start(bf16[64,384]{1,0:T(8,128)(2,1)S(1)} %get-tuple-element.99), channel_id=1, source_target_pairs={{0,12},{4,8},{8,4},{12,0},{16,28},{20,24},{24,20},{28,16},{1,13},{... | collective-permute-start | bytes 147464 | tf_op jit(solution)/shard_map/ppermute | solution.py:28
  136.3 9.2 %copy-start.1 = (f32[128,1024]{1,0:T(8,128)S(1)}, f32[128,1024]{1,0:T(8,128)}, u32[]{:S(2)}) copy-start(f32[128,1024]{1,0:T(8,128)} %get-tuple-element.91.refs_2_) | copy-start | bytes 1572868
  (5 other events, 3.3 us)
